TPU v7x, 32 devices: a whole 2x2x4 slice. The times are simulated.
32 devices in a mesh: band: 4 (over y, core), tile: 8 (over z, x).
Axes of the slice: x: 2, y: 2, z: 4, core: 2. Of those that a mesh axis runs over, the one named last changes fastest.
Arguments:
- cond_x: float32 [8, 512, 2048], P('band', 'tile'), may hold values from 0.2 to 5
- cond_y: float32 [8, 512, 2048], P('band', 'tile'), may hold values from 0.2 to 5
- via_cond: float32 [8, 512, 2048], P('band', 'tile'), may hold values from 0.5 to 8
- via_mask: int32 [8, 512, 2048], P('band', 'tile'), may hold values 0 or 1
- capacitance: float32 [8, 512, 2048], P('band', 'tile'), may hold values from 0.5 to 4
- pad_mask: int32 [8, 512, 2048], P('band', 'tile'), may hold values 0 or 1
- observe: float32 [2, 8, 512, 2048], P(None, 'band', 'tile'), may hold values from -40 to 40
Outputs:
- adjoint: float32 [2, 8, 512, 2048], P(None, 'band', 'tile')
All inputs are finite; a program needn't handle non-finite values. No bound on the sum of `via_mask` or of `pad_mask` on one device may be relied on, other than what follows from the above.
Results may differ from a plain program's by a relative error of at most 0.0003.
Values sent between devices are 32-bit elements; how exact they have to be, the bound alone decides.
No kernel may reach another device: no remote copies, remote signals or barrier semaphores. Data moves between devices by JAX's collectives and lax.ppermute only.
A program may use at most 128 MiB of HBM per device.

v0:
```python
import jax
import jax.numpy as jnp
from jax import lax
from jax.sharding import PartitionSpec as P

NB = 8
STEPS = 2
ITERS = 2


pad_conductance = 4.0


def from_behind(x, axis, by):
    devices = lax.axis_size(axis)
    pairs = [(i, i + by) for i in range(devices) if 0 <= i + by < devices]
    return lax.ppermute(x, axis, pairs)


def with_halo(block, sides, width):
    for axis, dim in sides:
        count = lax.axis_size(axis)
        forward = [(i, i + 1) for i in range(count - 1)]
        backward = [(target, source) for source, target in forward]
        low = lax.ppermute(
            lax.slice_in_dim(block, block.shape[dim] - width, None, axis=dim), axis, forward
        )
        high = lax.ppermute(lax.slice_in_dim(block, 0, width, axis=dim), axis, backward)
        block = jnp.concatenate([low, block, high], axis=dim)
    return block


def apply_operator(padded, rims_coeff, diagonal):
    center = padded[1:-1, 1:-1, 1:-1]
    here = rims_coeff[:, 1:-1, 1:-1, 1:-1]
    total = diagonal * center
    total = (
        total
        + here[0] * (center - padded[1:-1, 2:, 1:-1])
        + rims_coeff[0, 1:-1, :-2, 1:-1] * (center - padded[1:-1, :-2, 1:-1])
    )
    total = (
        total
        + here[1] * (center - padded[1:-1, 1:-1, 2:])
        + rims_coeff[1, 1:-1, 1:-1, :-2] * (center - padded[1:-1, 1:-1, :-2])
    )
    total = (
        total
        + here[2] * (center - padded[2:, 1:-1, 1:-1])
        + rims_coeff[2, :-2, 1:-1, 1:-1] * (center - padded[:-2, 1:-1, 1:-1])
    )
    return total


def jacobi_scale(rims_coeff, diagonal):
    here = rims_coeff[:, 1:-1, 1:-1, 1:-1]
    return (
        diagonal
        + here[0]
        + here[1]
        + here[2]
        + rims_coeff[0, 1:-1, :-2, 1:-1]
        + rims_coeff[1, 1:-1, 1:-1, :-2]
        + rims_coeff[2, :-2, 1:-1, 1:-1]
    )


def assemble_rims(cond_xs, cond_ys, via_gs, x_before, y_before, v_before):
    x_part = jnp.concatenate([x_before, cond_xs, jnp.zeros_like(x_before)], 1)
    x_part = jnp.pad(x_part, ((1, 1), (0, 0), (1, 1)))
    y_part = jnp.concatenate([y_before, cond_ys, jnp.zeros_like(y_before)], 2)
    y_part = jnp.pad(y_part, ((1, 1), (1, 1), (0, 0)))
    v_part = jnp.concatenate([v_before, via_gs, jnp.zeros_like(v_before)], 0)
    v_part = jnp.pad(v_part, ((0, 0), (1, 1), (1, 1)))
    return jnp.stack([x_part, y_part, v_part])


def norm_total(value):
    return lax.psum(value, ("band", "tile"))


def curve_total(value):
    return lax.psum(value, ("band", "tile"))


def solve_two(right_side, start, operator_fn, scale):
    residual = right_side - operator_fn(start)
    search = residual / scale
    norm_now = norm_total(jnp.sum(residual * search))
    answer = start
    for iteration in range(ITERS):
        image_vec = operator_fn(search)
        step_len = norm_now / curve_total(jnp.sum(search * image_vec))
        answer = answer + step_len * search
        residual = residual - step_len * image_vec
        if iteration + 1 < ITERS:
            precond_res = residual / scale
            norm_next = norm_total(jnp.sum(residual * precond_res))
            search = precond_res + norm_next / norm_now * search
            norm_now = norm_next
    return answer


def on_device(cond_x, cond_y, via_cond, via_mask, capacitance, pad_mask, observe):
    local_bands = cond_x.shape[0]
    band_start = lax.axis_index("band") * local_bands
    keep = (band_start + jnp.arange(local_bands) < NB - 1).astype(jnp.float32)[:, None, None]
    via_g = via_cond * via_mask.astype(jnp.float32) * keep
    diagonal = capacitance + pad_conductance * pad_mask.astype(jnp.float32)
    v_before = from_behind(via_g[-1:], "band", 1)
    x_before = from_behind(cond_x[:, -1:, :], "tile", 1)
    y_before = jnp.zeros_like(cond_y[:, :, :1])
    rims_coeff = assemble_rims(cond_x, cond_y, via_g, x_before, y_before, v_before)

    def operator_fn(values):
        padded = jnp.pad(with_halo(values, (("band", 0), ("tile", 1)), 1), ((0, 0), (0, 0), (1, 1)))
        return apply_operator(padded, rims_coeff, diagonal)

    scale = jacobi_scale(rims_coeff, diagonal)
    later = jnp.zeros_like(capacitance)
    results = [later] * STEPS
    for time_step in range(STEPS - 1, -1, -1):
        right_side = capacitance * later + observe[time_step]
        if time_step == STEPS - 1:
            start = right_side / scale
        else:
            start = later
        later = solve_two(right_side, start, operator_fn, scale)
        results[time_step] = later
    adjoint = jnp.stack(results)
    return adjoint


def solution(mesh):
    placed = (
        P("band", "tile", None),
        P("band", "tile", None),
        P("band", "tile", None),
        P("band", "tile", None),
        P("band", "tile", None),
        P("band", "tile", None),
        P(None, "band", "tile", None),
    )
    return jax.shard_map(
        on_device,
        mesh=mesh,
        in_specs=placed,
        out_specs=P(None, "band", "tile", None),
        check_vma=False,
    )
```

profile of v0, /device:TPU:0, one launch (start us, length us, event | category | flops | bytes accessed | tf_op | source)
XLA Modules:
  0.0 448.8 jit_solution(18229549004551273559)
XLA Ops:
  0.0 1.6 slice.338
  1.6 5.4 %collective-permute-start = (f32[2,1,2048]{2,1,0:T(1,128)}, f32[2,1,2048]{2,1,0:T(1,128)}, u32[]{:S(2)}, u32[]{:S(2)}) collective-permute-start(f32[2,1,2048]{2,1,0:T(1,128)} %slice.338), channel_id=1, source_target_pairs={{0,1},{1,2},{2,3},{3,4},{4,5},{5,6},{6,7},{8,9},{9,10},{10,11},{11... | collective-permute-start | bytes 49160 | tf_op jit(solution)/shard_map/ppermute | solution.py:17
  7.0 1.7 multiply_multiply_fusion
  9.6 2.3 collective-permute-start.1
  13.2 1.5 pad_bitcast_fusion.1
  16.2 1.7 maximum_maximum_fusion
  20.1 1.7 fusion.105
  23.3 5.5 %collective-permute-start.2 = (f32[1,64,2048]{2,1,0:T(8,128)S(1)}, f32[1,64,2048]{2,1,0:T(8,128)S(1)}, u32[]{:S(2)}, u32[]{:S(2)}) collective-permute-start(f32[1,64,2048]{2,1,0:T(8,128)S(1)} %get-tuple-element.45), channel_id=1, source_target_pairs={{0,8},{8,16},{16,24},{1,9},{9,17},{17,25},{2,10},{10,18},{18,26},{... | collective-permute-start | bytes 1572872 | tf_op jit(solution)/shard_map/ppermute | solution.py:25
  28.8 1.5 collective-permute-done.2
  30.4 2.9 collective-permute-start.5
  34.8 4.2 collective-permute-done.4
  39.9 2.5 fusion.110
  43.9 8.2 %collective-permute-start.6 = (f32[1,64,2048]{2,1,0:T(8,128)S(1)}, f32[1,64,2048]{2,1,0:T(8,128)S(1)}, u32[]{:S(2)}, u32[]{:S(2)}) collective-permute-start(f32[1,64,2048]{2,1,0:T(8,128)S(1)} %get-tuple-element.43), channel_id=1, source_target_pairs={{0,8},{8,16},{16,24},{1,9},{9,17},{17,25},{2,10},{10,18},{18,26},{... | collective-permute-start | bytes 1572872 | tf_op jit(solution)/shard_map/ppermute | solution.py:25
  52.1 1.5 collective-permute-done.6
  53.6 4.3 collective-permute-start.9
  59.5 4.2 collective-permute-done.8
  64.7 4.0 multiply_reduce_fusion.4
  68.7 49.9 %all-reduce.10 = (f32[]{:T(128)}, f32[]{:T(128)}) all-reduce(f32[]{:T(128)} %get-tuple-element.8, f32[]{:T(128)} %get-tuple-element.7), channel_id=1, replica_groups=mesh['band'=4,'tile'=8] {'band','tile'}, use_global_device_ids=true, to_apply=%region_1.2 | all-reduce | flops 2 | bytes 16 | tf_op jit(solution)/shard_map/psum | solution.py:79
  119.8 2.4 multiply_reduce_fusion.3
  122.2 39.2 %psum.58 = f32[]{:T(128)} all-reduce(f32[]{:T(128)} %multiply_reduce_fusion.3), channel_id=1, replica_groups=mesh['band'=4,'tile'=8] {'band','tile'}, use_global_device_ids=true, to_apply=%region_5.6 | all-reduce | flops 1 | bytes 8 | tf_op jit(solution)/shard_map/psum | solution.py:79
  162.6 2.2 multiply_add_fusion.2
  166.2 3.1 collective-permute-start.10
  169.3 1.5 collective-permute-done.10
  170.8 4.4 collective-permute-start.13
  176.9 4.2 collective-permute-done.12
  182.0 3.1 fusion.56
  185.1 48.1 %psum.59 = f32[]{:T(128)} all-reduce(f32[]{:T(128)} %fusion.56), channel_id=1, replica_groups=mesh['band'=4,'tile'=8] {'band','tile'}, use_global_device_ids=true, to_apply=%region_7.8 | all-reduce | flops 1 | bytes 8 | tf_op jit(solution)/shard_map/psum | solution.py:83
  234.5 2.2 multiply_add_fusion.1
  238.3 3.1 collective-permute-start.14
  242.9 4.4 collective-permute-start.17
  248.9 4.2 collective-permute-done.16
  254.1 2.6 fusion.107
  258.1 5.9 %collective-permute-start.18 = (f32[1,64,2048]{2,1,0:T(8,128)S(1)}, f32[1,64,2048]{2,1,0:T(8,128)S(1)}, u32[]{:S(2)}, u32[]{:S(2)}) collective-permute-start(f32[1,64,2048]{2,1,0:T(8,128)S(1)} %get-tuple-element.37), channel_id=1, source_target_pairs={{0,8},{8,16},{16,24},{1,9},{9,17},{17,25},{2,10},{10,18},{18,26},{... | collective-permute-start | bytes 1572872 | tf_op jit(solution)/shard_map/ppermute | solution.py:25
  265.6 4.5 %collective-permute-start.21 = (f32[4,1,2048]{2,1,0:T(1,128)S(1)}, f32[4,1,2048]{2,1,0:T(1,128)S(1)}, u32[]{:S(2)}, u32[]{:S(2)}) collective-permute-start(f32[4,1,2048]{2,1,0:T(1,128)S(1)} %get-tuple-element.24), channel_id=1, source_target_pairs={{0,1},{1,2},{2,3},{3,4},{4,5},{5,6},{6,7},{8,9},{9,10},{10,11},{11... | collective-permute-start | bytes 98312 | tf_op jit(solution)/shard_map/ppermute | solution.py:25
  271.7 4.2 collective-permute-done.20
  276.8 4.0 multiply_reduce_fusion.1
  280.8 48.4 %all-reduce.9 = (f32[]{:T(128)}, f32[]{:T(128)}) all-reduce(f32[]{:T(128)} %get-tuple-element.6, f32[]{:T(128)} %get-tuple-element.5), channel_id=1, replica_groups=mesh['band'=4,'tile'=8] {'band','tile'}, use_global_device_ids=true, to_apply=%region_9.10 | all-reduce | flops 2 | bytes 16 | tf_op jit(solution)/shard_map/psum | solution.py:79
  330.3 2.4 multiply_reduce_fusion
  332.8 40.8 %psum.62 = f32[]{:T(128)} all-reduce(f32[]{:T(128)} %multiply_reduce_fusion), channel_id=1, replica_groups=mesh['band'=4,'tile'=8] {'band','tile'}, use_global_device_ids=true, to_apply=%region_13.14 | all-reduce | flops 1 | bytes 8 | tf_op jit(solution)/shard_map/psum | solution.py:79
  374.8 2.2 multiply_add_fusion
  378.4 3.1 collective-permute-start.22
  381.4 1.5 collective-permute-done.22
  383.0 4.4 collective-permute-start.25
  387.4 1.5 collective-permute-start.24
  389.0 4.2 collective-permute-done.24
  394.2 3.1 fusion.5
  397.3 47.1 %psum.63 = f32[]{:T(128)} all-reduce(f32[]{:T(128)} %fusion.5), channel_id=1, replica_groups=mesh['band'=4,'tile'=8] {'band','tile'}, use_global_device_ids=true, to_apply=%region_15.16 | all-reduce | flops 1 | bytes 8 | tf_op jit(solution)/shard_map/psum | solution.py:83
  445.6 1.8 add_bitcast_fusion
  (111 shorter events, 32.1 us)
Async XLA Ops:
  0.0 11.9 %copy-start.27 = (f32[2,64,2048]{2,1,0:T(8,128)S(1)}, f32[2,64,2048]{2,1,0:T(8,128)}, u32[]{:S(2)}) copy-start(f32[2,64,2048]{2,1,0:T(8,128)} %param.8) | copy-start | bytes 3145732
  1.6 13.3 %collective-permute-start = (f32[2,1,2048]{2,1,0:T(1,128)}, f32[2,1,2048]{2,1,0:T(1,128)}, u32[]{:S(2)}, u32[]{:S(2)}) collective-permute-start(f32[2,1,2048]{2,1,0:T(1,128)} %slice.338), channel_id=1, source_target_pairs={{0,1},{1,2},{2,3},{3,4},{4,5},{5,6},{6,7},{8,9},{9,10},{10,11},{11... | collective-permute-start | bytes 49160 | tf_op jit(solution)/shard_map/ppermute | solution.py:17
  9.6 6.6 %collective-permute-start.1 = (f32[1,64,2048]{2,1,0:T(8,128)}, f32[1,64,2048]{2,1,0:T(8,128)}, u32[]{:S(2)}, u32[]{:S(2)}) collective-permute-start(f32[1,64,2048]{2,1,0:T(8,128)} %slice.409), channel_id=1, source_target_pairs={{0,8},{8,16},{16,24},{1,9},{9,17},{17,25},{2,10},{10,18},{18,26},{... | collective-permute-start | bytes 1572872 | tf_op jit(solution)/shard_map/ppermute | solution.py:17
  16.2 48.4 %copy-start = (f32[1,4,66,2050]{3,2,1,0:T(8,128)}, f32[1,4,66,2050]{3,2,1,0:T(8,128)S(1)}, u32[]{:S(2)}) copy-start(f32[1,4,66,2050]{3,2,1,0:T(8,128)S(1)} %pad_bitcast_fusion.2) | copy-start | bytes 6494404
  20.1 44.5 %copy-start.4 = (f32[1,4,66,2050]{3,2,1,0:T(8,128)}, f32[1,4,66,2050]{3,2,1,0:T(8,128)S(1)}, u32[]{:S(2)}) copy-start(f32[1,4,66,2050]{3,2,1,0:T(8,128)S(1)} %pad_bitcast_fusion) | copy-start | bytes 6494404
  21.9 18.1 %copy-start.16 = (f32[2,64,2048]{2,1,0:T(8,128)}, f32[2,64,2048]{2,1,0:T(8,128)S(1)}, u32[]{:S(2)}) copy-start(f32[2,64,2048]{2,1,0:T(8,128)S(1)} %get-tuple-element.19) | copy-start | bytes 3145732
  21.9 42.8 %copy-start.10 = (f32[2,64,2048]{2,1,0:T(8,128)}, f32[2,64,2048]{2,1,0:T(8,128)S(1)}, u32[]{:S(2)}) copy-start(f32[2,64,2048]{2,1,0:T(8,128)S(1)} %get-tuple-element.21) | copy-start | bytes 3145732
  22.0 6.8 %collective-permute-start.3 = (f32[1,64,2048]{2,1,0:T(8,128)S(1)}, f32[1,64,2048]{2,1,0:T(8,128)S(1)}, u32[]{:S(2)}, u32[]{:S(2)}) collective-permute-start(f32[1,64,2048]{2,1,0:T(8,128)S(1)} %get-tuple-element.44), channel_id=1, source_target_pairs={{8,0},{16,8},{24,16},{9,1},{17,9},{25,17},{10,2},{18,10},{26,18},{... | collective-permute-start | bytes 1572872 | tf_op jit(solution)/shard_map/ppermute | solution.py:28
  23.3 7.0 %collective-permute-start.2 = (f32[1,64,2048]{2,1,0:T(8,128)S(1)}, f32[1,64,2048]{2,1,0:T(8,128)S(1)}, u32[]{:S(2)}, u32[]{:S(2)}) collective-permute-start(f32[1,64,2048]{2,1,0:T(8,128)S(1)} %get-tuple-element.45), channel_id=1, source_target_pairs={{0,8},{8,16},{16,24},{1,9},{9,17},{17,25},{2,10},{10,18},{18,26},{... | collective-permute-start | bytes 1572872 | tf_op jit(solution)/shard_map/ppermute | solution.py:25
  30.4 4.5 collective-permute-start.5
  33.3 5.8 %collective-permute-start.4 = (f32[4,1,2048]{2,1,0:T(1,128)S(1)}, f32[4,1,2048]{2,1,0:T(1,128)S(1)}, u32[]{:S(2)}, u32[]{:S(2)}) collective-permute-start(f32[4,1,2048]{2,1,0:T(1,128)S(1)} %get-tuple-element.33), channel_id=1, source_target_pairs={{1,0},{2,1},{3,2},{4,3},{5,4},{6,5},{7,6},{9,8},{10,9},{11,10},{12... | collective-permute-start | bytes 98312 | tf_op jit(solution)/shard_map/ppermute | solution.py:28
  42.5 22.2 %copy-start.15 = (f32[2,64,2048]{2,1,0:T(8,128)}, f32[2,64,2048]{2,1,0:T(8,128)S(1)}, u32[]{:S(2)}) copy-start(f32[2,64,2048]{2,1,0:T(8,128)S(1)} %get-tuple-element.17) | copy-start | bytes 3145732
  42.5 22.2 %copy-start.20 = (f32[2,64,2048]{2,1,0:T(8,128)}, f32[2,64,2048]{2,1,0:T(8,128)S(1)}, u32[]{:S(2)}) copy-start(f32[2,64,2048]{2,1,0:T(8,128)S(1)} %get-tuple-element.18) | copy-start | bytes 3145732
  42.6 9.5 %collective-permute-start.7 = (f32[1,64,2048]{2,1,0:T(8,128)S(1)}, f32[1,64,2048]{2,1,0:T(8,128)S(1)}, u32[]{:S(2)}, u32[]{:S(2)}) collective-permute-start(f32[1,64,2048]{2,1,0:T(8,128)S(1)} %get-tuple-element.42), channel_id=1, source_target_pairs={{8,0},{16,8},{24,16},{9,1},{17,9},{25,17},{10,2},{18,10},{26,18},{... | collective-permute-start | bytes 1572872 | tf_op jit(solution)/shard_map/ppermute | solution.py:28
  43.9 9.7 %collective-permute-start.6 = (f32[1,64,2048]{2,1,0:T(8,128)S(1)}, f32[1,64,2048]{2,1,0:T(8,128)S(1)}, u32[]{:S(2)}, u32[]{:S(2)}) collective-permute-start(f32[1,64,2048]{2,1,0:T(8,128)S(1)} %get-tuple-element.43), channel_id=1, source_target_pairs={{0,8},{8,16},{16,24},{1,9},{9,17},{17,25},{2,10},{10,18},{18,26},{... | collective-permute-start | bytes 1572872 | tf_op jit(solution)/shard_map/ppermute | solution.py:25
  53.6 5.9 %collective-permute-start.9 = (f32[4,1,2048]{2,1,0:T(1,128)S(1)}, f32[4,1,2048]{2,1,0:T(1,128)S(1)}, u32[]{:S(2)}, u32[]{:S(2)}) collective-permute-start(f32[4,1,2048]{2,1,0:T(1,128)S(1)} %get-tuple-element.30), channel_id=1, source_target_pairs={{0,1},{1,2},{2,3},{3,4},{4,5},{5,6},{6,7},{8,9},{9,10},{10,11},{11... | collective-permute-start | bytes 98312 | tf_op jit(solution)/shard_map/ppermute | solution.py:25
  57.9 5.8 %collective-permute-start.8 = (f32[4,1,2048]{2,1,0:T(1,128)S(1)}, f32[4,1,2048]{2,1,0:T(1,128)S(1)}, u32[]{:S(2)}, u32[]{:S(2)}) collective-permute-start(f32[4,1,2048]{2,1,0:T(1,128)S(1)} %get-tuple-element.31), channel_id=1, source_target_pairs={{1,0},{2,1},{3,2},{4,3},{5,4},{6,5},{7,6},{9,8},{10,9},{11,10},{12... | collective-permute-start | bytes 98312 | tf_op jit(solution)/shard_map/ppermute | solution.py:28
  164.8 17.2 %copy-start.18 = (f32[2,64,2048]{2,1,0:T(8,128)}, f32[2,64,2048]{2,1,0:T(8,128)S(1)}, u32[]{:S(2)}) copy-start(f32[2,64,2048]{2,1,0:T(8,128)S(1)} %multiply_add_fusion.2) | copy-start | bytes 3145732
  164.9 4.4 collective-permute-start.11
  166.2 4.6 %collective-permute-start.10 = (f32[1,64,2048]{2,1,0:T(8,128)S(1)}, f32[1,64,2048]{2,1,0:T(8,128)S(1)}, u32[]{:S(2)}, u32[]{:S(2)}) collective-permute-start(f32[1,64,2048]{2,1,0:T(8,128)S(1)} %get-tuple-element.41), channel_id=1, source_target_pairs={{0,8},{8,16},{16,24},{1,9},{9,17},{17,25},{2,10},{10,18},{18,26},{... | collective-permute-start | bytes 1572872 | tf_op jit(solution)/shard_map/ppermute | solution.py:25
  170.8 11.2 %copy-start.5 = (f32[1,4,66,2050]{3,2,1,0:T(8,128)S(1)}, f32[1,4,66,2050]{3,2,1,0:T(8,128)}, u32[]{:S(2)}) copy-start(f32[1,4,66,2050]{3,2,1,0:T(8,128)} %copy-done.4) | copy-start | bytes 6494404
  170.8 11.2 %copy-start.1 = (f32[1,4,66,2050]{3,2,1,0:T(8,128)S(1)}, f32[1,4,66,2050]{3,2,1,0:T(8,128)}, u32[]{:S(2)}) copy-start(f32[1,4,66,2050]{3,2,1,0:T(8,128)} %copy-done) | copy-start | bytes 6494404
  170.8 11.2 %copy-start.11 = (f32[2,64,2048]{2,1,0:T(8,128)S(1)}, f32[2,64,2048]{2,1,0:T(8,128)}, u32[]{:S(2)}) copy-start(f32[2,64,2048]{2,1,0:T(8,128)} %copy-done.10) | copy-start | bytes 3145732
  170.8 6.0 %collective-permute-start.13 = (f32[4,1,2048]{2,1,0:T(1,128)S(1)}, f32[4,1,2048]{2,1,0:T(1,128)S(1)}, u32[]{:S(2)}, u32[]{:S(2)}) collective-permute-start(f32[4,1,2048]{2,1,0:T(1,128)S(1)} %get-tuple-element.28), channel_id=1, source_target_pairs={{0,1},{1,2},{2,3},{3,4},{4,5},{5,6},{6,7},{8,9},{9,10},{10,11},{11... | collective-permute-start | bytes 98312 | tf_op jit(solution)/shard_map/ppermute | solution.py:25
  175.3 5.8 %collective-permute-start.12 = (f32[4,1,2048]{2,1,0:T(1,128)S(1)}, f32[4,1,2048]{2,1,0:T(1,128)S(1)}, u32[]{:S(2)}, u32[]{:S(2)}) collective-permute-start(f32[4,1,2048]{2,1,0:T(1,128)S(1)} %get-tuple-element.29), channel_id=1, source_target_pairs={{1,0},{2,1},{3,2},{4,3},{5,4},{6,5},{7,6},{9,8},{10,9},{11,10},{12... | collective-permute-start | bytes 98312 | tf_op jit(solution)/shard_map/ppermute | solution.py:28
  234.5 19.6 %copy-start.24 = (f32[2,2,64,2048]{3,2,1,0:T(8,128)S(1)}, f32[2,2,64,2048]{3,2,1,0:T(8,128)}, u32[]{:S(2)}) copy-start(f32[2,2,64,2048]{3,2,1,0:T(8,128)} %param.13) | copy-start | bytes 6291460
  236.7 17.3 %copy-start.8 = (f32[2,64,2048]{2,1,0:T(8,128)}, f32[2,64,2048]{2,1,0:T(8,128)S(1)}, u32[]{:S(2)}) copy-start(f32[2,64,2048]{2,1,0:T(8,128)S(1)} %multiply_add_fusion.1) | copy-start | bytes 3145732
  236.7 17.3 %copy-start.22 = (f32[2,64,2048]{2,1,0:T(8,128)S(1)}, f32[2,64,2048]{2,1,0:T(8,128)}, u32[]{:S(2)}) copy-start(f32[2,64,2048]{2,1,0:T(8,128)} %param.11) | copy-start | bytes 3145732
  236.8 4.5 %collective-permute-start.15 = (f32[1,64,2048]{2,1,0:T(8,128)S(1)}, f32[1,64,2048]{2,1,0:T(8,128)S(1)}, u32[]{:S(2)}, u32[]{:S(2)}) collective-permute-start(f32[1,64,2048]{2,1,0:T(8,128)S(1)} %get-tuple-element.38), channel_id=1, source_target_pairs={{8,0},{16,8},{24,16},{9,1},{17,9},{25,17},{10,2},{18,10},{26,18},{... | collective-permute-start | bytes 1572872 | tf_op jit(solution)/shard_map/ppermute | solution.py:28
  238.3 4.6 %collective-permute-start.14 = (f32[1,64,2048]{2,1,0:T(8,128)S(1)}, f32[1,64,2048]{2,1,0:T(8,128)S(1)}, u32[]{:S(2)}, u32[]{:S(2)}) collective-permute-start(f32[1,64,2048]{2,1,0:T(8,128)S(1)} %get-tuple-element.39), channel_id=1, source_target_pairs={{0,8},{8,16},{16,24},{1,9},{9,17},{17,25},{2,10},{10,18},{18,26},{... | collective-permute-start | bytes 1572872 | tf_op jit(solution)/shard_map/ppermute | solution.py:25
  242.8 11.2 %copy-start.6 = (f32[1,4,66,2050]{3,2,1,0:T(8,128)S(1)}, f32[1,4,66,2050]{3,2,1,0:T(8,128)}, u32[]{:S(2)}) copy-start(f32[1,4,66,2050]{3,2,1,0:T(8,128)} %copy-done.4) | copy-start | bytes 6494404
  242.9 11.2 %copy-start.2 = (f32[1,4,66,2050]{3,2,1,0:T(8,128)S(1)}, f32[1,4,66,2050]{3,2,1,0:T(8,128)}, u32[]{:S(2)}) copy-start(f32[1,4,66,2050]{3,2,1,0:T(8,128)} %copy-done) | copy-start | bytes 6494404
  242.9 11.2 %copy-start.12 = (f32[2,64,2048]{2,1,0:T(8,128)S(1)}, f32[2,64,2048]{2,1,0:T(8,128)}, u32[]{:S(2)}) copy-start(f32[2,64,2048]{2,1,0:T(8,128)} %copy-done.10) | copy-start | bytes 3145732
  242.9 6.0 %collective-permute-start.17 = (f32[4,1,2048]{2,1,0:T(1,128)S(1)}, f32[4,1,2048]{2,1,0:T(1,128)S(1)}, u32[]{:S(2)}, u32[]{:S(2)}) collective-permute-start(f32[4,1,2048]{2,1,0:T(1,128)S(1)} %get-tuple-element.26), channel_id=1, source_target_pairs={{0,1},{1,2},{2,3},{3,4},{4,5},{5,6},{6,7},{8,9},{9,10},{10,11},{11... | collective-permute-start | bytes 98312 | tf_op jit(solution)/shard_map/ppermute | solution.py:25
  247.4 5.8 %collective-permute-start.16 = (f32[4,1,2048]{2,1,0:T(1,128)S(1)}, f32[4,1,2048]{2,1,0:T(1,128)S(1)}, u32[]{:S(2)}, u32[]{:S(2)}) collective-permute-start(f32[4,1,2048]{2,1,0:T(1,128)S(1)} %get-tuple-element.27), channel_id=1, source_target_pairs={{1,0},{2,1},{3,2},{4,3},{5,4},{6,5},{7,6},{9,8},{10,9},{11,10},{12... | collective-permute-start | bytes 98312 | tf_op jit(solution)/shard_map/ppermute | solution.py:28
  256.7 20.1 %copy-start.14 = (f32[2,64,2048]{2,1,0:T(8,128)}, f32[2,64,2048]{2,1,0:T(8,128)S(1)}, u32[]{:S(2)}) copy-start(f32[2,64,2048]{2,1,0:T(8,128)S(1)} %get-tuple-element.14) | copy-start | bytes 3145732
  256.7 20.1 %copy-start.19 = (f32[2,64,2048]{2,1,0:T(8,128)}, f32[2,64,2048]{2,1,0:T(8,128)S(1)}, u32[]{:S(2)}) copy-start(f32[2,64,2048]{2,1,0:T(8,128)S(1)} %get-tuple-element.15) | copy-start | bytes 3145732
  256.8 7.2 %collective-permute-start.19 = (f32[1,64,2048]{2,1,0:T(8,128)S(1)}, f32[1,64,2048]{2,1,0:T(8,128)S(1)}, u32[]{:S(2)}, u32[]{:S(2)}) collective-permute-start(f32[1,64,2048]{2,1,0:T(8,128)S(1)} %get-tuple-element.36), channel_id=1, source_target_pairs={{8,0},{16,8},{24,16},{9,1},{17,9},{25,17},{10,2},{18,10},{26,18},{... | collective-permute-start | bytes 1572872 | tf_op jit(solution)/shard_map/ppermute | solution.py:28
  258.1 7.4 %collective-permute-start.18 = (f32[1,64,2048]{2,1,0:T(8,128)S(1)}, f32[1,64,2048]{2,1,0:T(8,128)S(1)}, u32[]{:S(2)}, u32[]{:S(2)}) collective-permute-start(f32[1,64,2048]{2,1,0:T(8,128)S(1)} %get-tuple-element.37), channel_id=1, source_target_pairs={{0,8},{8,16},{16,24},{1,9},{9,17},{17,25},{2,10},{10,18},{18,26},{... | collective-permute-start | bytes 1572872 | tf_op jit(solution)/shard_map/ppermute | solution.py:25
  265.6 6.1 %collective-permute-start.21 = (f32[4,1,2048]{2,1,0:T(1,128)S(1)}, f32[4,1,2048]{2,1,0:T(1,128)S(1)}, u32[]{:S(2)}, u32[]{:S(2)}) collective-permute-start(f32[4,1,2048]{2,1,0:T(1,128)S(1)} %get-tuple-element.24), channel_id=1, source_target_pairs={{0,1},{1,2},{2,3},{3,4},{4,5},{5,6},{6,7},{8,9},{9,10},{10,11},{11... | collective-permute-start | bytes 98312 | tf_op jit(solution)/shard_map/ppermute | solution.py:25
  270.1 5.8 %collective-permute-start.20 = (f32[4,1,2048]{2,1,0:T(1,128)S(1)}, f32[4,1,2048]{2,1,0:T(1,128)S(1)}, u32[]{:S(2)}, u32[]{:S(2)}) collective-permute-start(f32[4,1,2048]{2,1,0:T(1,128)S(1)} %get-tuple-element.25), channel_id=1, source_target_pairs={{1,0},{2,1},{3,2},{4,3},{5,4},{6,5},{7,6},{9,8},{10,9},{11,10},{12... | collective-permute-start | bytes 98312 | tf_op jit(solution)/shard_map/ppermute | solution.py:28
  376.9 17.2 %copy-start.17 = (f32[2,64,2048]{2,1,0:T(8,128)}, f32[2,64,2048]{2,1,0:T(8,128)S(1)}, u32[]{:S(2)}) copy-start(f32[2,64,2048]{2,1,0:T(8,128)S(1)} %multiply_add_fusion) | copy-start | bytes 3145732
  377.1 4.4 collective-permute-start.23
  378.4 4.6 %collective-permute-start.22 = (f32[1,64,2048]{2,1,0:T(8,128)S(1)}, f32[1,64,2048]{2,1,0:T(8,128)S(1)}, u32[]{:S(2)}, u32[]{:S(2)}) collective-permute-start(f32[1,64,2048]{2,1,0:T(8,128)S(1)} %get-tuple-element.35), channel_id=1, source_target_pairs={{0,8},{8,16},{16,24},{1,9},{9,17},{17,25},{2,10},{10,18},{18,26},{... | collective-permute-start | bytes 1572872 | tf_op jit(solution)/shard_map/ppermute | solution.py:25
  382.9 11.2 %copy-start.7 = (f32[1,4,66,2050]{3,2,1,0:T(8,128)S(1)}, f32[1,4,66,2050]{3,2,1,0:T(8,128)}, u32[]{:S(2)}) copy-start(f32[1,4,66,2050]{3,2,1,0:T(8,128)} %copy-done.4) | copy-start | bytes 6494404
  383.0 6.0 %collective-permute-start.25 = (f32[4,1,2048]{2,1,0:T(1,128)S(1)}, f32[4,1,2048]{2,1,0:T(1,128)S(1)}, u32[]{:S(2)}, u32[]{:S(2)}) collective-permute-start(f32[4,1,2048]{2,1,0:T(1,128)S(1)} %get-tuple-element.22), channel_id=1, source_target_pairs={{0,1},{1,2},{2,3},{3,4},{4,5},{5,6},{6,7},{8,9},{9,10},{10,11},{11... | collective-permute-start | bytes 98312 | tf_op jit(solution)/shard_map/ppermute | solution.py:25
  387.4 5.8 %collective-permute-start.24 = (f32[4,1,2048]{2,1,0:T(1,128)S(1)}, f32[4,1,2048]{2,1,0:T(1,128)S(1)}, u32[]{:S(2)}, u32[]{:S(2)}) collective-permute-start(f32[4,1,2048]{2,1,0:T(1,128)S(1)} %get-tuple-element.23), channel_id=1, source_target_pairs={{1,0},{2,1},{3,2},{4,3},{5,4},{6,5},{7,6},{9,8},{10,9},{11,10},{12... | collective-permute-start | bytes 98312 | tf_op jit(solution)/shard_map/ppermute | solution.py:28
  394.1 51.5 %copy-start.9 = (f32[2,64,2048]{2,1,0:T(8,128)S(1)}, f32[2,64,2048]{2,1,0:T(8,128)}, u32[]{:S(2)}) copy-start(f32[2,64,2048]{2,1,0:T(8,128)} %copy-done.8) | copy-start | bytes 3145732
  (6 other events, 29.3 us)
where the time goes:
time: 451 us; the launch traced here: 449 us
  blocking collectives  273 us (61%)
  starting transfers between devices  77.4 us (17%)
  other arithmetic  45.5 us (10%)
  waiting for transfers between devices  35.7 us (8%)
  local copies, waits for them, and re-layouts  8.64 us (2%)
  between operations  8.09 us (2%)
    psum x4, blocking collectives, norm_total(): return lax.psum(value, ('band', 'tile'))  178 us
    psum x2, blocking collectives, curve_total(): return lax.psum(value, ('band', 'tile'))  95.2 us
    ppermute x12, starting transfers between devices, with_halo(): lax.ppermute(lax.slice_in_dim(block, block.shape[dim] - width, None, axis...  53.9 us
    ppermute x12, waiting for transfers between devices, with_halo(): lax.ppermute(lax.slice_in_dim(block, 0, width, axis=dim), axis, backward)  25.4 us
    ppermute x12, starting transfers between devices, with_halo(): lax.ppermute(lax.slice_in_dim(block, 0, width, axis=dim), axis, backward)  15.9 us
    reduce_sum x4, other arithmetic, solve_two(): step_len = norm_now / curve_total(jnp.sum(search * image_vec))  14.2 us
    ppermute x12, waiting for transfers between devices, with_halo(): lax.ppermute(lax.slice_in_dim(block, block.shape[dim] - width, None, axis...  10.3 us
  transfers between devices with their start and end apart: 26, of which 18 were waited for; matrix products, arithmetic and copies ran while one was open for 2% of the time, Pallas kernels for 0%

commit v1 on v0

v1 whole, which is shorter than its diff:
```python
import jax
import jax.numpy as jnp
from jax import lax
from jax.experimental import pallas as pl
from jax.experimental.pallas import tpu as pltpu
from jax.sharding import PartitionSpec as P

NB = 8
ROWS = 8
AXES = ("band", "tile")
F32 = jnp.float32

pad_conductance = 4.0


def sizes():
    return lax.axis_size("band"), lax.axis_size("tile")


def joint_permute(x, partner):
    nb, nt = sizes()
    pairs = []
    for b in range(nb):
        for t in range(nt):
            pb, pt = partner(b, t)
            pairs.append((b * nt + t, pb * nt + pt))
    return lax.ppermute(x, AXES, pairs)


def core_swap(x):
    nb, _ = sizes()
    return lax.ppermute(x, "band", [(b, b ^ 1) for b in range(nb)])


def outer_swap(x):
    nb, nt = sizes()

    def partner(b, t):
        if b in (0, nb - 1):
            return b, t ^ 2
        return (b + 1 if b % 2 else b - 1), t

    return joint_permute(x, partner)


def even_swap(x):
    _, nt = sizes()
    return lax.ppermute(x, "tile", [(t, t ^ 1) for t in range(nt)])


def odd_swap(x):
    nb, nt = sizes()

    def partner(b, t):
        if t in (0, nt - 1):
            return b ^ 1, t
        return b, (t + 1 if t % 2 else t - 1)

    return joint_permute(x, partner)


def all_total(parts):
    return lax.all_to_all(parts, AXES, 0, 0, tiled=True)


def call(body, outs, *args, name):
    vmem = pl.BlockSpec(memory_space=pltpu.VMEM)
    moved = sum(a.size for a in args) + sum(o.size for o in outs)
    return pl.pallas_call(
        body,
        out_shape=outs,
        in_specs=[vmem] * len(args),
        out_specs=[vmem] * len(outs),
        name=name,
        cost_estimate=pl.CostEstimate(flops=moved * 4, bytes_accessed=moved, transcendentals=0),
        compiler_params=pltpu.CompilerParams(vmem_limit_bytes=40 * 1024 * 1024),
    )(*args)


def shape(*dims):
    return jax.ShapeDtypeStruct(dims, F32)


def inner_at():
    return 1 - lax.rem(lax.axis_index("band"), 2)


def tile_is_odd():
    return lax.rem(lax.axis_index("tile"), 2) == 1


def put_rows(first, last, even_ref, odd_ref):
    odd = tile_is_odd()
    even_ref[...] = jnp.where(odd, first, last)
    odd_ref[...] = jnp.where(odd, last, first)


def take_rows(even_ref, odd_ref):
    odd = tile_is_odd()
    tile = lax.axis_index("tile")
    even, other = even_ref[...], odd_ref[...]
    above = jnp.where(tile == 0, 0.0, jnp.where(odd, even, other))
    below = jnp.where(tile == lax.axis_size("tile") - 1, 0.0, jnp.where(odd, other, even))
    return above, below


def row_at(width, at):
    return lax.broadcasted_iota(jnp.int32, (ROWS, width), 0) == at


def fold(total):
    width = total.shape[1]
    acc = total[:, :128]
    for at in range(128, width, 128):
        acc = acc + total[:, at : at + 128]
    return acc


def in_band(v_ref, cond_x_ref, at, cond_y, carried, below, k, chunks):
    width = v_ref.shape[-1]
    r = k * ROWS
    x = v_ref[r : r + ROWS, :]
    cx = cond_x_ref[at, r : r + ROWS, :]
    cy = cond_y[r : r + ROWS, :]
    after = below if k == chunks - 1 else v_ref[r + ROWS : r + ROWS + 1, :]
    down = jnp.where(row_at(width, ROWS - 1), after, pltpu.roll(x, ROWS - 1, 0))
    flux = cx * x
    up = jnp.where(row_at(width, 0), carried, pltpu.roll(flux, 1, 0))
    total = cx * down + up + cy * pltpu.roll(x, width - 1, 1) + pltpu.roll(cy * x, 1, 1)
    return x, total, flux[ROWS - 1 :, :]


def first_kernel(via_ref, mask_ref, cond_x_ref, link_ref, even_ref, odd_ref):
    local = via_ref.shape[0]
    top = lax.axis_index("band") * local + local - 1
    keep = jnp.where(top < NB - 1, 1.0, 0.0)
    link_ref[...] = via_ref[local - 1] * (mask_ref[local - 1].astype(F32) * keep)
    i = inner_at()
    rows = cond_x_ref.shape[1]
    last = jnp.concatenate([cond_x_ref[i, rows - 1 :, :], cond_x_ref[1 - i, rows - 1 :, :]], 0)
    put_rows(last, last, even_ref, odd_ref)


def prepare_kernel(
    cond_x_ref, cond_y_ref, via_ref, mask_ref, cap_ref, pad_ref, observe_ref, link_ref, near_ref, far_ref, even_ref, odd_ref,
    cy_ref, c_io_ref, c_in_ref, c_out_ref, diag_ref, inv_ref, s_i_ref, s_o_ref, edge_ref, s_even_ref, s_odd_ref,
):
    rows, width = s_i_ref.shape
    chunks = rows // ROWS
    i = inner_at()
    band = lax.axis_index("band")
    above, _ = take_rows(even_ref, odd_ref)
    edge_ref[...] = above
    lane = lax.broadcasted_iota(jnp.int32, (ROWS, width), 1)
    has_outer = jnp.where(jnp.logical_and(i == 1, band == 0), 0.0, 1.0)
    firsts, lasts = [], []
    carried = [above[0:1], above[1:2]]
    for k in range(chunks):
        rs = slice(k * ROWS, (k + 1) * ROWS)
        c_io = via_ref[0, rs, :] * mask_ref[0, rs, :].astype(F32)
        link = link_ref[rs, :]
        c_in = jnp.where(i == 1, link, near_ref[rs, :])
        c_out = jnp.where(i == 1, far_ref[rs, :] * has_outer, link)
        c_io_ref[rs, :] = c_io
        c_in_ref[rs, :] = c_in
        c_out_ref[rs, :] = c_out
        for side, at, to, out in ((0, i, c_in, s_i_ref), (1, 1 - i, c_out, s_o_ref)):
            cx = cond_x_ref[at, rs, :]
            cy = cond_y_ref[at, rs, :]
            cut = jnp.where(lane == width - 1, 0.0, cy)
            cy_ref[side, rs, :] = cut
            cx_up = jnp.where(row_at(width, 0), carried[side], pltpu.roll(cx, 1, 0))
            carried[side] = cx[ROWS - 1 :, :]
            diag = cap_ref[at, rs, :] + pad_conductance * pad_ref[at, rs, :].astype(F32)
            diag = diag + cx + cy + c_io + to + cx_up + pltpu.roll(cut, 1, 1)
            inv = 1.0 / diag
            diag_ref[side, rs, :] = diag
            inv_ref[side, rs, :] = inv
            s = observe_ref[0, at, rs, :] * inv
            out[rs, :] = s
            if k == 0:
                firsts.append(s[:1])
            if k == chunks - 1:
                lasts.append(s[ROWS - 1 :])
    put_rows(jnp.concatenate(firsts, 0), jnp.concatenate(lasts, 0), s_even_ref, s_odd_ref)


def spread_kernel(
    n_sums, u_i_ref, u_o_ref, near_ref, even_ref, odd_ref, cond_x_ref, cy_ref, c_io_ref, c_in_ref, inv_ref, edge_ref,
    v_i_ref, part_ref, sums_ref,
):
    rows, width = u_i_ref.shape
    chunks = rows // ROWS
    i = inner_at()
    above, below = take_rows(even_ref, odd_ref)
    flux = above * edge_ref[...]
    carry_i, carry_o = flux[0:1], flux[1:2]
    sums = [jnp.zeros((ROWS, width), F32) for _ in range(2)]
    for k in range(chunks):
        rs = slice(k * ROWS, (k + 1) * ROWS)
        x_i, part_i, carry_i = in_band(u_i_ref, cond_x_ref, i, cy_ref[0], carry_i, below[0:1], k, chunks)
        x_o, part_o, carry_o = in_band(u_o_ref, cond_x_ref, 1 - i, cy_ref[1], carry_o, below[1:2], k, chunks)
        c_io = c_io_ref[rs, :]
        part_i = part_i + c_io * x_o + c_in_ref[rs, :] * near_ref[rs, :]
        part_ref[rs, :] = part_o + c_io * x_i
        v_i = inv_ref[0, rs, :] * part_i
        v_i_ref[rs, :] = v_i
        sums[0] = sums[0] + x_i * part_i
        sums[1] = sums[1] + v_i * part_i
    sums_ref[0:ROWS, :] = fold(sums[0])
    sums_ref[ROWS : 2 * ROWS, :] = fold(sums[1])


def finish_kernel(
    u_o_ref, part_ref, far_ref, c_out_ref, inv_ref, v_i_ref, sums_ref,
    v_o_ref, even_ref, odd_ref, totals_ref,
):
    rows, width = u_o_ref.shape
    sums = [jnp.zeros((ROWS, width), F32) for _ in range(2)]
    for k in range(rows // ROWS):
        rs = slice(k * ROWS, (k + 1) * ROWS)
        part = part_ref[rs, :] + c_out_ref[rs, :] * far_ref[rs, :]
        v = inv_ref[1, rs, :] * part
        v_o_ref[rs, :] = v
        sums[0] = sums[0] + u_o_ref[rs, :] * part
        sums[1] = sums[1] + v * part
    totals_ref[0:ROWS, :] = fold(sums[0]) + sums_ref[0:ROWS, :]
    totals_ref[ROWS : 2 * ROWS, :] = fold(sums[1]) + sums_ref[ROWS : 2 * ROWS, :]
    put_rows(
        jnp.concatenate([v_i_ref[0:1, :], v_o_ref[0:1, :]], 0),
        jnp.concatenate([v_i_ref[rows - 1 :, :], v_o_ref[rows - 1 :, :]], 0),
        even_ref,
        odd_ref,
    )


def mail_kernel(t0_ref, t1_ref, t2_ref, mail_ref, *, picks):
    refs = (t0_ref, t1_ref, t2_ref)
    rows = [jnp.sum(refs[a][b * ROWS : (b + 1) * ROWS, :], 0, keepdims=True) for a, b in picks]
    block = jnp.concatenate(rows + rows, 0)
    for at in range(0, mail_ref.shape[0], ROWS):
        mail_ref[at : at + ROWS, :] = block


def weights(mail_ref):
    block = mail_ref[0:ROWS, :]
    for at in range(ROWS, mail_ref.shape[0], ROWS):
        block = block + mail_ref[at : at + ROWS, :]
    g = jnp.sum(block[0:4] + block[4:8], 1, keepdims=True)
    g0, g1, g2, g3 = (g[k : k + 1] for k in range(4))
    mu = g1 / g0
    h = g2 - mu * g1
    t = h / (h - (g3 - 2.0 * mu * g2 + mu * mu * g1))
    a = g0 / (g0 - g1 - h * t)
    b = t * a
    return a - mu * b, b


def step_kernel(
    mail_ref, s_i_ref, s_o_ref, v1_i_ref, v1_o_ref, v2_i_ref, v2_o_ref, v3_i_ref, v3_o_ref, cap_ref, observe_ref, diag_ref, inv_ref,
    x_ref, z_i_ref, z_o_ref, even_ref, odd_ref, sums_ref,
):
    rows, width = s_i_ref.shape
    i = inner_at()
    a, b = weights(mail_ref)
    total = jnp.zeros((ROWS, width), F32)
    for k in range(rows // ROWS):
        rs = slice(k * ROWS, (k + 1) * ROWS)
        for side, at, s_ref, p_ref, q_ref, r_ref, z_ref in (
            (0, i, s_i_ref, v1_i_ref, v2_i_ref, v3_i_ref, z_i_ref),
            (1, 1 - i, s_o_ref, v1_o_ref, v2_o_ref, v3_o_ref, z_o_ref),
        ):
            p, q = p_ref[rs, :], q_ref[rs, :]
            x = s_ref[rs, :] + a * p + b * q
            spread = p + a * q + b * r_ref[rs, :]
            x_ref[at, rs, :] = x
            residual = cap_ref[at, rs, :] * x + observe_ref[0, at, rs, :] - diag_ref[side, rs, :] * (x - spread)
            z = residual * inv_ref[side, rs, :]
            z_ref[rs, :] = z
            total = total + residual * z
    sums_ref[...] = fold(total)
    put_rows(
        jnp.concatenate([z_i_ref[0:1, :], z_o_ref[0:1, :]], 0),
        jnp.concatenate([z_i_ref[rows - 1 :, :], z_o_ref[rows - 1 :, :]], 0),
        even_ref,
        odd_ref,
    )


def last_kernel(mail_ref, x_ref, z_i_ref, z_o_ref, q_i_ref, q_o_ref, out_ref):
    rows, width = z_i_ref.shape
    i = inner_at()
    a, b = weights(mail_ref)
    for k in range(rows // ROWS):
        rs = slice(k * ROWS, (k + 1) * ROWS)
        for at, z_ref, q_ref in ((i, z_i_ref, q_i_ref), (1 - i, z_o_ref, q_o_ref)):
            x = x_ref[at, rs, :]
            out_ref[1, at, rs, :] = x
            out_ref[0, at, rs, :] = x + a * z_ref[rs, :] + b * q_ref[rs, :]


def on_device(cond_x, cond_y, via_cond, via_mask, capacitance, pad_mask, observe):
    bands, rows, width = cond_x.shape
    field, edge = shape(rows, width), shape(2, width)
    both = shape(bands, rows, width)
    n_devices = lax.axis_size("band") * lax.axis_size("tile")
    mail = shape(n_devices * 4, 128)
    two = shape(2 * ROWS, 128)
    one = shape(ROWS, 128)

    link, even, odd = call(first_kernel, [field, edge, edge], via_cond, via_mask, cond_x, name="links")
    far, near, even, odd = outer_swap(link), core_swap(link), even_swap(even), odd_swap(odd)
    cy, c_io, c_in, c_out, diag, inv, s_i, s_o, cx_edge, even, odd = call(
        prepare_kernel,
        [both, field, field, field, both, both, field, field, edge, edge, edge],
        cond_x, cond_y, via_cond, via_mask, capacitance, pad_mask, observe[1:2], link, near, far, even, odd,
        name="prepare",
    )

    def spread(u_i, u_o, even, odd, name):
        far, near, even, odd = outer_swap(u_o), core_swap(u_i), even_swap(even), odd_swap(odd)
        v_i, part, sums = call(
            lambda *refs: spread_kernel(2, *refs), [field, field, two],
            u_i, u_o, near, even, odd, cond_x, cy, c_io, c_in, inv, cx_edge, name=name + "_spread",
        )
        v_o, even, odd, totals = call(
            finish_kernel, [field, edge, edge, two], u_o, part, far, c_out, inv, v_i, sums, name=name + "_finish"
        )
        return v_i, v_o, even, odd, totals

    def send(t0, t1, t2, picks, name):
        (parts,) = call(
            lambda *refs: mail_kernel(*refs, picks=picks), [mail], t0, t1, t2, name=name
        )
        return all_total(parts)

    v1_i, v1_o, even, odd, t1 = spread(s_i, s_o, even, odd, "first")
    v2_i, v2_o, even, odd, t2 = spread(v1_i, v1_o, even, odd, "second")
    v3_i, v3_o, _, _, t3 = spread(v2_i, v2_o, even, odd, "third")
    got = send(t1, t2, t3, ((0, 1), (1, 0), (1, 1), (2, 0)), "later_mail")
    x, z_i, z_o, even, odd, t0 = call(
        step_kernel, [both, field, field, edge, edge, one],
        got, s_i, s_o, v1_i, v1_o, v2_i, v2_o, v3_i, v3_o, capacitance, observe[0:1], diag, inv, name="step",
    )
    q_i, q_o, even, odd, t1 = spread(z_i, z_o, even, odd, "fourth")
    _, _, _, _, t2 = spread(q_i, q_o, even, odd, "fifth")
    got = send(t0, t1, t2, ((0, 0), (1, 0), (1, 1), (2, 0)), "earlier_mail")
    (out,) = call(last_kernel, [shape(2, bands, rows, width)], got, x, z_i, z_o, q_i, q_o, name="last")
    return out


def solution(mesh):
    placed = (P("band", "tile", None),) * 6 + (P(None, "band", "tile", None),)
    return jax.shard_map(
        on_device,
        mesh=mesh,
        in_specs=placed,
        out_specs=P(None, "band", "tile", None),
        check_vma=False,
    )
```

time: 451 us -> 94.2 us (0.21)
  blocking collectives: 273 us -> 23.1 us
  starting transfers between devices: 77.4 us -> 19.1 us
  other arithmetic: 45.5 us -> 0 us
  Pallas kernels: 0 us -> 11.3 us
  between operations: 8.09 us -> 0.14 us
    psum x6 -> x0, blocking collectives: 273 us -> none  [the longest x4 178 us: norm_total(): return lax.psum(value, ('band', 'tile'))]
    ppermute x26 -> x24, starting transfers between devices: 77.4 us -> 19.1 us  [the longest x12 14.6 us: joint_permute(): return lax.ppermute(x, AXES, pairs)]
    all_to_all x0 -> x2, blocking collectives: none -> 23.1 us  [all_total(): return lax.all_to_all(parts, AXES, 0, 0, tiled=True)]
    reduce_sum x6 -> x0, other arithmetic: 19 us -> none  [the longest x4 14.2 us: solve_two(): step_len = norm_now / curve_total(jnp.sum(search * image_vec))]
    pallas_call x0 -> x16, Pallas kernels: none -> 11.3 us  [call(): pl.pallas_call(body, out_shape=outs, in_specs=[vmem] * len(args), out_spe...]
    concatenate x14 -> x0, other arithmetic: 8.1 us -> none  [the longest x12 5.48 us: with_halo(): block = jnp.concatenate([low, block, high], axis=dim)]
    div x3 -> x0, other arithmetic: 6.83 us -> none  [the longest x2 5.09 us: solve_two(): search = residual / scale]
    add x3 -> x0, other arithmetic: 6.58 us -> none  [the longest x2 4.36 us: solve_two(): search = precond_res + norm_next / norm_now * search]
  transfers between devices with their start and end apart: 26 -> 24, of which waited for: 18 -> 12; matrix products, arithmetic and copies ran while one was open for 2% -> 1% of each run, Pallas kernels for 0% -> 5%
where the time goes in v1:
time: 94.2 us; the launch traced here: 93.9 us
  waiting for transfers between devices  35.5 us (38%)
  blocking collectives  23.1 us (25%)
  starting transfers between devices  19.1 us (20%)
  Pallas kernels  11.3 us (12%)
  local copies, waits for them, and re-layouts  4.85 us (5%)
    all_to_all x2, blocking collectives, all_total(): return lax.all_to_all(parts, AXES, 0, 0, tiled=True)  23.1 us
    ppermute x12, waiting for transfers between devices, joint_permute(): return lax.ppermute(x, AXES, pairs)  18.8 us
    ppermute x6, waiting for transfers between devices, even_swap(): return lax.ppermute(x, 'tile', [(t, t ^ 1) for t in range(nt)])  16.7 us
    ppermute x12, starting transfers between devices, joint_permute(): return lax.ppermute(x, AXES, pairs)  14.6 us
    pallas_call x16, Pallas kernels, call(): pl.pallas_call(body, out_shape=outs, in_specs=[vmem] * len(args), out_spe...  11.3 us
    ppermute x6, starting transfers between devices, even_swap(): return lax.ppermute(x, 'tile', [(t, t ^ 1) for t in range(nt)])  3.99 us
    unnamed x16, local copies, waits for them, and re-layouts  3.69 us
  transfers between devices with their start and end apart: 24, of which 12 were waited for; matrix products, arithmetic and copies ran while one was open for 1% of the time, Pallas kernels for 5%

profile of v1, /device:TPU:0, one launch (start us, length us, event | category | flops | bytes accessed | tf_op | source)
XLA Modules:
  0.0 93.9 jit_solution(7266226838135367682)
XLA Ops:
  0.0 1.2 %copy-done = f32[2,64,2048]{2,1,0:T(8,128)S(1)} copy-done((f32[2,64,2048]{2,1,0:T(8,128)S(1)}, f32[2,64,2048]{2,1,0:T(8,128)}, u32[]{:S(2)}) %copy-start) | copy-done | bytes 1048600
  1.2 1.2 %copy-done.2 = f32[2,64,2048]{2,1,0:T(8,128)S(1)} copy-done((f32[2,64,2048]{2,1,0:T(8,128)S(1)}, f32[2,64,2048]{2,1,0:T(8,128)}, u32[]{:S(2)}) %copy-start.2) | copy-done | bytes 1048600
  2.5 1.2 %copy-done.3 = s32[2,64,2048]{2,1,0:T(8,128)S(1)} copy-done((s32[2,64,2048]{2,1,0:T(8,128)S(1)}, s32[2,64,2048]{2,1,0:T(8,128)}, u32[]{:S(2)}) %copy-start.3) | copy-done | bytes 1048600
  3.7 0.1 links.1
  3.8 3.1 %collective-permute-start.1 = (f32[64,2048]{1,0:T(8,128)S(1)}, f32[64,2048]{1,0:T(8,128)S(1)}, u32[]{:S(2)}, u32[]{:S(2)}) collective-permute-start(f32[64,2048]{1,0:T(8,128)S(1)} %get-tuple-element.55.link_ref), channel_id=1, source_target_pairs={{0,2},{1,3},{2,0},{3,1},{4,6},{5,7},{6,4},{7,5},{8,16},{9,17},{10,... | collective-permute-start | bytes 1572872 | tf_op jit(solution)/shard_map/ppermute | solution.py:27
  6.9 1.5 %collective-permute-start.2 = (f32[2,2048]{1,0:T(2,128)S(1)}, f32[2,2048]{1,0:T(2,128)S(1)}, u32[]{:S(2)}, u32[]{:S(2)}) collective-permute-start(f32[2,2048]{1,0:T(2,128)S(1)} %get-tuple-element.56), channel_id=1, source_target_pairs={{0,1},{1,0},{2,3},{3,2},{4,5},{5,4},{6,7},{7,6},{8,9},{9,8},{10,11... | collective-permute-start | bytes 49160 | tf_op jit(solution)/shard_map/ppermute | solution.py:48
  8.4 0.2 collective-permute-start.3
  8.6 1.2 %fusion = (f32[1,2,64,2048]{3,2,1,0:T(8,128)S(1)}, f32[1,2,64,2048]{3,2,1,0:T(8,128)}) fusion(f32[2,2,64,2048]{3,2,1,0:T(8,128)S(1)} %copy-done.7), kind=kLoop, calls=%fused_computation | loop fusion | bytes 4194304 | tf_op jit(solution)/shard_map/slice | solution.py:343
  9.7 0.9 collective-permute-done.2.even_ref
  10.6 3.5 %collective-permute-done.1.far_ref = f32[64,2048]{1,0:T(8,128)S(1)} collective-permute-done((f32[64,2048]{1,0:T(8,128)S(1)}, f32[64,2048]{1,0:T(8,128)S(1)}, u32[]{:S(2)}, u32[]{:S(2)}) %collective-permute-start.1) | collective-permute-done | bytes 524320 | tf_op jit(solution)/shard_map/ppermute | solution.py:27
  14.2 2.0 %prepare.1 = (f32[2,64,2048]{2,1,0:T(8,128)S(1)}, f32[64,2048]{1,0:T(8,128)S(1)}, f32[64,2048]{1,0:T(8,128)S(1)}, f32[64,2048]{1,0:T(8,128)S(1)}, f32[2,64,2048]...) custom-call(f32[2,64,2048]{2,1,0:T(8,128)S(1)} %copy-done, ...), custom_call_target="tpu_custom_call" | custom-call | flops 14761984 | bytes 3690496 | tf_op jit(solution)/shard_map/prepare/pallas_call | solution.py:69
  16.3 3.2 %collective-permute-start.7 = (f32[64,2048]{1,0:T(8,128)S(1)}, f32[64,2048]{1,0:T(8,128)S(1)}, u32[]{:S(2)}, u32[]{:S(2)}) collective-permute-start(f32[64,2048]{1,0:T(8,128)S(1)} %get-tuple-element.58.refs_1_.u_o_ref.s_o_ref), channel_id=1, source_target_pairs={{0,2},{1,3},{2,0},{3,1},{4,6},{5,7},{6,4},{7,5},{8,16},{9,17},{10,... | collective-permute-start | bytes 1572872 | tf_op jit(solution)/shard_map/ppermute | solution.py:27
  19.5 0.4 collective-permute-start.5
  19.9 3.4 %collective-permute-done.5.refs_3_ = f32[2,2048]{1,0:T(2,128)S(1)} collective-permute-done((f32[2,2048]{1,0:T(2,128)S(1)}, f32[2,2048]{1,0:T(2,128)S(1)}, u32[]{:S(2)}, u32[]{:S(2)}) %collective-permute-start.5) | collective-permute-done | bytes 16416 | tf_op jit(solution)/shard_map/ppermute | solution.py:48
  23.3 0.8 first_spread.1
  24.1 0.1 collective-permute-start.8
  24.2 2.7 %collective-permute-done.7.far_ref = f32[64,2048]{1,0:T(8,128)S(1)} collective-permute-done((f32[64,2048]{1,0:T(8,128)S(1)}, f32[64,2048]{1,0:T(8,128)S(1)}, u32[]{:S(2)}, u32[]{:S(2)}) %collective-permute-start.7) | collective-permute-done | bytes 524320 | tf_op jit(solution)/shard_map/ppermute | solution.py:27
  26.9 0.2 first_finish.1
  27.1 3.0 %collective-permute-start.11 = (f32[64,2048]{1,0:T(8,128)S(1)}, f32[64,2048]{1,0:T(8,128)S(1)}, u32[]{:S(2)}, u32[]{:S(2)}) collective-permute-start(f32[64,2048]{1,0:T(8,128)S(1)} %get-tuple-element.72.refs_1_.u_o_ref.v1_o_ref), channel_id=1, source_target_pairs={{0,2},{1,3},{2,0},{3,1},{4,6},{5,7},{6,4},{7,5},{8,16},{9,17},{10,... | collective-permute-start | bytes 1572872 | tf_op jit(solution)/shard_map/ppermute | solution.py:27
  30.1 3.7 %collective-permute-done.9.refs_3_ = f32[2,2048]{1,0:T(2,128)S(1)} collective-permute-done((f32[2,2048]{1,0:T(2,128)S(1)}, f32[2,2048]{1,0:T(2,128)S(1)}, u32[]{:S(2)}, u32[]{:S(2)}) %collective-permute-start.9) | collective-permute-done | bytes 16416 | tf_op jit(solution)/shard_map/ppermute | solution.py:48
  33.8 0.9 second_spread.1
  34.8 2.6 %collective-permute-done.11.far_ref = f32[64,2048]{1,0:T(8,128)S(1)} collective-permute-done((f32[64,2048]{1,0:T(8,128)S(1)}, f32[64,2048]{1,0:T(8,128)S(1)}, u32[]{:S(2)}, u32[]{:S(2)}) %collective-permute-start.11) | collective-permute-done | bytes 524320 | tf_op jit(solution)/shard_map/ppermute | solution.py:27
  37.4 0.2 second_finish.1
  37.6 2.3 %collective-permute-start.15 = (f32[64,2048]{1,0:T(8,128)S(1)}, f32[64,2048]{1,0:T(8,128)S(1)}, u32[]{:S(2)}, u32[]{:S(2)}) collective-permute-start(f32[64,2048]{1,0:T(8,128)S(1)} %get-tuple-element.79.refs_1_.u_o_ref.v2_o_ref), channel_id=1, source_target_pairs={{0,2},{1,3},{2,0},{3,1},{4,6},{5,7},{6,4},{7,5},{8,16},{9,17},{10,... | collective-permute-start | bytes 1572872 | tf_op jit(solution)/shard_map/ppermute | solution.py:27
  39.9 0.5 collective-permute-start.13
  40.4 0.2 collective-permute-start.14
  40.6 3.1 %collective-permute-done.13.refs_3_ = f32[2,2048]{1,0:T(2,128)S(1)} collective-permute-done((f32[2,2048]{1,0:T(2,128)S(1)}, f32[2,2048]{1,0:T(2,128)S(1)}, u32[]{:S(2)}, u32[]{:S(2)}) %collective-permute-start.13) | collective-permute-done | bytes 16416 | tf_op jit(solution)/shard_map/ppermute | solution.py:48
  43.7 0.8 third_spread.1
  44.5 2.8 %collective-permute-done.15.far_ref = f32[64,2048]{1,0:T(8,128)S(1)} collective-permute-done((f32[64,2048]{1,0:T(8,128)S(1)}, f32[64,2048]{1,0:T(8,128)S(1)}, u32[]{:S(2)}, u32[]{:S(2)}) %collective-permute-start.15) | collective-permute-done | bytes 524320 | tf_op jit(solution)/shard_map/ppermute | solution.py:27
  47.3 0.8 third_finish.1
  48.1 12.3 %all_to_all.22 = f32[32,4,128]{2,1,0:T(4,128)S(1)} all-to-all(f32[32,4,128]{2,1,0:T(4,128)S(1)} %bitcast.5), channel_id=1, replica_groups=mesh['band'=4,'tile'=8] {'band','tile'}, dimensions={0} | all-to-all | bytes 131072 | tf_op jit(solution)/shard_map/all_to_all | solution.py:63
  60.4 0.9 step.1
  61.3 0.2 collective-permute-start.16
  61.5 0.4 collective-permute-start.19
  61.9 1.0 %collective-permute-start.17 = (f32[2,2048]{1,0:T(2,128)S(1)}, f32[2,2048]{1,0:T(2,128)S(1)}, u32[]{:S(2)}, u32[]{:S(2)}) collective-permute-start(f32[2,2048]{1,0:T(2,128)S(1)} %get-tuple-element.91), channel_id=1, source_target_pairs={{0,1},{1,0},{2,3},{3,2},{4,5},{5,4},{6,7},{7,6},{8,9},{9,8},{10,11... | collective-permute-start | bytes 49160 | tf_op jit(solution)/shard_map/ppermute | solution.py:48
  62.9 2.8 %collective-permute-done.17.refs_3_ = f32[2,2048]{1,0:T(2,128)S(1)} collective-permute-done((f32[2,2048]{1,0:T(2,128)S(1)}, f32[2,2048]{1,0:T(2,128)S(1)}, u32[]{:S(2)}, u32[]{:S(2)}) %collective-permute-start.17) | collective-permute-done | bytes 16416 | tf_op jit(solution)/shard_map/ppermute | solution.py:48
  65.7 0.8 fourth_spread.1
  66.6 4.3 %collective-permute-done.19.far_ref = f32[64,2048]{1,0:T(8,128)S(1)} collective-permute-done((f32[64,2048]{1,0:T(8,128)S(1)}, f32[64,2048]{1,0:T(8,128)S(1)}, u32[]{:S(2)}, u32[]{:S(2)}) %collective-permute-start.19) | collective-permute-done | bytes 524320 | tf_op jit(solution)/shard_map/ppermute | solution.py:27
  70.8 0.2 fourth_finish.1
  71.1 2.0 %collective-permute-start.23 = (f32[64,2048]{1,0:T(8,128)S(1)}, f32[64,2048]{1,0:T(8,128)S(1)}, u32[]{:S(2)}, u32[]{:S(2)}) collective-permute-start(f32[64,2048]{1,0:T(8,128)S(1)} %get-tuple-element.97.refs_1_.u_o_ref.q_o_ref), channel_id=1, source_target_pairs={{0,2},{1,3},{2,0},{3,1},{4,6},{5,7},{6,4},{7,5},{8,16},{9,17},{10,... | collective-permute-start | bytes 1572872 | tf_op jit(solution)/shard_map/ppermute | solution.py:27
  73.1 0.7 collective-permute-start.21
  73.8 0.2 collective-permute-start.22
  74.0 2.8 %collective-permute-done.21.refs_3_ = f32[2,2048]{1,0:T(2,128)S(1)} collective-permute-done((f32[2,2048]{1,0:T(2,128)S(1)}, f32[2,2048]{1,0:T(2,128)S(1)}, u32[]{:S(2)}, u32[]{:S(2)}) %collective-permute-start.21) | collective-permute-done | bytes 16416 | tf_op jit(solution)/shard_map/ppermute | solution.py:48
  76.8 0.8 fifth_spread.1
  77.6 2.9 %collective-permute-done.23.far_ref = f32[64,2048]{1,0:T(8,128)S(1)} collective-permute-done((f32[64,2048]{1,0:T(8,128)S(1)}, f32[64,2048]{1,0:T(8,128)S(1)}, u32[]{:S(2)}, u32[]{:S(2)}) %collective-permute-start.23) | collective-permute-done | bytes 524320 | tf_op jit(solution)/shard_map/ppermute | solution.py:27
  80.5 1.0 %fifth_finish.1 = (f32[64,2048]{1,0:T(8,128)}, f32[2,2048]{1,0:T(2,128)}, f32[2,2048]{1,0:T(2,128)}, f32[16,128]{1,0:T(8,128)S(1)}) custom-call(f32[64,2048]{1,0:T(8,128)S(1)} %get-tuple-element.97.refs_1_.u_o_ref.q_o_ref, f32[64,2048]{1,0:T(8,128)S(1)} %get-tuple-element.100.part_ref, f32[64,2048]{1,0:T(8,128)S(1)} %collective-permute-done.23.far_ref, ...), custom_call_target="tpu_custom_call" | custom-call | flops 4243456 | bytes 1060864 | tf_op jit(solution)/shard_map/fifth_finish/pallas_call | solution.py:69
  81.5 10.7 %all_to_all.23 = f32[32,4,128]{2,1,0:T(4,128)S(1)} all-to-all(f32[32,4,128]{2,1,0:T(4,128)S(1)} %bitcast.6), channel_id=1, replica_groups=mesh['band'=4,'tile'=8] {'band','tile'}, dimensions={0} | all-to-all | bytes 131072 | tf_op jit(solution)/shard_map/all_to_all | solution.py:63
  92.2 1.7 %last.1 = f32[2,2,64,2048]{3,2,1,0:T(8,128)} custom-call(f32[128,128]{1,0:T(8,128)S(1)} %bitcast.7, f32[2,64,2048]{2,1,0:T(8,128)S(1)} %get-tuple-element.104.x_ref, f32[64,2048]{1,0:T(8,128)S(1)} %get-tuple-element.90.refs_0_.z_i_ref, f32[64,2048]{1,0:T(8,128)S(1)} %get-tuple-element.89.refs_1_.u_o_ref.z_o_ref, ...), custom_call_target="tpu_custom_call" | custom-call | flops 5308416 | bytes 1327104 | tf_op jit(solution)/shard_map/last/pallas_call | solution.py:69
  (35 shorter events, 0.4 us)
Async XLA Ops:
  0.0 1.2 %copy-start = (f32[2,64,2048]{2,1,0:T(8,128)S(1)}, f32[2,64,2048]{2,1,0:T(8,128)}, u32[]{:S(2)}) copy-start(f32[2,64,2048]{2,1,0:T(8,128)} %refs_5_.9) | copy-start | bytes 3145732
  1.2 1.2 %copy-start.2 = (f32[2,64,2048]{2,1,0:T(8,128)S(1)}, f32[2,64,2048]{2,1,0:T(8,128)}, u32[]{:S(2)}) copy-start(f32[2,64,2048]{2,1,0:T(8,128)} %via_ref.3) | copy-start | bytes 3145732
  2.5 1.2 %copy-start.3 = (s32[2,64,2048]{2,1,0:T(8,128)S(1)}, s32[2,64,2048]{2,1,0:T(8,128)}, u32[]{:S(2)}) copy-start(s32[2,64,2048]{2,1,0:T(8,128)} %mask_ref.3) | copy-start | bytes 3145732
  3.7 4.9 %copy-start.7 = (f32[2,2,64,2048]{3,2,1,0:T(8,128)S(1)}, f32[2,2,64,2048]{3,2,1,0:T(8,128)}, u32[]{:S(2)}) copy-start(f32[2,2,64,2048]{3,2,1,0:T(8,128)} %param.13) | copy-start | bytes 6291460
  3.8 10.4 %collective-permute-start.1 = (f32[64,2048]{1,0:T(8,128)S(1)}, f32[64,2048]{1,0:T(8,128)S(1)}, u32[]{:S(2)}, u32[]{:S(2)}) collective-permute-start(f32[64,2048]{1,0:T(8,128)S(1)} %get-tuple-element.55.link_ref), channel_id=1, source_target_pairs={{0,2},{1,3},{2,0},{3,1},{4,6},{5,7},{6,4},{7,5},{8,16},{9,17},{10,... | collective-permute-start | bytes 1572872 | tf_op jit(solution)/shard_map/ppermute | solution.py:27
  6.8 7.3 %collective-permute-start = (f32[64,2048]{1,0:T(8,128)S(1)}, f32[64,2048]{1,0:T(8,128)S(1)}, u32[]{:S(2)}, u32[]{:S(2)}) collective-permute-start(f32[64,2048]{1,0:T(8,128)S(1)} %get-tuple-element.55.link_ref), channel_id=1, source_target_pairs={{0,8},{8,0},{16,24},{24,16},{1,9},{9,1},{17,25},{25,17},{2,10},{10... | collective-permute-start | bytes 1572872 | tf_op jit(solution)/shard_map/ppermute | solution.py:32
  6.9 3.7 %collective-permute-start.2 = (f32[2,2048]{1,0:T(2,128)S(1)}, f32[2,2048]{1,0:T(2,128)S(1)}, u32[]{:S(2)}, u32[]{:S(2)}) collective-permute-start(f32[2,2048]{1,0:T(2,128)S(1)} %get-tuple-element.56), channel_id=1, source_target_pairs={{0,1},{1,0},{2,3},{3,2},{4,5},{5,4},{6,7},{7,6},{8,9},{9,8},{10,11... | collective-permute-start | bytes 49160 | tf_op jit(solution)/shard_map/ppermute | solution.py:48
  8.4 5.8 %copy-start.4 = (f32[2,64,2048]{2,1,0:T(8,128)S(1)}, f32[2,64,2048]{2,1,0:T(8,128)}, u32[]{:S(2)}) copy-start(f32[2,64,2048]{2,1,0:T(8,128)} %cap_ref.3) | copy-start | bytes 3145732
  8.4 5.8 %copy-start.5 = (f32[2,64,2048]{2,1,0:T(8,128)S(1)}, f32[2,64,2048]{2,1,0:T(8,128)}, u32[]{:S(2)}) copy-start(f32[2,64,2048]{2,1,0:T(8,128)} %cond_y_ref.1) | copy-start | bytes 3145732
  8.4 5.8 %copy-start.6 = (s32[2,64,2048]{2,1,0:T(8,128)S(1)}, s32[2,64,2048]{2,1,0:T(8,128)}, u32[]{:S(2)}) copy-start(s32[2,64,2048]{2,1,0:T(8,128)} %pad_ref.1) | copy-start | bytes 3145732
  8.4 2.2 %collective-permute-start.3 = (f32[2,2048]{1,0:T(2,128)S(1)}, f32[2,2048]{1,0:T(2,128)S(1)}, u32[]{:S(2)}, u32[]{:S(2)}) collective-permute-start(f32[2,2048]{1,0:T(2,128)S(1)} %get-tuple-element.57), channel_id=1, source_target_pairs={{0,8},{1,2},{2,1},{3,4},{4,3},{5,6},{6,5},{7,15},{8,0},{9,10},{10,... | collective-permute-start | bytes 49160 | tf_op jit(solution)/shard_map/ppermute | solution.py:27
  14.2 9.1 %copy-start.1 = (f32[2,64,2048]{2,1,0:T(8,128)S(1)}, f32[2,64,2048]{2,1,0:T(8,128)}, u32[]{:S(2)}) copy-start(f32[2,64,2048]{2,1,0:T(8,128)} %refs_5_.9) | copy-start | bytes 3145732
  16.2 7.0 %collective-permute-start.4 = (f32[64,2048]{1,0:T(8,128)S(1)}, f32[64,2048]{1,0:T(8,128)S(1)}, u32[]{:S(2)}, u32[]{:S(2)}) collective-permute-start(f32[64,2048]{1,0:T(8,128)S(1)} %get-tuple-element.59.refs_0_.s_i_ref), channel_id=1, source_target_pairs={{0,8},{8,0},{16,24},{24,16},{1,9},{9,1},{17,25},{25,17},{2,10},{10... | collective-permute-start | bytes 1572872 | tf_op jit(solution)/shard_map/ppermute | solution.py:32
  16.3 10.5 %collective-permute-start.7 = (f32[64,2048]{1,0:T(8,128)S(1)}, f32[64,2048]{1,0:T(8,128)S(1)}, u32[]{:S(2)}, u32[]{:S(2)}) collective-permute-start(f32[64,2048]{1,0:T(8,128)S(1)} %get-tuple-element.58.refs_1_.u_o_ref.s_o_ref), channel_id=1, source_target_pairs={{0,2},{1,3},{2,0},{3,1},{4,6},{5,7},{6,4},{7,5},{8,16},{9,17},{10,... | collective-permute-start | bytes 1572872 | tf_op jit(solution)/shard_map/ppermute | solution.py:27
  19.5 3.7 %collective-permute-start.5 = (f32[2,2048]{1,0:T(2,128)S(1)}, f32[2,2048]{1,0:T(2,128)S(1)}, u32[]{:S(2)}, u32[]{:S(2)}) collective-permute-start(f32[2,2048]{1,0:T(2,128)S(1)} %get-tuple-element.60), channel_id=1, source_target_pairs={{0,1},{1,0},{2,3},{3,2},{4,5},{5,4},{6,7},{7,6},{8,9},{9,8},{10,11... | collective-permute-start | bytes 49160 | tf_op jit(solution)/shard_map/ppermute | solution.py:48
  19.9 3.4 %collective-permute-start.6 = (f32[2,2048]{1,0:T(2,128)S(1)}, f32[2,2048]{1,0:T(2,128)S(1)}, u32[]{:S(2)}, u32[]{:S(2)}) collective-permute-start(f32[2,2048]{1,0:T(2,128)S(1)} %get-tuple-element.61), channel_id=1, source_target_pairs={{0,8},{1,2},{2,1},{3,4},{4,3},{5,6},{6,5},{7,15},{8,0},{9,10},{10,... | collective-permute-start | bytes 49160 | tf_op jit(solution)/shard_map/ppermute | solution.py:27
  24.1 9.7 %collective-permute-start.8 = (f32[64,2048]{1,0:T(8,128)S(1)}, f32[64,2048]{1,0:T(8,128)S(1)}, u32[]{:S(2)}, u32[]{:S(2)}) collective-permute-start(f32[64,2048]{1,0:T(8,128)S(1)} %get-tuple-element.69.v_i_ref.refs_0_.v1_i_ref), channel_id=1, source_target_pairs={{0,8},{8,0},{16,24},{24,16},{1,9},{9,1},{17,25},{25,17},{2,10},{10... | collective-permute-start | bytes 1572872 | tf_op jit(solution)/shard_map/ppermute | solution.py:32
  27.1 10.3 %collective-permute-start.11 = (f32[64,2048]{1,0:T(8,128)S(1)}, f32[64,2048]{1,0:T(8,128)S(1)}, u32[]{:S(2)}, u32[]{:S(2)}) collective-permute-start(f32[64,2048]{1,0:T(8,128)S(1)} %get-tuple-element.72.refs_1_.u_o_ref.v1_o_ref), channel_id=1, source_target_pairs={{0,2},{1,3},{2,0},{3,1},{4,6},{5,7},{6,4},{7,5},{8,16},{9,17},{10,... | collective-permute-start | bytes 1572872 | tf_op jit(solution)/shard_map/ppermute | solution.py:27
  30.1 3.7 %collective-permute-start.9 = (f32[2,2048]{1,0:T(2,128)S(1)}, f32[2,2048]{1,0:T(2,128)S(1)}, u32[]{:S(2)}, u32[]{:S(2)}) collective-permute-start(f32[2,2048]{1,0:T(2,128)S(1)} %get-tuple-element.73), channel_id=1, source_target_pairs={{0,1},{1,0},{2,3},{3,2},{4,5},{5,4},{6,7},{7,6},{8,9},{9,8},{10,11... | collective-permute-start | bytes 49160 | tf_op jit(solution)/shard_map/ppermute | solution.py:48
  30.1 3.7 %collective-permute-start.10 = (f32[2,2048]{1,0:T(2,128)S(1)}, f32[2,2048]{1,0:T(2,128)S(1)}, u32[]{:S(2)}, u32[]{:S(2)}) collective-permute-start(f32[2,2048]{1,0:T(2,128)S(1)} %get-tuple-element.74), channel_id=1, source_target_pairs={{0,8},{1,2},{2,1},{3,4},{4,3},{5,6},{6,5},{7,15},{8,0},{9,10},{10,... | collective-permute-start | bytes 49160 | tf_op jit(solution)/shard_map/ppermute | solution.py:27
  34.7 9.0 %collective-permute-start.12 = (f32[64,2048]{1,0:T(8,128)S(1)}, f32[64,2048]{1,0:T(8,128)S(1)}, u32[]{:S(2)}, u32[]{:S(2)}) collective-permute-start(f32[64,2048]{1,0:T(8,128)S(1)} %get-tuple-element.76.v_i_ref.refs_0_.v2_i_ref), channel_id=1, source_target_pairs={{0,8},{8,0},{16,24},{24,16},{1,9},{9,1},{17,25},{25,17},{2,10},{10... | collective-permute-start | bytes 1572872 | tf_op jit(solution)/shard_map/ppermute | solution.py:32
  37.6 9.6 %collective-permute-start.15 = (f32[64,2048]{1,0:T(8,128)S(1)}, f32[64,2048]{1,0:T(8,128)S(1)}, u32[]{:S(2)}, u32[]{:S(2)}) collective-permute-start(f32[64,2048]{1,0:T(8,128)S(1)} %get-tuple-element.79.refs_1_.u_o_ref.v2_o_ref), channel_id=1, source_target_pairs={{0,2},{1,3},{2,0},{3,1},{4,6},{5,7},{6,4},{7,5},{8,16},{9,17},{10,... | collective-permute-start | bytes 1572872 | tf_op jit(solution)/shard_map/ppermute | solution.py:27
  39.9 3.7 %collective-permute-start.13 = (f32[2,2048]{1,0:T(2,128)S(1)}, f32[2,2048]{1,0:T(2,128)S(1)}, u32[]{:S(2)}, u32[]{:S(2)}) collective-permute-start(f32[2,2048]{1,0:T(2,128)S(1)} %get-tuple-element.80), channel_id=1, source_target_pairs={{0,1},{1,0},{2,3},{3,2},{4,5},{5,4},{6,7},{7,6},{8,9},{9,8},{10,11... | collective-permute-start | bytes 49160 | tf_op jit(solution)/shard_map/ppermute | solution.py:48
  40.4 3.3 %collective-permute-start.14 = (f32[2,2048]{1,0:T(2,128)S(1)}, f32[2,2048]{1,0:T(2,128)S(1)}, u32[]{:S(2)}, u32[]{:S(2)}) collective-permute-start(f32[2,2048]{1,0:T(2,128)S(1)} %get-tuple-element.81), channel_id=1, source_target_pairs={{0,8},{1,2},{2,1},{3,4},{4,3},{5,6},{6,5},{7,15},{8,0},{9,10},{10,... | collective-permute-start | bytes 49160 | tf_op jit(solution)/shard_map/ppermute | solution.py:27
  61.3 4.4 %collective-permute-start.16 = (f32[64,2048]{1,0:T(8,128)S(1)}, f32[64,2048]{1,0:T(8,128)S(1)}, u32[]{:S(2)}, u32[]{:S(2)}) collective-permute-start(f32[64,2048]{1,0:T(8,128)S(1)} %get-tuple-element.90.refs_0_.z_i_ref), channel_id=1, source_target_pairs={{0,8},{8,0},{16,24},{24,16},{1,9},{9,1},{17,25},{25,17},{2,10},{10... | collective-permute-start | bytes 1572872 | tf_op jit(solution)/shard_map/ppermute | solution.py:32
  61.5 9.4 %collective-permute-start.19 = (f32[64,2048]{1,0:T(8,128)S(1)}, f32[64,2048]{1,0:T(8,128)S(1)}, u32[]{:S(2)}, u32[]{:S(2)}) collective-permute-start(f32[64,2048]{1,0:T(8,128)S(1)} %get-tuple-element.89.refs_1_.u_o_ref.z_o_ref), channel_id=1, source_target_pairs={{0,2},{1,3},{2,0},{3,1},{4,6},{5,7},{6,4},{7,5},{8,16},{9,17},{10,... | collective-permute-start | bytes 1572872 | tf_op jit(solution)/shard_map/ppermute | solution.py:27
  61.9 3.7 %collective-permute-start.17 = (f32[2,2048]{1,0:T(2,128)S(1)}, f32[2,2048]{1,0:T(2,128)S(1)}, u32[]{:S(2)}, u32[]{:S(2)}) collective-permute-start(f32[2,2048]{1,0:T(2,128)S(1)} %get-tuple-element.91), channel_id=1, source_target_pairs={{0,1},{1,0},{2,3},{3,2},{4,5},{5,4},{6,7},{7,6},{8,9},{9,8},{10,11... | collective-permute-start | bytes 49160 | tf_op jit(solution)/shard_map/ppermute | solution.py:48
  62.9 2.8 %collective-permute-start.18 = (f32[2,2048]{1,0:T(2,128)S(1)}, f32[2,2048]{1,0:T(2,128)S(1)}, u32[]{:S(2)}, u32[]{:S(2)}) collective-permute-start(f32[2,2048]{1,0:T(2,128)S(1)} %get-tuple-element.92), channel_id=1, source_target_pairs={{0,8},{1,2},{2,1},{3,4},{4,3},{5,6},{6,5},{7,15},{8,0},{9,10},{10,... | collective-permute-start | bytes 49160 | tf_op jit(solution)/shard_map/ppermute | solution.py:27
  66.5 10.3 %collective-permute-start.20 = (f32[64,2048]{1,0:T(8,128)S(1)}, f32[64,2048]{1,0:T(8,128)S(1)}, u32[]{:S(2)}, u32[]{:S(2)}) collective-permute-start(f32[64,2048]{1,0:T(8,128)S(1)} %get-tuple-element.94.v_i_ref.refs_0_.q_i_ref), channel_id=1, source_target_pairs={{0,8},{8,0},{16,24},{24,16},{1,9},{9,1},{17,25},{25,17},{2,10},{10... | collective-permute-start | bytes 1572872 | tf_op jit(solution)/shard_map/ppermute | solution.py:32
  71.1 9.4 %collective-permute-start.23 = (f32[64,2048]{1,0:T(8,128)S(1)}, f32[64,2048]{1,0:T(8,128)S(1)}, u32[]{:S(2)}, u32[]{:S(2)}) collective-permute-start(f32[64,2048]{1,0:T(8,128)S(1)} %get-tuple-element.97.refs_1_.u_o_ref.q_o_ref), channel_id=1, source_target_pairs={{0,2},{1,3},{2,0},{3,1},{4,6},{5,7},{6,4},{7,5},{8,16},{9,17},{10,... | collective-permute-start | bytes 1572872 | tf_op jit(solution)/shard_map/ppermute | solution.py:27
  73.1 3.7 %collective-permute-start.21 = (f32[2,2048]{1,0:T(2,128)S(1)}, f32[2,2048]{1,0:T(2,128)S(1)}, u32[]{:S(2)}, u32[]{:S(2)}) collective-permute-start(f32[2,2048]{1,0:T(2,128)S(1)} %get-tuple-element.98), channel_id=1, source_target_pairs={{0,1},{1,0},{2,3},{3,2},{4,5},{5,4},{6,7},{7,6},{8,9},{9,8},{10,11... | collective-permute-start | bytes 49160 | tf_op jit(solution)/shard_map/ppermute | solution.py:48
  73.8 3.0 %collective-permute-start.22 = (f32[2,2048]{1,0:T(2,128)S(1)}, f32[2,2048]{1,0:T(2,128)S(1)}, u32[]{:S(2)}, u32[]{:S(2)}) collective-permute-start(f32[2,2048]{1,0:T(2,128)S(1)} %get-tuple-element.99), channel_id=1, source_target_pairs={{0,8},{1,2},{2,1},{3,4},{4,3},{5,6},{6,5},{7,15},{8,0},{9,10},{10,... | collective-permute-start | bytes 49160 | tf_op jit(solution)/shard_map/ppermute | solution.py:27

commit v2 on v0

v2 whole, which is shorter than its diff:
```python
import jax
import jax.numpy as jnp
from jax import lax
from jax.experimental import pallas as pl
from jax.experimental.pallas import tpu as pltpu
from jax.sharding import PartitionSpec as P

NB = 8
ROWS = 8
AXES = ("band", "tile")
F32 = jnp.float32

pad_conductance = 4.0


def sizes():
    return lax.axis_size("band"), lax.axis_size("tile")


def core():
    return lax.rem(lax.axis_index("band"), 2)


def upper_chip():
    return lax.axis_index("band") >= 2


def core_swap(x):
    nb, _ = sizes()
    return lax.ppermute(x, "band", [(b, b ^ 1) for b in range(nb)])


def outer_swap(x):
    nb, _ = sizes()
    return lax.ppermute(x, "band", [(b, b ^ 2) for b in range(nb)])


def next_tile(x):
    _, nt = sizes()
    return lax.ppermute(x, "tile", [(t, (t + 1) % nt) for t in range(nt)])


def cross_swap(x):
    nb, nt = sizes()
    pairs = []
    for b in range(nb):
        for t in range(nt):
            other = (t + 1) % nt if b % 2 else (t - 1) % nt
            pairs.append((b * nt + t, (b ^ 1) * nt + other))
    return lax.ppermute(x, AXES, pairs)


def all_total(parts):
    return lax.all_to_all(parts, AXES, 0, 0, tiled=True)


def call(body, outs, *args, name, place=pltpu.VMEM, out_place=pltpu.VMEM, scratch=(), limit=10, cost=10):
    if place == pltpu.HBM:
        args = [pltpu.with_memory_space_constraint(a, pltpu.HBM) for a in args]
    return pl.pallas_call(
        body,
        out_shape=outs,
        in_specs=[pl.BlockSpec(memory_space=place)] * len(args),
        out_specs=[pl.BlockSpec(memory_space=out_place)] * len(outs),
        scratch_shapes=list(scratch),
        name=name,
        cost_estimate=pl.CostEstimate(flops=cost * 10**9, bytes_accessed=cost * 10**6, transcendentals=0),
        compiler_params=pltpu.CompilerParams(vmem_limit_bytes=limit * 1024 * 1024),
    )(*args)


def shape(*dims):
    return jax.ShapeDtypeStruct(dims, F32)


def row_at(width, at):
    return lax.broadcasted_iota(jnp.int32, (ROWS, width), 0) == at


def stack_rows(rows):
    return jnp.concatenate(rows, 0)


def put_rows(first, last, core_ref, cross_ref):
    lower = core() == 1
    core_ref[...] = jnp.where(lower, first, last)
    cross_ref[...] = jnp.where(lower, last, first)


def take_rows(core_ref, cross_ref):
    lower = core() == 1
    tile = lax.axis_index("tile")
    cross = cross_ref[...]
    near = core_ref[0 : cross.shape[0], :]
    above = jnp.where(lower, near, jnp.where(tile == 0, 0.0, cross))
    below = jnp.where(lower, jnp.where(tile == lax.axis_size("tile") - 1, 0.0, cross), near)
    return above, below


def fold(total):
    acc = total[:, :128]
    for at in range(128, total.shape[1], 128):
        acc = acc + total[:, at : at + 128]
    return acc


def band_of(u_o_ref, u_i_ref, j):
    return u_o_ref if j == 0 else u_i_ref.at[j - 1]


def in_band(v_ref, cx_ref, cy_ref, carried, below, k, chunks):
    width = v_ref.shape[-1]
    r = k * ROWS
    x = v_ref[r : r + ROWS, :]
    cx = cx_ref[r : r + ROWS, :]
    cy = cy_ref[r : r + ROWS, :]
    after = below if k == chunks - 1 else v_ref[r + ROWS : r + ROWS + 1, :]
    down = jnp.where(row_at(width, ROWS - 1), after, pltpu.roll(x, ROWS - 1, 0))
    flux = cx * x
    up = jnp.where(row_at(width, 0), carried, pltpu.roll(flux, 1, 0))
    total = cx * down + up + cy * pltpu.roll(x, width - 1, 1) + pltpu.roll(cy * x, 1, 1)
    return x, total, flux[ROWS - 1 :, :]


def couple(xs, parts, c_ref, rs):
    parts = list(parts)
    for j in range(1, len(xs)):
        c = c_ref[j, rs, :]
        parts[j] = parts[j] + c * xs[j - 1]
        parts[j - 1] = parts[j - 1] + c * xs[j]
    return parts


def half_of(which, half):
    return pl.ds(pl.multiple_of(which * half, ROWS), half)


def run_copies(pairs, sems):
    copies = [pltpu.make_async_copy(source, to, sems.at[n]) for n, (source, to) in enumerate(pairs)]
    for copy in copies:
        copy.start()
    for copy in copies:
        copy.wait()


def load_kernel(
    cond_x_ref, cond_y_ref, via_ref, mask_ref, cap_ref, pad_ref, observe_ref,
    mine_ref, send_ref, pay_mine_ref, pay_send_ref, last_ref, middle_ref, via_at, mask_at, pad_at, sems,
):
    half = send_ref.shape[1]
    me = core()
    pairs = [(via_ref, via_at), (mask_ref, mask_at), (pad_ref, pad_at)]
    halves = ((send_ref, pay_send_ref, 1 - me), (mine_ref, pay_mine_ref, me))
    for ref, _, which in halves:
        rs = half_of(which, half)
        pairs += [
            (cond_x_ref.at[:, rs, :], ref.at[0:2]),
            (cond_y_ref.at[:, rs, :], ref.at[2:4]),
            (observe_ref.at[1, :, rs, :], ref.at[8:10]),
            (cap_ref.at[:, rs, :], ref.at[10:12]),
            (observe_ref.at[0, :, rs, :], ref.at[12:14]),
        ]
    run_copies(pairs, sems)
    for ref, pay_ref, which in halves:
        rs = half_of(which, half)
        for band in range(2):
            ref[4 + band] = via_at[band, rs, :] * mask_at[band, rs, :].astype(F32)
            ref[6 + band] = ref[10 + band] + pad_conductance * pad_at[band, rs, :].astype(F32)
        pay_ref[...] = jnp.where(upper_chip(), ref[8], ref[5])
    for band in range(2):
        own, other = mine_ref[band, half - 1 :, :], send_ref[band, half - 1 :, :]
        last_ref[band : band + 1, :] = jnp.where(me == 1, own, other)
        middle_ref[band : band + 1, :] = jnp.where(me == 1, other, own)


def pay_kernel(mine_ref, got_ref, pay_ref):
    pay_ref[...] = jnp.where((core() == 1) == upper_chip(), got_ref[...], mine_ref[...])


def edge_kernel(middle_ref, before_ref, own_ref, send_ref):
    lower = core() == 1
    middle, before = middle_ref[...], before_ref[...]
    own_ref[...] = jnp.where(lower, middle, before)
    send_ref[...] = jnp.where(lower, before, middle)


def place_of(owner, band):
    n = 2 * owner + band
    return jnp.where(upper_chip(), n, 3 - n)


def prepare_kernel(
    mine_ref, got_ref, own_edge_ref, got_edge_ref, link_ref,
    cx_ref, cy_ref, c_ref, diag_ref, inv_i_ref, s_i_ref, inv_o_ref, s_o_ref, edge_ref, core_ref, cross_ref, cap_ref, seen_ref,
):
    half, width = s_o_ref.shape
    me = core()
    upper = upper_chip()
    lane = lax.broadcasted_iota(jnp.int32, (ROWS, width), 1)
    first_tile = jnp.logical_and(me == 0, lax.axis_index("tile") == 0)
    places = []
    for owner, ref, edges in ((me, mine_ref, own_edge_ref), (1 - me, got_ref, got_edge_ref)):
        for band in range(2):
            j = place_of(owner, band)
            places.append((j, ref, band))
            carried = jnp.where(first_tile, 0.0, edges[band : band + 1, :])
            edge_ref[pl.ds(j, 1), :] = carried
            cx_ref[j] = ref[band]
            cap_ref[j] = ref[10 + band]
            seen_ref[j] = ref[12 + band]
            via_at = jnp.where(upper, j + 1, j)

            @pl.when(via_at < 4)
            def _():
                c_ref[via_at] = ref[4 + band]

            for k in range(half // ROWS):
                rs = slice(k * ROWS, (k + 1) * ROWS)
                cx, cy, diag = (ref[2 * n + band, rs, :] for n in (0, 1, 3))
                cut = jnp.where(lane == width - 1, 0.0, cy)
                up = jnp.where(row_at(width, 0), carried, pltpu.roll(cx, 1, 0))
                carried = cx[ROWS - 1 :, :]
                cy_ref[j, rs, :] = cut
                diag_ref[j, rs, :] = diag + cx + cy + up + pltpu.roll(cut, 1, 1)

    @pl.when(upper)
    def _():
        c_ref[0] = link_ref[...]

    for j, ref, band in places:
        @pl.when(j == 0)
        def _():
            s_o_ref[...] = ref[8 + band]

        @pl.when(j > 0)
        def _():
            s_i_ref[j - 1] = ref[8 + band]

    for k in range(half // ROWS):
        rs = slice(k * ROWS, (k + 1) * ROWS)
        c = [c_ref[j, rs, :] for j in range(4)]
        for j in range(4):
            diag = diag_ref[j, rs, :] + c[j]
            if j < 3:
                diag = diag + c[j + 1]
            inv = 1.0 / diag
            diag_ref[j, rs, :] = diag
            band_of(inv_o_ref, inv_i_ref, j)[rs, :] = inv
            s_ref = band_of(s_o_ref, s_i_ref, j)
            s_ref[rs, :] = s_ref[rs, :] * inv
    ends = []
    for r in (0, half - 1):
        at = slice(r, r + 1)
        rows = [band_of(s_o_ref, s_i_ref, j)[at, :] for j in range(4)]
        ends.append(stack_rows(rows + [inv_o_ref[at, :], c_ref[0, at, :]]))
    put_rows(ends[0], ends[1], core_ref, cross_ref)


def own_parts(u_o_ref, u_i_ref, cx_ref, cy_ref, c_ref, pay_ref, scratch_ref):
    rows, width = u_o_ref.shape
    chunks = rows // ROWS
    none = jnp.zeros((1, width), F32)
    carried = none
    for k in range(chunks):
        rs = slice(k * ROWS, (k + 1) * ROWS)
        x, part, carried = in_band(u_o_ref, cx_ref.at[0], cy_ref.at[0], carried, none, k, chunks)
        pay_ref[rs, :] = x
        scratch_ref[rs, :] = part + c_ref[1, rs, :] * u_i_ref[0, rs, :]
    size = pay_ref.shape[0] - rows
    first = jnp.where(upper_chip(), 0, rows - size)
    pay_ref[rows:, :] = scratch_ref[pl.ds(pl.multiple_of(first, ROWS), size), :]


def spread_kernel(
    u_o_ref, u_i_ref, core_ref, cross_ref, cx_ref, cy_ref, c_ref, inv_i_ref, edge_ref,
    v_i_ref, part_ref, sums_ref, tail_ref=None, v_core_ref=None, v_cross_ref=None,
):
    rows, width = u_o_ref.shape
    chunks = rows // ROWS
    above, below = take_rows(core_ref, cross_ref)
    carried = [edge_ref[j : j + 1, :] * above[j : j + 1] for j in range(4)]
    sums = [jnp.zeros((ROWS, width), F32) for _ in range(2)]
    ends = [None, None]
    for k in range(chunks):
        rs = slice(k * ROWS, (k + 1) * ROWS)
        xs, parts = [], []
        for j in range(4):
            x, part, carried[j] = in_band(
                band_of(u_o_ref, u_i_ref, j), cx_ref.at[j], cy_ref.at[j], carried[j], below[j : j + 1], k, chunks
            )
            xs.append(x)
            parts.append(part)
        parts = couple(xs, parts, c_ref, rs)
        part_ref[rs, :] = parts[0]
        vs = [parts[0]]
        for j in range(1, 4):
            v = inv_i_ref[j - 1, rs, :] * parts[j]
            v_i_ref[j - 1, rs, :] = v
            sums[0] = sums[0] + xs[j] * parts[j]
            sums[1] = sums[1] + v * parts[j]
            vs.append(v)
        if k == 0:
            ends[0] = stack_rows([v[:1] for v in vs])
        if k == chunks - 1:
            ends[1] = stack_rows([v[ROWS - 1 :] for v in vs])
    sums_ref[0:ROWS, :] = fold(sums[0])
    sums_ref[ROWS : 2 * ROWS, :] = fold(sums[1])
    if tail_ref is not None:
        fluxes = [edge_ref[0:1, :] * above[0:1], cx_ref[0, rows - 1 :, :] * below[0:1]]
        tail_ref[...] = stack_rows([above[0:1], below[0:1], *fluxes, jnp.zeros((ROWS - 4, width), F32)])
        put_rows(ends[0], ends[1], v_core_ref, v_cross_ref)


def far_first_kernel(
    u_o_ref, part_ref, far_ref, c_ref, inv_ref, v_i_ref, sums_ref, cx_ref, cy_ref, v_ref, core_ref, cross_ref, total_ref, pay_ref,
    scratch_ref,
):
    rows, width = u_o_ref.shape
    total = jnp.zeros((ROWS, width), F32)
    for k in range(rows // ROWS):
        rs = slice(k * ROWS, (k + 1) * ROWS)
        part = part_ref[rs, :] + c_ref[0, rs, :] * far_ref[rs, :]
        v = inv_ref[rs, :] * part
        v_ref[rs, :] = v
        total = total + v * part
    total_ref[...] = fold(total) + sums_ref[ROWS : 2 * ROWS, :]
    ends = [
        stack_rows([v_ref[r : r + 1, :]] + [v_i_ref[j, r : r + 1, :] for j in range(3)]) for r in (0, rows - 1)
    ]
    put_rows(ends[0], ends[1], core_ref, cross_ref)
    own_parts(v_ref, v_i_ref, cx_ref, cy_ref, c_ref, pay_ref, scratch_ref)


def far_kernel(u_o_ref, part_ref, far_ref, c_ref, inv_ref, sums_ref, v_ref, totals_ref):
    rows, width = u_o_ref.shape
    sums = [jnp.zeros((ROWS, width), F32) for _ in range(2)]
    for k in range(rows // ROWS):
        rs = slice(k * ROWS, (k + 1) * ROWS)
        part = part_ref[rs, :] + c_ref[0, rs, :] * far_ref[rs, :]
        v = inv_ref[rs, :] * part
        v_ref[rs, :] = v
        sums[0] = sums[0] + u_o_ref[rs, :] * part
        sums[1] = sums[1] + v * part
    totals_ref[0:ROWS, :] = fold(sums[0]) + sums_ref[0:ROWS, :]
    totals_ref[ROWS : 2 * ROWS, :] = fold(sums[1]) + sums_ref[ROWS : 2 * ROWS, :]


def again_kernel(
    v_o_ref, v_i_ref, core_ref, cross_ref, cx_ref, cy_ref, c_ref, inv_i_ref, edge_ref,
    total_ref, w_i_ref=None, part_ref=None,
):
    rows, width = v_o_ref.shape
    chunks = rows // ROWS
    above, below = take_rows(core_ref, cross_ref)
    none = jnp.zeros((1, width), F32)
    carried = [none] + [edge_ref[j : j + 1, :] * above[j : j + 1] for j in range(1, 4)]
    after = [none] + [below[j : j + 1] for j in range(1, 4)]
    total = jnp.zeros((ROWS, width), F32)
    for k in range(chunks):
        rs = slice(k * ROWS, (k + 1) * ROWS)
        xs, parts = [], []
        for j in range(4):
            x, part, carried[j] = in_band(
                band_of(v_o_ref, v_i_ref, j), cx_ref.at[j], cy_ref.at[j], carried[j], after[j], k, chunks
            )
            xs.append(x)
            parts.append(part)
        parts = couple(xs, parts, c_ref, rs)
        for x, part in zip(xs, parts):
            total = total + x * part
        if w_i_ref is not None:
            part_ref[rs, :] = parts[0]
            for j in range(1, 4):
                w_i_ref[j - 1, rs, :] = inv_i_ref[j - 1, rs, :] * parts[j]
    total_ref[...] = fold(total)


def cross_kernel(
    u_ref, v_ref, got_ref, tail_ref, core_ref, cross_ref, inv_far_ref, c_ref, cx_ref, edge_ref, side_core_ref, side_cross_ref,
    t0_ref, t1_ref, t2_ref, mail_ref, part_ref=None, inv_ref=None, w_ref=None,
):
    rows, width = u_ref.shape
    size = got_ref.shape[0] - rows
    chunks = size // ROWS
    first = jnp.where(upper_chip(), rows - size, 0)
    above, below = take_rows(core_ref, cross_ref)
    side_above, side_below = take_rows(side_core_ref, side_cross_ref)
    up = side_above[4:5] * (above[0:1] + side_above[5:6] * tail_ref[0:1, :])
    down = side_below[4:5] * (below[0:1] + side_below[5:6] * tail_ref[1:2, :])
    up = edge_ref[0:1, :] * up
    down = cx_ref[0, rows - 1 :, :] * down
    far_up = jnp.where(first == 0, tail_ref[2:3, :], 0.0)
    far_down = jnp.where(first + size == rows, tail_ref[3:4, :], 0.0)
    total = jnp.zeros((ROWS, width), F32)
    for k in range(chunks):
        rs = slice(k * ROWS, (k + 1) * ROWS)
        at = pl.ds(pl.multiple_of(first + k * ROWS, ROWS), ROWS)
        c_out = c_ref[0, at, :]
        part = got_ref[rows + k * ROWS : rows + (k + 1) * ROWS, :] + c_out * u_ref[at, :]
        if k == 0:
            part = part + jnp.where(row_at(width, 0), far_up, 0.0)
        if k == chunks - 1:
            part = part + jnp.where(row_at(width, ROWS - 1), far_down, 0.0)
        flow = c_out * (inv_far_ref[at, :] * part)
        total = total + v_ref[at, :] * flow
        if w_ref is not None:
            part = part_ref[rs, :] + flow
            if k == 0:
                part = part + jnp.where(row_at(width, 0), up, 0.0)
            if k == chunks - 1:
                part = part + jnp.where(row_at(width, ROWS - 1), down, 0.0)
            w_ref[rs, :] = inv_ref[rs, :] * part
    ends = up * v_ref[0:1, :] + down * v_ref[rows - 1 :, :]
    last = fold((rows // size) * total + jnp.where(row_at(width, 0), ends, 0.0)) + t2_ref[...]
    terms = (t0_ref[...], t1_ref[0:ROWS, :], t1_ref[ROWS : 2 * ROWS, :], last)
    lines = [jnp.sum(t, 0, keepdims=True) for t in terms]
    block = jnp.concatenate(lines + lines, 0)
    for at in range(0, mail_ref.shape[0], ROWS):
        mail_ref[at : at + ROWS, :] = block


def weights(mail_ref):
    block = mail_ref[0:ROWS, :]
    for at in range(ROWS, mail_ref.shape[0], ROWS):
        block = block + mail_ref[at : at + ROWS, :]
    g = jnp.sum(block[0:4] + block[4:8], 1, keepdims=True)
    g0, g1, g2, g3 = (g[k : k + 1] for k in range(4))
    mu = g1 / g0
    h = g2 - mu * g1
    t = h / (h - (g3 - 2.0 * mu * g2 + mu * mu * g1))
    a = g0 / (g0 - g1 - h * t)
    b = t * a
    return a - mu * b, b


def hand_out(j, value, k, mine_ref, send_ref, first, half):
    n = jnp.where(upper_chip(), j, 3 - j)
    owner, band = n // 2, lax.rem(n, 2)
    size = value.shape[0]

    @pl.when(owner == core())
    def _():
        mine_ref[band, k * ROWS : k * ROWS + size, :] = value

    @pl.when(owner != core())
    def _():
        send_ref[pl.ds(pl.multiple_of(first + band * half + k * ROWS, ROWS), size), :] = value


def step_kernel(
    mail_ref, s_o_ref, s_i_ref, v1_o_ref, v1_i_ref, v2_o_ref, v2_i_ref, v3_o_ref, v3_i_ref, cap_ref, seen_ref,
    diag_ref, inv_o_ref, inv_i_ref, cx_ref, cy_ref, c_ref,
    z_o_ref, z_i_ref, core_ref, cross_ref, total_ref, pay_ref, x_mine_ref, z_mine_ref, scratch_ref,
):
    rows, width = s_o_ref.shape
    chunks = rows // ROWS
    a, b = weights(mail_ref)
    total = jnp.zeros((ROWS, width), F32)
    firsts, lasts = [], []
    for j in range(4):
        for k in range(chunks):
            rs = slice(k * ROWS, (k + 1) * ROWS)
            s, p, q, r, inv = (
                band_of(o, i, j)[rs, :]
                for o, i in (
                    (s_o_ref, s_i_ref), (v1_o_ref, v1_i_ref), (v2_o_ref, v2_i_ref), (v3_o_ref, v3_i_ref),
                    (inv_o_ref, inv_i_ref),
                )
            )
            x = s + a * p + b * q
            residual = cap_ref[j, rs, :] * x + seen_ref[j, rs, :] - diag_ref[j, rs, :] * (x - (p + a * q + b * r))
            z = residual * inv
            band_of(z_o_ref, z_i_ref, j)[rs, :] = z
            total = total + residual * z
            hand_out(j, x, k, x_mine_ref, core_ref, ROWS, rows)
            hand_out(j, z, k, z_mine_ref, core_ref, ROWS + 2 * rows, rows)
            if k == 0:
                firsts.append(z[:1])
            if k == chunks - 1:
                lasts.append(z[ROWS - 1 :])
    total_ref[...] = fold(total)
    none = jnp.zeros((4, width), F32)
    put_rows(stack_rows(firsts + [none]), stack_rows(lasts + [none]), core_ref.at[0:ROWS], cross_ref)
    own_parts(z_o_ref, z_i_ref, cx_ref, cy_ref, c_ref, pay_ref, scratch_ref)


def give_kernel(q_o_ref, q_i_ref, mine_ref, send_ref):
    rows = q_o_ref.shape[0]
    for j in range(4):
        hand_out(j, band_of(q_o_ref, q_i_ref, j)[...], 0, mine_ref, send_ref, 0, rows)


def last_kernel(mail_ref, x_mine_ref, z_mine_ref, got_ref, q_mine_ref, q_got_ref, out_ref, answer, sems):
    half = x_mine_ref.shape[1]
    places = []
    for band in range(2):
        mine = [ref.at[band] for ref in (x_mine_ref, z_mine_ref, q_mine_ref)]
        places.append((band, core(), mine))
        at = ROWS + band * half
        got = [got_ref.at[at : at + half], got_ref.at[at + 2 * half : at + 3 * half]]
        places.append((band, 1 - core(), got + [q_got_ref.at[band * half : (band + 1) * half]]))
    copies = []
    for n, (band, which, (x_ref, _, _)) in enumerate(places):
        copies.append(pltpu.make_async_copy(x_ref, out_ref.at[1, band, half_of(which, half), :], sems.at[n]))
        copies[-1].start()
    a, b = weights(mail_ref)
    for n, (band, which, (x_ref, z_ref, q_ref)) in enumerate(places):
        answer[n] = x_ref[...] + a * z_ref[...] + b * q_ref[...]
        copies.append(
            pltpu.make_async_copy(answer.at[n], out_ref.at[0, band, half_of(which, half), :], sems.at[4 + n])
        )
        copies[-1].start()
    for copy in copies:
        copy.wait()


def on_device(cond_x, cond_y, via_cond, via_mask, capacitance, pad_mask, observe):
    _, rows, width = cond_x.shape
    half = rows // 2
    field, three, four, edge = shape(half, width), shape(3, half, width), shape(4, half, width), shape(4, width)
    six, rim, pair = shape(6, width), shape(2, width), shape(2, half, width)
    mail = shape(lax.axis_size("band") * lax.axis_size("tile") * 4, 128)
    one, two = shape(ROWS, 128), shape(2 * ROWS, 128)
    fourteen = shape(14, half, width)
    whole, whole_int = pltpu.VMEM((2, rows, width), F32), pltpu.VMEM((2, rows, width), jnp.int32)
    own, send, pay, pay_send, last, middle = call(
        load_kernel, [fourteen, fourteen, field, field, rim, rim],
        cond_x, cond_y, via_cond, via_mask, capacitance, pad_mask, observe, name="load", place=pltpu.HBM,
        scratch=[whole, whole_int, whole_int, pltpu.SemaphoreType.DMA((13,))],
    )
    got, before = core_swap(pay_send), next_tile(last)
    got, send = lax.optimization_barrier((got, send))
    (pay,) = call(pay_kernel, [field], pay, got, name="pay")
    link, traded = outer_swap(pay), core_swap(send)
    own_edge, send_edge = call(edge_kernel, [rim, rim], middle, before, name="edges")
    got_edge = core_swap(send_edge)
    cx, cy, c, diag, inv_i, s_i, inv_o, s_o, cx_edge, near, cross, cap, earlier = call(
        prepare_kernel, [four, four, four, four, three, three, field, field, edge, six, six, four, four],
        own, traded, own_edge, got_edge, link, name="prepare",
    )
    far, sides = outer_swap(s_o), (core_swap(near), cross_swap(cross))
    inv_far = outer_swap(inv_o)

    coeffs = (cx, cy, c, inv_i, cx_edge)
    parts_of = [pltpu.VMEM((half, width), F32)]
    v1_i, part, sums = call(spread_kernel, [three, field, two], s_o, s_i, *sides, *coeffs, name="first_spread", cost=0)
    v1_i, inv_far = lax.optimization_barrier((v1_i, inv_far))
    v1_o, near, cross, t0, pay = call(
        far_first_kernel, [field, edge, edge, one, shape(2 * half, width)],
        s_o, part, far, c, inv_o, v1_i, sums, cx, cy, name="first_far", scratch=parts_of,
    )

    def stage(u_o, u_i, pay, near, cross, t0, inv_far, name):
        got, cross, near = outer_swap(pay), cross_swap(cross), core_swap(near)
        whole = pay.shape[0] == 2 * half
        near, cross, inv_far = lax.optimization_barrier((near, cross, inv_far))
        held = near
        v_i, part, sums, tail, near, cross = call(
            spread_kernel, [three, field, two, shape(ROWS, width), edge, edge],
            u_o, u_i, near, cross, *coeffs, name=name + "_spread", cost=0,
        )
        cross, tail, near = cross_swap(cross), outer_swap(tail), core_swap(near)
        v_o, t1 = call(far_kernel, [field, two], u_o, part, got, c, inv_o, sums, name=name + "_far")
        given = ()
        if not whole:
            mine, send = call(give_kernel, [pair, shape(2 * half, width)], v_o, v_i, name="give")
            given = mine, core_swap(send)
        t2, *rest = call(
            again_kernel, [one] + [three, field] * whole, v_o, v_i, near, cross, *coeffs, name=name + "_again"
        )
        args = [u_o, v_o, got, tail, near, cross, inv_far, c, cx, cx_edge, *sides, t0, t1, t2]

        def finish(*refs):
            n = len(args)
            cross_kernel(*refs[:n], *((refs[n + 2], *refs[n : n + 2], refs[n + 3]) if whole else refs[n:]))

        more_args = [rest[1], inv_o] if whole else []
        parts, *w_o = call(finish, [mail] + [field] * whole, *args, *more_args, name=name + "_cross")
        parts, given = lax.optimization_barrier((parts, given))
        return v_o, v_i, all_total(parts), inv_far, held, given, (*w_o, *rest[:1])

    v2_o, v2_i, total, inv_far, _, _, (v3_o, v3_i) = stage(v1_o, v1_i, pay, near, cross, t0, inv_far, "later")
    z_o, z_i, near, cross, t0, pay, x_mine, z_mine = call(
        step_kernel,
        [field, three, shape(ROWS + 4 * half, width), shape(ROWS, width), one, shape(half + half // 2, width), pair, pair],
        total, s_o, s_i, v1_o, v1_i, v2_o, v2_i, v3_o, v3_i, cap, earlier, diag, inv_o, inv_i, cx, cy, c,
        name="step", scratch=parts_of,
    )
    _, _, total, _, got, given, _ = stage(z_o, z_i, pay, near, cross, t0, inv_far, "earlier")
    (out,) = call(
        last_kernel, [shape(2, 2, rows, width)], total, x_mine, z_mine, got, *given, name="last", out_place=pl.ANY,
        scratch=[pltpu.VMEM((4, half, width), F32), pltpu.SemaphoreType.DMA((8,))],
    )
    return out


def solution(mesh):
    placed = (P("band", "tile", None),) * 6 + (P(None, "band", "tile", None),)
    return jax.shard_map(
        on_device,
        mesh=mesh,
        in_specs=placed,
        out_specs=P(None, "band", "tile", None),
        check_vma=False,
    )
```

time: 451 us -> 85.9 us (0.19)
  blocking collectives: 273 us -> 19.3 us
  starting transfers between devices: 77.4 us -> 24.1 us
  other arithmetic: 45.5 us -> 0 us
  Pallas kernels: 0 us -> 13.2 us
  local copies, waits for them, and re-layouts: 8.64 us -> 0 us
  between operations: 8.09 us -> 0.14 us
  waiting for transfers between devices: 35.7 us -> 28.9 us
    psum x6 -> x0, blocking collectives: 273 us -> none  [the longest x4 178 us: norm_total(): return lax.psum(value, ('band', 'tile'))]
    ppermute x26 -> x22, starting transfers between devices: 77.4 us -> 24.1 us  [the longest x5 12 us: cross_swap(): return lax.ppermute(x, AXES, pairs)]
    all_to_all x0 -> x2, blocking collectives: none -> 19.3 us  [all_total(): return lax.all_to_all(parts, AXES, 0, 0, tiled=True)]
    reduce_sum x6 -> x0, other arithmetic: 19 us -> none  [the longest x4 14.2 us: solve_two(): step_len = norm_now / curve_total(jnp.sum(search * image_vec))]
    pallas_call x0 -> x17, Pallas kernels: none -> 13.2 us  [call(): pl.pallas_call(body, out_shape=outs, in_specs=[pl.BlockSpec(memory_space=...]
    concatenate x14 -> x0, other arithmetic: 8.1 us -> none  [the longest x12 5.48 us: with_halo(): block = jnp.concatenate([low, block, high], axis=dim)]
    div x3 -> x0, other arithmetic: 6.83 us -> none  [the longest x2 5.09 us: solve_two(): search = residual / scale]
    ppermute x26 -> x22, waiting for transfers between devices: 35.7 us -> 28.9 us  [the longest x5 15 us: cross_swap(): return lax.ppermute(x, AXES, pairs)]
  transfers between devices with their start and end apart: 26 -> 22, of which waited for: 18 -> 12; matrix products, arithmetic and copies ran while one was open for 2% -> 0% of each run, Pallas kernels for 0% -> 6%
where the time goes in v2:
time: 85.9 us; the launch traced here: 85.7 us
  waiting for transfers between devices  28.9 us (34%)
  starting transfers between devices  24.1 us (28%)
  blocking collectives  19.3 us (22%)
  Pallas kernels  13.2 us (15%)
    all_to_all x2, blocking collectives, all_total(): return lax.all_to_all(parts, AXES, 0, 0, tiled=True)  19.3 us
    ppermute x5, waiting for transfers between devices, cross_swap(): return lax.ppermute(x, AXES, pairs)  15 us
    pallas_call x17, Pallas kernels, call(): pl.pallas_call(body, out_shape=outs, in_specs=[pl.BlockSpec(memory_space=...  13.2 us
    ppermute x5, starting transfers between devices, cross_swap(): return lax.ppermute(x, AXES, pairs)  12 us
    ppermute x7, waiting for transfers between devices, outer_swap(): return lax.ppermute(x, 'band', [(b, b ^ 2) for b in range(nb)])  8.44 us
    ppermute x7, starting transfers between devices, outer_swap(): return lax.ppermute(x, 'band', [(b, b ^ 2) for b in range(nb)])  8.17 us
    ppermute x1, waiting for transfers between devices, next_tile(): return lax.ppermute(x, 'tile', [(t, (t + 1) % nt) for t in range(nt)])  3.11 us
    ppermute x1, starting transfers between devices, next_tile(): return lax.ppermute(x, 'tile', [(t, (t + 1) % nt) for t in range(nt)])  2.64 us
  transfers between devices with their start and end apart: 22, of which 12 were waited for; matrix products, arithmetic and copies ran while one was open for 0% of the time, Pallas kernels for 6%

profile of v2, /device:TPU:0, one launch (start us, length us, event | category | flops | bytes accessed | tf_op | source)
XLA Modules:
  0.0 85.7 jit_solution(11484149429109259679)
XLA Ops:
  0.0 3.8 %load.1 = (f32[14,32,2048]{2,1,0:T(8,128)S(1)}, f32[14,32,2048]{2,1,0:T(8,128)S(1)}, f32[32,2048]{1,0:T(8,128)S(1)}, f32[32,2048]{1,0:T(8,128)S(1)}, f32[2,2048]{1,0:T(2,128)S(1)}, /*index=5*/f32[2,2048]{1,0:T(2,128)S(1)}) custom-call(f32[2,64,2048]{2,1,0:T(8,128)} %cond_x_ref.1, f32[2,64,2048]{2,1,0:T(8,128)} %cond_y_ref.1, f32[2,64,2048]{2,1,0:T(8,128)} %via_ref.1, ...), custom_call_target="tpu_custom_call" | custom-call | flops 10000000000 | bytes 10000000 | tf_op jit(solution)/shard_map/load/pallas_call | solution.py:60
  3.8 0.5 collective-permute-start
  4.3 1.2 %collective-permute-done.got_ref = f32[32,2048]{1,0:T(8,128)S(1)} collective-permute-done((f32[32,2048]{1,0:T(8,128)S(1)}, f32[32,2048]{1,0:T(8,128)S(1)}, u32[]{:S(2)}, u32[]{:S(2)}) %collective-permute-start) | collective-permute-done | bytes 262176 | tf_op jit(solution)/shard_map/ppermute | solution.py:30
  5.5 0.4 collective-permute-start.1
  5.9 2.6 %collective-permute-start.2 = (f32[2,2048]{1,0:T(2,128)S(1)}, f32[2,2048]{1,0:T(2,128)S(1)}, u32[]{:S(2)}, u32[]{:S(2)}) collective-permute-start(f32[2,2048]{1,0:T(2,128)S(1)} %get-tuple-element.83), channel_id=1, source_target_pairs={{0,1},{1,2},{2,3},{3,4},{4,5},{5,6},{6,7},{7,0},{8,9},{9,10},{10,1... | collective-permute-start | bytes 49160 | tf_op jit(solution)/shard_map/ppermute | solution.py:40
  8.6 1.6 %collective-permute-start.4 = (f32[32,2048]{1,0:T(8,128)S(1)}, f32[32,2048]{1,0:T(8,128)S(1)}, u32[]{:S(2)}, u32[]{:S(2)}) collective-permute-start(f32[32,2048]{1,0:T(8,128)S(1)} %pay.1), channel_id=1, source_target_pairs={{0,16},{8,24},{16,0},{24,8},{1,17},{9,25},{17,1},{25,9},{2,18},{10... | collective-permute-start | bytes 786440 | tf_op jit(solution)/shard_map/ppermute | solution.py:35
  10.1 3.1 %collective-permute-done.2.before_ref = f32[2,2048]{1,0:T(2,128)S(1)} collective-permute-done((f32[2,2048]{1,0:T(2,128)S(1)}, f32[2,2048]{1,0:T(2,128)S(1)}, u32[]{:S(2)}, u32[]{:S(2)}) %collective-permute-start.2) | collective-permute-done | bytes 16416 | tf_op jit(solution)/shard_map/ppermute | solution.py:40
  13.3 1.2 %collective-permute-done.3.got_edge_ref = f32[2,2048]{1,0:T(2,128)S(1)} collective-permute-done((f32[2,2048]{1,0:T(2,128)S(1)}, f32[2,2048]{1,0:T(2,128)S(1)}, u32[]{:S(2)}, u32[]{:S(2)}) %collective-permute-start.3) | collective-permute-done | bytes 16416 | tf_op jit(solution)/shard_map/ppermute | solution.py:30
  14.4 2.5 %collective-permute-done.4.link_ref = f32[32,2048]{1,0:T(8,128)S(1)} collective-permute-done((f32[32,2048]{1,0:T(8,128)S(1)}, f32[32,2048]{1,0:T(8,128)S(1)}, u32[]{:S(2)}, u32[]{:S(2)}) %collective-permute-start.4) | collective-permute-done | bytes 262176 | tf_op jit(solution)/shard_map/ppermute | solution.py:35
  16.9 1.2 %prepare.1 = (f32[4,32,2048]{2,1,0:T(8,128)S(1)}, f32[4,32,2048]{2,1,0:T(8,128)S(1)}, f32[4,32,2048]{2,1,0:T(8,128)S(1)}, f32[4,32,2048]{2,1,0:T(8,128)S(1)}, f3...) custom-call(f32[14,32,2048]{2,1,0:T(8,128)S(1)} %get-tuple-element.7, ...), custom_call_target="tpu_custom_call" | custom-call | flops 10000000000 | bytes 10000000 | tf_op jit(solution)/shard_map/prepare/pallas_call | solution.py:60
  18.1 1.6 %collective-permute-start.8 = (f32[32,2048]{1,0:T(8,128)S(1)}, f32[32,2048]{1,0:T(8,128)S(1)}, u32[]{:S(2)}, u32[]{:S(2)}) collective-permute-start(f32[32,2048]{1,0:T(8,128)S(1)} %get-tuple-element.98.inv_ref.refs_16_.inv_o_ref), channel_id=1, source_target_pairs={{0,16},{8,24},{16,0},{24,8},{1,17},{9,25},{17,1},{25,9},{2,18},{10... | collective-permute-start | bytes 786440 | tf_op jit(solution)/shard_map/ppermute | solution.py:35
  19.7 0.5 collective-permute-start.7
  20.2 3.4 %collective-permute-start.6 = (f32[6,2048]{1,0:T(8,128)S(1)}, f32[6,2048]{1,0:T(8,128)S(1)}, u32[]{:S(2)}, u32[]{:S(2)}) collective-permute-start(f32[6,2048]{1,0:T(8,128)S(1)} %get-tuple-element.91), channel_id=1, source_target_pairs={{0,15},{1,8},{2,9},{3,10},{4,11},{5,12},{6,13},{7,14},{8,1},{9,2},... | collective-permute-start | bytes 147464 | tf_op jit(solution)/shard_map/ppermute | solution.py:50
  23.6 3.0 %collective-permute-done.6.cross_ref.refs_11_ = f32[6,2048]{1,0:T(8,128)S(1)} collective-permute-done((f32[6,2048]{1,0:T(8,128)S(1)}, f32[6,2048]{1,0:T(8,128)S(1)}, u32[]{:S(2)}, u32[]{:S(2)}) %collective-permute-start.6) | collective-permute-done | bytes 49184 | tf_op jit(solution)/shard_map/ppermute | solution.py:50
  26.6 0.9 %first_spread.1 = (f32[3,32,2048]{2,1,0:T(8,128)S(1)}, f32[32,2048]{1,0:T(8,128)S(1)}, f32[16,128]{1,0:T(8,128)S(1)}) custom-call(f32[32,2048]{1,0:T(8,128)S(1)} %get-tuple-element.88.u_o_ref.s_o_ref, f32[3,32,2048]{2,1,0:T(8,128)S(1)} %get-tuple-element.89.u_i_ref.s_i_ref, f32[6,2048]{1,0:T(8,128)S(1)} %collective-permute-done.5.core_ref.refs_10_, ...), custom_call_target="tpu_custom_call" | custom-call | tf_op jit(solution)/shard_map/first_spread/pallas_call | solution.py:60
  27.5 3.8 %collective-permute-done.7.far_ref = f32[32,2048]{1,0:T(8,128)S(1)} collective-permute-done((f32[32,2048]{1,0:T(8,128)S(1)}, f32[32,2048]{1,0:T(8,128)S(1)}, u32[]{:S(2)}, u32[]{:S(2)}) %collective-permute-start.7) | collective-permute-done | bytes 262176 | tf_op jit(solution)/shard_map/ppermute | solution.py:35
  31.2 0.3 first_far.1
  31.5 1.6 %collective-permute-start.11 = (f32[64,2048]{1,0:T(8,128)S(1)}, f32[64,2048]{1,0:T(8,128)S(1)}, u32[]{:S(2)}, u32[]{:S(2)}) collective-permute-start(f32[64,2048]{1,0:T(8,128)S(1)} %get-tuple-element.109), channel_id=1, source_target_pairs={{0,16},{8,24},{16,0},{24,8},{1,17},{9,25},{17,1},{25,9},{2,18},{10... | collective-permute-start | bytes 1572872 | tf_op jit(solution)/shard_map/ppermute | solution.py:35
  33.1 3.5 %collective-permute-start.10 = (f32[4,2048]{1,0:T(4,128)S(1)}, f32[4,2048]{1,0:T(4,128)S(1)}, u32[]{:S(2)}, u32[]{:S(2)}) collective-permute-start(f32[4,2048]{1,0:T(4,128)S(1)} %get-tuple-element.104), channel_id=1, source_target_pairs={{0,15},{1,8},{2,9},{3,10},{4,11},{5,12},{6,13},{7,14},{8,1},{9,2},... | collective-permute-start | bytes 98312 | tf_op jit(solution)/shard_map/ppermute | solution.py:50
  36.6 2.5 %collective-permute-done.10.cross_ref = f32[4,2048]{1,0:T(4,128)S(1)} collective-permute-done((f32[4,2048]{1,0:T(4,128)S(1)}, f32[4,2048]{1,0:T(4,128)S(1)}, u32[]{:S(2)}, u32[]{:S(2)}) %collective-permute-start.10) | collective-permute-done | bytes 32800 | tf_op jit(solution)/shard_map/ppermute | solution.py:50
  39.1 1.0 %later_spread.1 = (f32[3,32,2048]{2,1,0:T(8,128)S(1)}, f32[32,2048]{1,0:T(8,128)S(1)}, f32[16,128]{1,0:T(8,128)S(1)}, f32[8,2048]{1,0:T(8,128)S(1)}, f32[4,2048]{1,0:T(4,128)S(1)}, /*index=5*/f32[4,2048]{1,0:T(4,128)S(1)}) custom-call(f32[32,2048]{1,0:T(8,128)S(1)} %get-tuple-element.102.u_o_ref.refs_0_.v1_o_ref, ...), custom_call_target="tpu_custom_call" | custom-call | tf_op jit(solution)/shard_map/later_spread/pallas_call | solution.py:60
  40.2 0.1 collective-permute-start.13
  40.3 3.6 %collective-permute-start.14 = (f32[4,2048]{1,0:T(4,128)S(1)}, f32[4,2048]{1,0:T(4,128)S(1)}, u32[]{:S(2)}, u32[]{:S(2)}) collective-permute-start(f32[4,2048]{1,0:T(4,128)S(1)} %get-tuple-element.114), channel_id=1, source_target_pairs={{0,15},{1,8},{2,9},{3,10},{4,11},{5,12},{6,13},{7,14},{8,1},{9,2},... | collective-permute-start | bytes 98312 | tf_op jit(solution)/shard_map/ppermute | solution.py:50
  43.9 0.7 collective-permute-start.12
  44.6 0.1 later_far.1
  44.7 1.7 %collective-permute-done.14.cross_ref.refs_5_ = f32[4,2048]{1,0:T(4,128)S(1)} collective-permute-done((f32[4,2048]{1,0:T(4,128)S(1)}, f32[4,2048]{1,0:T(4,128)S(1)}, u32[]{:S(2)}, u32[]{:S(2)}) %collective-permute-start.14) | collective-permute-done | bytes 32800 | tf_op jit(solution)/shard_map/ppermute | solution.py:50
  46.4 0.8 later_again.1
  47.2 0.9 %collective-permute-done.12.refs_3_ = f32[8,2048]{1,0:T(8,128)S(1)} collective-permute-done((f32[8,2048]{1,0:T(8,128)S(1)}, f32[8,2048]{1,0:T(8,128)S(1)}, u32[]{:S(2)}, u32[]{:S(2)}) %collective-permute-start.12) | collective-permute-done | bytes 65568 | tf_op jit(solution)/shard_map/ppermute | solution.py:35
  48.1 0.2 later_cross.1
  48.3 10.2 %all_to_all.22 = f32[32,4,128]{2,1,0:T(4,128)S(1)} all-to-all(f32[32,4,128]{2,1,0:T(4,128)S(1)} %bitcast.6), channel_id=1, replica_groups=mesh['band'=4,'tile'=8] {'band','tile'}, dimensions={0} | all-to-all | bytes 131072 | tf_op jit(solution)/shard_map/all_to_all | solution.py:54
  58.6 1.4 %step.1 = (f32[32,2048]{1,0:T(8,128)S(1)}, f32[3,32,2048]{2,1,0:T(8,128)S(1)}, f32[136,2048]{1,0:T(8,128)S(1)}, f32[8,2048]{1,0:T(8,128)S(1)}, f32[8,128]{1,0:T(...) custom-call(f32[128,128]{1,0:T(8,128)S(1)} %bitcast.4, ...), custom_call_target="tpu_custom_call" | custom-call | flops 10000000000 | bytes 10000000 | tf_op jit(solution)/shard_map/step/pallas_call | solution.py:60
  59.9 0.2 collective-permute-start.15
  60.1 0.7 collective-permute-start.17
  60.8 0.7 collective-permute-start.16
  61.5 5.7 %collective-permute-done.16.cross_ref = f32[8,2048]{1,0:T(8,128)S(1)} collective-permute-done((f32[8,2048]{1,0:T(8,128)S(1)}, f32[8,2048]{1,0:T(8,128)S(1)}, u32[]{:S(2)}, u32[]{:S(2)}) %collective-permute-start.16) | collective-permute-done | bytes 65568 | tf_op jit(solution)/shard_map/ppermute | solution.py:50
  67.2 0.9 %earlier_spread.1 = (f32[3,32,2048]{2,1,0:T(8,128)S(1)}, f32[32,2048]{1,0:T(8,128)S(1)}, f32[16,128]{1,0:T(8,128)S(1)}, f32[8,2048]{1,0:T(8,128)S(1)}, f32[4,2048]{1,0:T(4,128)S(1)}, /*index=5*/f32[4,2048]{1,0:T(4,128)S(1)}) custom-call(f32[32,2048]{1,0:T(8,128)S(1)} %get-tuple-element.127.u_o_ref.refs_0_, f32[3,32,2048]{2,1,0:T(8,128)S(1)} %get-tuple-element.128.u_i_ref, ...), custom_call_target="tpu_custom_call" | custom-call | tf_op jit(solution)/shard_map/earlier_spread/pallas_call | solution.py:60
  68.1 0.1 collective-permute-start.19
  68.2 0.8 collective-permute-start.20
  68.9 1.5 %collective-permute-start.18 = (f32[8,2048]{1,0:T(8,128)S(1)}, f32[8,2048]{1,0:T(8,128)S(1)}, u32[]{:S(2)}, u32[]{:S(2)}) collective-permute-start(f32[8,2048]{1,0:T(8,128)S(1)} %get-tuple-element.137), channel_id=1, source_target_pairs={{0,16},{8,24},{16,0},{24,8},{1,17},{9,25},{17,1},{25,9},{2,18},{10... | collective-permute-start | bytes 196616 | tf_op jit(solution)/shard_map/ppermute | solution.py:35
  70.5 1.3 %collective-permute-done.17.far_ref.refs_2_ = f32[48,2048]{1,0:T(8,128)S(1)} collective-permute-done((f32[48,2048]{1,0:T(8,128)S(1)}, f32[48,2048]{1,0:T(8,128)S(1)}, u32[]{:S(2)}, u32[]{:S(2)}) %collective-permute-start.17) | collective-permute-done | bytes 393248 | tf_op jit(solution)/shard_map/ppermute | solution.py:35
  71.7 0.1 earlier_far.1
  71.8 0.1 give.1
  72.0 0.1 collective-permute-start.21
  72.1 2.2 %collective-permute-done.20.cross_ref.refs_5_ = f32[4,2048]{1,0:T(4,128)S(1)} collective-permute-done((f32[4,2048]{1,0:T(4,128)S(1)}, f32[4,2048]{1,0:T(4,128)S(1)}, u32[]{:S(2)}, u32[]{:S(2)}) %collective-permute-start.20) | collective-permute-done | bytes 32800 | tf_op jit(solution)/shard_map/ppermute | solution.py:50
  74.3 0.8 earlier_again.1.refs_14_
  75.1 0.1 earlier_cross.1
  75.2 9.1 %all_to_all.23 = f32[32,4,128]{2,1,0:T(4,128)S(1)} all-to-all(f32[32,4,128]{2,1,0:T(4,128)S(1)} %bitcast.5), channel_id=1, replica_groups=mesh['band'=4,'tile'=8] {'band','tile'}, dimensions={0} | all-to-all | bytes 131072 | tf_op jit(solution)/shard_map/all_to_all | solution.py:54
  84.3 1.4 %last.1 = f32[2,2,64,2048]{3,2,1,0:T(8,128)} custom-call(f32[128,128]{1,0:T(8,128)S(1)} %bitcast.7, f32[2,32,2048]{2,1,0:T(8,128)S(1)} %get-tuple-element.147.x_mine_ref, f32[2,32,2048]{2,1,0:T(8,128)S(1)} %get-tuple-element.148.z_mine_ref, f32[136,2048]{1,0:T(8,128)S(1)} %collective-permute-done.15.core_ref.got_ref, ...), custom_call_target="tpu_custom_call" | custom-call | flops 10000000000 | bytes 10000000 | tf_op jit(solution)/shard_map/last/pallas_call | solution.py:60
  (15 shorter events, 0.1 us)
Async XLA Ops:
  3.8 1.7 %collective-permute-start = (f32[32,2048]{1,0:T(8,128)S(1)}, f32[32,2048]{1,0:T(8,128)S(1)}, u32[]{:S(2)}, u32[]{:S(2)}) collective-permute-start(f32[32,2048]{1,0:T(8,128)S(1)} %get-tuple-element.79), channel_id=1, source_target_pairs={{0,8},{8,0},{16,24},{24,16},{1,9},{9,1},{17,25},{25,17},{2,10},{10... | collective-permute-start | bytes 786440 | tf_op jit(solution)/shard_map/ppermute | solution.py:30
  5.5 11.4 %collective-permute-start.1 = (f32[14,32,2048]{2,1,0:T(8,128)S(1)}, f32[14,32,2048]{2,1,0:T(8,128)S(1)}, u32[]{:S(2)}, u32[]{:S(2)}) collective-permute-start(f32[14,32,2048]{2,1,0:T(8,128)S(1)} %get-tuple-element.81), channel_id=1, source_target_pairs={{0,8},{8,0},{16,24},{24,16},{1,9},{9,1},{17,25},{25,17},{2,10},{10... | collective-permute-start | bytes 11010056 | tf_op jit(solution)/shard_map/ppermute | solution.py:30
  5.9 7.4 %collective-permute-start.2 = (f32[2,2048]{1,0:T(2,128)S(1)}, f32[2,2048]{1,0:T(2,128)S(1)}, u32[]{:S(2)}, u32[]{:S(2)}) collective-permute-start(f32[2,2048]{1,0:T(2,128)S(1)} %get-tuple-element.83), channel_id=1, source_target_pairs={{0,1},{1,2},{2,3},{3,4},{4,5},{5,6},{6,7},{7,0},{8,9},{9,10},{10,1... | collective-permute-start | bytes 49160 | tf_op jit(solution)/shard_map/ppermute | solution.py:40
  8.6 8.4 %collective-permute-start.4 = (f32[32,2048]{1,0:T(8,128)S(1)}, f32[32,2048]{1,0:T(8,128)S(1)}, u32[]{:S(2)}, u32[]{:S(2)}) collective-permute-start(f32[32,2048]{1,0:T(8,128)S(1)} %pay.1), channel_id=1, source_target_pairs={{0,16},{8,24},{16,0},{24,8},{1,17},{9,25},{17,1},{25,9},{2,18},{10... | collective-permute-start | bytes 786440 | tf_op jit(solution)/shard_map/ppermute | solution.py:35
  13.3 1.2 %collective-permute-start.3 = (f32[2,2048]{1,0:T(2,128)S(1)}, f32[2,2048]{1,0:T(2,128)S(1)}, u32[]{:S(2)}, u32[]{:S(2)}) collective-permute-start(f32[2,2048]{1,0:T(2,128)S(1)} %get-tuple-element.85), channel_id=1, source_target_pairs={{0,8},{8,0},{16,24},{24,16},{1,9},{9,1},{17,25},{25,17},{2,10},{10... | collective-permute-start | bytes 49160 | tf_op jit(solution)/shard_map/ppermute | solution.py:30
  18.1 9.4 %collective-permute-start.8 = (f32[32,2048]{1,0:T(8,128)S(1)}, f32[32,2048]{1,0:T(8,128)S(1)}, u32[]{:S(2)}, u32[]{:S(2)}) collective-permute-start(f32[32,2048]{1,0:T(8,128)S(1)} %get-tuple-element.98.inv_ref.refs_16_.inv_o_ref), channel_id=1, source_target_pairs={{0,16},{8,24},{16,0},{24,8},{1,17},{9,25},{17,1},{25,9},{2,18},{10... | collective-permute-start | bytes 786440 | tf_op jit(solution)/shard_map/ppermute | solution.py:35
  19.7 11.6 %collective-permute-start.7 = (f32[32,2048]{1,0:T(8,128)S(1)}, f32[32,2048]{1,0:T(8,128)S(1)}, u32[]{:S(2)}, u32[]{:S(2)}) collective-permute-start(f32[32,2048]{1,0:T(8,128)S(1)} %get-tuple-element.88.u_o_ref.s_o_ref), channel_id=1, source_target_pairs={{0,16},{8,24},{16,0},{24,8},{1,17},{9,25},{17,1},{25,9},{2,18},{10... | collective-permute-start | bytes 786440 | tf_op jit(solution)/shard_map/ppermute | solution.py:35
  20.2 3.4 %collective-permute-start.5 = (f32[6,2048]{1,0:T(8,128)S(1)}, f32[6,2048]{1,0:T(8,128)S(1)}, u32[]{:S(2)}, u32[]{:S(2)}) collective-permute-start(f32[6,2048]{1,0:T(8,128)S(1)} %get-tuple-element.90), channel_id=1, source_target_pairs={{0,8},{8,0},{16,24},{24,16},{1,9},{9,1},{17,25},{25,17},{2,10},{10... | collective-permute-start | bytes 147464 | tf_op jit(solution)/shard_map/ppermute | solution.py:30
  20.2 6.4 %collective-permute-start.6 = (f32[6,2048]{1,0:T(8,128)S(1)}, f32[6,2048]{1,0:T(8,128)S(1)}, u32[]{:S(2)}, u32[]{:S(2)}) collective-permute-start(f32[6,2048]{1,0:T(8,128)S(1)} %get-tuple-element.91), channel_id=1, source_target_pairs={{0,15},{1,8},{2,9},{3,10},{4,11},{5,12},{6,13},{7,14},{8,1},{9,2},... | collective-permute-start | bytes 147464 | tf_op jit(solution)/shard_map/ppermute | solution.py:50
  31.5 13.1 %collective-permute-start.11 = (f32[64,2048]{1,0:T(8,128)S(1)}, f32[64,2048]{1,0:T(8,128)S(1)}, u32[]{:S(2)}, u32[]{:S(2)}) collective-permute-start(f32[64,2048]{1,0:T(8,128)S(1)} %get-tuple-element.109), channel_id=1, source_target_pairs={{0,16},{8,24},{16,0},{24,8},{1,17},{9,25},{17,1},{25,9},{2,18},{10... | collective-permute-start | bytes 1572872 | tf_op jit(solution)/shard_map/ppermute | solution.py:35
  33.1 3.5 %collective-permute-start.9 = (f32[4,2048]{1,0:T(4,128)S(1)}, f32[4,2048]{1,0:T(4,128)S(1)}, u32[]{:S(2)}, u32[]{:S(2)}) collective-permute-start(f32[4,2048]{1,0:T(4,128)S(1)} %get-tuple-element.103), channel_id=1, source_target_pairs={{0,8},{8,0},{16,24},{24,16},{1,9},{9,1},{17,25},{25,17},{2,10},{10... | collective-permute-start | bytes 98312 | tf_op jit(solution)/shard_map/ppermute | solution.py:30
  33.1 6.0 %collective-permute-start.10 = (f32[4,2048]{1,0:T(4,128)S(1)}, f32[4,2048]{1,0:T(4,128)S(1)}, u32[]{:S(2)}, u32[]{:S(2)}) collective-permute-start(f32[4,2048]{1,0:T(4,128)S(1)} %get-tuple-element.104), channel_id=1, source_target_pairs={{0,15},{1,8},{2,9},{3,10},{4,11},{5,12},{6,13},{7,14},{8,1},{9,2},... | collective-permute-start | bytes 98312 | tf_op jit(solution)/shard_map/ppermute | solution.py:50
  40.2 4.5 %collective-permute-start.13 = (f32[4,2048]{1,0:T(4,128)S(1)}, f32[4,2048]{1,0:T(4,128)S(1)}, u32[]{:S(2)}, u32[]{:S(2)}) collective-permute-start(f32[4,2048]{1,0:T(4,128)S(1)} %get-tuple-element.113), channel_id=1, source_target_pairs={{0,8},{8,0},{16,24},{24,16},{1,9},{9,1},{17,25},{25,17},{2,10},{10... | collective-permute-start | bytes 98312 | tf_op jit(solution)/shard_map/ppermute | solution.py:30
  40.3 6.1 %collective-permute-start.14 = (f32[4,2048]{1,0:T(4,128)S(1)}, f32[4,2048]{1,0:T(4,128)S(1)}, u32[]{:S(2)}, u32[]{:S(2)}) collective-permute-start(f32[4,2048]{1,0:T(4,128)S(1)} %get-tuple-element.114), channel_id=1, source_target_pairs={{0,15},{1,8},{2,9},{3,10},{4,11},{5,12},{6,13},{7,14},{8,1},{9,2},... | collective-permute-start | bytes 98312 | tf_op jit(solution)/shard_map/ppermute | solution.py:50
  43.9 4.3 %collective-permute-start.12 = (f32[8,2048]{1,0:T(8,128)S(1)}, f32[8,2048]{1,0:T(8,128)S(1)}, u32[]{:S(2)}, u32[]{:S(2)}) collective-permute-start(f32[8,2048]{1,0:T(8,128)S(1)} %get-tuple-element.112), channel_id=1, source_target_pairs={{0,16},{8,24},{16,0},{24,8},{1,17},{9,25},{17,1},{25,9},{2,18},{10... | collective-permute-start | bytes 196616 | tf_op jit(solution)/shard_map/ppermute | solution.py:35
  59.9 7.2 %collective-permute-start.15 = (f32[136,2048]{1,0:T(8,128)S(1)}, f32[136,2048]{1,0:T(8,128)S(1)}, u32[]{:S(2)}, u32[]{:S(2)}) collective-permute-start(f32[136,2048]{1,0:T(8,128)S(1)} %get-tuple-element.129), channel_id=1, source_target_pairs={{0,8},{8,0},{16,24},{24,16},{1,9},{9,1},{17,25},{25,17},{2,10},{10... | collective-permute-start | bytes 3342344 | tf_op jit(solution)/shard_map/ppermute | solution.py:30
  60.1 11.6 %collective-permute-start.17 = (f32[48,2048]{1,0:T(8,128)S(1)}, f32[48,2048]{1,0:T(8,128)S(1)}, u32[]{:S(2)}, u32[]{:S(2)}) collective-permute-start(f32[48,2048]{1,0:T(8,128)S(1)} %get-tuple-element.134), channel_id=1, source_target_pairs={{0,16},{8,24},{16,0},{24,8},{1,17},{9,25},{17,1},{25,9},{2,18},{10... | collective-permute-start | bytes 1179656 | tf_op jit(solution)/shard_map/ppermute | solution.py:35
  60.8 6.4 %collective-permute-start.16 = (f32[8,2048]{1,0:T(8,128)S(1)}, f32[8,2048]{1,0:T(8,128)S(1)}, u32[]{:S(2)}, u32[]{:S(2)}) collective-permute-start(f32[8,2048]{1,0:T(8,128)S(1)} %get-tuple-element.130), channel_id=1, source_target_pairs={{0,15},{1,8},{2,9},{3,10},{4,11},{5,12},{6,13},{7,14},{8,1},{9,2},... | collective-permute-start | bytes 196616 | tf_op jit(solution)/shard_map/ppermute | solution.py:50
  68.1 4.0 %collective-permute-start.19 = (f32[4,2048]{1,0:T(4,128)S(1)}, f32[4,2048]{1,0:T(4,128)S(1)}, u32[]{:S(2)}, u32[]{:S(2)}) collective-permute-start(f32[4,2048]{1,0:T(4,128)S(1)} %get-tuple-element.138), channel_id=1, source_target_pairs={{0,8},{8,0},{16,24},{24,16},{1,9},{9,1},{17,25},{25,17},{2,10},{10... | collective-permute-start | bytes 98312 | tf_op jit(solution)/shard_map/ppermute | solution.py:30
  68.2 6.1 %collective-permute-start.20 = (f32[4,2048]{1,0:T(4,128)S(1)}, f32[4,2048]{1,0:T(4,128)S(1)}, u32[]{:S(2)}, u32[]{:S(2)}) collective-permute-start(f32[4,2048]{1,0:T(4,128)S(1)} %get-tuple-element.139), channel_id=1, source_target_pairs={{0,15},{1,8},{2,9},{3,10},{4,11},{5,12},{6,13},{7,14},{8,1},{9,2},... | collective-permute-start | bytes 98312 | tf_op jit(solution)/shard_map/ppermute | solution.py:50
  68.9 6.1 %collective-permute-start.18 = (f32[8,2048]{1,0:T(8,128)S(1)}, f32[8,2048]{1,0:T(8,128)S(1)}, u32[]{:S(2)}, u32[]{:S(2)}) collective-permute-start(f32[8,2048]{1,0:T(8,128)S(1)} %get-tuple-element.137), channel_id=1, source_target_pairs={{0,16},{8,24},{16,0},{24,8},{1,17},{9,25},{17,1},{25,9},{2,18},{10... | collective-permute-start | bytes 196616 | tf_op jit(solution)/shard_map/ppermute | solution.py:35
  72.0 3.2 %collective-permute-start.21 = (f32[64,2048]{1,0:T(8,128)S(1)}, f32[64,2048]{1,0:T(8,128)S(1)}, u32[]{:S(2)}, u32[]{:S(2)}) collective-permute-start(f32[64,2048]{1,0:T(8,128)S(1)} %get-tuple-element.145), channel_id=1, source_target_pairs={{0,8},{8,0},{16,24},{24,16},{1,9},{9,1},{17,25},{25,17},{2,10},{10... | collective-permute-start | bytes 1572872 | tf_op jit(solution)/shard_map/ppermute | solution.py:30

commit v3 on v2

--- a/solution.py
+++ b/solution.py
@@ -33,11 +33,6 @@
 def outer_swap(x):
     nb, _ = sizes()
     return lax.ppermute(x, "band", [(b, b ^ 2) for b in range(nb)])
-
-
-def next_tile(x):
-    _, nt = sizes()
-    return lax.ppermute(x, "tile", [(t, (t + 1) % nt) for t in range(nt)])
 
 
 def cross_swap(x):
@@ -85,6 +80,15 @@
     lower = core() == 1
     core_ref[...] = jnp.where(lower, first, last)
     cross_ref[...] = jnp.where(lower, last, first)
+
+
+def put_two_rows(u_o_ref, u_i_ref, core_ref, cross_ref):
+    rows = u_o_ref.shape[0]
+    ends = [
+        stack_rows([band_of(u_o_ref, u_i_ref, j)[r : r + 1, :] for r in pair for j in range(4)])
+        for pair in ((0, 1), (rows - 1, rows - 2))
+    ]
+    put_rows(ends[0], ends[1], core_ref, cross_ref)
 
 
 def take_rows(core_ref, cross_ref):
@@ -166,22 +170,20 @@
         for band in range(2):
             ref[4 + band] = via_at[band, rs, :] * mask_at[band, rs, :].astype(F32)
             ref[6 + band] = ref[10 + band] + pad_conductance * pad_at[band, rs, :].astype(F32)
-        pay_ref[...] = jnp.where(upper_chip(), ref[8], ref[5])
+        pay_ref[0:half, :] = jnp.where(upper_chip(), ref[8], ref[5])
     for band in range(2):
         own, other = mine_ref[band, half - 1 :, :], send_ref[band, half - 1 :, :]
         last_ref[band : band + 1, :] = jnp.where(me == 1, own, other)
         middle_ref[band : band + 1, :] = jnp.where(me == 1, other, own)
-
-
-def pay_kernel(mine_ref, got_ref, pay_ref):
-    pay_ref[...] = jnp.where((core() == 1) == upper_chip(), got_ref[...], mine_ref[...])
-
-
-def edge_kernel(middle_ref, before_ref, own_ref, send_ref):
-    lower = core() == 1
-    middle, before = middle_ref[...], before_ref[...]
-    own_ref[...] = jnp.where(lower, middle, before)
-    send_ref[...] = jnp.where(lower, before, middle)
+    none = jnp.zeros((ROWS - 4, middle_ref.shape[1]), F32)
+    pay_send_ref[half:, :] = stack_rows([middle_ref[...], last_ref[...], none])
+
+
+def pay_kernel(mine_ref, got_ref, last_ref, pay_ref, all_last_ref):
+    pay_ref[...] = jnp.where((core() == 1) == upper_chip(), got_ref[0 : pay_ref.shape[0], :], mine_ref[...])
+    half = pay_ref.shape[0]
+    own, other = last_ref[...], got_ref[half + 2 : half + 4, :]
+    all_last_ref[...] = stack_rows([jnp.where(core() == 0, own, other), jnp.where(core() == 0, other, own)])
 
 
 def place_of(owner, band):
@@ -190,7 +192,7 @@
 
 
 def prepare_kernel(
-    mine_ref, got_ref, own_edge_ref, got_edge_ref, link_ref,
+    mine_ref, got_ref, link_ref, middle_ref, more_ref, last_ref,
     cx_ref, cy_ref, c_ref, diag_ref, inv_i_ref, s_i_ref, inv_o_ref, s_o_ref, edge_ref, core_ref, cross_ref, cap_ref, seen_ref,
 ):
     half, width = s_o_ref.shape
@@ -199,7 +201,9 @@
     lane = lax.broadcasted_iota(jnp.int32, (ROWS, width), 1)
     first_tile = jnp.logical_and(me == 0, lax.axis_index("tile") == 0)
     places = []
-    for owner, ref, edges in ((me, mine_ref, own_edge_ref), (1 - me, got_ref, got_edge_ref)):
+    own_edge = jnp.where(me == 1, middle_ref[...], last_ref[0:2, :])
+    got_edge = jnp.where(me == 1, more_ref[half : half + 2, :], last_ref[2:4, :])
+    for owner, ref, edges in ((me, mine_ref, own_edge), (1 - me, got_ref, got_edge)):
         for band in range(2):
             j = place_of(owner, band)
             places.append((j, ref, band))
@@ -249,10 +253,13 @@
             s_ref = band_of(s_o_ref, s_i_ref, j)
             s_ref[rs, :] = s_ref[rs, :] * inv
     ends = []
-    for r in (0, half - 1):
+    for r, beyond in ((0, 0), (half - 1, half - 2)):
         at = slice(r, r + 1)
         rows = [band_of(s_o_ref, s_i_ref, j)[at, :] for j in range(4)]
-        ends.append(stack_rows(rows + [inv_o_ref[at, :], c_ref[0, at, :]]))
+        rows += [band_of(inv_o_ref, inv_i_ref, j)[at, :] for j in range(4)]
+        for ref, row in ((cy_ref, r), (c_ref, r), (cx_ref, beyond)):
+            rows += [ref[j, row : row + 1, :] for j in range(4)]
+        ends.append(stack_rows(rows))
     put_rows(ends[0], ends[1], core_ref, cross_ref)
 
 
@@ -266,21 +273,23 @@
         x, part, carried = in_band(u_o_ref, cx_ref.at[0], cy_ref.at[0], carried, none, k, chunks)
         pay_ref[rs, :] = x
         scratch_ref[rs, :] = part + c_ref[1, rs, :] * u_i_ref[0, rs, :]
-    size = pay_ref.shape[0] - rows
+    size = rows // 2
     first = jnp.where(upper_chip(), 0, rows - size)
-    pay_ref[rows:, :] = scratch_ref[pl.ds(pl.multiple_of(first, ROWS), size), :]
+    pay_ref[rows : rows + size, :] = scratch_ref[pl.ds(pl.multiple_of(first, ROWS), size), :]
 
 
 def spread_kernel(
-    u_o_ref, u_i_ref, core_ref, cross_ref, cx_ref, cy_ref, c_ref, inv_i_ref, edge_ref,
-    v_i_ref, part_ref, sums_ref, tail_ref=None, v_core_ref=None, v_cross_ref=None,
+    u_o_ref, u_i_ref, core_ref, cross_ref, cx_ref, cy_ref, c_ref, inv_i_ref, edge_ref, v_i_ref, part_ref, sums_ref
 ):
+    above, below = take_rows(core_ref, cross_ref)
+    spread_rows(u_o_ref, u_i_ref, above, below, cx_ref, cy_ref, c_ref, inv_i_ref, edge_ref, v_i_ref, part_ref, sums_ref)
+
+
+def spread_rows(u_o_ref, u_i_ref, above, below, cx_ref, cy_ref, c_ref, inv_i_ref, edge_ref, v_i_ref, part_ref, sums_ref):
     rows, width = u_o_ref.shape
     chunks = rows // ROWS
-    above, below = take_rows(core_ref, cross_ref)
     carried = [edge_ref[j : j + 1, :] * above[j : j + 1] for j in range(4)]
     sums = [jnp.zeros((ROWS, width), F32) for _ in range(2)]
-    ends = [None, None]
     for k in range(chunks):
         rs = slice(k * ROWS, (k + 1) * ROWS)
         xs, parts = [], []
@@ -292,23 +301,59 @@
             parts.append(part)
         parts = couple(xs, parts, c_ref, rs)
         part_ref[rs, :] = parts[0]
-        vs = [parts[0]]
         for j in range(1, 4):
             v = inv_i_ref[j - 1, rs, :] * parts[j]
             v_i_ref[j - 1, rs, :] = v
             sums[0] = sums[0] + xs[j] * parts[j]
             sums[1] = sums[1] + v * parts[j]
-            vs.append(v)
-        if k == 0:
-            ends[0] = stack_rows([v[:1] for v in vs])
-        if k == chunks - 1:
-            ends[1] = stack_rows([v[ROWS - 1 :] for v in vs])
     sums_ref[0:ROWS, :] = fold(sums[0])
     sums_ref[ROWS : 2 * ROWS, :] = fold(sums[1])
-    if tail_ref is not None:
-        fluxes = [edge_ref[0:1, :] * above[0:1], cx_ref[0, rows - 1 :, :] * below[0:1]]
-        tail_ref[...] = stack_rows([above[0:1], below[0:1], *fluxes, jnp.zeros((ROWS - 4, width), F32)])
-        put_rows(ends[0], ends[1], v_core_ref, v_cross_ref)
+
+
+def beside(u_o_ref, u_i_ref, above, below, side_above, side_below, edge_ref, cx_ref):
+    rows, width = u_o_ref.shape
+    here = stack_rows([above[0:4], below[0:4]])
+    beyond = stack_rows([above[4:8], below[4:8]])
+    inside = [band_of(u_o_ref, u_i_ref, j)[r : r + 1, :] for r in (0, rows - 1) for j in range(4)]
+    toward = stack_rows([edge_ref[...]] + [cx_ref[j, rows - 1 :, :] for j in range(4)])
+    inv, cy, c, away = (stack_rows([side_above[n : n + 4], side_below[n : n + 4]]) for n in (4, 8, 12, 16))
+    c = jnp.where(jnp.logical_or(row_at(width, 0), row_at(width, 4)), 0.0, c)
+    total = toward * stack_rows(inside) + away * beyond
+    total = total + cy * pltpu.roll(here, width - 1, 1) + pltpu.roll(cy * here, 1, 1)
+    return total + c * pltpu.roll(here, 1, 0) + pltpu.roll(c * here, ROWS - 1, 0), inv
+
+
+def two_spread_kernel(
+    u_o_ref, u_i_ref, core_ref, cross_ref, cx_ref, cy_ref, c_ref, inv_i_ref, edge_ref, side_core_ref, side_cross_ref,
+    v_i_ref, part_ref, sums_ref, tail_ref, beside_ref, total_ref, w_ref=None,
+):
+    rows, width = u_o_ref.shape
+    chunks = rows // ROWS
+    above, below = take_rows(core_ref, cross_ref)
+    spread_rows(u_o_ref, u_i_ref, above, below, cx_ref, cy_ref, c_ref, inv_i_ref, edge_ref, v_i_ref, part_ref, sums_ref)
+    fluxes = [edge_ref[0:1, :] * above[0:1], cx_ref[0, rows - 1 :, :] * below[0:1]]
+    tail_ref[...] = stack_rows([above[0:1], below[0:1], *fluxes, jnp.zeros((ROWS - 4, width), F32)])
+    side_above, side_below = take_rows(side_core_ref, side_cross_ref)
+    parts_there, inv = beside(u_o_ref, u_i_ref, above, below, side_above, side_below, edge_ref, cx_ref)
+    beside_ref[...] = parts_there
+    v_there = inv * parts_there
+    carried = [edge_ref[j : j + 1, :] * v_there[j : j + 1] for j in range(1, 4)]
+    total = jnp.zeros((ROWS, width), F32)
+    for k in range(chunks):
+        rs = slice(k * ROWS, (k + 1) * ROWS)
+        xs, parts = [], []
+        for j in range(1, 4):
+            x, part, carried[j - 1] = in_band(
+                v_i_ref.at[j - 1], cx_ref.at[j], cy_ref.at[j], carried[j - 1], v_there[4 + j : 5 + j], k, chunks
+            )
+            xs.append(x)
+            parts.append(part)
+        parts = couple(xs, parts, c_ref.at[pl.ds(1, 3)], rs)
+        for j in range(3):
+            total = total + xs[j] * parts[j]
+            if w_ref is not None:
+                w_ref[j, rs, :] = parts[j]
+    total_ref[...] = fold(total)
 
 
 def far_first_kernel(
@@ -324,95 +369,67 @@
         v_ref[rs, :] = v
         total = total + v * part
     total_ref[...] = fold(total) + sums_ref[ROWS : 2 * ROWS, :]
-    ends = [
-        stack_rows([v_ref[r : r + 1, :]] + [v_i_ref[j, r : r + 1, :] for j in range(3)]) for r in (0, rows - 1)
-    ]
-    put_rows(ends[0], ends[1], core_ref, cross_ref)
+    put_two_rows(v_ref, v_i_ref, core_ref, cross_ref)
     own_parts(v_ref, v_i_ref, cx_ref, cy_ref, c_ref, pay_ref, scratch_ref)
-
-
-def far_kernel(u_o_ref, part_ref, far_ref, c_ref, inv_ref, sums_ref, v_ref, totals_ref):
+    size = rows // 2
+    first = pl.multiple_of(jnp.where(upper_chip(), 0, rows - size), ROWS)
+    pay_ref[rows + size :, :] = inv_ref[pl.ds(first, size), :]
+
+
+def finish_kernel(
+    u_o_ref, got_ref, tail_ref, v_i_ref, part_ref, sums_ref, beside_ref, inner_ref, inv_far_ref,
+    cx_ref, cy_ref, c_ref, inv_ref, edge_ref, side_core_ref, side_cross_ref, t0_ref,
+    mail_ref, v_ref, *more,
+):
     rows, width = u_o_ref.shape
-    sums = [jnp.zeros((ROWS, width), F32) for _ in range(2)]
-    for k in range(rows // ROWS):
+    chunks = rows // ROWS
+    none = jnp.zeros((1, width), F32)
+    sums = [jnp.zeros((ROWS, width), F32) for _ in range(4)]
+    for k in range(chunks):
         rs = slice(k * ROWS, (k + 1) * ROWS)
-        part = part_ref[rs, :] + c_ref[0, rs, :] * far_ref[rs, :]
+        part = part_ref[rs, :] + c_ref[0, rs, :] * got_ref[rs, :]
         v = inv_ref[rs, :] * part
         v_ref[rs, :] = v
         sums[0] = sums[0] + u_o_ref[rs, :] * part
         sums[1] = sums[1] + v * part
-    totals_ref[0:ROWS, :] = fold(sums[0]) + sums_ref[0:ROWS, :]
-    totals_ref[ROWS : 2 * ROWS, :] = fold(sums[1]) + sums_ref[ROWS : 2 * ROWS, :]
-
-
-def again_kernel(
-    v_o_ref, v_i_ref, core_ref, cross_ref, cx_ref, cy_ref, c_ref, inv_i_ref, edge_ref,
-    total_ref, w_i_ref=None, part_ref=None,
-):
-    rows, width = v_o_ref.shape
-    chunks = rows // ROWS
-    above, below = take_rows(core_ref, cross_ref)
-    none = jnp.zeros((1, width), F32)
-    carried = [none] + [edge_ref[j : j + 1, :] * above[j : j + 1] for j in range(1, 4)]
-    after = [none] + [below[j : j + 1] for j in range(1, 4)]
-    total = jnp.zeros((ROWS, width), F32)
+    if len(more) == 2:
+        w_ref, fix_ref = more
+    else:
+        w_ref = fix_ref = None
+    carried = none
     for k in range(chunks):
         rs = slice(k * ROWS, (k + 1) * ROWS)
-        xs, parts = [], []
-        for j in range(4):
-            x, part, carried[j] = in_band(
-                band_of(v_o_ref, v_i_ref, j), cx_ref.at[j], cy_ref.at[j], carried[j], after[j], k, chunks
-            )
-            xs.append(x)
-            parts.append(part)
-        parts = couple(xs, parts, c_ref, rs)
-        for x, part in zip(xs, parts):
-            total = total + x * part
-        if w_i_ref is not None:
-            part_ref[rs, :] = parts[0]
-            for j in range(1, 4):
-                w_i_ref[j - 1, rs, :] = inv_i_ref[j - 1, rs, :] * parts[j]
-    total_ref[...] = fold(total)
-
-
-def cross_kernel(
-    u_ref, v_ref, got_ref, tail_ref, core_ref, cross_ref, inv_far_ref, c_ref, cx_ref, edge_ref, side_core_ref, side_cross_ref,
-    t0_ref, t1_ref, t2_ref, mail_ref, part_ref=None, inv_ref=None, w_ref=None,
-):
-    rows, width = u_ref.shape
-    size = got_ref.shape[0] - rows
-    chunks = size // ROWS
-    first = jnp.where(upper_chip(), rows - size, 0)
-    above, below = take_rows(core_ref, cross_ref)
+        v, part, carried = in_band(v_ref, cx_ref.at[0], cy_ref.at[0], carried, none, k, chunks)
+        coupled = c_ref[1, rs, :] * v_i_ref[0, rs, :]
+        sums[2] = sums[2] + v * (part + 2.0 * coupled)
+        if w_ref is not None:
+            w_ref[rs, :] = part + coupled
     side_above, side_below = take_rows(side_core_ref, side_cross_ref)
-    up = side_above[4:5] * (above[0:1] + side_above[5:6] * tail_ref[0:1, :])
-    down = side_below[4:5] * (below[0:1] + side_below[5:6] * tail_ref[1:2, :])
+    up = side_above[4:5] * (beside_ref[0:1, :] + side_above[12:13] * tail_ref[0:1, :])
+    down = side_below[4:5] * (beside_ref[4:5, :] + side_below[12:13] * tail_ref[1:2, :])
     up = edge_ref[0:1, :] * up
     down = cx_ref[0, rows - 1 :, :] * down
+    if fix_ref is not None:
+        fix_ref[...] = stack_rows([up, down])
+    size = rows // 2
+    first = jnp.where(upper_chip(), rows - size, 0)
     far_up = jnp.where(first == 0, tail_ref[2:3, :], 0.0)
     far_down = jnp.where(first + size == rows, tail_ref[3:4, :], 0.0)
-    total = jnp.zeros((ROWS, width), F32)
-    for k in range(chunks):
-        rs = slice(k * ROWS, (k + 1) * ROWS)
+    for k in range(size // ROWS):
         at = pl.ds(pl.multiple_of(first + k * ROWS, ROWS), ROWS)
         c_out = c_ref[0, at, :]
-        part = got_ref[rows + k * ROWS : rows + (k + 1) * ROWS, :] + c_out * u_ref[at, :]
+        part = got_ref[rows + k * ROWS : rows + (k + 1) * ROWS, :] + c_out * u_o_ref[at, :]
         if k == 0:
             part = part + jnp.where(row_at(width, 0), far_up, 0.0)
-        if k == chunks - 1:
+        if k == size // ROWS - 1:
             part = part + jnp.where(row_at(width, ROWS - 1), far_down, 0.0)
-        flow = c_out * (inv_far_ref[at, :] * part)
-        total = total + v_ref[at, :] * flow
-        if w_ref is not None:
-            part = part_ref[rs, :] + flow
-            if k == 0:
-                part = part + jnp.where(row_at(width, 0), up, 0.0)
-            if k == chunks - 1:
-                part = part + jnp.where(row_at(width, ROWS - 1), down, 0.0)
-            w_ref[rs, :] = inv_ref[rs, :] * part
+        inv_far = inv_far_ref[rows + size + k * ROWS : rows + size + (k + 1) * ROWS, :]
+        sums[3] = sums[3] + v_ref[at, :] * (c_out * (inv_far * part))
     ends = up * v_ref[0:1, :] + down * v_ref[rows - 1 :, :]
-    last = fold((rows // size) * total + jnp.where(row_at(width, 0), ends, 0.0)) + t2_ref[...]
-    terms = (t0_ref[...], t1_ref[0:ROWS, :], t1_ref[ROWS : 2 * ROWS, :], last)
+    last = fold(sums[2] + 2.0 * sums[3] + jnp.where(row_at(width, 0), ends, 0.0)) + inner_ref[...]
+    terms = (
+        t0_ref[...], fold(sums[0]) + sums_ref[0:ROWS, :], fold(sums[1]) + sums_ref[ROWS : 2 * ROWS, :], last
+    )
     lines = [jnp.sum(t, 0, keepdims=True) for t in terms]
     block = jnp.concatenate(lines + lines, 0)
     for at in range(0, mail_ref.shape[0], ROWS):
@@ -448,7 +465,7 @@
 
 
 def step_kernel(
-    mail_ref, s_o_ref, s_i_ref, v1_o_ref, v1_i_ref, v2_o_ref, v2_i_ref, v3_o_ref, v3_i_ref, cap_ref, seen_ref,
+    mail_ref, s_o_ref, s_i_ref, v1_o_ref, v1_i_ref, v2_o_ref, v2_i_ref, part_i_ref, part_ref, far_ref, fix_ref, cap_ref, seen_ref,
     diag_ref, inv_o_ref, inv_i_ref, cx_ref, cy_ref, c_ref,
     z_o_ref, z_i_ref, core_ref, cross_ref, total_ref, pay_ref, x_mine_ref, z_mine_ref, scratch_ref,
 ):
@@ -456,17 +473,27 @@
     chunks = rows // ROWS
     a, b = weights(mail_ref)
     total = jnp.zeros((ROWS, width), F32)
-    firsts, lasts = [], []
     for j in range(4):
         for k in range(chunks):
             rs = slice(k * ROWS, (k + 1) * ROWS)
-            s, p, q, r, inv = (
+            s, p, q, inv = (
                 band_of(o, i, j)[rs, :]
                 for o, i in (
-                    (s_o_ref, s_i_ref), (v1_o_ref, v1_i_ref), (v2_o_ref, v2_i_ref), (v3_o_ref, v3_i_ref),
+                    (s_o_ref, s_i_ref), (v1_o_ref, v1_i_ref), (v2_o_ref, v2_i_ref),
                     (inv_o_ref, inv_i_ref),
                 )
             )
+            if j == 0:
+                part = part_ref[rs, :] + c_ref[0, rs, :] * far_ref[rs, :]
+                if k == 0:
+                    part = part + jnp.where(row_at(width, 0), fix_ref[0:1, :], 0.0)
+                if k == chunks - 1:
+                    part = part + jnp.where(row_at(width, ROWS - 1), fix_ref[1:2, :], 0.0)
+            else:
+                part = part_i_ref[j - 1, rs, :]
+                if j == 1:
+                    part = part + c_ref[1, rs, :] * v2_o_ref[rs, :]
+            r = inv * part
             x = s + a * p + b * q
             residual = cap_ref[j, rs, :] * x + seen_ref[j, rs, :] - diag_ref[j, rs, :] * (x - (p + a * q + b * r))
             z = residual * inv
@@ -474,13 +501,8 @@
             total = total + residual * z
             hand_out(j, x, k, x_mine_ref, core_ref, ROWS, rows)
             hand_out(j, z, k, z_mine_ref, core_ref, ROWS + 2 * rows, rows)
-            if k == 0:
-                firsts.append(z[:1])
-            if k == chunks - 1:
-                lasts.append(z[ROWS - 1 :])
     total_ref[...] = fold(total)
-    none = jnp.zeros((4, width), F32)
-    put_rows(stack_rows(firsts + [none]), stack_rows(lasts + [none]), core_ref.at[0:ROWS], cross_ref)
+    put_two_rows(z_o_ref, z_i_ref, core_ref.at[0:ROWS], cross_ref)
     own_parts(z_o_ref, z_i_ref, cx_ref, cy_ref, c_ref, pay_ref, scratch_ref)
 
 
@@ -518,75 +540,62 @@
     _, rows, width = cond_x.shape
     half = rows // 2
     field, three, four, edge = shape(half, width), shape(3, half, width), shape(4, half, width), shape(4, width)
-    six, rim, pair = shape(6, width), shape(2, width), shape(2, half, width)
+    eight, sides = shape(ROWS, width), shape(20, width)
+    rim, pair = shape(2, width), shape(2, half, width)
     mail = shape(lax.axis_size("band") * lax.axis_size("tile") * 4, 128)
     one, two = shape(ROWS, 128), shape(2 * ROWS, 128)
     fourteen = shape(14, half, width)
     whole, whole_int = pltpu.VMEM((2, rows, width), F32), pltpu.VMEM((2, rows, width), jnp.int32)
     own, send, pay, pay_send, last, middle = call(
-        load_kernel, [fourteen, fourteen, field, field, rim, rim],
+        load_kernel, [fourteen, fourteen, field, shape(half + ROWS, width), rim, rim],
         cond_x, cond_y, via_cond, via_mask, capacitance, pad_mask, observe, name="load", place=pltpu.HBM,
         scratch=[whole, whole_int, whole_int, pltpu.SemaphoreType.DMA((13,))],
     )
-    got, before = core_swap(pay_send), next_tile(last)
-    got, send = lax.optimization_barrier((got, send))
-    (pay,) = call(pay_kernel, [field], pay, got, name="pay")
-    link, traded = outer_swap(pay), core_swap(send)
-    own_edge, send_edge = call(edge_kernel, [rim, rim], middle, before, name="edges")
-    got_edge = core_swap(send_edge)
+    more = core_swap(pay_send)
+    more, send = lax.optimization_barrier((more, send))
+    pay, last = call(pay_kernel, [field, edge], pay, more, last, name="pay")
+    link, traded, last = outer_swap(pay), core_swap(send), cross_swap(last)
     cx, cy, c, diag, inv_i, s_i, inv_o, s_o, cx_edge, near, cross, cap, earlier = call(
-        prepare_kernel, [four, four, four, four, three, three, field, field, edge, six, six, four, four],
-        own, traded, own_edge, got_edge, link, name="prepare",
+        prepare_kernel,
+        [four, four, four, four, three, three, field, field, edge, sides, sides, four, four],
+        own, traded, link, middle, more, last, name="prepare",
     )
     far, sides = outer_swap(s_o), (core_swap(near), cross_swap(cross))
-    inv_far = outer_swap(inv_o)
 
     coeffs = (cx, cy, c, inv_i, cx_edge)
     parts_of = [pltpu.VMEM((half, width), F32)]
     v1_i, part, sums = call(spread_kernel, [three, field, two], s_o, s_i, *sides, *coeffs, name="first_spread", cost=0)
-    v1_i, inv_far = lax.optimization_barrier((v1_i, inv_far))
     v1_o, near, cross, t0, pay = call(
-        far_first_kernel, [field, edge, edge, one, shape(2 * half, width)],
+        far_first_kernel, [field, eight, eight, one, shape(2 * half, width)],
         s_o, part, far, c, inv_o, v1_i, sums, cx, cy, name="first_far", scratch=parts_of,
     )
 
-    def stage(u_o, u_i, pay, near, cross, t0, inv_far, name):
+    def stage(u_o, u_i, pay, near, cross, t0, inv_far, name, further):
         got, cross, near = outer_swap(pay), cross_swap(cross), core_swap(near)
-        whole = pay.shape[0] == 2 * half
-        near, cross, inv_far = lax.optimization_barrier((near, cross, inv_far))
-        held = near
-        v_i, part, sums, tail, near, cross = call(
-            spread_kernel, [three, field, two, shape(ROWS, width), edge, edge],
-            u_o, u_i, near, cross, *coeffs, name=name + "_spread", cost=0,
+        v_i, part, sums, tail, there, inner, *w_i = call(
+            two_spread_kernel, [three, field, two, eight, eight, one] + [three] * further,
+            u_o, u_i, near, cross, *coeffs, *sides, name=name + "_spread", cost=0,
         )
-        cross, tail, near = cross_swap(cross), outer_swap(tail), core_swap(near)
-        v_o, t1 = call(far_kernel, [field, two], u_o, part, got, c, inv_o, sums, name=name + "_far")
-        given = ()
-        if not whole:
+        parts, v_o, *more = call(
+            finish_kernel, [mail, field] + [field, rim] * further,
+            u_o, got, outer_swap(tail), v_i, part, sums, there, inner, got if further else inv_far,
+            cx, cy, c, inv_o, cx_edge, *sides, t0, name=name + "_finish",
+        )
+        if further:
+            more = *w_i, *more, outer_swap(v_o)
+        else:
             mine, send = call(give_kernel, [pair, shape(2 * half, width)], v_o, v_i, name="give")
-            given = mine, core_swap(send)
-        t2, *rest = call(
-            again_kernel, [one] + [three, field] * whole, v_o, v_i, near, cross, *coeffs, name=name + "_again"
-        )
-        args = [u_o, v_o, got, tail, near, cross, inv_far, c, cx, cx_edge, *sides, t0, t1, t2]
-
-        def finish(*refs):
-            n = len(args)
-            cross_kernel(*refs[:n], *((refs[n + 2], *refs[n : n + 2], refs[n + 3]) if whole else refs[n:]))
-
-        more_args = [rest[1], inv_o] if whole else []
-        parts, *w_o = call(finish, [mail] + [field] * whole, *args, *more_args, name=name + "_cross")
-        parts, given = lax.optimization_barrier((parts, given))
-        return v_o, v_i, all_total(parts), inv_far, held, given, (*w_o, *rest[:1])
-
-    v2_o, v2_i, total, inv_far, _, _, (v3_o, v3_i) = stage(v1_o, v1_i, pay, near, cross, t0, inv_far, "later")
+            more = mine, core_swap(send)
+        return v_o, v_i, all_total(parts), got, near, more
+
+    v2_o, v2_i, total, inv_far, _, (part_i, part, fix, far) = stage(v1_o, v1_i, pay, near, cross, t0, None, "later", True)
     z_o, z_i, near, cross, t0, pay, x_mine, z_mine = call(
         step_kernel,
         [field, three, shape(ROWS + 4 * half, width), shape(ROWS, width), one, shape(half + half // 2, width), pair, pair],
-        total, s_o, s_i, v1_o, v1_i, v2_o, v2_i, v3_o, v3_i, cap, earlier, diag, inv_o, inv_i, cx, cy, c,
+        total, s_o, s_i, v1_o, v1_i, v2_o, v2_i, part_i, part, far, fix, cap, earlier, diag, inv_o, inv_i, cx, cy, c,
         name="step", scratch=parts_of,
     )
-    _, _, total, _, got, given, _ = stage(z_o, z_i, pay, near, cross, t0, inv_far, "earlier")
+    _, _, total, _, got, given = stage(z_o, z_i, pay, near, cross, t0, inv_far, "earlier", False)
     (out,) = call(
         last_kernel, [shape(2, 2, rows, width)], total, x_mine, z_mine, got, *given, name="last", out_place=pl.ANY,
         scratch=[pltpu.VMEM((4, half, width), F32), pltpu.SemaphoreType.DMA((8,))],

time: 85.9 us -> 81.2 us (0.945)
  waiting for transfers between devices: 28.9 us -> 21.4 us
  blocking collectives: 19.3 us -> 21.3 us
    ppermute x1 -> x0, waiting for transfers between devices: 3.11 us -> none  [next_tile(): return lax.ppermute(x, 'tile', [(t, (t + 1) % nt) for t in range(nt)])]
    ppermute x1 -> x0, starting transfers between devices: 2.64 us -> none  [next_tile(): return lax.ppermute(x, 'tile', [(t, (t + 1) % nt) for t in range(nt)])]
    ppermute x5 -> x4, waiting for transfers between devices: 15 us -> 13.1 us  [cross_swap(): return lax.ppermute(x, AXES, pairs)]
    all_to_all x2, blocking collectives: 19.3 us -> 21.3 us  [all_total(): return lax.all_to_all(parts, AXES, 0, 0, tiled=True)]
    ppermute x5 -> x4, starting transfers between devices: 12 us -> 13.7 us  [cross_swap(): return lax.ppermute(x, AXES, pairs)]
    ppermute x7, starting transfers between devices: 8.17 us -> 9.74 us  [outer_swap(): return lax.ppermute(x, 'band', [(b, b ^ 2) for b in range(nb)])]
    ppermute x7, waiting for transfers between devices: 8.44 us -> 7.05 us  [outer_swap(): return lax.ppermute(x, 'band', [(b, b ^ 2) for b in range(nb)])]
    ppermute x9 -> x6, waiting for transfers between devices: 2.36 us -> 1.27 us  [core_swap(): return lax.ppermute(x, 'band', [(b, b ^ 1) for b in range(nb)])]
  transfers between devices with their start and end apart: 22 -> 17, of which waited for: 12 -> 9; matrix products, arithmetic and copies ran while one was open for 0% -> 0% of each run, Pallas kernels for 6% -> 5%
where the time goes in v3:
time: 81.2 us; the launch traced here: 81 us
  starting transfers between devices  24.6 us (30%)
  waiting for transfers between devices  21.4 us (26%)
  blocking collectives  21.3 us (26%)
  Pallas kernels  13.7 us (17%)
    all_to_all x2, blocking collectives, all_total(): return lax.all_to_all(parts, AXES, 0, 0, tiled=True)  21.3 us
    ppermute x4, starting transfers between devices, cross_swap(): return lax.ppermute(x, AXES, pairs)  13.7 us
    pallas_call x12, Pallas kernels, call(): pl.pallas_call(body, out_shape=outs, in_specs=[pl.BlockSpec(memory_space=...  13.7 us
    ppermute x4, waiting for transfers between devices, cross_swap(): return lax.ppermute(x, AXES, pairs)  13.1 us
    ppermute x7, starting transfers between devices, outer_swap(): return lax.ppermute(x, 'band', [(b, b ^ 2) for b in range(nb)])  9.74 us
    ppermute x7, waiting for transfers between devices, outer_swap(): return lax.ppermute(x, 'band', [(b, b ^ 2) for b in range(nb)])  7.05 us
  transfers between devices with their start and end apart: 17, of which 9 were waited for; matrix products, arithmetic and copies ran while one was open for 0% of the time, Pallas kernels for 5%

profile of v3, /device:TPU:0, one launch (start us, length us, event | category | flops | bytes accessed | tf_op | source)
XLA Modules:
  0.0 81.0 jit_solution(13157460925872607891)
XLA Ops:
  0.0 3.8 %load.1 = (f32[14,32,2048]{2,1,0:T(8,128)S(1)}, f32[14,32,2048]{2,1,0:T(8,128)S(1)}, f32[32,2048]{1,0:T(8,128)S(1)}, f32[40,2048]{1,0:T(8,128)S(1)}, f32[2,2048]{1,0:T(2,128)S(1)}, /*index=5*/f32[2,2048]{1,0:T(2,128)S(1)}) custom-call(f32[2,64,2048]{2,1,0:T(8,128)} %cond_x_ref.1, f32[2,64,2048]{2,1,0:T(8,128)} %cond_y_ref.1, f32[2,64,2048]{2,1,0:T(8,128)} %via_ref.1, ...), custom_call_target="tpu_custom_call" | custom-call | flops 10000000000 | bytes 10000000 | tf_op jit(solution)/shard_map/load/pallas_call | solution.py:55
  3.8 0.5 collective-permute-start
  4.4 1.3 %collective-permute-done.got_ref.more_ref = f32[40,2048]{1,0:T(8,128)S(1)} collective-permute-done((f32[40,2048]{1,0:T(8,128)S(1)}, f32[40,2048]{1,0:T(8,128)S(1)}, u32[]{:S(2)}, u32[]{:S(2)}) %collective-permute-start) | collective-permute-done | bytes 327712 | tf_op jit(solution)/shard_map/ppermute | solution.py:30
  5.6 0.4 collective-permute-start.1
  6.0 2.7 %collective-permute-start.2 = (f32[32,2048]{1,0:T(8,128)S(1)}, f32[32,2048]{1,0:T(8,128)S(1)}, u32[]{:S(2)}, u32[]{:S(2)}) collective-permute-start(f32[32,2048]{1,0:T(8,128)S(1)} %get-tuple-element.72), channel_id=1, source_target_pairs={{0,16},{8,24},{16,0},{24,8},{1,17},{9,25},{17,1},{25,9},{2,18},{10... | collective-permute-start | bytes 786440 | tf_op jit(solution)/shard_map/ppermute | solution.py:35
  8.8 4.2 %collective-permute-start.3 = (f32[4,2048]{1,0:T(4,128)S(1)}, f32[4,2048]{1,0:T(4,128)S(1)}, u32[]{:S(2)}, u32[]{:S(2)}) collective-permute-start(f32[4,2048]{1,0:T(4,128)S(1)} %get-tuple-element.74), channel_id=1, source_target_pairs={{0,15},{1,8},{2,9},{3,10},{4,11},{5,12},{6,13},{7,14},{8,1},{9,2},... | collective-permute-start | bytes 98312 | tf_op jit(solution)/shard_map/ppermute | solution.py:45
  13.0 1.8 %collective-permute-done.3.last_ref = f32[4,2048]{1,0:T(4,128)S(1)} collective-permute-done((f32[4,2048]{1,0:T(4,128)S(1)}, f32[4,2048]{1,0:T(4,128)S(1)}, u32[]{:S(2)}, u32[]{:S(2)}) %collective-permute-start.3) | collective-permute-done | bytes 32800 | tf_op jit(solution)/shard_map/ppermute | solution.py:45
  14.8 0.8 collective-permute-done.2.link_ref
  15.6 0.0 collective-permute-done.1.got_ref
  15.6 1.3 %prepare.1 = (f32[4,32,2048]{2,1,0:T(8,128)S(1)}, f32[4,32,2048]{2,1,0:T(8,128)S(1)}, f32[4,32,2048]{2,1,0:T(8,128)S(1)}, f32[4,32,2048]{2,1,0:T(8,128)S(1)}, f3...) custom-call(f32[14,32,2048]{2,1,0:T(8,128)S(1)} %get-tuple-element.6, ...), custom_call_target="tpu_custom_call" | custom-call | flops 10000000000 | bytes 10000000 | tf_op jit(solution)/shard_map/prepare/pallas_call | solution.py:55
  16.9 1.8 %collective-permute-start.6 = (f32[32,2048]{1,0:T(8,128)S(1)}, f32[32,2048]{1,0:T(8,128)S(1)}, u32[]{:S(2)}, u32[]{:S(2)}) collective-permute-start(f32[32,2048]{1,0:T(8,128)S(1)} %get-tuple-element.75.u_o_ref.s_o_ref), channel_id=1, source_target_pairs={{0,16},{8,24},{16,0},{24,8},{1,17},{9,25},{17,1},{25,9},{2,18},{10... | collective-permute-start | bytes 786440 | tf_op jit(solution)/shard_map/ppermute | solution.py:35
  18.7 0.0 collective-permute-start.4
  18.7 4.6 %collective-permute-start.5 = (f32[20,2048]{1,0:T(8,128)S(1)}, f32[20,2048]{1,0:T(8,128)S(1)}, u32[]{:S(2)}, u32[]{:S(2)}) collective-permute-start(f32[20,2048]{1,0:T(8,128)S(1)} %get-tuple-element.78), channel_id=1, source_target_pairs={{0,15},{1,8},{2,9},{3,10},{4,11},{5,12},{6,13},{7,14},{8,1},{9,2},... | collective-permute-start | bytes 491528 | tf_op jit(solution)/shard_map/ppermute | solution.py:45
  23.4 0.0 collective-permute-done.4.core_ref.side_core_ref
  23.4 3.3 %collective-permute-done.5.cross_ref.side_cross_ref = f32[20,2048]{1,0:T(8,128)S(1)} collective-permute-done((f32[20,2048]{1,0:T(8,128)S(1)}, f32[20,2048]{1,0:T(8,128)S(1)}, u32[]{:S(2)}, u32[]{:S(2)}) %collective-permute-start.5) | collective-permute-done | bytes 163872 | tf_op jit(solution)/shard_map/ppermute | solution.py:45
  26.7 0.9 %first_spread.1 = (f32[3,32,2048]{2,1,0:T(8,128)S(1)}, f32[32,2048]{1,0:T(8,128)S(1)}, f32[16,128]{1,0:T(8,128)S(1)}) custom-call(f32[32,2048]{1,0:T(8,128)S(1)} %get-tuple-element.75.u_o_ref.s_o_ref, f32[3,32,2048]{2,1,0:T(8,128)S(1)} %get-tuple-element.76.u_i_ref.s_i_ref, f32[20,2048]{1,0:T(8,128)S(1)} %collective-permute-done.4.core_ref.side_core_ref, ...), custom_call_target="tpu_custom_call" | custom-call | tf_op jit(solution)/shard_map/first_spread/pallas_call | solution.py:55
  27.6 0.0 collective-permute-done.6.far_ref
  27.6 0.4 first_far.1
  28.0 0.6 collective-permute-start.7
  28.6 0.0 collective-permute-start.8
  28.6 4.2 %collective-permute-start.9 = (f32[8,2048]{1,0:T(8,128)S(1)}, f32[8,2048]{1,0:T(8,128)S(1)}, u32[]{:S(2)}, u32[]{:S(2)}) collective-permute-start(f32[8,2048]{1,0:T(8,128)S(1)} %get-tuple-element.91), channel_id=1, source_target_pairs={{0,15},{1,8},{2,9},{3,10},{4,11},{5,12},{6,13},{7,14},{8,1},{9,2},... | collective-permute-start | bytes 196616 | tf_op jit(solution)/shard_map/ppermute | solution.py:45
  32.7 0.0 collective-permute-done.8.core_ref
  32.7 2.2 %collective-permute-done.9.cross_ref = f32[8,2048]{1,0:T(8,128)S(1)} collective-permute-done((f32[8,2048]{1,0:T(8,128)S(1)}, f32[8,2048]{1,0:T(8,128)S(1)}, u32[]{:S(2)}, u32[]{:S(2)}) %collective-permute-start.9) | collective-permute-done | bytes 65568 | tf_op jit(solution)/shard_map/ppermute | solution.py:45
  35.0 1.7 %later_spread.1 = (f32[3,32,2048]{2,1,0:T(8,128)S(1)}, f32[32,2048]{1,0:T(8,128)S(1)}, f32[16,128]{1,0:T(8,128)S(1)}, f32[8,2048]{1,0:T(8,128)S(1)}, f32[8,2048]...) custom-call(f32[32,2048]{1,0:T(8,128)S(1)} %get-tuple-element.88.u_o_ref.v1_o_ref, ...), custom_call_target="tpu_custom_call" | custom-call | tf_op jit(solution)/shard_map/later_spread/pallas_call | solution.py:55
  36.7 1.6 %collective-permute-start.10 = (f32[8,2048]{1,0:T(8,128)S(1)}, f32[8,2048]{1,0:T(8,128)S(1)}, u32[]{:S(2)}, u32[]{:S(2)}) collective-permute-start(f32[8,2048]{1,0:T(8,128)S(1)} %get-tuple-element.92), channel_id=1, source_target_pairs={{0,16},{8,24},{16,0},{24,8},{1,17},{9,25},{17,1},{25,9},{2,18},{10... | collective-permute-start | bytes 196616 | tf_op jit(solution)/shard_map/ppermute | solution.py:35
  38.2 3.4 %collective-permute-done.10.tail_ref = f32[8,2048]{1,0:T(8,128)S(1)} collective-permute-done((f32[8,2048]{1,0:T(8,128)S(1)}, f32[8,2048]{1,0:T(8,128)S(1)}, u32[]{:S(2)}, u32[]{:S(2)}) %collective-permute-start.10) | collective-permute-done | bytes 65568 | tf_op jit(solution)/shard_map/ppermute | solution.py:35
  41.6 0.0 collective-permute-done.7.got_ref.inv_far_ref
  41.6 0.4 later_finish.1
  42.0 0.9 %collective-permute-start.11 = (f32[32,2048]{1,0:T(8,128)S(1)}, f32[32,2048]{1,0:T(8,128)S(1)}, u32[]{:S(2)}, u32[]{:S(2)}) collective-permute-start(f32[32,2048]{1,0:T(8,128)S(1)} %get-tuple-element.100.v2_o_ref), channel_id=1, source_target_pairs={{0,16},{8,24},{16,0},{24,8},{1,17},{9,25},{17,1},{25,9},{2,18},{10... | collective-permute-start | bytes 786440 | tf_op jit(solution)/shard_map/ppermute | solution.py:35
  43.0 12.3 %all_to_all.22 = f32[32,4,128]{2,1,0:T(4,128)S(1)} all-to-all(f32[32,4,128]{2,1,0:T(4,128)S(1)} %bitcast.6), channel_id=1, replica_groups=mesh['band'=4,'tile'=8] {'band','tile'}, dimensions={0} | all-to-all | bytes 131072 | tf_op jit(solution)/shard_map/all_to_all | solution.py:49
  55.3 0.0 collective-permute-done.11.far_ref
  55.3 1.5 %step.1 = (f32[32,2048]{1,0:T(8,128)S(1)}, f32[3,32,2048]{2,1,0:T(8,128)S(1)}, f32[136,2048]{1,0:T(8,128)S(1)}, f32[8,2048]{1,0:T(8,128)S(1)}, f32[8,128]{1,0:T(...) custom-call(f32[128,128]{1,0:T(8,128)S(1)} %bitcast.4, ...), custom_call_target="tpu_custom_call" | custom-call | flops 10000000000 | bytes 10000000 | tf_op jit(solution)/shard_map/step/pallas_call | solution.py:55
  56.8 0.2 collective-permute-start.13
  57.0 0.7 collective-permute-start.12
  57.6 0.7 collective-permute-start.14
  58.3 5.7 %collective-permute-done.14.cross_ref = f32[8,2048]{1,0:T(8,128)S(1)} collective-permute-done((f32[8,2048]{1,0:T(8,128)S(1)}, f32[8,2048]{1,0:T(8,128)S(1)}, u32[]{:S(2)}, u32[]{:S(2)}) %collective-permute-start.14) | collective-permute-done | bytes 65568 | tf_op jit(solution)/shard_map/ppermute | solution.py:45
  64.0 0.0 collective-permute-done.13.core_ref.got_ref
  64.0 1.6 %earlier_spread.1 = (f32[3,32,2048]{2,1,0:T(8,128)S(1)}, f32[32,2048]{1,0:T(8,128)S(1)}, f32[16,128]{1,0:T(8,128)S(1)}, f32[8,2048]{1,0:T(8,128)S(1)}, f32[8,2048]{1,0:T(8,128)S(1)}, /*index=5*/f32[8,128]{1,0:T(8,128)S(1)}) custom-call(f32[32,2048]{1,0:T(8,128)S(1)} %get-tuple-element.107.u_o_ref, f32[3,32,2048]{2,1,0:T(8,128)S(1)} %get-tuple-element.109.u_i_ref, ...), custom_call_target="tpu_custom_call" | custom-call | tf_op jit(solution)/shard_map/earlier_spread/pallas_call | solution.py:55
  65.7 1.5 %collective-permute-start.15 = (f32[8,2048]{1,0:T(8,128)S(1)}, f32[8,2048]{1,0:T(8,128)S(1)}, u32[]{:S(2)}, u32[]{:S(2)}) collective-permute-start(f32[8,2048]{1,0:T(8,128)S(1)} %get-tuple-element.112), channel_id=1, source_target_pairs={{0,16},{8,24},{16,0},{24,8},{1,17},{9,25},{17,1},{25,9},{2,18},{10... | collective-permute-start | bytes 196616 | tf_op jit(solution)/shard_map/ppermute | solution.py:35
  67.1 1.8 %collective-permute-done.12.got_ref = f32[48,2048]{1,0:T(8,128)S(1)} collective-permute-done((f32[48,2048]{1,0:T(8,128)S(1)}, f32[48,2048]{1,0:T(8,128)S(1)}, u32[]{:S(2)}, u32[]{:S(2)}) %collective-permute-start.12) | collective-permute-done | bytes 393248 | tf_op jit(solution)/shard_map/ppermute | solution.py:35
  68.9 1.1 %collective-permute-done.15.tail_ref = f32[8,2048]{1,0:T(8,128)S(1)} collective-permute-done((f32[8,2048]{1,0:T(8,128)S(1)}, f32[8,2048]{1,0:T(8,128)S(1)}, u32[]{:S(2)}, u32[]{:S(2)}) %collective-permute-start.15) | collective-permute-done | bytes 65568 | tf_op jit(solution)/shard_map/ppermute | solution.py:35
  70.0 0.4 earlier_finish.1
  70.4 0.1 give.1
  70.6 0.1 collective-permute-start.16
  70.6 9.0 %all_to_all.23 = f32[32,4,128]{2,1,0:T(4,128)S(1)} all-to-all(f32[32,4,128]{2,1,0:T(4,128)S(1)} %bitcast.5), channel_id=1, replica_groups=mesh['band'=4,'tile'=8] {'band','tile'}, dimensions={0} | all-to-all | bytes 131072 | tf_op jit(solution)/shard_map/all_to_all | solution.py:49
  79.6 0.0 collective-permute-done.16.q_got_ref
  79.6 1.4 %last.1 = f32[2,2,64,2048]{3,2,1,0:T(8,128)} custom-call(f32[128,128]{1,0:T(8,128)S(1)} %bitcast.7, f32[2,32,2048]{2,1,0:T(8,128)S(1)} %get-tuple-element.120.x_mine_ref, f32[2,32,2048]{2,1,0:T(8,128)S(1)} %get-tuple-element.121.z_mine_ref, f32[136,2048]{1,0:T(8,128)S(1)} %collective-permute-done.13.core_ref.got_ref, ...), custom_call_target="tpu_custom_call" | custom-call | flops 10000000000 | bytes 10000000 | tf_op jit(solution)/shard_map/last/pallas_call | solution.py:55
  (1 shorter events, 0.0 us)
Async XLA Ops:
  3.8 1.8 %collective-permute-start = (f32[40,2048]{1,0:T(8,128)S(1)}, f32[40,2048]{1,0:T(8,128)S(1)}, u32[]{:S(2)}, u32[]{:S(2)}) collective-permute-start(f32[40,2048]{1,0:T(8,128)S(1)} %get-tuple-element.66), channel_id=1, source_target_pairs={{0,8},{8,0},{16,24},{24,16},{1,9},{9,1},{17,25},{25,17},{2,10},{10... | collective-permute-start | bytes 983048 | tf_op jit(solution)/shard_map/ppermute | solution.py:30
  5.6 10.0 %collective-permute-start.1 = (f32[14,32,2048]{2,1,0:T(8,128)S(1)}, f32[14,32,2048]{2,1,0:T(8,128)S(1)}, u32[]{:S(2)}, u32[]{:S(2)}) collective-permute-start(f32[14,32,2048]{2,1,0:T(8,128)S(1)} %get-tuple-element.68), channel_id=1, source_target_pairs={{0,8},{8,0},{16,24},{24,16},{1,9},{9,1},{17,25},{25,17},{2,10},{10... | collective-permute-start | bytes 11010056 | tf_op jit(solution)/shard_map/ppermute | solution.py:30
  6.0 9.6 %collective-permute-start.2 = (f32[32,2048]{1,0:T(8,128)S(1)}, f32[32,2048]{1,0:T(8,128)S(1)}, u32[]{:S(2)}, u32[]{:S(2)}) collective-permute-start(f32[32,2048]{1,0:T(8,128)S(1)} %get-tuple-element.72), channel_id=1, source_target_pairs={{0,16},{8,24},{16,0},{24,8},{1,17},{9,25},{17,1},{25,9},{2,18},{10... | collective-permute-start | bytes 786440 | tf_op jit(solution)/shard_map/ppermute | solution.py:35
  8.8 6.0 %collective-permute-start.3 = (f32[4,2048]{1,0:T(4,128)S(1)}, f32[4,2048]{1,0:T(4,128)S(1)}, u32[]{:S(2)}, u32[]{:S(2)}) collective-permute-start(f32[4,2048]{1,0:T(4,128)S(1)} %get-tuple-element.74), channel_id=1, source_target_pairs={{0,15},{1,8},{2,9},{3,10},{4,11},{5,12},{6,13},{7,14},{8,1},{9,2},... | collective-permute-start | bytes 98312 | tf_op jit(solution)/shard_map/ppermute | solution.py:45
  16.9 10.7 %collective-permute-start.6 = (f32[32,2048]{1,0:T(8,128)S(1)}, f32[32,2048]{1,0:T(8,128)S(1)}, u32[]{:S(2)}, u32[]{:S(2)}) collective-permute-start(f32[32,2048]{1,0:T(8,128)S(1)} %get-tuple-element.75.u_o_ref.s_o_ref), channel_id=1, source_target_pairs={{0,16},{8,24},{16,0},{24,8},{1,17},{9,25},{17,1},{25,9},{2,18},{10... | collective-permute-start | bytes 786440 | tf_op jit(solution)/shard_map/ppermute | solution.py:35
  18.7 4.6 %collective-permute-start.4 = (f32[20,2048]{1,0:T(8,128)S(1)}, f32[20,2048]{1,0:T(8,128)S(1)}, u32[]{:S(2)}, u32[]{:S(2)}) collective-permute-start(f32[20,2048]{1,0:T(8,128)S(1)} %get-tuple-element.77), channel_id=1, source_target_pairs={{0,8},{8,0},{16,24},{24,16},{1,9},{9,1},{17,25},{25,17},{2,10},{10... | collective-permute-start | bytes 491528 | tf_op jit(solution)/shard_map/ppermute | solution.py:30
  18.7 8.0 %collective-permute-start.5 = (f32[20,2048]{1,0:T(8,128)S(1)}, f32[20,2048]{1,0:T(8,128)S(1)}, u32[]{:S(2)}, u32[]{:S(2)}) collective-permute-start(f32[20,2048]{1,0:T(8,128)S(1)} %get-tuple-element.78), channel_id=1, source_target_pairs={{0,15},{1,8},{2,9},{3,10},{4,11},{5,12},{6,13},{7,14},{8,1},{9,2},... | collective-permute-start | bytes 491528 | tf_op jit(solution)/shard_map/ppermute | solution.py:45
  28.0 13.6 %collective-permute-start.7 = (f32[64,2048]{1,0:T(8,128)S(1)}, f32[64,2048]{1,0:T(8,128)S(1)}, u32[]{:S(2)}, u32[]{:S(2)}) collective-permute-start(f32[64,2048]{1,0:T(8,128)S(1)} %get-tuple-element.89), channel_id=1, source_target_pairs={{0,16},{8,24},{16,0},{24,8},{1,17},{9,25},{17,1},{25,9},{2,18},{10... | collective-permute-start | bytes 1572872 | tf_op jit(solution)/shard_map/ppermute | solution.py:35
  28.6 4.2 %collective-permute-start.8 = (f32[8,2048]{1,0:T(8,128)S(1)}, f32[8,2048]{1,0:T(8,128)S(1)}, u32[]{:S(2)}, u32[]{:S(2)}) collective-permute-start(f32[8,2048]{1,0:T(8,128)S(1)} %get-tuple-element.90), channel_id=1, source_target_pairs={{0,8},{8,0},{16,24},{24,16},{1,9},{9,1},{17,25},{25,17},{2,10},{10... | collective-permute-start | bytes 196616 | tf_op jit(solution)/shard_map/ppermute | solution.py:30
  28.6 6.4 %collective-permute-start.9 = (f32[8,2048]{1,0:T(8,128)S(1)}, f32[8,2048]{1,0:T(8,128)S(1)}, u32[]{:S(2)}, u32[]{:S(2)}) collective-permute-start(f32[8,2048]{1,0:T(8,128)S(1)} %get-tuple-element.91), channel_id=1, source_target_pairs={{0,15},{1,8},{2,9},{3,10},{4,11},{5,12},{6,13},{7,14},{8,1},{9,2},... | collective-permute-start | bytes 196616 | tf_op jit(solution)/shard_map/ppermute | solution.py:45
  36.7 5.0 %collective-permute-start.10 = (f32[8,2048]{1,0:T(8,128)S(1)}, f32[8,2048]{1,0:T(8,128)S(1)}, u32[]{:S(2)}, u32[]{:S(2)}) collective-permute-start(f32[8,2048]{1,0:T(8,128)S(1)} %get-tuple-element.92), channel_id=1, source_target_pairs={{0,16},{8,24},{16,0},{24,8},{1,17},{9,25},{17,1},{25,9},{2,18},{10... | collective-permute-start | bytes 196616 | tf_op jit(solution)/shard_map/ppermute | solution.py:35
  42.0 13.2 %collective-permute-start.11 = (f32[32,2048]{1,0:T(8,128)S(1)}, f32[32,2048]{1,0:T(8,128)S(1)}, u32[]{:S(2)}, u32[]{:S(2)}) collective-permute-start(f32[32,2048]{1,0:T(8,128)S(1)} %get-tuple-element.100.v2_o_ref), channel_id=1, source_target_pairs={{0,16},{8,24},{16,0},{24,8},{1,17},{9,25},{17,1},{25,9},{2,18},{10... | collective-permute-start | bytes 786440 | tf_op jit(solution)/shard_map/ppermute | solution.py:35
  56.8 7.2 %collective-permute-start.13 = (f32[136,2048]{1,0:T(8,128)S(1)}, f32[136,2048]{1,0:T(8,128)S(1)}, u32[]{:S(2)}, u32[]{:S(2)}) collective-permute-start(f32[136,2048]{1,0:T(8,128)S(1)} %get-tuple-element.110), channel_id=1, source_target_pairs={{0,8},{8,0},{16,24},{24,16},{1,9},{9,1},{17,25},{25,17},{2,10},{10... | collective-permute-start | bytes 3342344 | tf_op jit(solution)/shard_map/ppermute | solution.py:30
  57.0 12.0 %collective-permute-start.12 = (f32[48,2048]{1,0:T(8,128)S(1)}, f32[48,2048]{1,0:T(8,128)S(1)}, u32[]{:S(2)}, u32[]{:S(2)}) collective-permute-start(f32[48,2048]{1,0:T(8,128)S(1)} %get-tuple-element.108), channel_id=1, source_target_pairs={{0,16},{8,24},{16,0},{24,8},{1,17},{9,25},{17,1},{25,9},{2,18},{10... | collective-permute-start | bytes 1179656 | tf_op jit(solution)/shard_map/ppermute | solution.py:35
  57.6 6.4 %collective-permute-start.14 = (f32[8,2048]{1,0:T(8,128)S(1)}, f32[8,2048]{1,0:T(8,128)S(1)}, u32[]{:S(2)}, u32[]{:S(2)}) collective-permute-start(f32[8,2048]{1,0:T(8,128)S(1)} %get-tuple-element.111), channel_id=1, source_target_pairs={{0,15},{1,8},{2,9},{3,10},{4,11},{5,12},{6,13},{7,14},{8,1},{9,2},... | collective-permute-start | bytes 196616 | tf_op jit(solution)/shard_map/ppermute | solution.py:45
  65.7 4.3 %collective-permute-start.15 = (f32[8,2048]{1,0:T(8,128)S(1)}, f32[8,2048]{1,0:T(8,128)S(1)}, u32[]{:S(2)}, u32[]{:S(2)}) collective-permute-start(f32[8,2048]{1,0:T(8,128)S(1)} %get-tuple-element.112), channel_id=1, source_target_pairs={{0,16},{8,24},{16,0},{24,8},{1,17},{9,25},{17,1},{25,9},{2,18},{10... | collective-permute-start | bytes 196616 | tf_op jit(solution)/shard_map/ppermute | solution.py:35
  70.6 9.1 %collective-permute-start.16 = (f32[64,2048]{1,0:T(8,128)S(1)}, f32[64,2048]{1,0:T(8,128)S(1)}, u32[]{:S(2)}, u32[]{:S(2)}) collective-permute-start(f32[64,2048]{1,0:T(8,128)S(1)} %get-tuple-element.124), channel_id=1, source_target_pairs={{0,8},{8,0},{16,24},{24,16},{1,9},{9,1},{17,25},{25,17},{2,10},{10... | collective-permute-start | bytes 1572872 | tf_op jit(solution)/shard_map/ppermute | solution.py:30

commit v4 on v3

--- a/solution.py
+++ b/solution.py
@@ -139,12 +139,11 @@
     return pl.ds(pl.multiple_of(which * half, ROWS), half)
 
 
-def run_copies(pairs, sems):
+def start_copies(pairs, sems):
     copies = [pltpu.make_async_copy(source, to, sems.at[n]) for n, (source, to) in enumerate(pairs)]
     for copy in copies:
         copy.start()
-    for copy in copies:
-        copy.wait()
+    return copies
 
 
 def load_kernel(
@@ -162,27 +161,53 @@
             (cond_y_ref.at[:, rs, :], ref.at[2:4]),
             (observe_ref.at[1, :, rs, :], ref.at[8:10]),
             (cap_ref.at[:, rs, :], ref.at[10:12]),
-            (observe_ref.at[0, :, rs, :], ref.at[12:14]),
         ]
-    run_copies(pairs, sems)
+    for ref, _, which in halves:
+        pairs.append((observe_ref.at[0, :, half_of(which, half), :], ref.at[12:14]))
+    copies = start_copies(pairs, sems)
+    for copy in copies[:-2]:
+        copy.wait()
     for ref, pay_ref, which in halves:
         rs = half_of(which, half)
         for band in range(2):
             ref[4 + band] = via_at[band, rs, :] * mask_at[band, rs, :].astype(F32)
             ref[6 + band] = ref[10 + band] + pad_conductance * pad_at[band, rs, :].astype(F32)
-        pay_ref[0:half, :] = jnp.where(upper_chip(), ref[8], ref[5])
     for band in range(2):
         own, other = mine_ref[band, half - 1 :, :], send_ref[band, half - 1 :, :]
         last_ref[band : band + 1, :] = jnp.where(me == 1, own, other)
         middle_ref[band : band + 1, :] = jnp.where(me == 1, other, own)
-    none = jnp.zeros((ROWS - 4, middle_ref.shape[1]), F32)
-    pay_send_ref[half:, :] = stack_rows([middle_ref[...], last_ref[...], none])
-
-
-def pay_kernel(mine_ref, got_ref, last_ref, pay_ref, all_last_ref):
-    pay_ref[...] = jnp.where((core() == 1) == upper_chip(), got_ref[0 : pay_ref.shape[0], :], mine_ref[...])
+    width = middle_ref.shape[1]
+    lane = lax.broadcasted_iota(jnp.int32, (ROWS, width), 1)
+    upper = upper_chip()
+    band = jnp.where(upper, 0, 1)
+    for (ref, pay_ref, which), (other_ref, _, _) in (halves, halves[::-1]):
+        carried = jnp.where(which == 0, 0.0, other_ref[band, half - 1 :, :])
+        for k in range(half // ROWS):
+            rs = slice(k * ROWS, (k + 1) * ROWS)
+            cx, cy, seen, via = ref[band, rs, :], ref[2 + band, rs, :], ref[8 + band, rs, :], ref[5, rs, :]
+            up = jnp.where(row_at(width, 0), carried, pltpu.roll(cx, 1, 0))
+            carried = cx[ROWS - 1 :, :]
+            left = jnp.where(lane == 0, 0.0, pltpu.roll(cy, 1, 1))
+            diag = ref[6 + band, rs, :] + cx + cy + up + left + ref[4, rs, :]
+            pay_ref[rs, :] = jnp.where(upper, diag, via)
+            inv = 1.0 / (diag + via)
+            pay_ref[half + k * ROWS : half + (k + 1) * ROWS, :] = jnp.where(upper, seen, seen * inv)
+            if 2 * k * ROWS >= half:
+                at = 3 * half // 2 + k * ROWS
+                pay_ref[at : at + ROWS, :] = inv
+    none = jnp.zeros((ROWS - 4, width), F32)
+    pay_send_ref[5 * half // 2 :, :] = stack_rows([middle_ref[...], last_ref[...], none])
+    for copy in copies[-2:]:
+        copy.wait()
+
+
+def pay_kernel(mine_ref, got_ref, last_ref, pay_ref, more_ref, all_last_ref):
     half = pay_ref.shape[0]
-    own, other = last_ref[...], got_ref[half + 2 : half + 4, :]
+    theirs = (core() == 1) == upper_chip()
+    pay_ref[...] = jnp.where(theirs, got_ref[0:half, :], mine_ref[0:half, :])
+    more_ref[...] = jnp.where(theirs, got_ref[half : 5 * half // 2, :], mine_ref[half:, :])
+    at = 5 * half // 2
+    own, other = last_ref[...], got_ref[at + 2 : at + 4, :]
     all_last_ref[...] = stack_rows([jnp.where(core() == 0, own, other), jnp.where(core() == 0, other, own)])
 
 
@@ -192,26 +217,26 @@
 
 
 def prepare_kernel(
-    mine_ref, got_ref, link_ref, middle_ref, more_ref, last_ref,
-    cx_ref, cy_ref, c_ref, diag_ref, inv_i_ref, s_i_ref, inv_o_ref, s_o_ref, edge_ref, core_ref, cross_ref, cap_ref, seen_ref,
-):
-    half, width = s_o_ref.shape
+    mine_ref, got_ref, middle_ref, more_ref, last_ref,
+    cx_ref, cy_ref, c_ref, diag_ref, inv_ref, s_ref, part_ref, seen_o_ref, edge_ref, cap_ref, seen_ref, all_part, all_seen,
+):
+    half, width = part_ref.shape
     me = core()
     upper = upper_chip()
     lane = lax.broadcasted_iota(jnp.int32, (ROWS, width), 1)
     first_tile = jnp.logical_and(me == 0, lax.axis_index("tile") == 0)
-    places = []
     own_edge = jnp.where(me == 1, middle_ref[...], last_ref[0:2, :])
-    got_edge = jnp.where(me == 1, more_ref[half : half + 2, :], last_ref[2:4, :])
+    got_edge = jnp.where(me == 1, more_ref[5 * half // 2 : 5 * half // 2 + 2, :], last_ref[2:4, :])
+    c_ref[0] = jnp.zeros((half, width), F32)
     for owner, ref, edges in ((me, mine_ref, own_edge), (1 - me, got_ref, got_edge)):
         for band in range(2):
             j = place_of(owner, band)
-            places.append((j, ref, band))
             carried = jnp.where(first_tile, 0.0, edges[band : band + 1, :])
             edge_ref[pl.ds(j, 1), :] = carried
             cx_ref[j] = ref[band]
             cap_ref[j] = ref[10 + band]
             seen_ref[j] = ref[12 + band]
+            all_seen[j] = ref[8 + band]
             via_at = jnp.where(upper, j + 1, j)
 
             @pl.when(via_at < 4)
@@ -225,42 +250,47 @@
                 up = jnp.where(row_at(width, 0), carried, pltpu.roll(cx, 1, 0))
                 carried = cx[ROWS - 1 :, :]
                 cy_ref[j, rs, :] = cut
-                diag_ref[j, rs, :] = diag + cx + cy + up + pltpu.roll(cut, 1, 1)
-
-    @pl.when(upper)
-    def _():
-        c_ref[0] = link_ref[...]
-
-    for j, ref, band in places:
-        @pl.when(j == 0)
-        def _():
-            s_o_ref[...] = ref[8 + band]
-
-        @pl.when(j > 0)
-        def _():
-            s_i_ref[j - 1] = ref[8 + band]
-
-    for k in range(half // ROWS):
+                all_part[j, rs, :] = diag + cx + cy + up + pltpu.roll(cut, 1, 1)
+    part_ref[...] = all_part[0] + c_ref[1]
+    seen_o_ref[...] = all_seen[0]
+    for j in range(1, 4):
+        for k in range(half // ROWS):
+            rs = slice(k * ROWS, (k + 1) * ROWS)
+            diag = all_part[j, rs, :] + c_ref[j, rs, :]
+            if j < 3:
+                diag = diag + c_ref[j + 1, rs, :]
+            inv = 1.0 / diag
+            diag_ref[j - 1, rs, :] = diag
+            inv_ref[j - 1, rs, :] = inv
+            s_ref[j - 1, rs, :] = all_seen[j, rs, :] * inv
+
+
+def outer_kernel(
+    part_ref, seen_ref, link_ref, cx_ref, cy_ref, c_ref, inv_i_ref, s_i_ref,
+    c_out_ref, diag_ref, inv_ref, s_ref, core_ref, cross_ref, fix_ref,
+):
+    rows, width = part_ref.shape
+    upper = upper_chip()
+    for k in range(rows // ROWS):
         rs = slice(k * ROWS, (k + 1) * ROWS)
-        c = [c_ref[j, rs, :] for j in range(4)]
-        for j in range(4):
-            diag = diag_ref[j, rs, :] + c[j]
-            if j < 3:
-                diag = diag + c[j + 1]
-            inv = 1.0 / diag
-            diag_ref[j, rs, :] = diag
-            band_of(inv_o_ref, inv_i_ref, j)[rs, :] = inv
-            s_ref = band_of(s_o_ref, s_i_ref, j)
-            s_ref[rs, :] = s_ref[rs, :] * inv
+        c_out = jnp.where(upper, link_ref[rs, :], c_ref[0, rs, :])
+        diag = part_ref[rs, :] + c_out
+        inv = 1.0 / diag
+        c_out_ref[rs, :] = c_out
+        diag_ref[rs, :] = diag
+        inv_ref[rs, :] = inv
+        s_ref[rs, :] = seen_ref[rs, :] * inv
     ends = []
-    for r, beyond in ((0, 0), (half - 1, half - 2)):
+    for r, beyond in ((0, 0), (rows - 1, rows - 2)):
         at = slice(r, r + 1)
-        rows = [band_of(s_o_ref, s_i_ref, j)[at, :] for j in range(4)]
-        rows += [band_of(inv_o_ref, inv_i_ref, j)[at, :] for j in range(4)]
-        for ref, row in ((cy_ref, r), (c_ref, r), (cx_ref, beyond)):
-            rows += [ref[j, row : row + 1, :] for j in range(4)]
-        ends.append(stack_rows(rows))
+        lines = [band_of(s_ref, s_i_ref, j)[at, :] for j in range(4)]
+        lines += [band_of(inv_ref, inv_i_ref, j)[at, :] for j in range(4)]
+        lines += [cy_ref[j, at, :] for j in range(4)]
+        lines += [c_out_ref[at, :]] + [c_ref[j, at, :] for j in range(1, 4)]
+        lines += [cx_ref[j, beyond : beyond + 1, :] for j in range(4)]
+        ends.append(stack_rows(lines))
     put_rows(ends[0], ends[1], core_ref, cross_ref)
+    fix_ref[...] = jnp.where(upper, diag_ref[0:1, :], s_ref[0:1, :])
 
 
 def own_parts(u_o_ref, u_i_ref, cx_ref, cy_ref, c_ref, pay_ref, scratch_ref):
@@ -332,7 +362,7 @@
     above, below = take_rows(core_ref, cross_ref)
     spread_rows(u_o_ref, u_i_ref, above, below, cx_ref, cy_ref, c_ref, inv_i_ref, edge_ref, v_i_ref, part_ref, sums_ref)
     fluxes = [edge_ref[0:1, :] * above[0:1], cx_ref[0, rows - 1 :, :] * below[0:1]]
-    tail_ref[...] = stack_rows([above[0:1], below[0:1], *fluxes, jnp.zeros((ROWS - 4, width), F32)])
+    tail_ref[...] = stack_rows([above[0:1], below[0:1], *fluxes])
     side_above, side_below = take_rows(side_core_ref, side_cross_ref)
     parts_there, inv = beside(u_o_ref, u_i_ref, above, below, side_above, side_below, edge_ref, cx_ref)
     beside_ref[...] = parts_there
@@ -357,51 +387,62 @@
 
 
 def far_first_kernel(
-    u_o_ref, part_ref, far_ref, c_ref, inv_ref, v_i_ref, sums_ref, cx_ref, cy_ref, v_ref, core_ref, cross_ref, total_ref, pay_ref,
-    scratch_ref,
+    u_o_ref, part_ref, got_ref, more_ref, fix_ref, c_out_ref, inv_ref, v_i_ref, sums_ref, cx_ref, cy_ref, c_ref,
+    v_ref, core_ref, cross_ref, total_ref, pay_ref, inv_far_ref, scratch_ref,
 ):
     rows, width = u_o_ref.shape
+    upper = upper_chip()
     total = jnp.zeros((ROWS, width), F32)
     for k in range(rows // ROWS):
         rs = slice(k * ROWS, (k + 1) * ROWS)
-        part = part_ref[rs, :] + c_ref[0, rs, :] * far_ref[rs, :]
+        c_out = c_out_ref[rs, :]
+        diag, far = got_ref[rs, :] + c_out, more_ref[rs, :]
+        if k == 0:
+            first = jnp.broadcast_to(fix_ref[0:1, :], far.shape)
+            diag = jnp.where(row_at(width, 0), first, diag)
+            far = jnp.where(jnp.logical_and(upper, row_at(width, 0)), first, far)
+        inv_far = 1.0 / jnp.where(upper, 1.0, diag)
+        if k * ROWS < rows // 2:
+            inv_far_ref[rs, :] = jnp.where(upper, more_ref[rows + k * ROWS : rows + (k + 1) * ROWS, :], inv_far)
+        far = jnp.where(upper, far, far * inv_far)
+        part = part_ref[rs, :] + c_out * far
         v = inv_ref[rs, :] * part
         v_ref[rs, :] = v
         total = total + v * part
     total_ref[...] = fold(total) + sums_ref[ROWS : 2 * ROWS, :]
     put_two_rows(v_ref, v_i_ref, core_ref, cross_ref)
     own_parts(v_ref, v_i_ref, cx_ref, cy_ref, c_ref, pay_ref, scratch_ref)
-    size = rows // 2
-    first = pl.multiple_of(jnp.where(upper_chip(), 0, rows - size), ROWS)
-    pay_ref[rows + size :, :] = inv_ref[pl.ds(first, size), :]
-
-
-def finish_kernel(
-    u_o_ref, got_ref, tail_ref, v_i_ref, part_ref, sums_ref, beside_ref, inner_ref, inv_far_ref,
-    cx_ref, cy_ref, c_ref, inv_ref, edge_ref, side_core_ref, side_cross_ref, t0_ref,
-    mail_ref, v_ref, *more,
-):
+
+
+def far_kernel(u_o_ref, got_ref, part_ref, sums_ref, c_out_ref, inv_ref, v_ref, totals_ref):
     rows, width = u_o_ref.shape
-    chunks = rows // ROWS
-    none = jnp.zeros((1, width), F32)
-    sums = [jnp.zeros((ROWS, width), F32) for _ in range(4)]
-    for k in range(chunks):
+    sums = [jnp.zeros((ROWS, width), F32) for _ in range(2)]
+    for k in range(rows // ROWS):
         rs = slice(k * ROWS, (k + 1) * ROWS)
-        part = part_ref[rs, :] + c_ref[0, rs, :] * got_ref[rs, :]
+        part = part_ref[rs, :] + c_out_ref[rs, :] * got_ref[rs, :]
         v = inv_ref[rs, :] * part
         v_ref[rs, :] = v
         sums[0] = sums[0] + u_o_ref[rs, :] * part
         sums[1] = sums[1] + v * part
-    if len(more) == 2:
-        w_ref, fix_ref = more
-    else:
-        w_ref = fix_ref = None
+    totals_ref[0:ROWS, :] = fold(sums[0]) + sums_ref[0:ROWS, :]
+    totals_ref[ROWS : 2 * ROWS, :] = fold(sums[1]) + sums_ref[ROWS : 2 * ROWS, :]
+
+
+def finish_kernel(
+    u_o_ref, v_ref, got_ref, tail_ref, v_i_ref, totals_ref, beside_ref, inner_ref, inv_far_ref,
+    cx_ref, cy_ref, c_ref, c_out_ref, edge_ref, side_core_ref, side_cross_ref, t0_ref,
+    mail_ref, w_ref=None, fix_ref=None,
+):
+    rows, width = u_o_ref.shape
+    chunks = rows // ROWS
+    none = jnp.zeros((1, width), F32)
+    sums = [jnp.zeros((ROWS, width), F32) for _ in range(2)]
     carried = none
     for k in range(chunks):
         rs = slice(k * ROWS, (k + 1) * ROWS)
         v, part, carried = in_band(v_ref, cx_ref.at[0], cy_ref.at[0], carried, none, k, chunks)
         coupled = c_ref[1, rs, :] * v_i_ref[0, rs, :]
-        sums[2] = sums[2] + v * (part + 2.0 * coupled)
+        sums[0] = sums[0] + v * (part + 2.0 * coupled)
         if w_ref is not None:
             w_ref[rs, :] = part + coupled
     side_above, side_below = take_rows(side_core_ref, side_cross_ref)
@@ -417,31 +458,33 @@
     far_down = jnp.where(first + size == rows, tail_ref[3:4, :], 0.0)
     for k in range(size // ROWS):
         at = pl.ds(pl.multiple_of(first + k * ROWS, ROWS), ROWS)
-        c_out = c_ref[0, at, :]
+        c_out = c_out_ref[at, :]
         part = got_ref[rows + k * ROWS : rows + (k + 1) * ROWS, :] + c_out * u_o_ref[at, :]
         if k == 0:
             part = part + jnp.where(row_at(width, 0), far_up, 0.0)
         if k == size // ROWS - 1:
             part = part + jnp.where(row_at(width, ROWS - 1), far_down, 0.0)
-        inv_far = inv_far_ref[rows + size + k * ROWS : rows + size + (k + 1) * ROWS, :]
-        sums[3] = sums[3] + v_ref[at, :] * (c_out * (inv_far * part))
+        sums[1] = sums[1] + v_ref[at, :] * (c_out * (inv_far_ref[k * ROWS : (k + 1) * ROWS, :] * part))
     ends = up * v_ref[0:1, :] + down * v_ref[rows - 1 :, :]
-    last = fold(sums[2] + 2.0 * sums[3] + jnp.where(row_at(width, 0), ends, 0.0)) + inner_ref[...]
-    terms = (
-        t0_ref[...], fold(sums[0]) + sums_ref[0:ROWS, :], fold(sums[1]) + sums_ref[ROWS : 2 * ROWS, :], last
-    )
-    lines = [jnp.sum(t, 0, keepdims=True) for t in terms]
-    block = jnp.concatenate(lines + lines, 0)
+    last = fold(sums[0] + 2.0 * sums[1] + jnp.where(row_at(width, 0), ends, 0.0)) + inner_ref[...]
+    terms = (t0_ref[...], totals_ref[0:ROWS, :], totals_ref[ROWS : 2 * ROWS, :], last)
+    lane = lax.broadcasted_iota(jnp.int32, (ROWS, 128), 1)
+    row = jnp.zeros((ROWS, 128), F32)
+    for n, t in enumerate(terms):
+        t = t + pltpu.roll(t, 64, 1)
+        t = t + pltpu.roll(t, 32, 1)
+        row = jnp.where(lane // 32 == n, t, row)
+    row = jnp.broadcast_to(jnp.sum(row, 0, keepdims=True), (ROWS, 128))
     for at in range(0, mail_ref.shape[0], ROWS):
-        mail_ref[at : at + ROWS, :] = block
+        mail_ref[at : at + ROWS, :] = row
 
 
 def weights(mail_ref):
     block = mail_ref[0:ROWS, :]
     for at in range(ROWS, mail_ref.shape[0], ROWS):
         block = block + mail_ref[at : at + ROWS, :]
-    g = jnp.sum(block[0:4] + block[4:8], 1, keepdims=True)
-    g0, g1, g2, g3 = (g[k : k + 1] for k in range(4))
+    block = jnp.sum(block, 0, keepdims=True)
+    g0, g1, g2, g3 = (jnp.sum(block[:, 32 * k : 32 * (k + 1)], 1, keepdims=True) for k in range(4))
     mu = g1 / g0
     h = g2 - mu * g1
     t = h / (h - (g3 - 2.0 * mu * g2 + mu * mu * g1))
@@ -466,7 +509,7 @@
 
 def step_kernel(
     mail_ref, s_o_ref, s_i_ref, v1_o_ref, v1_i_ref, v2_o_ref, v2_i_ref, part_i_ref, part_ref, far_ref, fix_ref, cap_ref, seen_ref,
-    diag_ref, inv_o_ref, inv_i_ref, cx_ref, cy_ref, c_ref,
+    diag_o_ref, diag_i_ref, inv_o_ref, inv_i_ref, cx_ref, cy_ref, c_ref, c_out_ref,
     z_o_ref, z_i_ref, core_ref, cross_ref, total_ref, pay_ref, x_mine_ref, z_mine_ref, scratch_ref,
 ):
     rows, width = s_o_ref.shape
@@ -476,15 +519,15 @@
     for j in range(4):
         for k in range(chunks):
             rs = slice(k * ROWS, (k + 1) * ROWS)
-            s, p, q, inv = (
+            s, p, q, diag, inv = (
                 band_of(o, i, j)[rs, :]
                 for o, i in (
                     (s_o_ref, s_i_ref), (v1_o_ref, v1_i_ref), (v2_o_ref, v2_i_ref),
-                    (inv_o_ref, inv_i_ref),
+                    (diag_o_ref, diag_i_ref), (inv_o_ref, inv_i_ref),
                 )
             )
             if j == 0:
-                part = part_ref[rs, :] + c_ref[0, rs, :] * far_ref[rs, :]
+                part = part_ref[rs, :] + c_out_ref[rs, :] * far_ref[rs, :]
                 if k == 0:
                     part = part + jnp.where(row_at(width, 0), fix_ref[0:1, :], 0.0)
                 if k == chunks - 1:
@@ -495,7 +538,7 @@
                     part = part + c_ref[1, rs, :] * v2_o_ref[rs, :]
             r = inv * part
             x = s + a * p + b * q
-            residual = cap_ref[j, rs, :] * x + seen_ref[j, rs, :] - diag_ref[j, rs, :] * (x - (p + a * q + b * r))
+            residual = cap_ref[j, rs, :] * x + seen_ref[j, rs, :] - diag * (x - (p + a * q + b * r))
             z = residual * inv
             band_of(z_o_ref, z_i_ref, j)[rs, :] = z
             total = total + residual * z
@@ -540,62 +583,71 @@
     _, rows, width = cond_x.shape
     half = rows // 2
     field, three, four, edge = shape(half, width), shape(3, half, width), shape(4, half, width), shape(4, width)
-    eight, sides = shape(ROWS, width), shape(20, width)
+    eight, twenty = shape(ROWS, width), shape(20, width)
+    most, part_rows = shape(3 * half // 2, width), shape(half // 2, width)
     rim, pair = shape(2, width), shape(2, half, width)
-    mail = shape(lax.axis_size("band") * lax.axis_size("tile") * 4, 128)
+    mail = shape(lax.axis_size("band") * lax.axis_size("tile"), 128)
     one, two = shape(ROWS, 128), shape(2 * ROWS, 128)
     fourteen = shape(14, half, width)
     whole, whole_int = pltpu.VMEM((2, rows, width), F32), pltpu.VMEM((2, rows, width), jnp.int32)
     own, send, pay, pay_send, last, middle = call(
-        load_kernel, [fourteen, fourteen, field, shape(half + ROWS, width), rim, rim],
+        load_kernel, [fourteen, fourteen, shape(5 * half // 2, width), shape(5 * half // 2 + ROWS, width), rim, rim],
         cond_x, cond_y, via_cond, via_mask, capacitance, pad_mask, observe, name="load", place=pltpu.HBM,
         scratch=[whole, whole_int, whole_int, pltpu.SemaphoreType.DMA((13,))],
     )
     more = core_swap(pay_send)
     more, send = lax.optimization_barrier((more, send))
-    pay, last = call(pay_kernel, [field, edge], pay, more, last, name="pay")
+    pay, pay_more, last = call(pay_kernel, [field, most, edge], pay, more, last, name="pay")
     link, traded, last = outer_swap(pay), core_swap(send), cross_swap(last)
-    cx, cy, c, diag, inv_i, s_i, inv_o, s_o, cx_edge, near, cross, cap, earlier = call(
-        prepare_kernel,
-        [four, four, four, four, three, three, field, field, edge, sides, sides, four, four],
-        own, traded, link, middle, more, last, name="prepare",
+    pay_more, last = lax.optimization_barrier((pay_more, last))
+    far = outer_swap(pay_more)
+    cx, cy, c, diag_i, inv_i, s_i, part, seen, cx_edge, cap, earlier = call(
+        prepare_kernel, [four, four, four, three, three, three, field, field, edge, four, four],
+        own, traded, middle, more, last, name="prepare", cost=0,
+        scratch=[pltpu.VMEM((4, half, width), F32), pltpu.VMEM((4, half, width), F32)],
     )
-    far, sides = outer_swap(s_o), (core_swap(near), cross_swap(cross))
+    c_out, diag_o, inv_o, s_o, near, cross, fix = call(
+        outer_kernel, [field, field, field, field, twenty, twenty, shape(1, width)],
+        part, seen, link, cx, cy, c, inv_i, s_i, name="outer",
+    )
+    fix, sides = outer_swap(fix), (core_swap(near), cross_swap(cross))
 
     coeffs = (cx, cy, c, inv_i, cx_edge)
     parts_of = [pltpu.VMEM((half, width), F32)]
     v1_i, part, sums = call(spread_kernel, [three, field, two], s_o, s_i, *sides, *coeffs, name="first_spread", cost=0)
-    v1_o, near, cross, t0, pay = call(
-        far_first_kernel, [field, eight, eight, one, shape(2 * half, width)],
-        s_o, part, far, c, inv_o, v1_i, sums, cx, cy, name="first_far", scratch=parts_of,
+    v1_o, near, cross, t0, pay, inv_far = call(
+        far_first_kernel, [field, eight, eight, one, most, part_rows],
+        s_o, part, link, far, fix, c_out, inv_o, v1_i, sums, cx, cy, c, name="first_far", scratch=parts_of,
     )
 
-    def stage(u_o, u_i, pay, near, cross, t0, inv_far, name, further):
+    def stage(u_o, u_i, pay, near, cross, t0, name, further):
         got, cross, near = outer_swap(pay), cross_swap(cross), core_swap(near)
         v_i, part, sums, tail, there, inner, *w_i = call(
-            two_spread_kernel, [three, field, two, eight, eight, one] + [three] * further,
+            two_spread_kernel, [three, field, two, edge, eight, one] + [three] * further,
             u_o, u_i, near, cross, *coeffs, *sides, name=name + "_spread", cost=0,
         )
-        parts, v_o, *more = call(
-            finish_kernel, [mail, field] + [field, rim] * further,
-            u_o, got, outer_swap(tail), v_i, part, sums, there, inner, got if further else inv_far,
-            cx, cy, c, inv_o, cx_edge, *sides, t0, name=name + "_finish",
-        )
+        v_o, totals = call(far_kernel, [field, two], u_o, got, part, sums, c_out, inv_o, name=name + "_far")
         if further:
-            more = *w_i, *more, outer_swap(v_o)
+            more = (outer_swap(v_o),)
         else:
             mine, send = call(give_kernel, [pair, shape(2 * half, width)], v_o, v_i, name="give")
             more = mine, core_swap(send)
-        return v_o, v_i, all_total(parts), got, near, more
-
-    v2_o, v2_i, total, inv_far, _, (part_i, part, fix, far) = stage(v1_o, v1_i, pay, near, cross, t0, None, "later", True)
+        parts, *rest = call(
+            finish_kernel, [mail] + [field, rim] * further,
+            u_o, v_o, got, outer_swap(tail), v_i, totals, there, inner, inv_far,
+            cx, cy, c, c_out, cx_edge, *sides, t0, name=name + "_finish",
+        )
+        more = *w_i, *rest, *more
+        return v_o, v_i, all_total(parts), near, more
+
+    v2_o, v2_i, total, _, (part_i, part, fix, far) = stage(v1_o, v1_i, pay, near, cross, t0, "later", True)
     z_o, z_i, near, cross, t0, pay, x_mine, z_mine = call(
         step_kernel,
-        [field, three, shape(ROWS + 4 * half, width), shape(ROWS, width), one, shape(half + half // 2, width), pair, pair],
-        total, s_o, s_i, v1_o, v1_i, v2_o, v2_i, part_i, part, far, fix, cap, earlier, diag, inv_o, inv_i, cx, cy, c,
+        [field, three, shape(ROWS + 4 * half, width), eight, one, most, pair, pair],
+        total, s_o, s_i, v1_o, v1_i, v2_o, v2_i, part_i, part, far, fix, cap, earlier, diag_o, diag_i, inv_o, inv_i, cx, cy, c, c_out,
         name="step", scratch=parts_of,
     )
-    _, _, total, _, got, given = stage(z_o, z_i, pay, near, cross, t0, inv_far, "earlier", False)
+    _, _, total, got, given = stage(z_o, z_i, pay, near, cross, t0, "earlier", False)
     (out,) = call(
         last_kernel, [shape(2, 2, rows, width)], total, x_mine, z_mine, got, *given, name="last", out_place=pl.ANY,
         scratch=[pltpu.VMEM((4, half, width), F32), pltpu.SemaphoreType.DMA((8,))],

time: 81.2 us -> 75.8 us (0.933)
  blocking collectives: 21.3 us -> 18.3 us
  waiting for transfers between devices: 21.4 us -> 18.7 us
    all_to_all x2, blocking collectives: 21.3 us -> 18.3 us  [all_total(): return lax.all_to_all(parts, AXES, 0, 0, tiled=True)]
    ppermute x7 -> x8, waiting for transfers between devices: 7.05 us -> 4.22 us  [outer_swap(): return lax.ppermute(x, 'band', [(b, b ^ 2) for b in range(nb)])]
    ppermute x4, starting transfers between devices: 13.7 us -> 12.6 us  [cross_swap(): return lax.ppermute(x, AXES, pairs)]
    ppermute x7 -> x8, starting transfers between devices: 9.74 us -> 10.6 us  [outer_swap(): return lax.ppermute(x, 'band', [(b, b ^ 2) for b in range(nb)])]
    pallas_call x12 -> x15, Pallas kernels: 13.7 us -> 14.3 us  [call(): pl.pallas_call(body, out_shape=outs, in_specs=[pl.BlockSpec(memory_space=...]
  transfers between devices with their start and end apart: 17 -> 18, of which waited for: 9 -> 8; matrix products, arithmetic and copies ran while one was open for 0% -> 0% of each run, Pallas kernels for 5% -> 9%
where the time goes in v4:
time: 75.8 us; the launch traced here: 75.7 us
  starting transfers between devices  24.2 us (32%)
  waiting for transfers between devices  18.7 us (25%)
  blocking collectives  18.3 us (24%)
  Pallas kernels  14.3 us (19%)
    all_to_all x2, blocking collectives, all_total(): return lax.all_to_all(parts, AXES, 0, 0, tiled=True)  18.3 us
    pallas_call x15, Pallas kernels, call(): pl.pallas_call(body, out_shape=outs, in_specs=[pl.BlockSpec(memory_space=...  14.3 us
    ppermute x4, waiting for transfers between devices, cross_swap(): return lax.ppermute(x, AXES, pairs)  12.6 us
    ppermute x4, starting transfers between devices, cross_swap(): return lax.ppermute(x, AXES, pairs)  12.6 us
    ppermute x8, starting transfers between devices, outer_swap(): return lax.ppermute(x, 'band', [(b, b ^ 2) for b in range(nb)])  10.6 us
    ppermute x8, waiting for transfers between devices, outer_swap(): return lax.ppermute(x, 'band', [(b, b ^ 2) for b in range(nb)])  4.22 us
    ppermute x6, waiting for transfers between devices, core_swap(): return lax.ppermute(x, 'band', [(b, b ^ 1) for b in range(nb)])  1.83 us
  transfers between devices with their start and end apart: 18, of which 8 were waited for; matrix products, arithmetic and copies ran while one was open for 0% of the time, Pallas kernels for 9%

profile of v4, /device:TPU:0, one launch (start us, length us, event | category | flops | bytes accessed | tf_op | source)
XLA Modules:
  0.0 75.7 jit_solution(13892597136119592894)
XLA Ops:
  0.0 4.1 %load.1 = (f32[14,32,2048]{2,1,0:T(8,128)S(1)}, f32[14,32,2048]{2,1,0:T(8,128)S(1)}, f32[80,2048]{1,0:T(8,128)S(1)}, f32[88,2048]{1,0:T(8,128)S(1)}, f32[2,2048]{1,0:T(2,128)S(1)}, /*index=5*/f32[2,2048]{1,0:T(2,128)S(1)}) custom-call(f32[2,64,2048]{2,1,0:T(8,128)} %cond_x_ref.1, f32[2,64,2048]{2,1,0:T(8,128)} %cond_y_ref.1, f32[2,64,2048]{2,1,0:T(8,128)} %via_ref.1, ...), custom_call_target="tpu_custom_call" | custom-call | flops 10000000000 | bytes 10000000 | tf_op jit(solution)/shard_map/load/pallas_call | solution.py:55
  4.1 0.5 collective-permute-start
  4.6 1.8 %collective-permute-done.got_ref.more_ref = f32[88,2048]{1,0:T(8,128)S(1)} collective-permute-done((f32[88,2048]{1,0:T(8,128)S(1)}, f32[88,2048]{1,0:T(8,128)S(1)}, u32[]{:S(2)}, u32[]{:S(2)}) %collective-permute-start) | collective-permute-done | bytes 720928 | tf_op jit(solution)/shard_map/ppermute | solution.py:30
  6.4 0.4 collective-permute-start.1
  6.8 0.1 pay.1
  6.9 2.7 %collective-permute-start.3 = (f32[32,2048]{1,0:T(8,128)S(1)}, f32[32,2048]{1,0:T(8,128)S(1)}, u32[]{:S(2)}, u32[]{:S(2)}) collective-permute-start(f32[32,2048]{1,0:T(8,128)S(1)} %get-tuple-element.88), channel_id=1, source_target_pairs={{0,16},{8,24},{16,0},{24,8},{1,17},{9,25},{17,1},{25,9},{2,18},{10... | collective-permute-start | bytes 786440 | tf_op jit(solution)/shard_map/ppermute | solution.py:35
  9.6 4.2 %collective-permute-start.2 = (f32[4,2048]{1,0:T(4,128)S(1)}, f32[4,2048]{1,0:T(4,128)S(1)}, u32[]{:S(2)}, u32[]{:S(2)}) collective-permute-start(f32[4,2048]{1,0:T(4,128)S(1)} %get-tuple-element.84), channel_id=1, source_target_pairs={{0,15},{1,8},{2,9},{3,10},{4,11},{5,12},{6,13},{7,14},{8,1},{9,2},... | collective-permute-start | bytes 98312 | tf_op jit(solution)/shard_map/ppermute | solution.py:45
  13.8 1.8 %collective-permute-done.2.last_ref = f32[4,2048]{1,0:T(4,128)S(1)} collective-permute-done((f32[4,2048]{1,0:T(4,128)S(1)}, f32[4,2048]{1,0:T(4,128)S(1)}, u32[]{:S(2)}, u32[]{:S(2)}) %collective-permute-start.2) | collective-permute-done | bytes 32800 | tf_op jit(solution)/shard_map/ppermute | solution.py:45
  15.6 0.3 collective-permute-start.6
  15.9 0.0 collective-permute-done.1.got_ref
  15.9 1.0 %prepare.1 = (f32[4,32,2048]{2,1,0:T(8,128)S(1)}, f32[4,32,2048]{2,1,0:T(8,128)S(1)}, f32[4,32,2048]{2,1,0:T(8,128)S(1)}, f32[3,32,2048]{2,1,0:T(8,128)S(1)}, f3...) custom-call(f32[14,32,2048]{2,1,0:T(8,128)S(1)} %get-tuple-element.7, ...), custom_call_target="tpu_custom_call" | custom-call | tf_op jit(solution)/shard_map/prepare/pallas_call | solution.py:55
  17.0 0.0 collective-permute-done.3.link_ref.got_ref
  17.0 0.3 outer.1
  17.3 0.1 collective-permute-start.4
  17.4 4.3 %collective-permute-start.5 = (f32[20,2048]{1,0:T(8,128)S(1)}, f32[20,2048]{1,0:T(8,128)S(1)}, u32[]{:S(2)}, u32[]{:S(2)}) collective-permute-start(f32[20,2048]{1,0:T(8,128)S(1)} %get-tuple-element.96), channel_id=1, source_target_pairs={{0,15},{1,8},{2,9},{3,10},{4,11},{5,12},{6,13},{7,14},{8,1},{9,2},... | collective-permute-start | bytes 491528 | tf_op jit(solution)/shard_map/ppermute | solution.py:45
  21.7 1.5 %collective-permute-start.7 = (f32[1,2048]{1,0:T(1,128)S(1)}, f32[1,2048]{1,0:T(1,128)S(1)}, u32[]{:S(2)}, u32[]{:S(2)}) collective-permute-start(f32[1,2048]{1,0:T(1,128)S(1)} %get-tuple-element.100), channel_id=1, source_target_pairs={{0,16},{8,24},{16,0},{24,8},{1,17},{9,25},{17,1},{25,9},{2,18},{10... | collective-permute-start | bytes 24584 | tf_op jit(solution)/shard_map/ppermute | solution.py:35
  23.2 0.0 collective-permute-done.4.core_ref.side_core_ref
  23.2 2.1 %collective-permute-done.5.cross_ref.side_cross_ref = f32[20,2048]{1,0:T(8,128)S(1)} collective-permute-done((f32[20,2048]{1,0:T(8,128)S(1)}, f32[20,2048]{1,0:T(8,128)S(1)}, u32[]{:S(2)}, u32[]{:S(2)}) %collective-permute-start.5) | collective-permute-done | bytes 163872 | tf_op jit(solution)/shard_map/ppermute | solution.py:45
  25.3 0.9 %first_spread.1 = (f32[3,32,2048]{2,1,0:T(8,128)S(1)}, f32[32,2048]{1,0:T(8,128)S(1)}, f32[16,128]{1,0:T(8,128)S(1)}) custom-call(f32[32,2048]{1,0:T(8,128)S(1)} %get-tuple-element.94.u_o_ref.s_o_ref, f32[3,32,2048]{2,1,0:T(8,128)S(1)} %get-tuple-element.93.s_i_ref.u_i_ref, f32[20,2048]{1,0:T(8,128)S(1)} %collective-permute-done.4.core_ref.side_core_ref, ...), custom_call_target="tpu_custom_call" | custom-call | tf_op jit(solution)/shard_map/first_spread/pallas_call | solution.py:55
  26.2 0.0 collective-permute-done.7.fix_ref
  26.2 0.4 first_far.1
  26.7 1.8 %collective-permute-start.8 = (f32[48,2048]{1,0:T(8,128)S(1)}, f32[48,2048]{1,0:T(8,128)S(1)}, u32[]{:S(2)}, u32[]{:S(2)}) collective-permute-start(f32[48,2048]{1,0:T(8,128)S(1)} %get-tuple-element.106), channel_id=1, source_target_pairs={{0,16},{8,24},{16,0},{24,8},{1,17},{9,25},{17,1},{25,9},{2,18},{10... | collective-permute-start | bytes 1179656 | tf_op jit(solution)/shard_map/ppermute | solution.py:35
  28.4 0.0 collective-permute-start.9
  28.4 3.7 %collective-permute-start.10 = (f32[8,2048]{1,0:T(8,128)S(1)}, f32[8,2048]{1,0:T(8,128)S(1)}, u32[]{:S(2)}, u32[]{:S(2)}) collective-permute-start(f32[8,2048]{1,0:T(8,128)S(1)} %get-tuple-element.108), channel_id=1, source_target_pairs={{0,15},{1,8},{2,9},{3,10},{4,11},{5,12},{6,13},{7,14},{8,1},{9,2},... | collective-permute-start | bytes 196616 | tf_op jit(solution)/shard_map/ppermute | solution.py:45
  32.1 2.7 %collective-permute-done.10.cross_ref = f32[8,2048]{1,0:T(8,128)S(1)} collective-permute-done((f32[8,2048]{1,0:T(8,128)S(1)}, f32[8,2048]{1,0:T(8,128)S(1)}, u32[]{:S(2)}, u32[]{:S(2)}) %collective-permute-start.10) | collective-permute-done | bytes 65568 | tf_op jit(solution)/shard_map/ppermute | solution.py:45
  34.8 1.7 %later_spread.1 = (f32[3,32,2048]{2,1,0:T(8,128)S(1)}, f32[32,2048]{1,0:T(8,128)S(1)}, f32[16,128]{1,0:T(8,128)S(1)}, f32[4,2048]{1,0:T(4,128)S(1)}, f32[8,2048]...) custom-call(f32[32,2048]{1,0:T(8,128)S(1)} %get-tuple-element.105.u_o_ref.v1_o_ref, ...), custom_call_target="tpu_custom_call" | custom-call | tf_op jit(solution)/shard_map/later_spread/pallas_call | solution.py:55
  36.5 0.4 collective-permute-start.11
  36.9 0.1 later_far.1
  37.0 1.8 %collective-permute-start.12 = (f32[32,2048]{1,0:T(8,128)S(1)}, f32[32,2048]{1,0:T(8,128)S(1)}, u32[]{:S(2)}, u32[]{:S(2)}) collective-permute-start(f32[32,2048]{1,0:T(8,128)S(1)} %get-tuple-element.111.v_ref.v2_o_ref), channel_id=1, source_target_pairs={{0,16},{8,24},{16,0},{24,8},{1,17},{9,25},{17,1},{25,9},{2,18},{10... | collective-permute-start | bytes 786440 | tf_op jit(solution)/shard_map/ppermute | solution.py:35
  38.7 2.0 %collective-permute-done.11.tail_ref = f32[4,2048]{1,0:T(4,128)S(1)} collective-permute-done((f32[4,2048]{1,0:T(4,128)S(1)}, f32[4,2048]{1,0:T(4,128)S(1)}, u32[]{:S(2)}, u32[]{:S(2)}) %collective-permute-start.11) | collective-permute-done | bytes 32800 | tf_op jit(solution)/shard_map/ppermute | solution.py:35
  40.8 0.5 later_finish.1
  41.2 9.5 %all_to_all.22 = f32[32,1,128]{2,1,0:T(1,128)S(1)} all-to-all(f32[32,1,128]{2,1,0:T(1,128)S(1)} %bitcast.11), channel_id=1, replica_groups=mesh['band'=4,'tile'=8] {'band','tile'}, dimensions={0} | all-to-all | bytes 32768 | tf_op jit(solution)/shard_map/all_to_all | solution.py:49
  50.8 1.5 %step.1 = (f32[32,2048]{1,0:T(8,128)S(1)}, f32[3,32,2048]{2,1,0:T(8,128)S(1)}, f32[136,2048]{1,0:T(8,128)S(1)}, f32[8,2048]{1,0:T(8,128)S(1)}, f32[8,128]{1,0:T(...) custom-call(f32[32,128]{1,0:T(8,128)S(1)} %bitcast.8, ...), custom_call_target="tpu_custom_call" | custom-call | flops 10000000000 | bytes 10000000 | tf_op jit(solution)/shard_map/step/pallas_call | solution.py:55
  52.3 0.1 collective-permute-start.14
  52.4 0.7 collective-permute-start.13
  53.1 0.3 collective-permute-start.15
  53.4 6.1 %collective-permute-done.15.cross_ref = f32[8,2048]{1,0:T(8,128)S(1)} collective-permute-done((f32[8,2048]{1,0:T(8,128)S(1)}, f32[8,2048]{1,0:T(8,128)S(1)}, u32[]{:S(2)}, u32[]{:S(2)}) %collective-permute-start.15) | collective-permute-done | bytes 65568 | tf_op jit(solution)/shard_map/ppermute | solution.py:45
  59.5 0.0 collective-permute-done.14.core_ref.got_ref
  59.5 1.6 %earlier_spread.1 = (f32[3,32,2048]{2,1,0:T(8,128)S(1)}, f32[32,2048]{1,0:T(8,128)S(1)}, f32[16,128]{1,0:T(8,128)S(1)}, f32[4,2048]{1,0:T(4,128)S(1)}, f32[8,2048]{1,0:T(8,128)S(1)}, /*index=5*/f32[8,128]{1,0:T(8,128)S(1)}) custom-call(f32[32,2048]{1,0:T(8,128)S(1)} %get-tuple-element.127.u_o_ref, f32[3,32,2048]{2,1,0:T(8,128)S(1)} %get-tuple-element.129.u_i_ref, ...), custom_call_target="tpu_custom_call" | custom-call | tf_op jit(solution)/shard_map/earlier_spread/pallas_call | solution.py:55
  61.0 1.5 %collective-permute-start.16 = (f32[4,2048]{1,0:T(4,128)S(1)}, f32[4,2048]{1,0:T(4,128)S(1)}, u32[]{:S(2)}, u32[]{:S(2)}) collective-permute-start(f32[4,2048]{1,0:T(4,128)S(1)} %get-tuple-element.135), channel_id=1, source_target_pairs={{0,16},{8,24},{16,0},{24,8},{1,17},{9,25},{17,1},{25,9},{2,18},{10... | collective-permute-start | bytes 98312 | tf_op jit(solution)/shard_map/ppermute | solution.py:35
  62.5 1.8 %collective-permute-done.13.got_ref = f32[48,2048]{1,0:T(8,128)S(1)} collective-permute-done((f32[48,2048]{1,0:T(8,128)S(1)}, f32[48,2048]{1,0:T(8,128)S(1)}, u32[]{:S(2)}, u32[]{:S(2)}) %collective-permute-start.13) | collective-permute-done | bytes 393248 | tf_op jit(solution)/shard_map/ppermute | solution.py:35
  64.3 0.1 earlier_far.1
  64.4 0.1 give.1
  64.5 0.1 collective-permute-start.17
  64.6 0.4 collective-permute-done.16.tail_ref
  65.0 0.5 earlier_finish.1
  65.5 8.8 %all_to_all.23 = f32[32,1,128]{2,1,0:T(1,128)S(1)} all-to-all(f32[32,1,128]{2,1,0:T(1,128)S(1)} %bitcast.9), channel_id=1, replica_groups=mesh['band'=4,'tile'=8] {'band','tile'}, dimensions={0} | all-to-all | bytes 32768 | tf_op jit(solution)/shard_map/all_to_all | solution.py:49
  74.3 1.4 %last.1 = f32[2,2,64,2048]{3,2,1,0:T(8,128)} custom-call(f32[32,128]{1,0:T(8,128)S(1)} %bitcast.10, f32[2,32,2048]{2,1,0:T(8,128)S(1)} %get-tuple-element.141.x_mine_ref, f32[2,32,2048]{2,1,0:T(8,128)S(1)} %get-tuple-element.142.z_mine_ref, f32[136,2048]{1,0:T(8,128)S(1)} %collective-permute-done.14.core_ref.got_ref, ...), custom_call_target="tpu_custom_call" | custom-call | flops 10000000000 | bytes 10000000 | tf_op jit(solution)/shard_map/last/pallas_call | solution.py:55
  (5 shorter events, 0.0 us)
Async XLA Ops:
  4.1 2.3 %collective-permute-start = (f32[88,2048]{1,0:T(8,128)S(1)}, f32[88,2048]{1,0:T(8,128)S(1)}, u32[]{:S(2)}, u32[]{:S(2)}) collective-permute-start(f32[88,2048]{1,0:T(8,128)S(1)} %get-tuple-element.76), channel_id=1, source_target_pairs={{0,8},{8,0},{16,24},{24,16},{1,9},{9,1},{17,25},{25,17},{2,10},{10... | collective-permute-start | bytes 2162696 | tf_op jit(solution)/shard_map/ppermute | solution.py:30
  6.4 9.5 %collective-permute-start.1 = (f32[14,32,2048]{2,1,0:T(8,128)S(1)}, f32[14,32,2048]{2,1,0:T(8,128)S(1)}, u32[]{:S(2)}, u32[]{:S(2)}) collective-permute-start(f32[14,32,2048]{2,1,0:T(8,128)S(1)} %get-tuple-element.78), channel_id=1, source_target_pairs={{0,8},{8,0},{16,24},{24,16},{1,9},{9,1},{17,25},{25,17},{2,10},{10... | collective-permute-start | bytes 11010056 | tf_op jit(solution)/shard_map/ppermute | solution.py:30
  6.9 10.1 %collective-permute-start.3 = (f32[32,2048]{1,0:T(8,128)S(1)}, f32[32,2048]{1,0:T(8,128)S(1)}, u32[]{:S(2)}, u32[]{:S(2)}) collective-permute-start(f32[32,2048]{1,0:T(8,128)S(1)} %get-tuple-element.88), channel_id=1, source_target_pairs={{0,16},{8,24},{16,0},{24,8},{1,17},{9,25},{17,1},{25,9},{2,18},{10... | collective-permute-start | bytes 786440 | tf_op jit(solution)/shard_map/ppermute | solution.py:35
  9.6 6.0 %collective-permute-start.2 = (f32[4,2048]{1,0:T(4,128)S(1)}, f32[4,2048]{1,0:T(4,128)S(1)}, u32[]{:S(2)}, u32[]{:S(2)}) collective-permute-start(f32[4,2048]{1,0:T(4,128)S(1)} %get-tuple-element.84), channel_id=1, source_target_pairs={{0,15},{1,8},{2,9},{3,10},{4,11},{5,12},{6,13},{7,14},{8,1},{9,2},... | collective-permute-start | bytes 98312 | tf_op jit(solution)/shard_map/ppermute | solution.py:45
  15.6 10.6 %collective-permute-start.6 = (f32[48,2048]{1,0:T(8,128)S(1)}, f32[48,2048]{1,0:T(8,128)S(1)}, u32[]{:S(2)}, u32[]{:S(2)}) collective-permute-start(f32[48,2048]{1,0:T(8,128)S(1)} %get-tuple-element.99), channel_id=1, source_target_pairs={{0,16},{8,24},{16,0},{24,8},{1,17},{9,25},{17,1},{25,9},{2,18},{10... | collective-permute-start | bytes 1179656 | tf_op jit(solution)/shard_map/ppermute | solution.py:35
  17.3 5.9 %collective-permute-start.4 = (f32[20,2048]{1,0:T(8,128)S(1)}, f32[20,2048]{1,0:T(8,128)S(1)}, u32[]{:S(2)}, u32[]{:S(2)}) collective-permute-start(f32[20,2048]{1,0:T(8,128)S(1)} %get-tuple-element.95), channel_id=1, source_target_pairs={{0,8},{8,0},{16,24},{24,16},{1,9},{9,1},{17,25},{25,17},{2,10},{10... | collective-permute-start | bytes 491528 | tf_op jit(solution)/shard_map/ppermute | solution.py:30
  17.4 7.9 %collective-permute-start.5 = (f32[20,2048]{1,0:T(8,128)S(1)}, f32[20,2048]{1,0:T(8,128)S(1)}, u32[]{:S(2)}, u32[]{:S(2)}) collective-permute-start(f32[20,2048]{1,0:T(8,128)S(1)} %get-tuple-element.96), channel_id=1, source_target_pairs={{0,15},{1,8},{2,9},{3,10},{4,11},{5,12},{6,13},{7,14},{8,1},{9,2},... | collective-permute-start | bytes 491528 | tf_op jit(solution)/shard_map/ppermute | solution.py:45
  21.7 4.5 %collective-permute-start.7 = (f32[1,2048]{1,0:T(1,128)S(1)}, f32[1,2048]{1,0:T(1,128)S(1)}, u32[]{:S(2)}, u32[]{:S(2)}) collective-permute-start(f32[1,2048]{1,0:T(1,128)S(1)} %get-tuple-element.100), channel_id=1, source_target_pairs={{0,16},{8,24},{16,0},{24,8},{1,17},{9,25},{17,1},{25,9},{2,18},{10... | collective-permute-start | bytes 24584 | tf_op jit(solution)/shard_map/ppermute | solution.py:35
  26.7 10.2 %collective-permute-start.8 = (f32[48,2048]{1,0:T(8,128)S(1)}, f32[48,2048]{1,0:T(8,128)S(1)}, u32[]{:S(2)}, u32[]{:S(2)}) collective-permute-start(f32[48,2048]{1,0:T(8,128)S(1)} %get-tuple-element.106), channel_id=1, source_target_pairs={{0,16},{8,24},{16,0},{24,8},{1,17},{9,25},{17,1},{25,9},{2,18},{10... | collective-permute-start | bytes 1179656 | tf_op jit(solution)/shard_map/ppermute | solution.py:35
  28.4 3.7 %collective-permute-start.9 = (f32[8,2048]{1,0:T(8,128)S(1)}, f32[8,2048]{1,0:T(8,128)S(1)}, u32[]{:S(2)}, u32[]{:S(2)}) collective-permute-start(f32[8,2048]{1,0:T(8,128)S(1)} %get-tuple-element.107), channel_id=1, source_target_pairs={{0,8},{8,0},{16,24},{24,16},{1,9},{9,1},{17,25},{25,17},{2,10},{10... | collective-permute-start | bytes 196616 | tf_op jit(solution)/shard_map/ppermute | solution.py:30
  28.4 6.4 %collective-permute-start.10 = (f32[8,2048]{1,0:T(8,128)S(1)}, f32[8,2048]{1,0:T(8,128)S(1)}, u32[]{:S(2)}, u32[]{:S(2)}) collective-permute-start(f32[8,2048]{1,0:T(8,128)S(1)} %get-tuple-element.108), channel_id=1, source_target_pairs={{0,15},{1,8},{2,9},{3,10},{4,11},{5,12},{6,13},{7,14},{8,1},{9,2},... | collective-permute-start | bytes 196616 | tf_op jit(solution)/shard_map/ppermute | solution.py:45
  36.5 4.3 %collective-permute-start.11 = (f32[4,2048]{1,0:T(4,128)S(1)}, f32[4,2048]{1,0:T(4,128)S(1)}, u32[]{:S(2)}, u32[]{:S(2)}) collective-permute-start(f32[4,2048]{1,0:T(4,128)S(1)} %get-tuple-element.112), channel_id=1, source_target_pairs={{0,16},{8,24},{16,0},{24,8},{1,17},{9,25},{17,1},{25,9},{2,18},{10... | collective-permute-start | bytes 98312 | tf_op jit(solution)/shard_map/ppermute | solution.py:35
  37.0 13.8 %collective-permute-start.12 = (f32[32,2048]{1,0:T(8,128)S(1)}, f32[32,2048]{1,0:T(8,128)S(1)}, u32[]{:S(2)}, u32[]{:S(2)}) collective-permute-start(f32[32,2048]{1,0:T(8,128)S(1)} %get-tuple-element.111.v_ref.v2_o_ref), channel_id=1, source_target_pairs={{0,16},{8,24},{16,0},{24,8},{1,17},{9,25},{17,1},{25,9},{2,18},{10... | collective-permute-start | bytes 786440 | tf_op jit(solution)/shard_map/ppermute | solution.py:35
  52.3 7.1 %collective-permute-start.14 = (f32[136,2048]{1,0:T(8,128)S(1)}, f32[136,2048]{1,0:T(8,128)S(1)}, u32[]{:S(2)}, u32[]{:S(2)}) collective-permute-start(f32[136,2048]{1,0:T(8,128)S(1)} %get-tuple-element.130), channel_id=1, source_target_pairs={{0,8},{8,0},{16,24},{24,16},{1,9},{9,1},{17,25},{25,17},{2,10},{10... | collective-permute-start | bytes 3342344 | tf_op jit(solution)/shard_map/ppermute | solution.py:30
  52.4 11.9 %collective-permute-start.13 = (f32[48,2048]{1,0:T(8,128)S(1)}, f32[48,2048]{1,0:T(8,128)S(1)}, u32[]{:S(2)}, u32[]{:S(2)}) collective-permute-start(f32[48,2048]{1,0:T(8,128)S(1)} %get-tuple-element.128), channel_id=1, source_target_pairs={{0,16},{8,24},{16,0},{24,8},{1,17},{9,25},{17,1},{25,9},{2,18},{10... | collective-permute-start | bytes 1179656 | tf_op jit(solution)/shard_map/ppermute | solution.py:35
  53.1 6.4 %collective-permute-start.15 = (f32[8,2048]{1,0:T(8,128)S(1)}, f32[8,2048]{1,0:T(8,128)S(1)}, u32[]{:S(2)}, u32[]{:S(2)}) collective-permute-start(f32[8,2048]{1,0:T(8,128)S(1)} %get-tuple-element.131), channel_id=1, source_target_pairs={{0,15},{1,8},{2,9},{3,10},{4,11},{5,12},{6,13},{7,14},{8,1},{9,2},... | collective-permute-start | bytes 196616 | tf_op jit(solution)/shard_map/ppermute | solution.py:45
  61.0 4.0 %collective-permute-start.16 = (f32[4,2048]{1,0:T(4,128)S(1)}, f32[4,2048]{1,0:T(4,128)S(1)}, u32[]{:S(2)}, u32[]{:S(2)}) collective-permute-start(f32[4,2048]{1,0:T(4,128)S(1)} %get-tuple-element.135), channel_id=1, source_target_pairs={{0,16},{8,24},{16,0},{24,8},{1,17},{9,25},{17,1},{25,9},{2,18},{10... | collective-permute-start | bytes 98312 | tf_op jit(solution)/shard_map/ppermute | solution.py:35
  64.5 9.7 %collective-permute-start.17 = (f32[64,2048]{1,0:T(8,128)S(1)}, f32[64,2048]{1,0:T(8,128)S(1)}, u32[]{:S(2)}, u32[]{:S(2)}) collective-permute-start(f32[64,2048]{1,0:T(8,128)S(1)} %get-tuple-element.144), channel_id=1, source_target_pairs={{0,8},{8,0},{16,24},{24,16},{1,9},{9,1},{17,25},{25,17},{2,10},{10... | collective-permute-start | bytes 1572872 | tf_op jit(solution)/shard_map/ppermute | solution.py:30

commit v5 on v4

--- a/solution.py
+++ b/solution.py
@@ -11,6 +11,8 @@
 F32 = jnp.float32
 
 pad_conductance = 4.0
+
+COSTS = {"prepare": 0, "first_spread": 0, "later_spread": 0, "earlier_spread": 0, "later_out": 0}
 
 
 def sizes():
@@ -49,13 +51,15 @@
     return lax.all_to_all(parts, AXES, 0, 0, tiled=True)
 
 
-def call(body, outs, *args, name, place=pltpu.VMEM, out_place=pltpu.VMEM, scratch=(), limit=10, cost=10):
+def call(body, outs, *args, name, place=pltpu.VMEM, out_place=pltpu.VMEM, scratch=(), limit=10, reuse=False):
+    cost = COSTS.get(name, 10)
     if place == pltpu.HBM:
         args = [pltpu.with_memory_space_constraint(a, pltpu.HBM) for a in args]
     return pl.pallas_call(
         body,
         out_shape=outs,
-        in_specs=[pl.BlockSpec(memory_space=place)] * len(args),
+        in_specs=[pl.BlockSpec(memory_space=pl.ANY if reuse and n == 0 else place) for n in range(len(args))],
+        input_output_aliases={0: 0} if reuse else {},
         out_specs=[pl.BlockSpec(memory_space=out_place)] * len(outs),
         scratch_shapes=list(scratch),
         name=name,
@@ -148,12 +152,16 @@
 
 def load_kernel(
     cond_x_ref, cond_y_ref, via_ref, mask_ref, cap_ref, pad_ref, observe_ref,
-    mine_ref, send_ref, pay_mine_ref, pay_send_ref, last_ref, middle_ref, via_at, mask_at, pad_at, sems,
-):
-    half = send_ref.shape[1]
+    mine_ref, send_ref, pay_mine_ref, pay_send_ref, last_ref, middle_ref,
+    via_at, mask_at, pad_at, edge_at, sems,
+):
+    half, width = send_ref.shape[1:]
     me = core()
+    upper = upper_chip()
+    halves = ((send_ref, pay_send_ref, 1 - me), (mine_ref, pay_mine_ref, me))
     pairs = [(via_ref, via_at), (mask_ref, mask_at), (pad_ref, pad_at)]
-    halves = ((send_ref, pay_send_ref, 1 - me), (mine_ref, pay_mine_ref, me))
+    pairs.append((cond_x_ref.at[:, pl.ds(half - ROWS, ROWS), :], edge_at.at[0]))
+    pairs.append((cond_x_ref.at[:, pl.ds(2 * half - ROWS, ROWS), :], edge_at.at[1]))
     for ref, _, which in halves:
         rs = half_of(which, half)
         pairs += [
@@ -165,49 +173,49 @@
     for ref, _, which in halves:
         pairs.append((observe_ref.at[0, :, half_of(which, half), :], ref.at[12:14]))
     copies = start_copies(pairs, sems)
-    for copy in copies[:-2]:
+    for copy in copies[:5]:
         copy.wait()
-    for ref, pay_ref, which in halves:
+    for band in range(2):
+        middle_ref[band : band + 1, :] = edge_at[0, band, ROWS - 1 :, :]
+        last_ref[band : band + 1, :] = edge_at[1, band, ROWS - 1 :, :]
+    lane = lax.broadcasted_iota(jnp.int32, (ROWS, width), 1)
+    facing = jnp.where(upper, 0, 1)
+    for n, (ref, pay_ref, which) in enumerate(halves):
+        for copy in copies[5 + 4 * n : 9 + 4 * n]:
+            copy.wait()
         rs = half_of(which, half)
         for band in range(2):
             ref[4 + band] = via_at[band, rs, :] * mask_at[band, rs, :].astype(F32)
             ref[6 + band] = ref[10 + band] + pad_conductance * pad_at[band, rs, :].astype(F32)
-    for band in range(2):
-        own, other = mine_ref[band, half - 1 :, :], send_ref[band, half - 1 :, :]
-        last_ref[band : band + 1, :] = jnp.where(me == 1, own, other)
-        middle_ref[band : band + 1, :] = jnp.where(me == 1, other, own)
-    width = middle_ref.shape[1]
-    lane = lax.broadcasted_iota(jnp.int32, (ROWS, width), 1)
-    upper = upper_chip()
-    band = jnp.where(upper, 0, 1)
-    for (ref, pay_ref, which), (other_ref, _, _) in (halves, halves[::-1]):
-        carried = jnp.where(which == 0, 0.0, other_ref[band, half - 1 :, :])
+        carried = jnp.where(which == 0, 0.0, edge_at[0, facing, ROWS - 1 :, :])
         for k in range(half // ROWS):
             rs = slice(k * ROWS, (k + 1) * ROWS)
-            cx, cy, seen, via = ref[band, rs, :], ref[2 + band, rs, :], ref[8 + band, rs, :], ref[5, rs, :]
+            cx, cy, seen, via = ref[facing, rs, :], ref[2 + facing, rs, :], ref[8 + facing, rs, :], ref[5, rs, :]
             up = jnp.where(row_at(width, 0), carried, pltpu.roll(cx, 1, 0))
             carried = cx[ROWS - 1 :, :]
             left = jnp.where(lane == 0, 0.0, pltpu.roll(cy, 1, 1))
-            diag = ref[6 + band, rs, :] + cx + cy + up + left + ref[4, rs, :]
+            diag = ref[6 + facing, rs, :] + cx + cy + up + left + ref[4, rs, :]
+            inv = 1.0 / (diag + via)
             pay_ref[rs, :] = jnp.where(upper, diag, via)
-            inv = 1.0 / (diag + via)
             pay_ref[half + k * ROWS : half + (k + 1) * ROWS, :] = jnp.where(upper, seen, seen * inv)
             if 2 * k * ROWS >= half:
                 at = 3 * half // 2 + k * ROWS
                 pay_ref[at : at + ROWS, :] = inv
-    none = jnp.zeros((ROWS - 4, width), F32)
-    pay_send_ref[5 * half // 2 :, :] = stack_rows([middle_ref[...], last_ref[...], none])
+    pay_send_ref[5 * half // 2 :, :] = stack_rows([middle_ref[...], last_ref[...], jnp.zeros((ROWS - 4, width), F32)])
     for copy in copies[-2:]:
         copy.wait()
 
 
+def theirs():
+    return (core() == 1) == upper_chip()
+
+
 def pay_kernel(mine_ref, got_ref, last_ref, pay_ref, more_ref, all_last_ref):
     half = pay_ref.shape[0]
-    theirs = (core() == 1) == upper_chip()
-    pay_ref[...] = jnp.where(theirs, got_ref[0:half, :], mine_ref[0:half, :])
-    more_ref[...] = jnp.where(theirs, got_ref[half : 5 * half // 2, :], mine_ref[half:, :])
-    at = 5 * half // 2
-    own, other = last_ref[...], got_ref[at + 2 : at + 4, :]
+    end = 5 * half // 2
+    pay_ref[...] = jnp.where(theirs(), got_ref[0:half, :], mine_ref[0:half, :])
+    more_ref[...] = jnp.where(theirs(), got_ref[half:end, :], mine_ref[half:, :])
+    own, other = last_ref[...], got_ref[end + 2 : end + 4, :]
     all_last_ref[...] = stack_rows([jnp.where(core() == 0, own, other), jnp.where(core() == 0, other, own)])
 
 
@@ -493,18 +501,19 @@
     return a - mu * b, b
 
 
-def hand_out(j, value, k, mine_ref, send_ref, first, half):
-    n = jnp.where(upper_chip(), j, 3 - j)
-    owner, band = n // 2, lax.rem(n, 2)
+def hand_out(j, value, k, holds_outer, mine_ref, send_ref, first, half):
+    band = jnp.where(upper_chip(), j % 2, 1 - j % 2)
     size = value.shape[0]
-
-    @pl.when(owner == core())
-    def _():
+    if holds_outer == (j < 2):
         mine_ref[band, k * ROWS : k * ROWS + size, :] = value
-
-    @pl.when(owner != core())
-    def _():
+    else:
         send_ref[pl.ds(pl.multiple_of(first + band * half + k * ROWS, ROWS), size), :] = value
+
+
+def for_holder(body):
+    outer = (core() == 1) != upper_chip()
+    pl.when(outer)(lambda: body(True))
+    pl.when(jnp.logical_not(outer))(lambda: body(False))
 
 
 def step_kernel(
@@ -515,66 +524,82 @@
     rows, width = s_o_ref.shape
     chunks = rows // ROWS
     a, b = weights(mail_ref)
-    total = jnp.zeros((ROWS, width), F32)
-    for j in range(4):
-        for k in range(chunks):
-            rs = slice(k * ROWS, (k + 1) * ROWS)
-            s, p, q, diag, inv = (
-                band_of(o, i, j)[rs, :]
-                for o, i in (
-                    (s_o_ref, s_i_ref), (v1_o_ref, v1_i_ref), (v2_o_ref, v2_i_ref),
-                    (diag_o_ref, diag_i_ref), (inv_o_ref, inv_i_ref),
+
+    def run(holds_outer):
+        total = jnp.zeros((ROWS, width), F32)
+        for j in range(4):
+            for k in range(chunks):
+                rs = slice(k * ROWS, (k + 1) * ROWS)
+                s, p, q, diag, inv = (
+                    band_of(o, i, j)[rs, :]
+                    for o, i in (
+                        (s_o_ref, s_i_ref), (v1_o_ref, v1_i_ref), (v2_o_ref, v2_i_ref),
+                        (diag_o_ref, diag_i_ref), (inv_o_ref, inv_i_ref),
+                    )
                 )
-            )
-            if j == 0:
-                part = part_ref[rs, :] + c_out_ref[rs, :] * far_ref[rs, :]
-                if k == 0:
-                    part = part + jnp.where(row_at(width, 0), fix_ref[0:1, :], 0.0)
-                if k == chunks - 1:
-                    part = part + jnp.where(row_at(width, ROWS - 1), fix_ref[1:2, :], 0.0)
-            else:
-                part = part_i_ref[j - 1, rs, :]
-                if j == 1:
-                    part = part + c_ref[1, rs, :] * v2_o_ref[rs, :]
-            r = inv * part
-            x = s + a * p + b * q
-            residual = cap_ref[j, rs, :] * x + seen_ref[j, rs, :] - diag * (x - (p + a * q + b * r))
-            z = residual * inv
-            band_of(z_o_ref, z_i_ref, j)[rs, :] = z
-            total = total + residual * z
-            hand_out(j, x, k, x_mine_ref, core_ref, ROWS, rows)
-            hand_out(j, z, k, z_mine_ref, core_ref, ROWS + 2 * rows, rows)
-    total_ref[...] = fold(total)
+                if j == 0:
+                    part = part_ref[rs, :] + c_out_ref[rs, :] * far_ref[rs, :]
+                    if k == 0:
+                        part = part + jnp.where(row_at(width, 0), fix_ref[0:1, :], 0.0)
+                    if k == chunks - 1:
+                        part = part + jnp.where(row_at(width, ROWS - 1), fix_ref[1:2, :], 0.0)
+                else:
+                    part = part_i_ref[j - 1, rs, :]
+                    if j == 1:
+                        part = part + c_ref[1, rs, :] * v2_o_ref[rs, :]
+                r = inv * part
+                x = s + a * p + b * q
+                residual = cap_ref[j, rs, :] * x + seen_ref[j, rs, :] - diag * (x - (p + a * q + b * r))
+                z = residual * inv
+                band_of(z_o_ref, z_i_ref, j)[rs, :] = z
+                total = total + residual * z
+                hand_out(j, x, k, holds_outer, x_mine_ref, core_ref, ROWS, rows)
+                hand_out(j, z, k, holds_outer, z_mine_ref, core_ref, ROWS + 2 * rows, rows)
+        total_ref[...] = fold(total)
+
+    for_holder(run)
     put_two_rows(z_o_ref, z_i_ref, core_ref.at[0:ROWS], cross_ref)
     own_parts(z_o_ref, z_i_ref, cx_ref, cy_ref, c_ref, pay_ref, scratch_ref)
 
 
 def give_kernel(q_o_ref, q_i_ref, mine_ref, send_ref):
     rows = q_o_ref.shape[0]
-    for j in range(4):
-        hand_out(j, band_of(q_o_ref, q_i_ref, j)[...], 0, mine_ref, send_ref, 0, rows)
-
-
-def last_kernel(mail_ref, x_mine_ref, z_mine_ref, got_ref, q_mine_ref, q_got_ref, out_ref, answer, sems):
+
+    def run(holds_outer):
+        for j in range(4):
+            hand_out(j, band_of(q_o_ref, q_i_ref, j)[...], 0, holds_outer, mine_ref, send_ref, 0, rows)
+
+    for_holder(run)
+
+
+def out_rows(out_ref, step, band, which):
+    return out_ref.at[step, band, half_of(which, out_ref.shape[2] // 2), :]
+
+
+def later_out_kernel(x_mine_ref, got_ref, out_ref, sems):
     half = x_mine_ref.shape[1]
-    places = []
+    pairs = []
     for band in range(2):
+        at = ROWS + band * half
+        pairs.append((x_mine_ref.at[band], out_rows(out_ref, 1, band, core())))
+        pairs.append((got_ref.at[at : at + half], out_rows(out_ref, 1, band, 1 - core())))
+    for copy in start_copies(pairs, sems):
+        copy.wait()
+
+
+def last_kernel(_, mail_ref, x_mine_ref, z_mine_ref, got_ref, q_mine_ref, q_got_ref, out_ref, answer, sems):
+    half = x_mine_ref.shape[1]
+    a, b = weights(mail_ref)
+    copies = []
+    for band in range(2):
+        at = ROWS + band * half
+        got = got_ref.at[at : at + half], got_ref.at[at + 2 * half : at + 3 * half], q_got_ref.at[band * half : (band + 1) * half]
         mine = [ref.at[band] for ref in (x_mine_ref, z_mine_ref, q_mine_ref)]
-        places.append((band, core(), mine))
-        at = ROWS + band * half
-        got = [got_ref.at[at : at + half], got_ref.at[at + 2 * half : at + 3 * half]]
-        places.append((band, 1 - core(), got + [q_got_ref.at[band * half : (band + 1) * half]]))
-    copies = []
-    for n, (band, which, (x_ref, _, _)) in enumerate(places):
-        copies.append(pltpu.make_async_copy(x_ref, out_ref.at[1, band, half_of(which, half), :], sems.at[n]))
-        copies[-1].start()
-    a, b = weights(mail_ref)
-    for n, (band, which, (x_ref, z_ref, q_ref)) in enumerate(places):
-        answer[n] = x_ref[...] + a * z_ref[...] + b * q_ref[...]
-        copies.append(
-            pltpu.make_async_copy(answer.at[n], out_ref.at[0, band, half_of(which, half), :], sems.at[4 + n])
-        )
-        copies[-1].start()
+        for which, (x_ref, z_ref, q_ref) in ((core(), mine), (1 - core(), got)):
+            n = len(copies)
+            answer[n] = x_ref[...] + a * z_ref[...] + b * q_ref[...]
+            copies.append(pltpu.make_async_copy(answer.at[n], out_rows(out_ref, 0, band, which), sems.at[n]))
+            copies[-1].start()
     for copy in copies:
         copy.wait()
 
@@ -593,7 +618,7 @@
     own, send, pay, pay_send, last, middle = call(
         load_kernel, [fourteen, fourteen, shape(5 * half // 2, width), shape(5 * half // 2 + ROWS, width), rim, rim],
         cond_x, cond_y, via_cond, via_mask, capacitance, pad_mask, observe, name="load", place=pltpu.HBM,
-        scratch=[whole, whole_int, whole_int, pltpu.SemaphoreType.DMA((13,))],
+        scratch=[whole, whole_int, whole_int, pltpu.VMEM((2, 2, ROWS, width), F32), pltpu.SemaphoreType.DMA((15,))],
     )
     more = core_swap(pay_send)
     more, send = lax.optimization_barrier((more, send))
@@ -603,7 +628,7 @@
     far = outer_swap(pay_more)
     cx, cy, c, diag_i, inv_i, s_i, part, seen, cx_edge, cap, earlier = call(
         prepare_kernel, [four, four, four, three, three, three, field, field, edge, four, four],
-        own, traded, middle, more, last, name="prepare", cost=0,
+        own, traded, middle, more, last, name="prepare",
         scratch=[pltpu.VMEM((4, half, width), F32), pltpu.VMEM((4, half, width), F32)],
     )
     c_out, diag_o, inv_o, s_o, near, cross, fix = call(
@@ -614,43 +639,50 @@
 
     coeffs = (cx, cy, c, inv_i, cx_edge)
     parts_of = [pltpu.VMEM((half, width), F32)]
-    v1_i, part, sums = call(spread_kernel, [three, field, two], s_o, s_i, *sides, *coeffs, name="first_spread", cost=0)
+    v1_i, part, sums = call(spread_kernel, [three, field, two], s_o, s_i, *sides, *coeffs, name="first_spread")
     v1_o, near, cross, t0, pay, inv_far = call(
         far_first_kernel, [field, eight, eight, one, most, part_rows],
         s_o, part, link, far, fix, c_out, inv_o, v1_i, sums, cx, cy, c, name="first_far", scratch=parts_of,
     )
 
-    def stage(u_o, u_i, pay, near, cross, t0, name, further):
+    def stage(u_o, u_i, pay, near, cross, t0, name, x_mine=None):
+        further = x_mine is None
         got, cross, near = outer_swap(pay), cross_swap(cross), core_swap(near)
         v_i, part, sums, tail, there, inner, *w_i = call(
             two_spread_kernel, [three, field, two, edge, eight, one] + [three] * further,
-            u_o, u_i, near, cross, *coeffs, *sides, name=name + "_spread", cost=0,
+            u_o, u_i, near, cross, *coeffs, *sides, name=name + "_spread",
         )
+        if not further:
+            (out,) = call(
+                later_out_kernel, [shape(2, 2, rows, width)], x_mine, near, name="later_out", out_place=pl.ANY,
+                scratch=[pltpu.SemaphoreType.DMA((4,))],
+            )
+            part, out = lax.optimization_barrier((part, out))
         v_o, totals = call(far_kernel, [field, two], u_o, got, part, sums, c_out, inv_o, name=name + "_far")
         if further:
             more = (outer_swap(v_o),)
         else:
             mine, send = call(give_kernel, [pair, shape(2 * half, width)], v_o, v_i, name="give")
-            more = mine, core_swap(send)
+            more = out, near, mine, core_swap(send)
         parts, *rest = call(
             finish_kernel, [mail] + [field, rim] * further,
             u_o, v_o, got, outer_swap(tail), v_i, totals, there, inner, inv_far,
             cx, cy, c, c_out, cx_edge, *sides, t0, name=name + "_finish",
         )
         more = *w_i, *rest, *more
-        return v_o, v_i, all_total(parts), near, more
-
-    v2_o, v2_i, total, _, (part_i, part, fix, far) = stage(v1_o, v1_i, pay, near, cross, t0, "later", True)
+        return v_o, v_i, all_total(parts), more
+
+    v2_o, v2_i, total, (part_i, part, fix, far) = stage(v1_o, v1_i, pay, near, cross, t0, "later")
     z_o, z_i, near, cross, t0, pay, x_mine, z_mine = call(
         step_kernel,
         [field, three, shape(ROWS + 4 * half, width), eight, one, most, pair, pair],
         total, s_o, s_i, v1_o, v1_i, v2_o, v2_i, part_i, part, far, fix, cap, earlier, diag_o, diag_i, inv_o, inv_i, cx, cy, c, c_out,
         name="step", scratch=parts_of,
     )
-    _, _, total, got, given = stage(z_o, z_i, pay, near, cross, t0, "earlier", False)
+    _, _, total, (out, got, q_mine, q_got) = stage(z_o, z_i, pay, near, cross, t0, "earlier", x_mine)
     (out,) = call(
-        last_kernel, [shape(2, 2, rows, width)], total, x_mine, z_mine, got, *given, name="last", out_place=pl.ANY,
-        scratch=[pltpu.VMEM((4, half, width), F32), pltpu.SemaphoreType.DMA((8,))],
+        last_kernel, [shape(2, 2, rows, width)], out, total, x_mine, z_mine, got, q_mine, q_got, name="last",
+        out_place=pl.ANY, scratch=[pltpu.VMEM((4, half, width), F32), pltpu.SemaphoreType.DMA((4,))], reuse=True,
     )
     return out
 

time: 75.8 us -> 75.1 us (level)
  waiting for transfers between devices: 18.7 us -> 17.7 us
    ppermute x8, waiting for transfers between devices: 4.22 us -> 3.26 us  [outer_swap(): return lax.ppermute(x, 'band', [(b, b ^ 2) for b in range(nb)])]
    pallas_call x15 -> x16, Pallas kernels: 14.3 us -> 14.5 us  [call(): pl.pallas_call(body, out_shape=outs, in_specs=[pl.BlockSpec(memory_space=...]
  transfers between devices with their start and end apart: 18 -> 18, of which waited for: 8 -> 8; matrix products, arithmetic and copies ran while one was open for 0% -> 0% of each run, Pallas kernels for 9% -> 10%
where the time goes in v5:
time: 75.1 us; the launch traced here: 74.9 us
  starting transfers between devices  24.3 us (32%)
  blocking collectives  18.3 us (24%)
  waiting for transfers between devices  17.7 us (24%)
  Pallas kernels  14.5 us (19%)
    all_to_all x2, blocking collectives, all_total(): return lax.all_to_all(parts, AXES, 0, 0, tiled=True)  18.3 us
    pallas_call x16, Pallas kernels, call(): pl.pallas_call(body, out_shape=outs, in_specs=[pl.BlockSpec(memory_space=...  14.5 us
    ppermute x4, waiting for transfers between devices, cross_swap(): return lax.ppermute(x, AXES, pairs)  12.6 us
    ppermute x4, starting transfers between devices, cross_swap(): return lax.ppermute(x, AXES, pairs)  12.6 us
    ppermute x8, starting transfers between devices, outer_swap(): return lax.ppermute(x, 'band', [(b, b ^ 2) for b in range(nb)])  10.6 us
    ppermute x8, waiting for transfers between devices, outer_swap(): return lax.ppermute(x, 'band', [(b, b ^ 2) for b in range(nb)])  3.26 us
    ppermute x6, waiting for transfers between devices, core_swap(): return lax.ppermute(x, 'band', [(b, b ^ 1) for b in range(nb)])  1.83 us
  transfers between devices with their start and end apart: 18, of which 8 were waited for; matrix products, arithmetic and copies ran while one was open for 0% of the time, Pallas kernels for 10%

profile of v5, /device:TPU:0, one launch (start us, length us, event | category | flops | bytes accessed | tf_op | source)
XLA Modules:
  0.0 74.9 jit_solution(7875182044062832475)
XLA Ops:
  0.0 3.8 %load.1 = (f32[14,32,2048]{2,1,0:T(8,128)S(1)}, f32[14,32,2048]{2,1,0:T(8,128)S(1)}, f32[80,2048]{1,0:T(8,128)S(1)}, f32[88,2048]{1,0:T(8,128)S(1)}, f32[2,2048]{1,0:T(2,128)S(1)}, /*index=5*/f32[2,2048]{1,0:T(2,128)S(1)}) custom-call(f32[2,64,2048]{2,1,0:T(8,128)} %cond_x_ref.1, f32[2,64,2048]{2,1,0:T(8,128)} %cond_y_ref.1, f32[2,64,2048]{2,1,0:T(8,128)} %via_ref.1, ...), custom_call_target="tpu_custom_call" | custom-call | flops 10000000000 | bytes 10000000 | tf_op jit(solution)/shard_map/load/pallas_call | solution.py:58
  3.8 0.5 collective-permute-start
  4.3 1.8 %collective-permute-done.got_ref.more_ref = f32[88,2048]{1,0:T(8,128)S(1)} collective-permute-done((f32[88,2048]{1,0:T(8,128)S(1)}, f32[88,2048]{1,0:T(8,128)S(1)}, u32[]{:S(2)}, u32[]{:S(2)}) %collective-permute-start) | collective-permute-done | bytes 720928 | tf_op jit(solution)/shard_map/ppermute | solution.py:32
  6.1 0.4 collective-permute-start.1
  6.5 0.1 pay.1
  6.6 2.7 %collective-permute-start.3 = (f32[32,2048]{1,0:T(8,128)S(1)}, f32[32,2048]{1,0:T(8,128)S(1)}, u32[]{:S(2)}, u32[]{:S(2)}) collective-permute-start(f32[32,2048]{1,0:T(8,128)S(1)} %get-tuple-element.90), channel_id=1, source_target_pairs={{0,16},{8,24},{16,0},{24,8},{1,17},{9,25},{17,1},{25,9},{2,18},{10... | collective-permute-start | bytes 786440 | tf_op jit(solution)/shard_map/ppermute | solution.py:37
  9.3 4.2 %collective-permute-start.2 = (f32[4,2048]{1,0:T(4,128)S(1)}, f32[4,2048]{1,0:T(4,128)S(1)}, u32[]{:S(2)}, u32[]{:S(2)}) collective-permute-start(f32[4,2048]{1,0:T(4,128)S(1)} %get-tuple-element.86), channel_id=1, source_target_pairs={{0,15},{1,8},{2,9},{3,10},{4,11},{5,12},{6,13},{7,14},{8,1},{9,2},... | collective-permute-start | bytes 98312 | tf_op jit(solution)/shard_map/ppermute | solution.py:47
  13.5 1.8 %collective-permute-done.2.last_ref = f32[4,2048]{1,0:T(4,128)S(1)} collective-permute-done((f32[4,2048]{1,0:T(4,128)S(1)}, f32[4,2048]{1,0:T(4,128)S(1)}, u32[]{:S(2)}, u32[]{:S(2)}) %collective-permute-start.2) | collective-permute-done | bytes 32800 | tf_op jit(solution)/shard_map/ppermute | solution.py:47
  15.3 0.3 collective-permute-start.6
  15.6 0.0 collective-permute-done.1.got_ref
  15.6 1.0 %prepare.1 = (f32[4,32,2048]{2,1,0:T(8,128)S(1)}, f32[4,32,2048]{2,1,0:T(8,128)S(1)}, f32[4,32,2048]{2,1,0:T(8,128)S(1)}, f32[3,32,2048]{2,1,0:T(8,128)S(1)}, f3...) custom-call(f32[14,32,2048]{2,1,0:T(8,128)S(1)} %get-tuple-element.7, ...), custom_call_target="tpu_custom_call" | custom-call | tf_op jit(solution)/shard_map/prepare/pallas_call | solution.py:58
  16.7 0.0 collective-permute-done.3.link_ref.got_ref
  16.7 0.3 outer.1
  17.0 0.1 collective-permute-start.4
  17.1 4.3 %collective-permute-start.5 = (f32[20,2048]{1,0:T(8,128)S(1)}, f32[20,2048]{1,0:T(8,128)S(1)}, u32[]{:S(2)}, u32[]{:S(2)}) collective-permute-start(f32[20,2048]{1,0:T(8,128)S(1)} %get-tuple-element.98), channel_id=1, source_target_pairs={{0,15},{1,8},{2,9},{3,10},{4,11},{5,12},{6,13},{7,14},{8,1},{9,2},... | collective-permute-start | bytes 491528 | tf_op jit(solution)/shard_map/ppermute | solution.py:47
  21.4 1.5 %collective-permute-start.7 = (f32[1,2048]{1,0:T(1,128)S(1)}, f32[1,2048]{1,0:T(1,128)S(1)}, u32[]{:S(2)}, u32[]{:S(2)}) collective-permute-start(f32[1,2048]{1,0:T(1,128)S(1)} %get-tuple-element.102), channel_id=1, source_target_pairs={{0,16},{8,24},{16,0},{24,8},{1,17},{9,25},{17,1},{25,9},{2,18},{10... | collective-permute-start | bytes 24584 | tf_op jit(solution)/shard_map/ppermute | solution.py:37
  22.9 0.0 collective-permute-done.4.core_ref.side_core_ref
  22.9 2.1 %collective-permute-done.5.cross_ref.side_cross_ref = f32[20,2048]{1,0:T(8,128)S(1)} collective-permute-done((f32[20,2048]{1,0:T(8,128)S(1)}, f32[20,2048]{1,0:T(8,128)S(1)}, u32[]{:S(2)}, u32[]{:S(2)}) %collective-permute-start.5) | collective-permute-done | bytes 163872 | tf_op jit(solution)/shard_map/ppermute | solution.py:47
  25.0 0.9 %first_spread.1 = (f32[3,32,2048]{2,1,0:T(8,128)S(1)}, f32[32,2048]{1,0:T(8,128)S(1)}, f32[16,128]{1,0:T(8,128)S(1)}) custom-call(f32[32,2048]{1,0:T(8,128)S(1)} %get-tuple-element.96.u_o_ref.s_o_ref, f32[3,32,2048]{2,1,0:T(8,128)S(1)} %get-tuple-element.95.s_i_ref.u_i_ref, f32[20,2048]{1,0:T(8,128)S(1)} %collective-permute-done.4.core_ref.side_core_ref, ...), custom_call_target="tpu_custom_call" | custom-call | tf_op jit(solution)/shard_map/first_spread/pallas_call | solution.py:58
  25.9 0.0 collective-permute-done.7.fix_ref
  25.9 0.4 first_far.1
  26.3 1.8 %collective-permute-start.8 = (f32[48,2048]{1,0:T(8,128)S(1)}, f32[48,2048]{1,0:T(8,128)S(1)}, u32[]{:S(2)}, u32[]{:S(2)}) collective-permute-start(f32[48,2048]{1,0:T(8,128)S(1)} %get-tuple-element.108), channel_id=1, source_target_pairs={{0,16},{8,24},{16,0},{24,8},{1,17},{9,25},{17,1},{25,9},{2,18},{10... | collective-permute-start | bytes 1179656 | tf_op jit(solution)/shard_map/ppermute | solution.py:37
  28.1 0.0 collective-permute-start.9
  28.1 3.7 %collective-permute-start.10 = (f32[8,2048]{1,0:T(8,128)S(1)}, f32[8,2048]{1,0:T(8,128)S(1)}, u32[]{:S(2)}, u32[]{:S(2)}) collective-permute-start(f32[8,2048]{1,0:T(8,128)S(1)} %get-tuple-element.110), channel_id=1, source_target_pairs={{0,15},{1,8},{2,9},{3,10},{4,11},{5,12},{6,13},{7,14},{8,1},{9,2},... | collective-permute-start | bytes 196616 | tf_op jit(solution)/shard_map/ppermute | solution.py:47
  31.8 2.7 %collective-permute-done.10.cross_ref = f32[8,2048]{1,0:T(8,128)S(1)} collective-permute-done((f32[8,2048]{1,0:T(8,128)S(1)}, f32[8,2048]{1,0:T(8,128)S(1)}, u32[]{:S(2)}, u32[]{:S(2)}) %collective-permute-start.10) | collective-permute-done | bytes 65568 | tf_op jit(solution)/shard_map/ppermute | solution.py:47
  34.5 1.7 %later_spread.1 = (f32[3,32,2048]{2,1,0:T(8,128)S(1)}, f32[32,2048]{1,0:T(8,128)S(1)}, f32[16,128]{1,0:T(8,128)S(1)}, f32[4,2048]{1,0:T(4,128)S(1)}, f32[8,2048]...) custom-call(f32[32,2048]{1,0:T(8,128)S(1)} %get-tuple-element.107.u_o_ref.v1_o_ref, ...), custom_call_target="tpu_custom_call" | custom-call | tf_op jit(solution)/shard_map/later_spread/pallas_call | solution.py:58
  36.2 0.4 collective-permute-start.11
  36.6 0.1 later_far.1
  36.6 1.8 %collective-permute-start.12 = (f32[32,2048]{1,0:T(8,128)S(1)}, f32[32,2048]{1,0:T(8,128)S(1)}, u32[]{:S(2)}, u32[]{:S(2)}) collective-permute-start(f32[32,2048]{1,0:T(8,128)S(1)} %get-tuple-element.113.v_ref.v2_o_ref), channel_id=1, source_target_pairs={{0,16},{8,24},{16,0},{24,8},{1,17},{9,25},{17,1},{25,9},{2,18},{10... | collective-permute-start | bytes 786440 | tf_op jit(solution)/shard_map/ppermute | solution.py:37
  38.4 2.0 %collective-permute-done.11.tail_ref = f32[4,2048]{1,0:T(4,128)S(1)} collective-permute-done((f32[4,2048]{1,0:T(4,128)S(1)}, f32[4,2048]{1,0:T(4,128)S(1)}, u32[]{:S(2)}, u32[]{:S(2)}) %collective-permute-start.11) | collective-permute-done | bytes 32800 | tf_op jit(solution)/shard_map/ppermute | solution.py:37
  40.5 0.5 later_finish.1
  41.0 9.5 %all_to_all.22 = f32[32,1,128]{2,1,0:T(1,128)S(1)} all-to-all(f32[32,1,128]{2,1,0:T(1,128)S(1)} %bitcast.11), channel_id=1, replica_groups=mesh['band'=4,'tile'=8] {'band','tile'}, dimensions={0} | all-to-all | bytes 32768 | tf_op jit(solution)/shard_map/all_to_all | solution.py:51
  50.5 1.2 %step.1 = (f32[32,2048]{1,0:T(8,128)S(1)}, f32[3,32,2048]{2,1,0:T(8,128)S(1)}, f32[136,2048]{1,0:T(8,128)S(1)}, f32[8,2048]{1,0:T(8,128)S(1)}, f32[8,128]{1,0:T(...) custom-call(f32[32,128]{1,0:T(8,128)S(1)} %bitcast.8, ...), custom_call_target="tpu_custom_call" | custom-call | flops 10000000000 | bytes 10000000 | tf_op jit(solution)/shard_map/step/pallas_call | solution.py:58
  51.8 0.1 collective-permute-start.13
  51.8 0.6 collective-permute-start.15
  52.5 0.3 collective-permute-start.14
  52.8 6.1 %collective-permute-done.14.cross_ref = f32[8,2048]{1,0:T(8,128)S(1)} collective-permute-done((f32[8,2048]{1,0:T(8,128)S(1)}, f32[8,2048]{1,0:T(8,128)S(1)}, u32[]{:S(2)}, u32[]{:S(2)}) %collective-permute-start.14) | collective-permute-done | bytes 65568 | tf_op jit(solution)/shard_map/ppermute | solution.py:47
  58.9 1.6 %earlier_spread.1 = (f32[3,32,2048]{2,1,0:T(8,128)S(1)}, f32[32,2048]{1,0:T(8,128)S(1)}, f32[16,128]{1,0:T(8,128)S(1)}, f32[4,2048]{1,0:T(4,128)S(1)}, f32[8,2048]{1,0:T(8,128)S(1)}, /*index=5*/f32[8,128]{1,0:T(8,128)S(1)}) custom-call(f32[32,2048]{1,0:T(8,128)S(1)} %get-tuple-element.129.u_o_ref, f32[3,32,2048]{2,1,0:T(8,128)S(1)} %get-tuple-element.130.u_i_ref, ...), custom_call_target="tpu_custom_call" | custom-call | tf_op jit(solution)/shard_map/earlier_spread/pallas_call | solution.py:58
  60.4 1.5 %collective-permute-start.16 = (f32[4,2048]{1,0:T(4,128)S(1)}, f32[4,2048]{1,0:T(4,128)S(1)}, u32[]{:S(2)}, u32[]{:S(2)}) collective-permute-start(f32[4,2048]{1,0:T(4,128)S(1)} %get-tuple-element.140), channel_id=1, source_target_pairs={{0,16},{8,24},{16,0},{24,8},{1,17},{9,25},{17,1},{25,9},{2,18},{10... | collective-permute-start | bytes 98312 | tf_op jit(solution)/shard_map/ppermute | solution.py:37
  62.0 1.0 %later_out.1._ = f32[2,2,64,2048]{3,2,1,0:T(8,128)} custom-call(f32[2,32,2048]{2,1,0:T(8,128)S(1)} %get-tuple-element.134.x_mine_ref, f32[136,2048]{1,0:T(8,128)S(1)} %collective-permute-done.13.core_ref.got_ref), custom_call_target="tpu_custom_call" | custom-call | tf_op jit(solution)/shard_map/later_out/pallas_call | solution.py:58
  63.0 0.8 %collective-permute-done.15.got_ref = f32[48,2048]{1,0:T(8,128)S(1)} collective-permute-done((f32[48,2048]{1,0:T(8,128)S(1)}, f32[48,2048]{1,0:T(8,128)S(1)}, u32[]{:S(2)}, u32[]{:S(2)}) %collective-permute-start.15) | collective-permute-done | bytes 393248 | tf_op jit(solution)/shard_map/ppermute | solution.py:37
  63.7 0.1 earlier_far.1
  63.8 0.1 give.1
  63.9 0.1 collective-permute-start.17
  64.0 0.5 collective-permute-done.16.tail_ref
  64.4 0.5 earlier_finish.1
  64.9 8.8 %all_to_all.23 = f32[32,1,128]{2,1,0:T(1,128)S(1)} all-to-all(f32[32,1,128]{2,1,0:T(1,128)S(1)} %bitcast.9), channel_id=1, replica_groups=mesh['band'=4,'tile'=8] {'band','tile'}, dimensions={0} | all-to-all | bytes 32768 | tf_op jit(solution)/shard_map/all_to_all | solution.py:51
  73.7 1.2 %last.1 = f32[2,2,64,2048]{3,2,1,0:T(8,128)} custom-call(f32[2,2,64,2048]{3,2,1,0:T(8,128)} %later_out.1._, f32[32,128]{1,0:T(8,128)S(1)} %bitcast.10, f32[2,32,2048]{2,1,0:T(8,128)S(1)} %get-tuple-element.134.x_mine_ref, f32[2,32,2048]{2,1,0:T(8,128)S(1)} %get-tuple-element.146.z_mine_ref, ...), custom_call_target="tpu_custom_call", output_to_operand_aliasing={{}: (0, {})} | custom-call | flops 10000000000 | bytes 10000000 | tf_op jit(solution)/shard_map/last/pallas_call | solution.py:58
  (6 shorter events, 0.0 us)
Async XLA Ops:
  3.8 2.3 %collective-permute-start = (f32[88,2048]{1,0:T(8,128)S(1)}, f32[88,2048]{1,0:T(8,128)S(1)}, u32[]{:S(2)}, u32[]{:S(2)}) collective-permute-start(f32[88,2048]{1,0:T(8,128)S(1)} %get-tuple-element.78), channel_id=1, source_target_pairs={{0,8},{8,0},{16,24},{24,16},{1,9},{9,1},{17,25},{25,17},{2,10},{10... | collective-permute-start | bytes 2162696 | tf_op jit(solution)/shard_map/ppermute | solution.py:32
  6.1 9.5 %collective-permute-start.1 = (f32[14,32,2048]{2,1,0:T(8,128)S(1)}, f32[14,32,2048]{2,1,0:T(8,128)S(1)}, u32[]{:S(2)}, u32[]{:S(2)}) collective-permute-start(f32[14,32,2048]{2,1,0:T(8,128)S(1)} %get-tuple-element.80), channel_id=1, source_target_pairs={{0,8},{8,0},{16,24},{24,16},{1,9},{9,1},{17,25},{25,17},{2,10},{10... | collective-permute-start | bytes 11010056 | tf_op jit(solution)/shard_map/ppermute | solution.py:32
  6.6 10.1 %collective-permute-start.3 = (f32[32,2048]{1,0:T(8,128)S(1)}, f32[32,2048]{1,0:T(8,128)S(1)}, u32[]{:S(2)}, u32[]{:S(2)}) collective-permute-start(f32[32,2048]{1,0:T(8,128)S(1)} %get-tuple-element.90), channel_id=1, source_target_pairs={{0,16},{8,24},{16,0},{24,8},{1,17},{9,25},{17,1},{25,9},{2,18},{10... | collective-permute-start | bytes 786440 | tf_op jit(solution)/shard_map/ppermute | solution.py:37
  9.3 6.0 %collective-permute-start.2 = (f32[4,2048]{1,0:T(4,128)S(1)}, f32[4,2048]{1,0:T(4,128)S(1)}, u32[]{:S(2)}, u32[]{:S(2)}) collective-permute-start(f32[4,2048]{1,0:T(4,128)S(1)} %get-tuple-element.86), channel_id=1, source_target_pairs={{0,15},{1,8},{2,9},{3,10},{4,11},{5,12},{6,13},{7,14},{8,1},{9,2},... | collective-permute-start | bytes 98312 | tf_op jit(solution)/shard_map/ppermute | solution.py:47
  15.3 10.5 %collective-permute-start.6 = (f32[48,2048]{1,0:T(8,128)S(1)}, f32[48,2048]{1,0:T(8,128)S(1)}, u32[]{:S(2)}, u32[]{:S(2)}) collective-permute-start(f32[48,2048]{1,0:T(8,128)S(1)} %get-tuple-element.101), channel_id=1, source_target_pairs={{0,16},{8,24},{16,0},{24,8},{1,17},{9,25},{17,1},{25,9},{2,18},{10... | collective-permute-start | bytes 1179656 | tf_op jit(solution)/shard_map/ppermute | solution.py:37
  17.0 5.9 %collective-permute-start.4 = (f32[20,2048]{1,0:T(8,128)S(1)}, f32[20,2048]{1,0:T(8,128)S(1)}, u32[]{:S(2)}, u32[]{:S(2)}) collective-permute-start(f32[20,2048]{1,0:T(8,128)S(1)} %get-tuple-element.97), channel_id=1, source_target_pairs={{0,8},{8,0},{16,24},{24,16},{1,9},{9,1},{17,25},{25,17},{2,10},{10... | collective-permute-start | bytes 491528 | tf_op jit(solution)/shard_map/ppermute | solution.py:32
  17.1 7.9 %collective-permute-start.5 = (f32[20,2048]{1,0:T(8,128)S(1)}, f32[20,2048]{1,0:T(8,128)S(1)}, u32[]{:S(2)}, u32[]{:S(2)}) collective-permute-start(f32[20,2048]{1,0:T(8,128)S(1)} %get-tuple-element.98), channel_id=1, source_target_pairs={{0,15},{1,8},{2,9},{3,10},{4,11},{5,12},{6,13},{7,14},{8,1},{9,2},... | collective-permute-start | bytes 491528 | tf_op jit(solution)/shard_map/ppermute | solution.py:47
  21.4 4.5 %collective-permute-start.7 = (f32[1,2048]{1,0:T(1,128)S(1)}, f32[1,2048]{1,0:T(1,128)S(1)}, u32[]{:S(2)}, u32[]{:S(2)}) collective-permute-start(f32[1,2048]{1,0:T(1,128)S(1)} %get-tuple-element.102), channel_id=1, source_target_pairs={{0,16},{8,24},{16,0},{24,8},{1,17},{9,25},{17,1},{25,9},{2,18},{10... | collective-permute-start | bytes 24584 | tf_op jit(solution)/shard_map/ppermute | solution.py:37
  26.3 10.2 %collective-permute-start.8 = (f32[48,2048]{1,0:T(8,128)S(1)}, f32[48,2048]{1,0:T(8,128)S(1)}, u32[]{:S(2)}, u32[]{:S(2)}) collective-permute-start(f32[48,2048]{1,0:T(8,128)S(1)} %get-tuple-element.108), channel_id=1, source_target_pairs={{0,16},{8,24},{16,0},{24,8},{1,17},{9,25},{17,1},{25,9},{2,18},{10... | collective-permute-start | bytes 1179656 | tf_op jit(solution)/shard_map/ppermute | solution.py:37
  28.1 3.7 %collective-permute-start.9 = (f32[8,2048]{1,0:T(8,128)S(1)}, f32[8,2048]{1,0:T(8,128)S(1)}, u32[]{:S(2)}, u32[]{:S(2)}) collective-permute-start(f32[8,2048]{1,0:T(8,128)S(1)} %get-tuple-element.109), channel_id=1, source_target_pairs={{0,8},{8,0},{16,24},{24,16},{1,9},{9,1},{17,25},{25,17},{2,10},{10... | collective-permute-start | bytes 196616 | tf_op jit(solution)/shard_map/ppermute | solution.py:32
  28.1 6.4 %collective-permute-start.10 = (f32[8,2048]{1,0:T(8,128)S(1)}, f32[8,2048]{1,0:T(8,128)S(1)}, u32[]{:S(2)}, u32[]{:S(2)}) collective-permute-start(f32[8,2048]{1,0:T(8,128)S(1)} %get-tuple-element.110), channel_id=1, source_target_pairs={{0,15},{1,8},{2,9},{3,10},{4,11},{5,12},{6,13},{7,14},{8,1},{9,2},... | collective-permute-start | bytes 196616 | tf_op jit(solution)/shard_map/ppermute | solution.py:47
  36.2 4.3 %collective-permute-start.11 = (f32[4,2048]{1,0:T(4,128)S(1)}, f32[4,2048]{1,0:T(4,128)S(1)}, u32[]{:S(2)}, u32[]{:S(2)}) collective-permute-start(f32[4,2048]{1,0:T(4,128)S(1)} %get-tuple-element.114), channel_id=1, source_target_pairs={{0,16},{8,24},{16,0},{24,8},{1,17},{9,25},{17,1},{25,9},{2,18},{10... | collective-permute-start | bytes 98312 | tf_op jit(solution)/shard_map/ppermute | solution.py:37
  36.6 13.9 %collective-permute-start.12 = (f32[32,2048]{1,0:T(8,128)S(1)}, f32[32,2048]{1,0:T(8,128)S(1)}, u32[]{:S(2)}, u32[]{:S(2)}) collective-permute-start(f32[32,2048]{1,0:T(8,128)S(1)} %get-tuple-element.113.v_ref.v2_o_ref), channel_id=1, source_target_pairs={{0,16},{8,24},{16,0},{24,8},{1,17},{9,25},{17,1},{25,9},{2,18},{10... | collective-permute-start | bytes 786440 | tf_op jit(solution)/shard_map/ppermute | solution.py:37
  51.8 7.1 %collective-permute-start.13 = (f32[136,2048]{1,0:T(8,128)S(1)}, f32[136,2048]{1,0:T(8,128)S(1)}, u32[]{:S(2)}, u32[]{:S(2)}) collective-permute-start(f32[136,2048]{1,0:T(8,128)S(1)} %get-tuple-element.131), channel_id=1, source_target_pairs={{0,8},{8,0},{16,24},{24,16},{1,9},{9,1},{17,25},{25,17},{2,10},{10... | collective-permute-start | bytes 3342344 | tf_op jit(solution)/shard_map/ppermute | solution.py:32
  51.8 11.9 %collective-permute-start.15 = (f32[48,2048]{1,0:T(8,128)S(1)}, f32[48,2048]{1,0:T(8,128)S(1)}, u32[]{:S(2)}, u32[]{:S(2)}) collective-permute-start(f32[48,2048]{1,0:T(8,128)S(1)} %get-tuple-element.136), channel_id=1, source_target_pairs={{0,16},{8,24},{16,0},{24,8},{1,17},{9,25},{17,1},{25,9},{2,18},{10... | collective-permute-start | bytes 1179656 | tf_op jit(solution)/shard_map/ppermute | solution.py:37
  52.5 6.4 %collective-permute-start.14 = (f32[8,2048]{1,0:T(8,128)S(1)}, f32[8,2048]{1,0:T(8,128)S(1)}, u32[]{:S(2)}, u32[]{:S(2)}) collective-permute-start(f32[8,2048]{1,0:T(8,128)S(1)} %get-tuple-element.132), channel_id=1, source_target_pairs={{0,15},{1,8},{2,9},{3,10},{4,11},{5,12},{6,13},{7,14},{8,1},{9,2},... | collective-permute-start | bytes 196616 | tf_op jit(solution)/shard_map/ppermute | solution.py:47
  60.4 4.0 %collective-permute-start.16 = (f32[4,2048]{1,0:T(4,128)S(1)}, f32[4,2048]{1,0:T(4,128)S(1)}, u32[]{:S(2)}, u32[]{:S(2)}) collective-permute-start(f32[4,2048]{1,0:T(4,128)S(1)} %get-tuple-element.140), channel_id=1, source_target_pairs={{0,16},{8,24},{16,0},{24,8},{1,17},{9,25},{17,1},{25,9},{2,18},{10... | collective-permute-start | bytes 98312 | tf_op jit(solution)/shard_map/ppermute | solution.py:37
  63.9 9.8 %collective-permute-start.17 = (f32[64,2048]{1,0:T(8,128)S(1)}, f32[64,2048]{1,0:T(8,128)S(1)}, u32[]{:S(2)}, u32[]{:S(2)}) collective-permute-start(f32[64,2048]{1,0:T(8,128)S(1)} %get-tuple-element.148), channel_id=1, source_target_pairs={{0,8},{8,0},{16,24},{24,16},{1,9},{9,1},{17,25},{25,17},{2,10},{10... | collective-permute-start | bytes 1572872 | tf_op jit(solution)/shard_map/ppermute | solution.py:32

commit v6 on v5

--- a/solution.py
+++ b/solution.py
@@ -495,7 +495,7 @@
     g0, g1, g2, g3 = (jnp.sum(block[:, 32 * k : 32 * (k + 1)], 1, keepdims=True) for k in range(4))
     mu = g1 / g0
     h = g2 - mu * g1
-    t = h / (h - (g3 - 2.0 * mu * g2 + mu * mu * g1))
+    t = jnp.clip(h / (h - (g3 - 2.0 * mu * g2 + mu * mu * g1)), 0.5, 80.0)
     a = g0 / (g0 - g1 - h * t)
     b = t * a
     return a - mu * b, b

time: 75.1 us -> 75.1 us (level)
  no operation moved by 1% of the time
where the time goes in v6:
time: 75.1 us; the launch traced here: 74.9 us
  starting transfers between devices  24.3 us (32%)
  blocking collectives  18.3 us (24%)
  waiting for transfers between devices  17.7 us (24%)
  Pallas kernels  14.5 us (19%)
    all_to_all x2, blocking collectives, all_total(): return lax.all_to_all(parts, AXES, 0, 0, tiled=True)  18.3 us
    pallas_call x16, Pallas kernels, call(): pl.pallas_call(body, out_shape=outs, in_specs=[pl.BlockSpec(memory_space=...  14.5 us
    ppermute x4, waiting for transfers between devices, cross_swap(): return lax.ppermute(x, AXES, pairs)  12.6 us
    ppermute x4, starting transfers between devices, cross_swap(): return lax.ppermute(x, AXES, pairs)  12.6 us
    ppermute x8, starting transfers between devices, outer_swap(): return lax.ppermute(x, 'band', [(b, b ^ 2) for b in range(nb)])  10.6 us
    ppermute x8, waiting for transfers between devices, outer_swap(): return lax.ppermute(x, 'band', [(b, b ^ 2) for b in range(nb)])  3.26 us
    ppermute x6, waiting for transfers between devices, core_swap(): return lax.ppermute(x, 'band', [(b, b ^ 1) for b in range(nb)])  1.83 us
  transfers between devices with their start and end apart: 18, of which 8 were waited for; matrix products, arithmetic and copies ran while one was open for 0% of the time, Pallas kernels for 10%

profile of v6, /device:TPU:0, one launch (start us, length us, event | category | flops | bytes accessed | tf_op | source)
XLA Modules:
  0.0 74.9 jit_solution(11729572498986945359)
XLA Ops:
  0.0 3.8 %load.1 = (f32[14,32,2048]{2,1,0:T(8,128)S(1)}, f32[14,32,2048]{2,1,0:T(8,128)S(1)}, f32[80,2048]{1,0:T(8,128)S(1)}, f32[88,2048]{1,0:T(8,128)S(1)}, f32[2,2048]{1,0:T(2,128)S(1)}, /*index=5*/f32[2,2048]{1,0:T(2,128)S(1)}) custom-call(f32[2,64,2048]{2,1,0:T(8,128)} %cond_x_ref.1, f32[2,64,2048]{2,1,0:T(8,128)} %cond_y_ref.1, f32[2,64,2048]{2,1,0:T(8,128)} %via_ref.1, ...), custom_call_target="tpu_custom_call" | custom-call | flops 10000000000 | bytes 10000000 | tf_op jit(solution)/shard_map/load/pallas_call | solution.py:58
  3.8 0.5 collective-permute-start
  4.3 1.8 %collective-permute-done.got_ref.more_ref = f32[88,2048]{1,0:T(8,128)S(1)} collective-permute-done((f32[88,2048]{1,0:T(8,128)S(1)}, f32[88,2048]{1,0:T(8,128)S(1)}, u32[]{:S(2)}, u32[]{:S(2)}) %collective-permute-start) | collective-permute-done | bytes 720928 | tf_op jit(solution)/shard_map/ppermute | solution.py:32
  6.1 0.4 collective-permute-start.1
  6.5 0.1 pay.1
  6.6 2.7 %collective-permute-start.3 = (f32[32,2048]{1,0:T(8,128)S(1)}, f32[32,2048]{1,0:T(8,128)S(1)}, u32[]{:S(2)}, u32[]{:S(2)}) collective-permute-start(f32[32,2048]{1,0:T(8,128)S(1)} %get-tuple-element.90), channel_id=1, source_target_pairs={{0,16},{8,24},{16,0},{24,8},{1,17},{9,25},{17,1},{25,9},{2,18},{10... | collective-permute-start | bytes 786440 | tf_op jit(solution)/shard_map/ppermute | solution.py:37
  9.3 4.2 %collective-permute-start.2 = (f32[4,2048]{1,0:T(4,128)S(1)}, f32[4,2048]{1,0:T(4,128)S(1)}, u32[]{:S(2)}, u32[]{:S(2)}) collective-permute-start(f32[4,2048]{1,0:T(4,128)S(1)} %get-tuple-element.86), channel_id=1, source_target_pairs={{0,15},{1,8},{2,9},{3,10},{4,11},{5,12},{6,13},{7,14},{8,1},{9,2},... | collective-permute-start | bytes 98312 | tf_op jit(solution)/shard_map/ppermute | solution.py:47
  13.5 1.8 %collective-permute-done.2.last_ref = f32[4,2048]{1,0:T(4,128)S(1)} collective-permute-done((f32[4,2048]{1,0:T(4,128)S(1)}, f32[4,2048]{1,0:T(4,128)S(1)}, u32[]{:S(2)}, u32[]{:S(2)}) %collective-permute-start.2) | collective-permute-done | bytes 32800 | tf_op jit(solution)/shard_map/ppermute | solution.py:47
  15.3 0.3 collective-permute-start.6
  15.6 0.0 collective-permute-done.1.got_ref
  15.6 1.0 %prepare.1 = (f32[4,32,2048]{2,1,0:T(8,128)S(1)}, f32[4,32,2048]{2,1,0:T(8,128)S(1)}, f32[4,32,2048]{2,1,0:T(8,128)S(1)}, f32[3,32,2048]{2,1,0:T(8,128)S(1)}, f3...) custom-call(f32[14,32,2048]{2,1,0:T(8,128)S(1)} %get-tuple-element.7, ...), custom_call_target="tpu_custom_call" | custom-call | tf_op jit(solution)/shard_map/prepare/pallas_call | solution.py:58
  16.7 0.3 outer.1
  17.0 0.1 collective-permute-start.4
  17.1 4.3 %collective-permute-start.5 = (f32[20,2048]{1,0:T(8,128)S(1)}, f32[20,2048]{1,0:T(8,128)S(1)}, u32[]{:S(2)}, u32[]{:S(2)}) collective-permute-start(f32[20,2048]{1,0:T(8,128)S(1)} %get-tuple-element.98), channel_id=1, source_target_pairs={{0,15},{1,8},{2,9},{3,10},{4,11},{5,12},{6,13},{7,14},{8,1},{9,2},... | collective-permute-start | bytes 491528 | tf_op jit(solution)/shard_map/ppermute | solution.py:47
  21.4 1.5 %collective-permute-start.7 = (f32[1,2048]{1,0:T(1,128)S(1)}, f32[1,2048]{1,0:T(1,128)S(1)}, u32[]{:S(2)}, u32[]{:S(2)}) collective-permute-start(f32[1,2048]{1,0:T(1,128)S(1)} %get-tuple-element.102), channel_id=1, source_target_pairs={{0,16},{8,24},{16,0},{24,8},{1,17},{9,25},{17,1},{25,9},{2,18},{10... | collective-permute-start | bytes 24584 | tf_op jit(solution)/shard_map/ppermute | solution.py:37
  22.9 0.0 collective-permute-done.4.core_ref.side_core_ref
  22.9 2.1 %collective-permute-done.5.cross_ref.side_cross_ref = f32[20,2048]{1,0:T(8,128)S(1)} collective-permute-done((f32[20,2048]{1,0:T(8,128)S(1)}, f32[20,2048]{1,0:T(8,128)S(1)}, u32[]{:S(2)}, u32[]{:S(2)}) %collective-permute-start.5) | collective-permute-done | bytes 163872 | tf_op jit(solution)/shard_map/ppermute | solution.py:47
  25.0 0.9 %first_spread.1 = (f32[3,32,2048]{2,1,0:T(8,128)S(1)}, f32[32,2048]{1,0:T(8,128)S(1)}, f32[16,128]{1,0:T(8,128)S(1)}) custom-call(f32[32,2048]{1,0:T(8,128)S(1)} %get-tuple-element.96.u_o_ref.s_o_ref, f32[3,32,2048]{2,1,0:T(8,128)S(1)} %get-tuple-element.95.s_i_ref.u_i_ref, f32[20,2048]{1,0:T(8,128)S(1)} %collective-permute-done.4.core_ref.side_core_ref, ...), custom_call_target="tpu_custom_call" | custom-call | tf_op jit(solution)/shard_map/first_spread/pallas_call | solution.py:58
  25.9 0.0 collective-permute-done.7.fix_ref
  25.9 0.4 first_far.1
  26.3 1.8 %collective-permute-start.8 = (f32[48,2048]{1,0:T(8,128)S(1)}, f32[48,2048]{1,0:T(8,128)S(1)}, u32[]{:S(2)}, u32[]{:S(2)}) collective-permute-start(f32[48,2048]{1,0:T(8,128)S(1)} %get-tuple-element.108), channel_id=1, source_target_pairs={{0,16},{8,24},{16,0},{24,8},{1,17},{9,25},{17,1},{25,9},{2,18},{10... | collective-permute-start | bytes 1179656 | tf_op jit(solution)/shard_map/ppermute | solution.py:37
  28.1 0.0 collective-permute-start.9
  28.1 3.7 %collective-permute-start.10 = (f32[8,2048]{1,0:T(8,128)S(1)}, f32[8,2048]{1,0:T(8,128)S(1)}, u32[]{:S(2)}, u32[]{:S(2)}) collective-permute-start(f32[8,2048]{1,0:T(8,128)S(1)} %get-tuple-element.110), channel_id=1, source_target_pairs={{0,15},{1,8},{2,9},{3,10},{4,11},{5,12},{6,13},{7,14},{8,1},{9,2},... | collective-permute-start | bytes 196616 | tf_op jit(solution)/shard_map/ppermute | solution.py:47
  31.8 2.7 %collective-permute-done.10.cross_ref = f32[8,2048]{1,0:T(8,128)S(1)} collective-permute-done((f32[8,2048]{1,0:T(8,128)S(1)}, f32[8,2048]{1,0:T(8,128)S(1)}, u32[]{:S(2)}, u32[]{:S(2)}) %collective-permute-start.10) | collective-permute-done | bytes 65568 | tf_op jit(solution)/shard_map/ppermute | solution.py:47
  34.5 1.7 %later_spread.1 = (f32[3,32,2048]{2,1,0:T(8,128)S(1)}, f32[32,2048]{1,0:T(8,128)S(1)}, f32[16,128]{1,0:T(8,128)S(1)}, f32[4,2048]{1,0:T(4,128)S(1)}, f32[8,2048]...) custom-call(f32[32,2048]{1,0:T(8,128)S(1)} %get-tuple-element.107.u_o_ref.v1_o_ref, ...), custom_call_target="tpu_custom_call" | custom-call | tf_op jit(solution)/shard_map/later_spread/pallas_call | solution.py:58
  36.2 0.4 collective-permute-start.11
  36.6 0.1 later_far.1
  36.6 1.8 %collective-permute-start.12 = (f32[32,2048]{1,0:T(8,128)S(1)}, f32[32,2048]{1,0:T(8,128)S(1)}, u32[]{:S(2)}, u32[]{:S(2)}) collective-permute-start(f32[32,2048]{1,0:T(8,128)S(1)} %get-tuple-element.113.v_ref.v2_o_ref), channel_id=1, source_target_pairs={{0,16},{8,24},{16,0},{24,8},{1,17},{9,25},{17,1},{25,9},{2,18},{10... | collective-permute-start | bytes 786440 | tf_op jit(solution)/shard_map/ppermute | solution.py:37
  38.4 2.0 %collective-permute-done.11.tail_ref = f32[4,2048]{1,0:T(4,128)S(1)} collective-permute-done((f32[4,2048]{1,0:T(4,128)S(1)}, f32[4,2048]{1,0:T(4,128)S(1)}, u32[]{:S(2)}, u32[]{:S(2)}) %collective-permute-start.11) | collective-permute-done | bytes 32800 | tf_op jit(solution)/shard_map/ppermute | solution.py:37
  40.5 0.5 later_finish.1
  41.0 9.5 %all_to_all.22 = f32[32,1,128]{2,1,0:T(1,128)S(1)} all-to-all(f32[32,1,128]{2,1,0:T(1,128)S(1)} %bitcast.11), channel_id=1, replica_groups=mesh['band'=4,'tile'=8] {'band','tile'}, dimensions={0} | all-to-all | bytes 32768 | tf_op jit(solution)/shard_map/all_to_all | solution.py:51
  50.5 1.2 %step.1 = (f32[32,2048]{1,0:T(8,128)S(1)}, f32[3,32,2048]{2,1,0:T(8,128)S(1)}, f32[136,2048]{1,0:T(8,128)S(1)}, f32[8,2048]{1,0:T(8,128)S(1)}, f32[8,128]{1,0:T(...) custom-call(f32[32,128]{1,0:T(8,128)S(1)} %bitcast.8, ...), custom_call_target="tpu_custom_call" | custom-call | flops 10000000000 | bytes 10000000 | tf_op jit(solution)/shard_map/step/pallas_call | solution.py:58
  51.8 0.1 collective-permute-start.13
  51.8 0.6 collective-permute-start.15
  52.5 0.3 collective-permute-start.14
  52.8 6.1 %collective-permute-done.14.cross_ref = f32[8,2048]{1,0:T(8,128)S(1)} collective-permute-done((f32[8,2048]{1,0:T(8,128)S(1)}, f32[8,2048]{1,0:T(8,128)S(1)}, u32[]{:S(2)}, u32[]{:S(2)}) %collective-permute-start.14) | collective-permute-done | bytes 65568 | tf_op jit(solution)/shard_map/ppermute | solution.py:47
  58.9 0.0 collective-permute-done.13.core_ref.got_ref
  58.9 1.6 %earlier_spread.1 = (f32[3,32,2048]{2,1,0:T(8,128)S(1)}, f32[32,2048]{1,0:T(8,128)S(1)}, f32[16,128]{1,0:T(8,128)S(1)}, f32[4,2048]{1,0:T(4,128)S(1)}, f32[8,2048]{1,0:T(8,128)S(1)}, /*index=5*/f32[8,128]{1,0:T(8,128)S(1)}) custom-call(f32[32,2048]{1,0:T(8,128)S(1)} %get-tuple-element.129.u_o_ref, f32[3,32,2048]{2,1,0:T(8,128)S(1)} %get-tuple-element.130.u_i_ref, ...), custom_call_target="tpu_custom_call" | custom-call | tf_op jit(solution)/shard_map/earlier_spread/pallas_call | solution.py:58
  60.4 1.5 %collective-permute-start.16 = (f32[4,2048]{1,0:T(4,128)S(1)}, f32[4,2048]{1,0:T(4,128)S(1)}, u32[]{:S(2)}, u32[]{:S(2)}) collective-permute-start(f32[4,2048]{1,0:T(4,128)S(1)} %get-tuple-element.140), channel_id=1, source_target_pairs={{0,16},{8,24},{16,0},{24,8},{1,17},{9,25},{17,1},{25,9},{2,18},{10... | collective-permute-start | bytes 98312 | tf_op jit(solution)/shard_map/ppermute | solution.py:37
  62.0 1.0 %later_out.1._ = f32[2,2,64,2048]{3,2,1,0:T(8,128)} custom-call(f32[2,32,2048]{2,1,0:T(8,128)S(1)} %get-tuple-element.134.x_mine_ref, f32[136,2048]{1,0:T(8,128)S(1)} %collective-permute-done.13.core_ref.got_ref), custom_call_target="tpu_custom_call" | custom-call | tf_op jit(solution)/shard_map/later_out/pallas_call | solution.py:58
  63.0 0.8 %collective-permute-done.15.got_ref = f32[48,2048]{1,0:T(8,128)S(1)} collective-permute-done((f32[48,2048]{1,0:T(8,128)S(1)}, f32[48,2048]{1,0:T(8,128)S(1)}, u32[]{:S(2)}, u32[]{:S(2)}) %collective-permute-start.15) | collective-permute-done | bytes 393248 | tf_op jit(solution)/shard_map/ppermute | solution.py:37
  63.7 0.1 earlier_far.1
  63.8 0.1 give.1
  63.9 0.1 collective-permute-start.17
  64.0 0.5 collective-permute-done.16.tail_ref
  64.4 0.5 earlier_finish.1
  64.9 8.8 %all_to_all.23 = f32[32,1,128]{2,1,0:T(1,128)S(1)} all-to-all(f32[32,1,128]{2,1,0:T(1,128)S(1)} %bitcast.9), channel_id=1, replica_groups=mesh['band'=4,'tile'=8] {'band','tile'}, dimensions={0} | all-to-all | bytes 32768 | tf_op jit(solution)/shard_map/all_to_all | solution.py:51
  73.7 1.2 %last.1 = f32[2,2,64,2048]{3,2,1,0:T(8,128)} custom-call(f32[2,2,64,2048]{3,2,1,0:T(8,128)} %later_out.1._, f32[32,128]{1,0:T(8,128)S(1)} %bitcast.10, f32[2,32,2048]{2,1,0:T(8,128)S(1)} %get-tuple-element.134.x_mine_ref, f32[2,32,2048]{2,1,0:T(8,128)S(1)} %get-tuple-element.146.z_mine_ref, ...), custom_call_target="tpu_custom_call", output_to_operand_aliasing={{}: (0, {})} | custom-call | flops 10000000000 | bytes 10000000 | tf_op jit(solution)/shard_map/last/pallas_call | solution.py:58
  (6 shorter events, 0.0 us)
Async XLA Ops:
  3.8 2.3 %collective-permute-start = (f32[88,2048]{1,0:T(8,128)S(1)}, f32[88,2048]{1,0:T(8,128)S(1)}, u32[]{:S(2)}, u32[]{:S(2)}) collective-permute-start(f32[88,2048]{1,0:T(8,128)S(1)} %get-tuple-element.78), channel_id=1, source_target_pairs={{0,8},{8,0},{16,24},{24,16},{1,9},{9,1},{17,25},{25,17},{2,10},{10... | collective-permute-start | bytes 2162696 | tf_op jit(solution)/shard_map/ppermute | solution.py:32
  6.1 9.5 %collective-permute-start.1 = (f32[14,32,2048]{2,1,0:T(8,128)S(1)}, f32[14,32,2048]{2,1,0:T(8,128)S(1)}, u32[]{:S(2)}, u32[]{:S(2)}) collective-permute-start(f32[14,32,2048]{2,1,0:T(8,128)S(1)} %get-tuple-element.80), channel_id=1, source_target_pairs={{0,8},{8,0},{16,24},{24,16},{1,9},{9,1},{17,25},{25,17},{2,10},{10... | collective-permute-start | bytes 11010056 | tf_op jit(solution)/shard_map/ppermute | solution.py:32
  6.6 10.1 %collective-permute-start.3 = (f32[32,2048]{1,0:T(8,128)S(1)}, f32[32,2048]{1,0:T(8,128)S(1)}, u32[]{:S(2)}, u32[]{:S(2)}) collective-permute-start(f32[32,2048]{1,0:T(8,128)S(1)} %get-tuple-element.90), channel_id=1, source_target_pairs={{0,16},{8,24},{16,0},{24,8},{1,17},{9,25},{17,1},{25,9},{2,18},{10... | collective-permute-start | bytes 786440 | tf_op jit(solution)/shard_map/ppermute | solution.py:37
  9.3 6.0 %collective-permute-start.2 = (f32[4,2048]{1,0:T(4,128)S(1)}, f32[4,2048]{1,0:T(4,128)S(1)}, u32[]{:S(2)}, u32[]{:S(2)}) collective-permute-start(f32[4,2048]{1,0:T(4,128)S(1)} %get-tuple-element.86), channel_id=1, source_target_pairs={{0,15},{1,8},{2,9},{3,10},{4,11},{5,12},{6,13},{7,14},{8,1},{9,2},... | collective-permute-start | bytes 98312 | tf_op jit(solution)/shard_map/ppermute | solution.py:47
  15.3 10.5 %collective-permute-start.6 = (f32[48,2048]{1,0:T(8,128)S(1)}, f32[48,2048]{1,0:T(8,128)S(1)}, u32[]{:S(2)}, u32[]{:S(2)}) collective-permute-start(f32[48,2048]{1,0:T(8,128)S(1)} %get-tuple-element.101), channel_id=1, source_target_pairs={{0,16},{8,24},{16,0},{24,8},{1,17},{9,25},{17,1},{25,9},{2,18},{10... | collective-permute-start | bytes 1179656 | tf_op jit(solution)/shard_map/ppermute | solution.py:37
  17.0 5.9 %collective-permute-start.4 = (f32[20,2048]{1,0:T(8,128)S(1)}, f32[20,2048]{1,0:T(8,128)S(1)}, u32[]{:S(2)}, u32[]{:S(2)}) collective-permute-start(f32[20,2048]{1,0:T(8,128)S(1)} %get-tuple-element.97), channel_id=1, source_target_pairs={{0,8},{8,0},{16,24},{24,16},{1,9},{9,1},{17,25},{25,17},{2,10},{10... | collective-permute-start | bytes 491528 | tf_op jit(solution)/shard_map/ppermute | solution.py:32
  17.1 7.9 %collective-permute-start.5 = (f32[20,2048]{1,0:T(8,128)S(1)}, f32[20,2048]{1,0:T(8,128)S(1)}, u32[]{:S(2)}, u32[]{:S(2)}) collective-permute-start(f32[20,2048]{1,0:T(8,128)S(1)} %get-tuple-element.98), channel_id=1, source_target_pairs={{0,15},{1,8},{2,9},{3,10},{4,11},{5,12},{6,13},{7,14},{8,1},{9,2},... | collective-permute-start | bytes 491528 | tf_op jit(solution)/shard_map/ppermute | solution.py:47
  21.4 4.5 %collective-permute-start.7 = (f32[1,2048]{1,0:T(1,128)S(1)}, f32[1,2048]{1,0:T(1,128)S(1)}, u32[]{:S(2)}, u32[]{:S(2)}) collective-permute-start(f32[1,2048]{1,0:T(1,128)S(1)} %get-tuple-element.102), channel_id=1, source_target_pairs={{0,16},{8,24},{16,0},{24,8},{1,17},{9,25},{17,1},{25,9},{2,18},{10... | collective-permute-start | bytes 24584 | tf_op jit(solution)/shard_map/ppermute | solution.py:37
  26.3 10.2 %collective-permute-start.8 = (f32[48,2048]{1,0:T(8,128)S(1)}, f32[48,2048]{1,0:T(8,128)S(1)}, u32[]{:S(2)}, u32[]{:S(2)}) collective-permute-start(f32[48,2048]{1,0:T(8,128)S(1)} %get-tuple-element.108), channel_id=1, source_target_pairs={{0,16},{8,24},{16,0},{24,8},{1,17},{9,25},{17,1},{25,9},{2,18},{10... | collective-permute-start | bytes 1179656 | tf_op jit(solution)/shard_map/ppermute | solution.py:37
  28.1 3.7 %collective-permute-start.9 = (f32[8,2048]{1,0:T(8,128)S(1)}, f32[8,2048]{1,0:T(8,128)S(1)}, u32[]{:S(2)}, u32[]{:S(2)}) collective-permute-start(f32[8,2048]{1,0:T(8,128)S(1)} %get-tuple-element.109), channel_id=1, source_target_pairs={{0,8},{8,0},{16,24},{24,16},{1,9},{9,1},{17,25},{25,17},{2,10},{10... | collective-permute-start | bytes 196616 | tf_op jit(solution)/shard_map/ppermute | solution.py:32
  28.1 6.4 %collective-permute-start.10 = (f32[8,2048]{1,0:T(8,128)S(1)}, f32[8,2048]{1,0:T(8,128)S(1)}, u32[]{:S(2)}, u32[]{:S(2)}) collective-permute-start(f32[8,2048]{1,0:T(8,128)S(1)} %get-tuple-element.110), channel_id=1, source_target_pairs={{0,15},{1,8},{2,9},{3,10},{4,11},{5,12},{6,13},{7,14},{8,1},{9,2},... | collective-permute-start | bytes 196616 | tf_op jit(solution)/shard_map/ppermute | solution.py:47
  36.2 4.3 %collective-permute-start.11 = (f32[4,2048]{1,0:T(4,128)S(1)}, f32[4,2048]{1,0:T(4,128)S(1)}, u32[]{:S(2)}, u32[]{:S(2)}) collective-permute-start(f32[4,2048]{1,0:T(4,128)S(1)} %get-tuple-element.114), channel_id=1, source_target_pairs={{0,16},{8,24},{16,0},{24,8},{1,17},{9,25},{17,1},{25,9},{2,18},{10... | collective-permute-start | bytes 98312 | tf_op jit(solution)/shard_map/ppermute | solution.py:37
  36.6 13.9 %collective-permute-start.12 = (f32[32,2048]{1,0:T(8,128)S(1)}, f32[32,2048]{1,0:T(8,128)S(1)}, u32[]{:S(2)}, u32[]{:S(2)}) collective-permute-start(f32[32,2048]{1,0:T(8,128)S(1)} %get-tuple-element.113.v_ref.v2_o_ref), channel_id=1, source_target_pairs={{0,16},{8,24},{16,0},{24,8},{1,17},{9,25},{17,1},{25,9},{2,18},{10... | collective-permute-start | bytes 786440 | tf_op jit(solution)/shard_map/ppermute | solution.py:37
  51.8 7.1 %collective-permute-start.13 = (f32[136,2048]{1,0:T(8,128)S(1)}, f32[136,2048]{1,0:T(8,128)S(1)}, u32[]{:S(2)}, u32[]{:S(2)}) collective-permute-start(f32[136,2048]{1,0:T(8,128)S(1)} %get-tuple-element.131), channel_id=1, source_target_pairs={{0,8},{8,0},{16,24},{24,16},{1,9},{9,1},{17,25},{25,17},{2,10},{10... | collective-permute-start | bytes 3342344 | tf_op jit(solution)/shard_map/ppermute | solution.py:32
  51.8 11.9 %collective-permute-start.15 = (f32[48,2048]{1,0:T(8,128)S(1)}, f32[48,2048]{1,0:T(8,128)S(1)}, u32[]{:S(2)}, u32[]{:S(2)}) collective-permute-start(f32[48,2048]{1,0:T(8,128)S(1)} %get-tuple-element.136), channel_id=1, source_target_pairs={{0,16},{8,24},{16,0},{24,8},{1,17},{9,25},{17,1},{25,9},{2,18},{10... | collective-permute-start | bytes 1179656 | tf_op jit(solution)/shard_map/ppermute | solution.py:37
  52.5 6.4 %collective-permute-start.14 = (f32[8,2048]{1,0:T(8,128)S(1)}, f32[8,2048]{1,0:T(8,128)S(1)}, u32[]{:S(2)}, u32[]{:S(2)}) collective-permute-start(f32[8,2048]{1,0:T(8,128)S(1)} %get-tuple-element.132), channel_id=1, source_target_pairs={{0,15},{1,8},{2,9},{3,10},{4,11},{5,12},{6,13},{7,14},{8,1},{9,2},... | collective-permute-start | bytes 196616 | tf_op jit(solution)/shard_map/ppermute | solution.py:47
  60.4 4.0 %collective-permute-start.16 = (f32[4,2048]{1,0:T(4,128)S(1)}, f32[4,2048]{1,0:T(4,128)S(1)}, u32[]{:S(2)}, u32[]{:S(2)}) collective-permute-start(f32[4,2048]{1,0:T(4,128)S(1)} %get-tuple-element.140), channel_id=1, source_target_pairs={{0,16},{8,24},{16,0},{24,8},{1,17},{9,25},{17,1},{25,9},{2,18},{10... | collective-permute-start | bytes 98312 | tf_op jit(solution)/shard_map/ppermute | solution.py:37
  63.9 9.8 %collective-permute-start.17 = (f32[64,2048]{1,0:T(8,128)S(1)}, f32[64,2048]{1,0:T(8,128)S(1)}, u32[]{:S(2)}, u32[]{:S(2)}) collective-permute-start(f32[64,2048]{1,0:T(8,128)S(1)} %get-tuple-element.148), channel_id=1, source_target_pairs={{0,8},{8,0},{16,24},{24,16},{1,9},{9,1},{17,25},{25,17},{2,10},{10... | collective-permute-start | bytes 1572872 | tf_op jit(solution)/shard_map/ppermute | solution.py:32

commit v7 on v6

--- a/solution.py
+++ b/solution.py
@@ -323,7 +323,9 @@
     spread_rows(u_o_ref, u_i_ref, above, below, cx_ref, cy_ref, c_ref, inv_i_ref, edge_ref, v_i_ref, part_ref, sums_ref)
 
 
-def spread_rows(u_o_ref, u_i_ref, above, below, cx_ref, cy_ref, c_ref, inv_i_ref, edge_ref, v_i_ref, part_ref, sums_ref):
+def spread_rows(
+    u_o_ref, u_i_ref, above, below, cx_ref, cy_ref, c_ref, inv_i_ref, edge_ref, v_i_ref, part_ref, sums_ref, diag_i_ref=None
+):
     rows, width = u_o_ref.shape
     chunks = rows // ROWS
     carried = [edge_ref[j : j + 1, :] * above[j : j + 1] for j in range(4)]
@@ -341,9 +343,13 @@
         part_ref[rs, :] = parts[0]
         for j in range(1, 4):
             v = inv_i_ref[j - 1, rs, :] * parts[j]
+            weighted = parts[j]
+            if diag_i_ref is not None:
+                v = xs[j] - v
+                weighted = diag_i_ref[j - 1, rs, :] * xs[j] - weighted
             v_i_ref[j - 1, rs, :] = v
-            sums[0] = sums[0] + xs[j] * parts[j]
-            sums[1] = sums[1] + v * parts[j]
+            sums[0] = sums[0] + xs[j] * weighted
+            sums[1] = sums[1] + v * weighted
     sums_ref[0:ROWS, :] = fold(sums[0])
     sums_ref[ROWS : 2 * ROWS, :] = fold(sums[1])
 
@@ -363,26 +369,26 @@
 
 def two_spread_kernel(
     u_o_ref, u_i_ref, core_ref, cross_ref, cx_ref, cy_ref, c_ref, inv_i_ref, edge_ref, side_core_ref, side_cross_ref,
-    v_i_ref, part_ref, sums_ref, tail_ref, beside_ref, total_ref, w_ref=None,
+    diag_i_ref, d_i_ref, part_ref, sums_ref, tail_ref, beside_ref, total_ref, w_ref=None,
 ):
     rows, width = u_o_ref.shape
     chunks = rows // ROWS
     above, below = take_rows(core_ref, cross_ref)
-    spread_rows(u_o_ref, u_i_ref, above, below, cx_ref, cy_ref, c_ref, inv_i_ref, edge_ref, v_i_ref, part_ref, sums_ref)
+    spread_rows(u_o_ref, u_i_ref, above, below, cx_ref, cy_ref, c_ref, inv_i_ref, edge_ref, d_i_ref, part_ref, sums_ref, diag_i_ref)
     fluxes = [edge_ref[0:1, :] * above[0:1], cx_ref[0, rows - 1 :, :] * below[0:1]]
     tail_ref[...] = stack_rows([above[0:1], below[0:1], *fluxes])
     side_above, side_below = take_rows(side_core_ref, side_cross_ref)
     parts_there, inv = beside(u_o_ref, u_i_ref, above, below, side_above, side_below, edge_ref, cx_ref)
     beside_ref[...] = parts_there
-    v_there = inv * parts_there
-    carried = [edge_ref[j : j + 1, :] * v_there[j : j + 1] for j in range(1, 4)]
+    there = stack_rows([above[0:4], below[0:4]]) - inv * parts_there
+    carried = [edge_ref[j : j + 1, :] * there[j : j + 1] for j in range(1, 4)]
     total = jnp.zeros((ROWS, width), F32)
     for k in range(chunks):
         rs = slice(k * ROWS, (k + 1) * ROWS)
         xs, parts = [], []
         for j in range(1, 4):
             x, part, carried[j - 1] = in_band(
-                v_i_ref.at[j - 1], cx_ref.at[j], cy_ref.at[j], carried[j - 1], v_there[4 + j : 5 + j], k, chunks
+                d_i_ref.at[j - 1], cx_ref.at[j], cy_ref.at[j], carried[j - 1], there[4 + j : 5 + j], k, chunks
             )
             xs.append(x)
             parts.append(part)
@@ -422,22 +428,24 @@
     own_parts(v_ref, v_i_ref, cx_ref, cy_ref, c_ref, pay_ref, scratch_ref)
 
 
-def far_kernel(u_o_ref, got_ref, part_ref, sums_ref, c_out_ref, inv_ref, v_ref, totals_ref):
+def far_kernel(u_o_ref, got_ref, part_ref, sums_ref, c_out_ref, inv_ref, diag_ref, d_ref, totals_ref):
     rows, width = u_o_ref.shape
     sums = [jnp.zeros((ROWS, width), F32) for _ in range(2)]
     for k in range(rows // ROWS):
         rs = slice(k * ROWS, (k + 1) * ROWS)
+        u = u_o_ref[rs, :]
         part = part_ref[rs, :] + c_out_ref[rs, :] * got_ref[rs, :]
-        v = inv_ref[rs, :] * part
-        v_ref[rs, :] = v
-        sums[0] = sums[0] + u_o_ref[rs, :] * part
-        sums[1] = sums[1] + v * part
+        d = u - inv_ref[rs, :] * part
+        weighted = diag_ref[rs, :] * u - part
+        d_ref[rs, :] = d
+        sums[0] = sums[0] + u * weighted
+        sums[1] = sums[1] + d * weighted
     totals_ref[0:ROWS, :] = fold(sums[0]) + sums_ref[0:ROWS, :]
     totals_ref[ROWS : 2 * ROWS, :] = fold(sums[1]) + sums_ref[ROWS : 2 * ROWS, :]
 
 
 def finish_kernel(
-    u_o_ref, v_ref, got_ref, tail_ref, v_i_ref, totals_ref, beside_ref, inner_ref, inv_far_ref,
+    u_o_ref, d_ref, got_ref, tail_ref, own_tail_ref, d_i_ref, totals_ref, beside_ref, inner_ref, inv_far_ref,
     cx_ref, cy_ref, c_ref, c_out_ref, edge_ref, side_core_ref, side_cross_ref, t0_ref,
     mail_ref, w_ref=None, fix_ref=None,
 ):
@@ -448,16 +456,16 @@
     carried = none
     for k in range(chunks):
         rs = slice(k * ROWS, (k + 1) * ROWS)
-        v, part, carried = in_band(v_ref, cx_ref.at[0], cy_ref.at[0], carried, none, k, chunks)
-        coupled = c_ref[1, rs, :] * v_i_ref[0, rs, :]
-        sums[0] = sums[0] + v * (part + 2.0 * coupled)
+        d, part, carried = in_band(d_ref, cx_ref.at[0], cy_ref.at[0], carried, none, k, chunks)
+        coupled = c_ref[1, rs, :] * d_i_ref[0, rs, :]
+        sums[0] = sums[0] + d * (part + 2.0 * coupled)
         if w_ref is not None:
             w_ref[rs, :] = part + coupled
     side_above, side_below = take_rows(side_core_ref, side_cross_ref)
     up = side_above[4:5] * (beside_ref[0:1, :] + side_above[12:13] * tail_ref[0:1, :])
     down = side_below[4:5] * (beside_ref[4:5, :] + side_below[12:13] * tail_ref[1:2, :])
-    up = edge_ref[0:1, :] * up
-    down = cx_ref[0, rows - 1 :, :] * down
+    up = edge_ref[0:1, :] * (own_tail_ref[0:1, :] - up)
+    down = cx_ref[0, rows - 1 :, :] * (own_tail_ref[1:2, :] - down)
     if fix_ref is not None:
         fix_ref[...] = stack_rows([up, down])
     size = rows // 2
@@ -472,8 +480,9 @@
             part = part + jnp.where(row_at(width, 0), far_up, 0.0)
         if k == size // ROWS - 1:
             part = part + jnp.where(row_at(width, ROWS - 1), far_down, 0.0)
-        sums[1] = sums[1] + v_ref[at, :] * (c_out * (inv_far_ref[k * ROWS : (k + 1) * ROWS, :] * part))
-    ends = up * v_ref[0:1, :] + down * v_ref[rows - 1 :, :]
+        far = got_ref[at, :] - inv_far_ref[k * ROWS : (k + 1) * ROWS, :] * part
+        sums[1] = sums[1] + d_ref[at, :] * (c_out * far)
+    ends = up * d_ref[0:1, :] + down * d_ref[rows - 1 :, :]
     last = fold(sums[0] + 2.0 * sums[1] + jnp.where(row_at(width, 0), ends, 0.0)) + inner_ref[...]
     terms = (t0_ref[...], totals_ref[0:ROWS, :], totals_ref[ROWS : 2 * ROWS, :], last)
     lane = lax.broadcasted_iota(jnp.int32, (ROWS, 128), 1)
@@ -492,13 +501,13 @@
     for at in range(ROWS, mail_ref.shape[0], ROWS):
         block = block + mail_ref[at : at + ROWS, :]
     block = jnp.sum(block, 0, keepdims=True)
-    g0, g1, g2, g3 = (jnp.sum(block[:, 32 * k : 32 * (k + 1)], 1, keepdims=True) for k in range(4))
-    mu = g1 / g0
-    h = g2 - mu * g1
-    t = jnp.clip(h / (h - (g3 - 2.0 * mu * g2 + mu * mu * g1)), 0.5, 80.0)
-    a = g0 / (g0 - g1 - h * t)
-    b = t * a
-    return a - mu * b, b
+    k0, k1, k2, spread = (jnp.sum(block[:, 32 * k : 32 * (k + 1)], 1, keepdims=True) for k in range(4))
+    k3 = k2 - spread
+    nu = k1 / k0
+    h = k2 - nu * k1
+    t = jnp.clip(h / (k3 - 2.0 * nu * k2 + nu * nu * k1), 0.5, 80.0)
+    a = k0 / (k1 - h * t)
+    return a * (1.0 + t * nu), -t * a
 
 
 def hand_out(j, value, k, holds_outer, mine_ref, send_ref, first, half):
@@ -517,7 +526,7 @@
 
 
 def step_kernel(
-    mail_ref, s_o_ref, s_i_ref, v1_o_ref, v1_i_ref, v2_o_ref, v2_i_ref, part_i_ref, part_ref, far_ref, fix_ref, cap_ref, seen_ref,
+    mail_ref, s_o_ref, s_i_ref, v1_o_ref, v1_i_ref, d_o_ref, d_i_ref, part_i_ref, part_ref, far_ref, fix_ref, cap_ref, seen_ref,
     diag_o_ref, diag_i_ref, inv_o_ref, inv_i_ref, cx_ref, cy_ref, c_ref, c_out_ref,
     z_o_ref, z_i_ref, core_ref, cross_ref, total_ref, pay_ref, x_mine_ref, z_mine_ref, scratch_ref,
 ):
@@ -530,10 +539,10 @@
         for j in range(4):
             for k in range(chunks):
                 rs = slice(k * ROWS, (k + 1) * ROWS)
-                s, p, q, diag, inv = (
+                s, p, d, diag, inv = (
                     band_of(o, i, j)[rs, :]
                     for o, i in (
-                        (s_o_ref, s_i_ref), (v1_o_ref, v1_i_ref), (v2_o_ref, v2_i_ref),
+                        (s_o_ref, s_i_ref), (v1_o_ref, v1_i_ref), (d_o_ref, d_i_ref),
                         (diag_o_ref, diag_i_ref), (inv_o_ref, inv_i_ref),
                     )
                 )
@@ -546,10 +555,10 @@
                 else:
                     part = part_i_ref[j - 1, rs, :]
                     if j == 1:
-                        part = part + c_ref[1, rs, :] * v2_o_ref[rs, :]
+                        part = part + c_ref[1, rs, :] * d_o_ref[rs, :]
                 r = inv * part
-                x = s + a * p + b * q
-                residual = cap_ref[j, rs, :] * x + seen_ref[j, rs, :] - diag * (x - (p + a * q + b * r))
+                x = s + a * p + b * d
+                residual = cap_ref[j, rs, :] * x + seen_ref[j, rs, :] - diag * (x - (p + a * (p - d) + b * r))
                 z = residual * inv
                 band_of(z_o_ref, z_i_ref, j)[rs, :] = z
                 total = total + residual * z
@@ -648,9 +657,9 @@
     def stage(u_o, u_i, pay, near, cross, t0, name, x_mine=None):
         further = x_mine is None
         got, cross, near = outer_swap(pay), cross_swap(cross), core_swap(near)
-        v_i, part, sums, tail, there, inner, *w_i = call(
+        d_i, part, sums, tail, there, inner, *w_i = call(
             two_spread_kernel, [three, field, two, edge, eight, one] + [three] * further,
-            u_o, u_i, near, cross, *coeffs, *sides, name=name + "_spread",
+            u_o, u_i, near, cross, *coeffs, *sides, diag_i, name=name + "_spread",
         )
         if not further:
             (out,) = call(
@@ -658,25 +667,25 @@
                 scratch=[pltpu.SemaphoreType.DMA((4,))],
             )
             part, out = lax.optimization_barrier((part, out))
-        v_o, totals = call(far_kernel, [field, two], u_o, got, part, sums, c_out, inv_o, name=name + "_far")
+        d_o, totals = call(far_kernel, [field, two], u_o, got, part, sums, c_out, inv_o, diag_o, name=name + "_far")
         if further:
-            more = (outer_swap(v_o),)
+            more = (outer_swap(d_o),)
         else:
-            mine, send = call(give_kernel, [pair, shape(2 * half, width)], v_o, v_i, name="give")
+            mine, send = call(give_kernel, [pair, shape(2 * half, width)], d_o, d_i, name="give")
             more = out, near, mine, core_swap(send)
         parts, *rest = call(
             finish_kernel, [mail] + [field, rim] * further,
-            u_o, v_o, got, outer_swap(tail), v_i, totals, there, inner, inv_far,
+            u_o, d_o, got, outer_swap(tail), tail, d_i, totals, there, inner, inv_far,
             cx, cy, c, c_out, cx_edge, *sides, t0, name=name + "_finish",
         )
         more = *w_i, *rest, *more
-        return v_o, v_i, all_total(parts), more
-
-    v2_o, v2_i, total, (part_i, part, fix, far) = stage(v1_o, v1_i, pay, near, cross, t0, "later")
+        return d_o, d_i, all_total(parts), more
+
+    d_o, d_i, total, (part_i, part, fix, far) = stage(v1_o, v1_i, pay, near, cross, t0, "later")
     z_o, z_i, near, cross, t0, pay, x_mine, z_mine = call(
         step_kernel,
         [field, three, shape(ROWS + 4 * half, width), eight, one, most, pair, pair],
-        total, s_o, s_i, v1_o, v1_i, v2_o, v2_i, part_i, part, far, fix, cap, earlier, diag_o, diag_i, inv_o, inv_i, cx, cy, c, c_out,
+        total, s_o, s_i, v1_o, v1_i, d_o, d_i, part_i, part, far, fix, cap, earlier, diag_o, diag_i, inv_o, inv_i, cx, cy, c, c_out,
         name="step", scratch=parts_of,
     )
     _, _, total, (out, got, q_mine, q_got) = stage(z_o, z_i, pay, near, cross, t0, "earlier", x_mine)

time: 75.1 us -> 75.2 us (level)
  transfers between devices with their start and end apart: 18 -> 18, of which waited for: 8 -> 8; matrix products, arithmetic and copies ran while one was open for 0% -> 0% of each run, Pallas kernels for 10% -> 11%
where the time goes in v7:
time: 75.2 us; the launch traced here: 75.1 us
  starting transfers between devices  24.3 us (32%)
  blocking collectives  18.3 us (24%)
  waiting for transfers between devices  17.6 us (23%)
  Pallas kernels  14.7 us (20%)
    all_to_all x2, blocking collectives, all_total(): return lax.all_to_all(parts, AXES, 0, 0, tiled=True)  18.3 us
    pallas_call x16, Pallas kernels, call(): pl.pallas_call(body, out_shape=outs, in_specs=[pl.BlockSpec(memory_space=...  14.7 us
    ppermute x4, waiting for transfers between devices, cross_swap(): return lax.ppermute(x, AXES, pairs)  12.6 us
    ppermute x4, starting transfers between devices, cross_swap(): return lax.ppermute(x, AXES, pairs)  12.6 us
    ppermute x8, starting transfers between devices, outer_swap(): return lax.ppermute(x, 'band', [(b, b ^ 2) for b in range(nb)])  10.6 us
    ppermute x8, waiting for transfers between devices, outer_swap(): return lax.ppermute(x, 'band', [(b, b ^ 2) for b in range(nb)])  3.21 us
    ppermute x6, waiting for transfers between devices, core_swap(): return lax.ppermute(x, 'band', [(b, b ^ 1) for b in range(nb)])  1.83 us
  transfers between devices with their start and end apart: 18, of which 8 were waited for; matrix products, arithmetic and copies ran while one was open for 0% of the time, Pallas kernels for 11%

profile of v7, /device:TPU:0, one launch (start us, length us, event | category | flops | bytes accessed | tf_op | source)
XLA Modules:
  0.0 75.1 jit_solution(8241668459987969754)
XLA Ops:
  0.0 3.8 %load.1 = (f32[14,32,2048]{2,1,0:T(8,128)S(1)}, f32[14,32,2048]{2,1,0:T(8,128)S(1)}, f32[80,2048]{1,0:T(8,128)S(1)}, f32[88,2048]{1,0:T(8,128)S(1)}, f32[2,2048]{1,0:T(2,128)S(1)}, /*index=5*/f32[2,2048]{1,0:T(2,128)S(1)}) custom-call(f32[2,64,2048]{2,1,0:T(8,128)} %cond_x_ref.1, f32[2,64,2048]{2,1,0:T(8,128)} %cond_y_ref.1, f32[2,64,2048]{2,1,0:T(8,128)} %via_ref.1, ...), custom_call_target="tpu_custom_call" | custom-call | flops 10000000000 | bytes 10000000 | tf_op jit(solution)/shard_map/load/pallas_call | solution.py:58
  3.8 0.5 collective-permute-start
  4.3 1.8 %collective-permute-done.got_ref.more_ref = f32[88,2048]{1,0:T(8,128)S(1)} collective-permute-done((f32[88,2048]{1,0:T(8,128)S(1)}, f32[88,2048]{1,0:T(8,128)S(1)}, u32[]{:S(2)}, u32[]{:S(2)}) %collective-permute-start) | collective-permute-done | bytes 720928 | tf_op jit(solution)/shard_map/ppermute | solution.py:32
  6.1 0.4 collective-permute-start.1
  6.5 0.1 pay.1
  6.6 2.7 %collective-permute-start.3 = (f32[32,2048]{1,0:T(8,128)S(1)}, f32[32,2048]{1,0:T(8,128)S(1)}, u32[]{:S(2)}, u32[]{:S(2)}) collective-permute-start(f32[32,2048]{1,0:T(8,128)S(1)} %get-tuple-element.90), channel_id=1, source_target_pairs={{0,16},{8,24},{16,0},{24,8},{1,17},{9,25},{17,1},{25,9},{2,18},{10... | collective-permute-start | bytes 786440 | tf_op jit(solution)/shard_map/ppermute | solution.py:37
  9.3 4.2 %collective-permute-start.2 = (f32[4,2048]{1,0:T(4,128)S(1)}, f32[4,2048]{1,0:T(4,128)S(1)}, u32[]{:S(2)}, u32[]{:S(2)}) collective-permute-start(f32[4,2048]{1,0:T(4,128)S(1)} %get-tuple-element.86), channel_id=1, source_target_pairs={{0,15},{1,8},{2,9},{3,10},{4,11},{5,12},{6,13},{7,14},{8,1},{9,2},... | collective-permute-start | bytes 98312 | tf_op jit(solution)/shard_map/ppermute | solution.py:47
  13.5 1.8 %collective-permute-done.2.last_ref = f32[4,2048]{1,0:T(4,128)S(1)} collective-permute-done((f32[4,2048]{1,0:T(4,128)S(1)}, f32[4,2048]{1,0:T(4,128)S(1)}, u32[]{:S(2)}, u32[]{:S(2)}) %collective-permute-start.2) | collective-permute-done | bytes 32800 | tf_op jit(solution)/shard_map/ppermute | solution.py:47
  15.3 0.3 collective-permute-start.6
  15.6 0.0 collective-permute-done.1.got_ref
  15.6 1.0 %prepare.1 = (f32[4,32,2048]{2,1,0:T(8,128)S(1)}, f32[4,32,2048]{2,1,0:T(8,128)S(1)}, f32[4,32,2048]{2,1,0:T(8,128)S(1)}, f32[3,32,2048]{2,1,0:T(8,128)S(1)}, f3...) custom-call(f32[14,32,2048]{2,1,0:T(8,128)S(1)} %get-tuple-element.7, ...), custom_call_target="tpu_custom_call" | custom-call | tf_op jit(solution)/shard_map/prepare/pallas_call | solution.py:58
  16.7 0.3 outer.1
  17.0 0.1 collective-permute-start.4
  17.1 4.3 %collective-permute-start.5 = (f32[20,2048]{1,0:T(8,128)S(1)}, f32[20,2048]{1,0:T(8,128)S(1)}, u32[]{:S(2)}, u32[]{:S(2)}) collective-permute-start(f32[20,2048]{1,0:T(8,128)S(1)} %get-tuple-element.98), channel_id=1, source_target_pairs={{0,15},{1,8},{2,9},{3,10},{4,11},{5,12},{6,13},{7,14},{8,1},{9,2},... | collective-permute-start | bytes 491528 | tf_op jit(solution)/shard_map/ppermute | solution.py:47
  21.4 1.5 %collective-permute-start.7 = (f32[1,2048]{1,0:T(1,128)S(1)}, f32[1,2048]{1,0:T(1,128)S(1)}, u32[]{:S(2)}, u32[]{:S(2)}) collective-permute-start(f32[1,2048]{1,0:T(1,128)S(1)} %get-tuple-element.102), channel_id=1, source_target_pairs={{0,16},{8,24},{16,0},{24,8},{1,17},{9,25},{17,1},{25,9},{2,18},{10... | collective-permute-start | bytes 24584 | tf_op jit(solution)/shard_map/ppermute | solution.py:37
  22.9 0.0 collective-permute-done.4.core_ref.side_core_ref
  22.9 2.1 %collective-permute-done.5.cross_ref.side_cross_ref = f32[20,2048]{1,0:T(8,128)S(1)} collective-permute-done((f32[20,2048]{1,0:T(8,128)S(1)}, f32[20,2048]{1,0:T(8,128)S(1)}, u32[]{:S(2)}, u32[]{:S(2)}) %collective-permute-start.5) | collective-permute-done | bytes 163872 | tf_op jit(solution)/shard_map/ppermute | solution.py:47
  25.0 0.9 %first_spread.1 = (f32[3,32,2048]{2,1,0:T(8,128)S(1)}, f32[32,2048]{1,0:T(8,128)S(1)}, f32[16,128]{1,0:T(8,128)S(1)}) custom-call(f32[32,2048]{1,0:T(8,128)S(1)} %get-tuple-element.96.u_o_ref.s_o_ref, f32[3,32,2048]{2,1,0:T(8,128)S(1)} %get-tuple-element.95.s_i_ref.u_i_ref, f32[20,2048]{1,0:T(8,128)S(1)} %collective-permute-done.4.core_ref.side_core_ref, ...), custom_call_target="tpu_custom_call" | custom-call | tf_op jit(solution)/shard_map/first_spread/pallas_call | solution.py:58
  25.9 0.0 collective-permute-done.6.more_ref
  25.9 0.4 first_far.1
  26.3 1.8 %collective-permute-start.8 = (f32[48,2048]{1,0:T(8,128)S(1)}, f32[48,2048]{1,0:T(8,128)S(1)}, u32[]{:S(2)}, u32[]{:S(2)}) collective-permute-start(f32[48,2048]{1,0:T(8,128)S(1)} %get-tuple-element.108), channel_id=1, source_target_pairs={{0,16},{8,24},{16,0},{24,8},{1,17},{9,25},{17,1},{25,9},{2,18},{10... | collective-permute-start | bytes 1179656 | tf_op jit(solution)/shard_map/ppermute | solution.py:37
  28.1 0.0 collective-permute-start.9
  28.1 3.7 %collective-permute-start.10 = (f32[8,2048]{1,0:T(8,128)S(1)}, f32[8,2048]{1,0:T(8,128)S(1)}, u32[]{:S(2)}, u32[]{:S(2)}) collective-permute-start(f32[8,2048]{1,0:T(8,128)S(1)} %get-tuple-element.110), channel_id=1, source_target_pairs={{0,15},{1,8},{2,9},{3,10},{4,11},{5,12},{6,13},{7,14},{8,1},{9,2},... | collective-permute-start | bytes 196616 | tf_op jit(solution)/shard_map/ppermute | solution.py:47
  31.8 0.0 collective-permute-done.9.core_ref
  31.8 2.7 %collective-permute-done.10.cross_ref = f32[8,2048]{1,0:T(8,128)S(1)} collective-permute-done((f32[8,2048]{1,0:T(8,128)S(1)}, f32[8,2048]{1,0:T(8,128)S(1)}, u32[]{:S(2)}, u32[]{:S(2)}) %collective-permute-start.10) | collective-permute-done | bytes 65568 | tf_op jit(solution)/shard_map/ppermute | solution.py:47
  34.5 1.8 %later_spread.1 = (f32[3,32,2048]{2,1,0:T(8,128)S(1)}, f32[32,2048]{1,0:T(8,128)S(1)}, f32[16,128]{1,0:T(8,128)S(1)}, f32[4,2048]{1,0:T(4,128)S(1)}, f32[8,2048]...) custom-call(f32[32,2048]{1,0:T(8,128)S(1)} %get-tuple-element.107.u_o_ref.v1_o_ref, ...), custom_call_target="tpu_custom_call" | custom-call | tf_op jit(solution)/shard_map/later_spread/pallas_call | solution.py:58
  36.3 0.4 collective-permute-start.11
  36.6 0.1 later_far.1
  36.7 1.8 %collective-permute-start.12 = (f32[32,2048]{1,0:T(8,128)S(1)}, f32[32,2048]{1,0:T(8,128)S(1)}, u32[]{:S(2)}, u32[]{:S(2)}) collective-permute-start(f32[32,2048]{1,0:T(8,128)S(1)} %get-tuple-element.115.d_ref.d_o_ref), channel_id=1, source_target_pairs={{0,16},{8,24},{16,0},{24,8},{1,17},{9,25},{17,1},{25,9},{2,18},{10... | collective-permute-start | bytes 786440 | tf_op jit(solution)/shard_map/ppermute | solution.py:37
  38.5 2.0 %collective-permute-done.11.tail_ref = f32[4,2048]{1,0:T(4,128)S(1)} collective-permute-done((f32[4,2048]{1,0:T(4,128)S(1)}, f32[4,2048]{1,0:T(4,128)S(1)}, u32[]{:S(2)}, u32[]{:S(2)}) %collective-permute-start.11) | collective-permute-done | bytes 32800 | tf_op jit(solution)/shard_map/ppermute | solution.py:37
  40.5 0.5 later_finish.1
  41.0 9.5 %all_to_all.22 = f32[32,1,128]{2,1,0:T(1,128)S(1)} all-to-all(f32[32,1,128]{2,1,0:T(1,128)S(1)} %bitcast.11), channel_id=1, replica_groups=mesh['band'=4,'tile'=8] {'band','tile'}, dimensions={0} | all-to-all | bytes 32768 | tf_op jit(solution)/shard_map/all_to_all | solution.py:51
  50.6 1.2 %step.1 = (f32[32,2048]{1,0:T(8,128)S(1)}, f32[3,32,2048]{2,1,0:T(8,128)S(1)}, f32[136,2048]{1,0:T(8,128)S(1)}, f32[8,2048]{1,0:T(8,128)S(1)}, f32[8,128]{1,0:T(...) custom-call(f32[32,128]{1,0:T(8,128)S(1)} %bitcast.8, ...), custom_call_target="tpu_custom_call" | custom-call | flops 10000000000 | bytes 10000000 | tf_op jit(solution)/shard_map/step/pallas_call | solution.py:58
  51.8 0.1 collective-permute-start.13
  51.9 0.6 collective-permute-start.15
  52.5 0.3 collective-permute-start.14
  52.9 6.1 %collective-permute-done.14.cross_ref = f32[8,2048]{1,0:T(8,128)S(1)} collective-permute-done((f32[8,2048]{1,0:T(8,128)S(1)}, f32[8,2048]{1,0:T(8,128)S(1)}, u32[]{:S(2)}, u32[]{:S(2)}) %collective-permute-start.14) | collective-permute-done | bytes 65568 | tf_op jit(solution)/shard_map/ppermute | solution.py:47
  58.9 1.7 %earlier_spread.1 = (f32[3,32,2048]{2,1,0:T(8,128)S(1)}, f32[32,2048]{1,0:T(8,128)S(1)}, f32[16,128]{1,0:T(8,128)S(1)}, f32[4,2048]{1,0:T(4,128)S(1)}, f32[8,2048]{1,0:T(8,128)S(1)}, /*index=5*/f32[8,128]{1,0:T(8,128)S(1)}) custom-call(f32[32,2048]{1,0:T(8,128)S(1)} %get-tuple-element.129.u_o_ref, f32[3,32,2048]{2,1,0:T(8,128)S(1)} %get-tuple-element.130.u_i_ref, ...), custom_call_target="tpu_custom_call" | custom-call | tf_op jit(solution)/shard_map/earlier_spread/pallas_call | solution.py:58
  60.6 1.5 %collective-permute-start.16 = (f32[4,2048]{1,0:T(4,128)S(1)}, f32[4,2048]{1,0:T(4,128)S(1)}, u32[]{:S(2)}, u32[]{:S(2)}) collective-permute-start(f32[4,2048]{1,0:T(4,128)S(1)} %get-tuple-element.140.own_tail_ref), channel_id=1, source_target_pairs={{0,16},{8,24},{16,0},{24,8},{1,17},{9,25},{17,1},{25,9},{2,18},{10... | collective-permute-start | bytes 98312 | tf_op jit(solution)/shard_map/ppermute | solution.py:37
  62.1 1.0 %later_out.1._ = f32[2,2,64,2048]{3,2,1,0:T(8,128)} custom-call(f32[2,32,2048]{2,1,0:T(8,128)S(1)} %get-tuple-element.134.x_mine_ref, f32[136,2048]{1,0:T(8,128)S(1)} %collective-permute-done.13.core_ref.got_ref), custom_call_target="tpu_custom_call" | custom-call | tf_op jit(solution)/shard_map/later_out/pallas_call | solution.py:58
  63.1 0.7 collective-permute-done.15.got_ref
  63.8 0.1 earlier_far.1
  63.9 0.1 give.1
  64.0 0.1 collective-permute-start.17
  64.0 0.5 collective-permute-done.16.tail_ref
  64.6 0.5 earlier_finish.1
  65.0 8.8 %all_to_all.23 = f32[32,1,128]{2,1,0:T(1,128)S(1)} all-to-all(f32[32,1,128]{2,1,0:T(1,128)S(1)} %bitcast.9), channel_id=1, replica_groups=mesh['band'=4,'tile'=8] {'band','tile'}, dimensions={0} | all-to-all | bytes 32768 | tf_op jit(solution)/shard_map/all_to_all | solution.py:51
  73.8 1.2 %last.1 = f32[2,2,64,2048]{3,2,1,0:T(8,128)} custom-call(f32[2,2,64,2048]{3,2,1,0:T(8,128)} %later_out.1._, f32[32,128]{1,0:T(8,128)S(1)} %bitcast.10, f32[2,32,2048]{2,1,0:T(8,128)S(1)} %get-tuple-element.134.x_mine_ref, f32[2,32,2048]{2,1,0:T(8,128)S(1)} %get-tuple-element.146.z_mine_ref, ...), custom_call_target="tpu_custom_call", output_to_operand_aliasing={{}: (0, {})} | custom-call | flops 10000000000 | bytes 10000000 | tf_op jit(solution)/shard_map/last/pallas_call | solution.py:58
  (6 shorter events, 0.0 us)
Async XLA Ops:
  3.8 2.3 %collective-permute-start = (f32[88,2048]{1,0:T(8,128)S(1)}, f32[88,2048]{1,0:T(8,128)S(1)}, u32[]{:S(2)}, u32[]{:S(2)}) collective-permute-start(f32[88,2048]{1,0:T(8,128)S(1)} %get-tuple-element.78), channel_id=1, source_target_pairs={{0,8},{8,0},{16,24},{24,16},{1,9},{9,1},{17,25},{25,17},{2,10},{10... | collective-permute-start | bytes 2162696 | tf_op jit(solution)/shard_map/ppermute | solution.py:32
  6.1 9.5 %collective-permute-start.1 = (f32[14,32,2048]{2,1,0:T(8,128)S(1)}, f32[14,32,2048]{2,1,0:T(8,128)S(1)}, u32[]{:S(2)}, u32[]{:S(2)}) collective-permute-start(f32[14,32,2048]{2,1,0:T(8,128)S(1)} %get-tuple-element.80), channel_id=1, source_target_pairs={{0,8},{8,0},{16,24},{24,16},{1,9},{9,1},{17,25},{25,17},{2,10},{10... | collective-permute-start | bytes 11010056 | tf_op jit(solution)/shard_map/ppermute | solution.py:32
  6.6 10.1 %collective-permute-start.3 = (f32[32,2048]{1,0:T(8,128)S(1)}, f32[32,2048]{1,0:T(8,128)S(1)}, u32[]{:S(2)}, u32[]{:S(2)}) collective-permute-start(f32[32,2048]{1,0:T(8,128)S(1)} %get-tuple-element.90), channel_id=1, source_target_pairs={{0,16},{8,24},{16,0},{24,8},{1,17},{9,25},{17,1},{25,9},{2,18},{10... | collective-permute-start | bytes 786440 | tf_op jit(solution)/shard_map/ppermute | solution.py:37
  9.3 6.0 %collective-permute-start.2 = (f32[4,2048]{1,0:T(4,128)S(1)}, f32[4,2048]{1,0:T(4,128)S(1)}, u32[]{:S(2)}, u32[]{:S(2)}) collective-permute-start(f32[4,2048]{1,0:T(4,128)S(1)} %get-tuple-element.86), channel_id=1, source_target_pairs={{0,15},{1,8},{2,9},{3,10},{4,11},{5,12},{6,13},{7,14},{8,1},{9,2},... | collective-permute-start | bytes 98312 | tf_op jit(solution)/shard_map/ppermute | solution.py:47
  15.3 10.5 %collective-permute-start.6 = (f32[48,2048]{1,0:T(8,128)S(1)}, f32[48,2048]{1,0:T(8,128)S(1)}, u32[]{:S(2)}, u32[]{:S(2)}) collective-permute-start(f32[48,2048]{1,0:T(8,128)S(1)} %get-tuple-element.101), channel_id=1, source_target_pairs={{0,16},{8,24},{16,0},{24,8},{1,17},{9,25},{17,1},{25,9},{2,18},{10... | collective-permute-start | bytes 1179656 | tf_op jit(solution)/shard_map/ppermute | solution.py:37
  17.0 5.9 %collective-permute-start.4 = (f32[20,2048]{1,0:T(8,128)S(1)}, f32[20,2048]{1,0:T(8,128)S(1)}, u32[]{:S(2)}, u32[]{:S(2)}) collective-permute-start(f32[20,2048]{1,0:T(8,128)S(1)} %get-tuple-element.97), channel_id=1, source_target_pairs={{0,8},{8,0},{16,24},{24,16},{1,9},{9,1},{17,25},{25,17},{2,10},{10... | collective-permute-start | bytes 491528 | tf_op jit(solution)/shard_map/ppermute | solution.py:32
  17.1 7.9 %collective-permute-start.5 = (f32[20,2048]{1,0:T(8,128)S(1)}, f32[20,2048]{1,0:T(8,128)S(1)}, u32[]{:S(2)}, u32[]{:S(2)}) collective-permute-start(f32[20,2048]{1,0:T(8,128)S(1)} %get-tuple-element.98), channel_id=1, source_target_pairs={{0,15},{1,8},{2,9},{3,10},{4,11},{5,12},{6,13},{7,14},{8,1},{9,2},... | collective-permute-start | bytes 491528 | tf_op jit(solution)/shard_map/ppermute | solution.py:47
  21.4 4.5 %collective-permute-start.7 = (f32[1,2048]{1,0:T(1,128)S(1)}, f32[1,2048]{1,0:T(1,128)S(1)}, u32[]{:S(2)}, u32[]{:S(2)}) collective-permute-start(f32[1,2048]{1,0:T(1,128)S(1)} %get-tuple-element.102), channel_id=1, source_target_pairs={{0,16},{8,24},{16,0},{24,8},{1,17},{9,25},{17,1},{25,9},{2,18},{10... | collective-permute-start | bytes 24584 | tf_op jit(solution)/shard_map/ppermute | solution.py:37
  26.3 10.3 %collective-permute-start.8 = (f32[48,2048]{1,0:T(8,128)S(1)}, f32[48,2048]{1,0:T(8,128)S(1)}, u32[]{:S(2)}, u32[]{:S(2)}) collective-permute-start(f32[48,2048]{1,0:T(8,128)S(1)} %get-tuple-element.108), channel_id=1, source_target_pairs={{0,16},{8,24},{16,0},{24,8},{1,17},{9,25},{17,1},{25,9},{2,18},{10... | collective-permute-start | bytes 1179656 | tf_op jit(solution)/shard_map/ppermute | solution.py:37
  28.1 3.7 %collective-permute-start.9 = (f32[8,2048]{1,0:T(8,128)S(1)}, f32[8,2048]{1,0:T(8,128)S(1)}, u32[]{:S(2)}, u32[]{:S(2)}) collective-permute-start(f32[8,2048]{1,0:T(8,128)S(1)} %get-tuple-element.109), channel_id=1, source_target_pairs={{0,8},{8,0},{16,24},{24,16},{1,9},{9,1},{17,25},{25,17},{2,10},{10... | collective-permute-start | bytes 196616 | tf_op jit(solution)/shard_map/ppermute | solution.py:32
  28.1 6.4 %collective-permute-start.10 = (f32[8,2048]{1,0:T(8,128)S(1)}, f32[8,2048]{1,0:T(8,128)S(1)}, u32[]{:S(2)}, u32[]{:S(2)}) collective-permute-start(f32[8,2048]{1,0:T(8,128)S(1)} %get-tuple-element.110), channel_id=1, source_target_pairs={{0,15},{1,8},{2,9},{3,10},{4,11},{5,12},{6,13},{7,14},{8,1},{9,2},... | collective-permute-start | bytes 196616 | tf_op jit(solution)/shard_map/ppermute | solution.py:47
  36.3 4.3 %collective-permute-start.11 = (f32[4,2048]{1,0:T(4,128)S(1)}, f32[4,2048]{1,0:T(4,128)S(1)}, u32[]{:S(2)}, u32[]{:S(2)}) collective-permute-start(f32[4,2048]{1,0:T(4,128)S(1)} %get-tuple-element.116.own_tail_ref), channel_id=1, source_target_pairs={{0,16},{8,24},{16,0},{24,8},{1,17},{9,25},{17,1},{25,9},{2,18},{10... | collective-permute-start | bytes 98312 | tf_op jit(solution)/shard_map/ppermute | solution.py:37
  36.7 13.9 %collective-permute-start.12 = (f32[32,2048]{1,0:T(8,128)S(1)}, f32[32,2048]{1,0:T(8,128)S(1)}, u32[]{:S(2)}, u32[]{:S(2)}) collective-permute-start(f32[32,2048]{1,0:T(8,128)S(1)} %get-tuple-element.115.d_ref.d_o_ref), channel_id=1, source_target_pairs={{0,16},{8,24},{16,0},{24,8},{1,17},{9,25},{17,1},{25,9},{2,18},{10... | collective-permute-start | bytes 786440 | tf_op jit(solution)/shard_map/ppermute | solution.py:37
  51.8 7.1 %collective-permute-start.13 = (f32[136,2048]{1,0:T(8,128)S(1)}, f32[136,2048]{1,0:T(8,128)S(1)}, u32[]{:S(2)}, u32[]{:S(2)}) collective-permute-start(f32[136,2048]{1,0:T(8,128)S(1)} %get-tuple-element.131), channel_id=1, source_target_pairs={{0,8},{8,0},{16,24},{24,16},{1,9},{9,1},{17,25},{25,17},{2,10},{10... | collective-permute-start | bytes 3342344 | tf_op jit(solution)/shard_map/ppermute | solution.py:32
  51.9 11.9 %collective-permute-start.15 = (f32[48,2048]{1,0:T(8,128)S(1)}, f32[48,2048]{1,0:T(8,128)S(1)}, u32[]{:S(2)}, u32[]{:S(2)}) collective-permute-start(f32[48,2048]{1,0:T(8,128)S(1)} %get-tuple-element.136), channel_id=1, source_target_pairs={{0,16},{8,24},{16,0},{24,8},{1,17},{9,25},{17,1},{25,9},{2,18},{10... | collective-permute-start | bytes 1179656 | tf_op jit(solution)/shard_map/ppermute | solution.py:37
  52.5 6.4 %collective-permute-start.14 = (f32[8,2048]{1,0:T(8,128)S(1)}, f32[8,2048]{1,0:T(8,128)S(1)}, u32[]{:S(2)}, u32[]{:S(2)}) collective-permute-start(f32[8,2048]{1,0:T(8,128)S(1)} %get-tuple-element.132), channel_id=1, source_target_pairs={{0,15},{1,8},{2,9},{3,10},{4,11},{5,12},{6,13},{7,14},{8,1},{9,2},... | collective-permute-start | bytes 196616 | tf_op jit(solution)/shard_map/ppermute | solution.py:47
  60.6 4.0 %collective-permute-start.16 = (f32[4,2048]{1,0:T(4,128)S(1)}, f32[4,2048]{1,0:T(4,128)S(1)}, u32[]{:S(2)}, u32[]{:S(2)}) collective-permute-start(f32[4,2048]{1,0:T(4,128)S(1)} %get-tuple-element.140.own_tail_ref), channel_id=1, source_target_pairs={{0,16},{8,24},{16,0},{24,8},{1,17},{9,25},{17,1},{25,9},{2,18},{10... | collective-permute-start | bytes 98312 | tf_op jit(solution)/shard_map/ppermute | solution.py:37
  64.0 9.9 %collective-permute-start.17 = (f32[64,2048]{1,0:T(8,128)S(1)}, f32[64,2048]{1,0:T(8,128)S(1)}, u32[]{:S(2)}, u32[]{:S(2)}) collective-permute-start(f32[64,2048]{1,0:T(8,128)S(1)} %get-tuple-element.148), channel_id=1, source_target_pairs={{0,8},{8,0},{16,24},{24,16},{1,9},{9,1},{17,25},{25,17},{2,10},{10... | collective-permute-start | bytes 1572872 | tf_op jit(solution)/shard_map/ppermute | solution.py:32

commit v8 on v7

--- a/solution.py
+++ b/solution.py
@@ -348,7 +348,8 @@
                 v = xs[j] - v
                 weighted = diag_i_ref[j - 1, rs, :] * xs[j] - weighted
             v_i_ref[j - 1, rs, :] = v
-            sums[0] = sums[0] + xs[j] * weighted
+            if diag_i_ref is not None:
+                sums[0] = sums[0] + xs[j] * weighted
             sums[1] = sums[1] + v * weighted
     sums_ref[0:ROWS, :] = fold(sums[0])
     sums_ref[ROWS : 2 * ROWS, :] = fold(sums[1])

time: 75.2 us -> 75.2 us (level)
  no operation moved by 1% of the time
where the time goes in v8:
time: 75.2 us; the launch traced here: 75 us
  starting transfers between devices  24.3 us (32%)
  blocking collectives  18.3 us (24%)
  waiting for transfers between devices  17.6 us (23%)
  Pallas kernels  14.6 us (19%)
    all_to_all x2, blocking collectives, all_total(): return lax.all_to_all(parts, AXES, 0, 0, tiled=True)  18.3 us
    pallas_call x16, Pallas kernels, call(): pl.pallas_call(body, out_shape=outs, in_specs=[pl.BlockSpec(memory_space=...  14.6 us
    ppermute x4, waiting for transfers between devices, cross_swap(): return lax.ppermute(x, AXES, pairs)  12.6 us
    ppermute x4, starting transfers between devices, cross_swap(): return lax.ppermute(x, AXES, pairs)  12.6 us
    ppermute x8, starting transfers between devices, outer_swap(): return lax.ppermute(x, 'band', [(b, b ^ 2) for b in range(nb)])  10.6 us
    ppermute x8, waiting for transfers between devices, outer_swap(): return lax.ppermute(x, 'band', [(b, b ^ 2) for b in range(nb)])  3.21 us
    ppermute x6, waiting for transfers between devices, core_swap(): return lax.ppermute(x, 'band', [(b, b ^ 1) for b in range(nb)])  1.83 us
  transfers between devices with their start and end apart: 18, of which 8 were waited for; matrix products, arithmetic and copies ran while one was open for 0% of the time, Pallas kernels for 11%

profile of v8, /device:TPU:0, one launch (start us, length us, event | category | flops | bytes accessed | tf_op | source)
XLA Modules:
  0.0 75.0 jit_solution(14490010215683230185)
XLA Ops:
  0.0 3.8 %load.1 = (f32[14,32,2048]{2,1,0:T(8,128)S(1)}, f32[14,32,2048]{2,1,0:T(8,128)S(1)}, f32[80,2048]{1,0:T(8,128)S(1)}, f32[88,2048]{1,0:T(8,128)S(1)}, f32[2,2048]{1,0:T(2,128)S(1)}, /*index=5*/f32[2,2048]{1,0:T(2,128)S(1)}) custom-call(f32[2,64,2048]{2,1,0:T(8,128)} %cond_x_ref.1, f32[2,64,2048]{2,1,0:T(8,128)} %cond_y_ref.1, f32[2,64,2048]{2,1,0:T(8,128)} %via_ref.1, ...), custom_call_target="tpu_custom_call" | custom-call | flops 10000000000 | bytes 10000000 | tf_op jit(solution)/shard_map/load/pallas_call | solution.py:58
  3.8 0.5 collective-permute-start
  4.3 1.8 %collective-permute-done.got_ref.more_ref = f32[88,2048]{1,0:T(8,128)S(1)} collective-permute-done((f32[88,2048]{1,0:T(8,128)S(1)}, f32[88,2048]{1,0:T(8,128)S(1)}, u32[]{:S(2)}, u32[]{:S(2)}) %collective-permute-start) | collective-permute-done | bytes 720928 | tf_op jit(solution)/shard_map/ppermute | solution.py:32
  6.1 0.4 collective-permute-start.1
  6.5 0.1 pay.1
  6.6 2.7 %collective-permute-start.3 = (f32[32,2048]{1,0:T(8,128)S(1)}, f32[32,2048]{1,0:T(8,128)S(1)}, u32[]{:S(2)}, u32[]{:S(2)}) collective-permute-start(f32[32,2048]{1,0:T(8,128)S(1)} %get-tuple-element.90), channel_id=1, source_target_pairs={{0,16},{8,24},{16,0},{24,8},{1,17},{9,25},{17,1},{25,9},{2,18},{10... | collective-permute-start | bytes 786440 | tf_op jit(solution)/shard_map/ppermute | solution.py:37
  9.3 4.2 %collective-permute-start.2 = (f32[4,2048]{1,0:T(4,128)S(1)}, f32[4,2048]{1,0:T(4,128)S(1)}, u32[]{:S(2)}, u32[]{:S(2)}) collective-permute-start(f32[4,2048]{1,0:T(4,128)S(1)} %get-tuple-element.86), channel_id=1, source_target_pairs={{0,15},{1,8},{2,9},{3,10},{4,11},{5,12},{6,13},{7,14},{8,1},{9,2},... | collective-permute-start | bytes 98312 | tf_op jit(solution)/shard_map/ppermute | solution.py:47
  13.5 1.8 %collective-permute-done.2.last_ref = f32[4,2048]{1,0:T(4,128)S(1)} collective-permute-done((f32[4,2048]{1,0:T(4,128)S(1)}, f32[4,2048]{1,0:T(4,128)S(1)}, u32[]{:S(2)}, u32[]{:S(2)}) %collective-permute-start.2) | collective-permute-done | bytes 32800 | tf_op jit(solution)/shard_map/ppermute | solution.py:47
  15.3 0.3 collective-permute-start.6
  15.6 0.0 collective-permute-done.1.got_ref
  15.6 1.0 %prepare.1 = (f32[4,32,2048]{2,1,0:T(8,128)S(1)}, f32[4,32,2048]{2,1,0:T(8,128)S(1)}, f32[4,32,2048]{2,1,0:T(8,128)S(1)}, f32[3,32,2048]{2,1,0:T(8,128)S(1)}, f3...) custom-call(f32[14,32,2048]{2,1,0:T(8,128)S(1)} %get-tuple-element.7, ...), custom_call_target="tpu_custom_call" | custom-call | tf_op jit(solution)/shard_map/prepare/pallas_call | solution.py:58
  16.7 0.3 outer.1
  17.0 0.1 collective-permute-start.4
  17.1 4.3 %collective-permute-start.5 = (f32[20,2048]{1,0:T(8,128)S(1)}, f32[20,2048]{1,0:T(8,128)S(1)}, u32[]{:S(2)}, u32[]{:S(2)}) collective-permute-start(f32[20,2048]{1,0:T(8,128)S(1)} %get-tuple-element.98), channel_id=1, source_target_pairs={{0,15},{1,8},{2,9},{3,10},{4,11},{5,12},{6,13},{7,14},{8,1},{9,2},... | collective-permute-start | bytes 491528 | tf_op jit(solution)/shard_map/ppermute | solution.py:47
  21.4 1.5 %collective-permute-start.7 = (f32[1,2048]{1,0:T(1,128)S(1)}, f32[1,2048]{1,0:T(1,128)S(1)}, u32[]{:S(2)}, u32[]{:S(2)}) collective-permute-start(f32[1,2048]{1,0:T(1,128)S(1)} %get-tuple-element.102), channel_id=1, source_target_pairs={{0,16},{8,24},{16,0},{24,8},{1,17},{9,25},{17,1},{25,9},{2,18},{10... | collective-permute-start | bytes 24584 | tf_op jit(solution)/shard_map/ppermute | solution.py:37
  22.9 0.0 collective-permute-done.4.core_ref.side_core_ref
  22.9 2.1 %collective-permute-done.5.cross_ref.side_cross_ref = f32[20,2048]{1,0:T(8,128)S(1)} collective-permute-done((f32[20,2048]{1,0:T(8,128)S(1)}, f32[20,2048]{1,0:T(8,128)S(1)}, u32[]{:S(2)}, u32[]{:S(2)}) %collective-permute-start.5) | collective-permute-done | bytes 163872 | tf_op jit(solution)/shard_map/ppermute | solution.py:47
  25.0 0.8 %first_spread.1 = (f32[3,32,2048]{2,1,0:T(8,128)S(1)}, f32[32,2048]{1,0:T(8,128)S(1)}, f32[16,128]{1,0:T(8,128)S(1)}) custom-call(f32[32,2048]{1,0:T(8,128)S(1)} %get-tuple-element.96.u_o_ref.s_o_ref, f32[3,32,2048]{2,1,0:T(8,128)S(1)} %get-tuple-element.95.s_i_ref.u_i_ref, f32[20,2048]{1,0:T(8,128)S(1)} %collective-permute-done.4.core_ref.side_core_ref, ...), custom_call_target="tpu_custom_call" | custom-call | tf_op jit(solution)/shard_map/first_spread/pallas_call | solution.py:58
  25.8 0.0 collective-permute-done.6.more_ref
  25.8 0.4 first_far.1
  26.2 1.8 %collective-permute-start.8 = (f32[48,2048]{1,0:T(8,128)S(1)}, f32[48,2048]{1,0:T(8,128)S(1)}, u32[]{:S(2)}, u32[]{:S(2)}) collective-permute-start(f32[48,2048]{1,0:T(8,128)S(1)} %get-tuple-element.108), channel_id=1, source_target_pairs={{0,16},{8,24},{16,0},{24,8},{1,17},{9,25},{17,1},{25,9},{2,18},{10... | collective-permute-start | bytes 1179656 | tf_op jit(solution)/shard_map/ppermute | solution.py:37
  28.0 0.0 collective-permute-start.9
  28.0 3.7 %collective-permute-start.10 = (f32[8,2048]{1,0:T(8,128)S(1)}, f32[8,2048]{1,0:T(8,128)S(1)}, u32[]{:S(2)}, u32[]{:S(2)}) collective-permute-start(f32[8,2048]{1,0:T(8,128)S(1)} %get-tuple-element.110), channel_id=1, source_target_pairs={{0,15},{1,8},{2,9},{3,10},{4,11},{5,12},{6,13},{7,14},{8,1},{9,2},... | collective-permute-start | bytes 196616 | tf_op jit(solution)/shard_map/ppermute | solution.py:47
  31.8 2.7 %collective-permute-done.10.cross_ref = f32[8,2048]{1,0:T(8,128)S(1)} collective-permute-done((f32[8,2048]{1,0:T(8,128)S(1)}, f32[8,2048]{1,0:T(8,128)S(1)}, u32[]{:S(2)}, u32[]{:S(2)}) %collective-permute-start.10) | collective-permute-done | bytes 65568 | tf_op jit(solution)/shard_map/ppermute | solution.py:47
  34.4 1.8 %later_spread.1 = (f32[3,32,2048]{2,1,0:T(8,128)S(1)}, f32[32,2048]{1,0:T(8,128)S(1)}, f32[16,128]{1,0:T(8,128)S(1)}, f32[4,2048]{1,0:T(4,128)S(1)}, f32[8,2048]...) custom-call(f32[32,2048]{1,0:T(8,128)S(1)} %get-tuple-element.107.u_o_ref.v1_o_ref, ...), custom_call_target="tpu_custom_call" | custom-call | tf_op jit(solution)/shard_map/later_spread/pallas_call | solution.py:58
  36.2 0.4 collective-permute-start.11
  36.6 0.0 collective-permute-done.8.got_ref
  36.6 0.1 later_far.1
  36.7 1.8 %collective-permute-start.12 = (f32[32,2048]{1,0:T(8,128)S(1)}, f32[32,2048]{1,0:T(8,128)S(1)}, u32[]{:S(2)}, u32[]{:S(2)}) collective-permute-start(f32[32,2048]{1,0:T(8,128)S(1)} %get-tuple-element.115.d_ref.d_o_ref), channel_id=1, source_target_pairs={{0,16},{8,24},{16,0},{24,8},{1,17},{9,25},{17,1},{25,9},{2,18},{10... | collective-permute-start | bytes 786440 | tf_op jit(solution)/shard_map/ppermute | solution.py:37
  38.5 2.0 %collective-permute-done.11.tail_ref = f32[4,2048]{1,0:T(4,128)S(1)} collective-permute-done((f32[4,2048]{1,0:T(4,128)S(1)}, f32[4,2048]{1,0:T(4,128)S(1)}, u32[]{:S(2)}, u32[]{:S(2)}) %collective-permute-start.11) | collective-permute-done | bytes 32800 | tf_op jit(solution)/shard_map/ppermute | solution.py:37
  40.5 0.5 later_finish.1
  41.0 9.5 %all_to_all.22 = f32[32,1,128]{2,1,0:T(1,128)S(1)} all-to-all(f32[32,1,128]{2,1,0:T(1,128)S(1)} %bitcast.11), channel_id=1, replica_groups=mesh['band'=4,'tile'=8] {'band','tile'}, dimensions={0} | all-to-all | bytes 32768 | tf_op jit(solution)/shard_map/all_to_all | solution.py:51
  50.5 1.2 %step.1 = (f32[32,2048]{1,0:T(8,128)S(1)}, f32[3,32,2048]{2,1,0:T(8,128)S(1)}, f32[136,2048]{1,0:T(8,128)S(1)}, f32[8,2048]{1,0:T(8,128)S(1)}, f32[8,128]{1,0:T(...) custom-call(f32[32,128]{1,0:T(8,128)S(1)} %bitcast.8, ...), custom_call_target="tpu_custom_call" | custom-call | flops 10000000000 | bytes 10000000 | tf_op jit(solution)/shard_map/step/pallas_call | solution.py:58
  51.7 0.1 collective-permute-start.13
  51.8 0.6 collective-permute-start.15
  52.5 0.3 collective-permute-start.14
  52.8 6.1 %collective-permute-done.14.cross_ref = f32[8,2048]{1,0:T(8,128)S(1)} collective-permute-done((f32[8,2048]{1,0:T(8,128)S(1)}, f32[8,2048]{1,0:T(8,128)S(1)}, u32[]{:S(2)}, u32[]{:S(2)}) %collective-permute-start.14) | collective-permute-done | bytes 65568 | tf_op jit(solution)/shard_map/ppermute | solution.py:47
  58.9 1.7 %earlier_spread.1 = (f32[3,32,2048]{2,1,0:T(8,128)S(1)}, f32[32,2048]{1,0:T(8,128)S(1)}, f32[16,128]{1,0:T(8,128)S(1)}, f32[4,2048]{1,0:T(4,128)S(1)}, f32[8,2048]{1,0:T(8,128)S(1)}, /*index=5*/f32[8,128]{1,0:T(8,128)S(1)}) custom-call(f32[32,2048]{1,0:T(8,128)S(1)} %get-tuple-element.129.u_o_ref, f32[3,32,2048]{2,1,0:T(8,128)S(1)} %get-tuple-element.130.u_i_ref, ...), custom_call_target="tpu_custom_call" | custom-call | tf_op jit(solution)/shard_map/earlier_spread/pallas_call | solution.py:58
  60.5 1.5 %collective-permute-start.16 = (f32[4,2048]{1,0:T(4,128)S(1)}, f32[4,2048]{1,0:T(4,128)S(1)}, u32[]{:S(2)}, u32[]{:S(2)}) collective-permute-start(f32[4,2048]{1,0:T(4,128)S(1)} %get-tuple-element.140.own_tail_ref), channel_id=1, source_target_pairs={{0,16},{8,24},{16,0},{24,8},{1,17},{9,25},{17,1},{25,9},{2,18},{10... | collective-permute-start | bytes 98312 | tf_op jit(solution)/shard_map/ppermute | solution.py:37
  62.1 1.0 %later_out.1._ = f32[2,2,64,2048]{3,2,1,0:T(8,128)} custom-call(f32[2,32,2048]{2,1,0:T(8,128)S(1)} %get-tuple-element.134.x_mine_ref, f32[136,2048]{1,0:T(8,128)S(1)} %collective-permute-done.13.core_ref.got_ref), custom_call_target="tpu_custom_call" | custom-call | tf_op jit(solution)/shard_map/later_out/pallas_call | solution.py:58
  63.1 0.7 collective-permute-done.15.got_ref
  63.7 0.1 earlier_far.1
  63.8 0.1 give.1
  63.9 0.1 collective-permute-start.17
  64.0 0.5 collective-permute-done.16.tail_ref
  64.5 0.5 earlier_finish.1
  65.0 8.8 %all_to_all.23 = f32[32,1,128]{2,1,0:T(1,128)S(1)} all-to-all(f32[32,1,128]{2,1,0:T(1,128)S(1)} %bitcast.9), channel_id=1, replica_groups=mesh['band'=4,'tile'=8] {'band','tile'}, dimensions={0} | all-to-all | bytes 32768 | tf_op jit(solution)/shard_map/all_to_all | solution.py:51
  73.8 1.2 %last.1 = f32[2,2,64,2048]{3,2,1,0:T(8,128)} custom-call(f32[2,2,64,2048]{3,2,1,0:T(8,128)} %later_out.1._, f32[32,128]{1,0:T(8,128)S(1)} %bitcast.10, f32[2,32,2048]{2,1,0:T(8,128)S(1)} %get-tuple-element.134.x_mine_ref, f32[2,32,2048]{2,1,0:T(8,128)S(1)} %get-tuple-element.146.z_mine_ref, ...), custom_call_target="tpu_custom_call", output_to_operand_aliasing={{}: (0, {})} | custom-call | flops 10000000000 | bytes 10000000 | tf_op jit(solution)/shard_map/last/pallas_call | solution.py:58
  (6 shorter events, 0.0 us)
Async XLA Ops:
  3.8 2.3 %collective-permute-start = (f32[88,2048]{1,0:T(8,128)S(1)}, f32[88,2048]{1,0:T(8,128)S(1)}, u32[]{:S(2)}, u32[]{:S(2)}) collective-permute-start(f32[88,2048]{1,0:T(8,128)S(1)} %get-tuple-element.78), channel_id=1, source_target_pairs={{0,8},{8,0},{16,24},{24,16},{1,9},{9,1},{17,25},{25,17},{2,10},{10... | collective-permute-start | bytes 2162696 | tf_op jit(solution)/shard_map/ppermute | solution.py:32
  6.1 9.5 %collective-permute-start.1 = (f32[14,32,2048]{2,1,0:T(8,128)S(1)}, f32[14,32,2048]{2,1,0:T(8,128)S(1)}, u32[]{:S(2)}, u32[]{:S(2)}) collective-permute-start(f32[14,32,2048]{2,1,0:T(8,128)S(1)} %get-tuple-element.80), channel_id=1, source_target_pairs={{0,8},{8,0},{16,24},{24,16},{1,9},{9,1},{17,25},{25,17},{2,10},{10... | collective-permute-start | bytes 11010056 | tf_op jit(solution)/shard_map/ppermute | solution.py:32
  6.6 10.1 %collective-permute-start.3 = (f32[32,2048]{1,0:T(8,128)S(1)}, f32[32,2048]{1,0:T(8,128)S(1)}, u32[]{:S(2)}, u32[]{:S(2)}) collective-permute-start(f32[32,2048]{1,0:T(8,128)S(1)} %get-tuple-element.90), channel_id=1, source_target_pairs={{0,16},{8,24},{16,0},{24,8},{1,17},{9,25},{17,1},{25,9},{2,18},{10... | collective-permute-start | bytes 786440 | tf_op jit(solution)/shard_map/ppermute | solution.py:37
  9.3 6.0 %collective-permute-start.2 = (f32[4,2048]{1,0:T(4,128)S(1)}, f32[4,2048]{1,0:T(4,128)S(1)}, u32[]{:S(2)}, u32[]{:S(2)}) collective-permute-start(f32[4,2048]{1,0:T(4,128)S(1)} %get-tuple-element.86), channel_id=1, source_target_pairs={{0,15},{1,8},{2,9},{3,10},{4,11},{5,12},{6,13},{7,14},{8,1},{9,2},... | collective-permute-start | bytes 98312 | tf_op jit(solution)/shard_map/ppermute | solution.py:47
  15.3 10.5 %collective-permute-start.6 = (f32[48,2048]{1,0:T(8,128)S(1)}, f32[48,2048]{1,0:T(8,128)S(1)}, u32[]{:S(2)}, u32[]{:S(2)}) collective-permute-start(f32[48,2048]{1,0:T(8,128)S(1)} %get-tuple-element.101), channel_id=1, source_target_pairs={{0,16},{8,24},{16,0},{24,8},{1,17},{9,25},{17,1},{25,9},{2,18},{10... | collective-permute-start | bytes 1179656 | tf_op jit(solution)/shard_map/ppermute | solution.py:37
  17.0 5.9 %collective-permute-start.4 = (f32[20,2048]{1,0:T(8,128)S(1)}, f32[20,2048]{1,0:T(8,128)S(1)}, u32[]{:S(2)}, u32[]{:S(2)}) collective-permute-start(f32[20,2048]{1,0:T(8,128)S(1)} %get-tuple-element.97), channel_id=1, source_target_pairs={{0,8},{8,0},{16,24},{24,16},{1,9},{9,1},{17,25},{25,17},{2,10},{10... | collective-permute-start | bytes 491528 | tf_op jit(solution)/shard_map/ppermute | solution.py:32
  17.1 7.9 %collective-permute-start.5 = (f32[20,2048]{1,0:T(8,128)S(1)}, f32[20,2048]{1,0:T(8,128)S(1)}, u32[]{:S(2)}, u32[]{:S(2)}) collective-permute-start(f32[20,2048]{1,0:T(8,128)S(1)} %get-tuple-element.98), channel_id=1, source_target_pairs={{0,15},{1,8},{2,9},{3,10},{4,11},{5,12},{6,13},{7,14},{8,1},{9,2},... | collective-permute-start | bytes 491528 | tf_op jit(solution)/shard_map/ppermute | solution.py:47
  21.4 4.4 %collective-permute-start.7 = (f32[1,2048]{1,0:T(1,128)S(1)}, f32[1,2048]{1,0:T(1,128)S(1)}, u32[]{:S(2)}, u32[]{:S(2)}) collective-permute-start(f32[1,2048]{1,0:T(1,128)S(1)} %get-tuple-element.102), channel_id=1, source_target_pairs={{0,16},{8,24},{16,0},{24,8},{1,17},{9,25},{17,1},{25,9},{2,18},{10... | collective-permute-start | bytes 24584 | tf_op jit(solution)/shard_map/ppermute | solution.py:37
  26.2 10.3 %collective-permute-start.8 = (f32[48,2048]{1,0:T(8,128)S(1)}, f32[48,2048]{1,0:T(8,128)S(1)}, u32[]{:S(2)}, u32[]{:S(2)}) collective-permute-start(f32[48,2048]{1,0:T(8,128)S(1)} %get-tuple-element.108), channel_id=1, source_target_pairs={{0,16},{8,24},{16,0},{24,8},{1,17},{9,25},{17,1},{25,9},{2,18},{10... | collective-permute-start | bytes 1179656 | tf_op jit(solution)/shard_map/ppermute | solution.py:37
  28.0 3.7 %collective-permute-start.9 = (f32[8,2048]{1,0:T(8,128)S(1)}, f32[8,2048]{1,0:T(8,128)S(1)}, u32[]{:S(2)}, u32[]{:S(2)}) collective-permute-start(f32[8,2048]{1,0:T(8,128)S(1)} %get-tuple-element.109), channel_id=1, source_target_pairs={{0,8},{8,0},{16,24},{24,16},{1,9},{9,1},{17,25},{25,17},{2,10},{10... | collective-permute-start | bytes 196616 | tf_op jit(solution)/shard_map/ppermute | solution.py:32
  28.0 6.4 %collective-permute-start.10 = (f32[8,2048]{1,0:T(8,128)S(1)}, f32[8,2048]{1,0:T(8,128)S(1)}, u32[]{:S(2)}, u32[]{:S(2)}) collective-permute-start(f32[8,2048]{1,0:T(8,128)S(1)} %get-tuple-element.110), channel_id=1, source_target_pairs={{0,15},{1,8},{2,9},{3,10},{4,11},{5,12},{6,13},{7,14},{8,1},{9,2},... | collective-permute-start | bytes 196616 | tf_op jit(solution)/shard_map/ppermute | solution.py:47
  36.2 4.3 %collective-permute-start.11 = (f32[4,2048]{1,0:T(4,128)S(1)}, f32[4,2048]{1,0:T(4,128)S(1)}, u32[]{:S(2)}, u32[]{:S(2)}) collective-permute-start(f32[4,2048]{1,0:T(4,128)S(1)} %get-tuple-element.116.own_tail_ref), channel_id=1, source_target_pairs={{0,16},{8,24},{16,0},{24,8},{1,17},{9,25},{17,1},{25,9},{2,18},{10... | collective-permute-start | bytes 98312 | tf_op jit(solution)/shard_map/ppermute | solution.py:37
  36.7 13.9 %collective-permute-start.12 = (f32[32,2048]{1,0:T(8,128)S(1)}, f32[32,2048]{1,0:T(8,128)S(1)}, u32[]{:S(2)}, u32[]{:S(2)}) collective-permute-start(f32[32,2048]{1,0:T(8,128)S(1)} %get-tuple-element.115.d_ref.d_o_ref), channel_id=1, source_target_pairs={{0,16},{8,24},{16,0},{24,8},{1,17},{9,25},{17,1},{25,9},{2,18},{10... | collective-permute-start | bytes 786440 | tf_op jit(solution)/shard_map/ppermute | solution.py:37
  51.7 7.1 %collective-permute-start.13 = (f32[136,2048]{1,0:T(8,128)S(1)}, f32[136,2048]{1,0:T(8,128)S(1)}, u32[]{:S(2)}, u32[]{:S(2)}) collective-permute-start(f32[136,2048]{1,0:T(8,128)S(1)} %get-tuple-element.131), channel_id=1, source_target_pairs={{0,8},{8,0},{16,24},{24,16},{1,9},{9,1},{17,25},{25,17},{2,10},{10... | collective-permute-start | bytes 3342344 | tf_op jit(solution)/shard_map/ppermute | solution.py:32
  51.8 11.9 %collective-permute-start.15 = (f32[48,2048]{1,0:T(8,128)S(1)}, f32[48,2048]{1,0:T(8,128)S(1)}, u32[]{:S(2)}, u32[]{:S(2)}) collective-permute-start(f32[48,2048]{1,0:T(8,128)S(1)} %get-tuple-element.136), channel_id=1, source_target_pairs={{0,16},{8,24},{16,0},{24,8},{1,17},{9,25},{17,1},{25,9},{2,18},{10... | collective-permute-start | bytes 1179656 | tf_op jit(solution)/shard_map/ppermute | solution.py:37
  52.5 6.4 %collective-permute-start.14 = (f32[8,2048]{1,0:T(8,128)S(1)}, f32[8,2048]{1,0:T(8,128)S(1)}, u32[]{:S(2)}, u32[]{:S(2)}) collective-permute-start(f32[8,2048]{1,0:T(8,128)S(1)} %get-tuple-element.132), channel_id=1, source_target_pairs={{0,15},{1,8},{2,9},{3,10},{4,11},{5,12},{6,13},{7,14},{8,1},{9,2},... | collective-permute-start | bytes 196616 | tf_op jit(solution)/shard_map/ppermute | solution.py:47
  60.5 4.0 %collective-permute-start.16 = (f32[4,2048]{1,0:T(4,128)S(1)}, f32[4,2048]{1,0:T(4,128)S(1)}, u32[]{:S(2)}, u32[]{:S(2)}) collective-permute-start(f32[4,2048]{1,0:T(4,128)S(1)} %get-tuple-element.140.own_tail_ref), channel_id=1, source_target_pairs={{0,16},{8,24},{16,0},{24,8},{1,17},{9,25},{17,1},{25,9},{2,18},{10... | collective-permute-start | bytes 98312 | tf_op jit(solution)/shard_map/ppermute | solution.py:37
  63.9 9.9 %collective-permute-start.17 = (f32[64,2048]{1,0:T(8,128)S(1)}, f32[64,2048]{1,0:T(8,128)S(1)}, u32[]{:S(2)}, u32[]{:S(2)}) collective-permute-start(f32[64,2048]{1,0:T(8,128)S(1)} %get-tuple-element.148), channel_id=1, source_target_pairs={{0,8},{8,0},{16,24},{24,16},{1,9},{9,1},{17,25},{25,17},{2,10},{10... | collective-permute-start | bytes 1572872 | tf_op jit(solution)/shard_map/ppermute | solution.py:32
